TPU v7x, 32 devices: a whole 2x2x4 slice. The times are simulated.
32 devices in a mesh: fsdp: 8 (over y, x, core), tp: 4 (over z).
Axes of the slice: x: 2, y: 2, z: 4, core: 2. Of those that a mesh axis runs over, the one named last changes fastest.
Arguments:
- image_tokens: bfloat16 [16, 1024, 1536], P('fsdp', 'tp'), may hold values from -6 to 6
- text_tokens: bfloat16 [1280, 1536], P(('fsdp', 'tp')), may hold values from -6 to 6
- conditioning: float32 [16, 1536], P('fsdp'), may hold values from -6 to 6
- text_lengths: int32 [8, 2], P('fsdp'), may hold values from 1 to 154, as said below
- adapter_index: int32 [16], P('fsdp'), may hold values from 0 to 7
- adapters: float32 [4, 2260992], P('tp', 'fsdp'), may hold values from -0.24 to 0.24
- mod_weight: bfloat16 [2, 1536, 9216], P(None, 'fsdp', 'tp'), may hold values from -0.15625 to 0.15625
- qkv_weight: bfloat16 [2, 1536, 4608], P(None, 'fsdp', 'tp'), may hold values from -0.15625 to 0.15625
- out_weight: bfloat16 [2, 1536, 1536], P(None, 'tp', 'fsdp'), may hold values from -0.4375 to 0.4375
- fc1_weight: bfloat16 [2, 1536, 6144], P(None, 'fsdp', 'tp'), may hold values from -0.15625 to 0.15625
- fc2_weight: bfloat16 [2, 6144, 1536], P(None, 'tp', 'fsdp'), may hold values from -0.109375 to 0.109375
- image_cot: bfloat16 [16, 1024, 1536], P('fsdp', 'tp'), may hold values from -6 to 6
- text_cot: bfloat16 [1280, 1536], P(('fsdp', 'tp')), may hold values from -6 to 6
Outputs:
- image_out: bfloat16 [16, 1024, 1536], P('fsdp', 'tp')
- text_out: bfloat16 [1280, 1536], P(('fsdp', 'tp'))
- image_grad: float32 [16, 1024, 1536], P('fsdp', 'tp')
- text_grad: float32 [1280, 1536], P(('fsdp', 'tp'))
- cond_grad: float32 [16, 1536], P('fsdp')
- adapter_grad: float32 [4, 2260992], P('tp', 'fsdp')
Inputs may be any that keep to these rules, and one draw needn't show every extreme that they name: `text_lengths`: each group's 2 lengths sum to 160, and its largest is exactly 154.
All inputs are finite; a program needn't handle non-finite values.
Results may differ from a plain program's by a relative error of at most 0.015.
The roundings to bfloat16 on the way count: a program that leaves them out, or rounds other values in their place, can miss the bound.
Values may be sent and summed in bfloat16 or wider, within the bound.
A program may use at most 384 MiB of HBM per device.

v0:
```python
import jax
import jax.numpy as jnp
from jax import lax
from jax.sharding import PartitionSpec as P

HD = 64
FF = 6144
NAD = 8
RANK = 16


EPS = 1e-06
HIGH = lax.Precision.HIGHEST


def matmul(left, right):
    return jnp.dot(left, right, preferred_element_type=jnp.float32)


def exact(left, right):
    return jnp.dot(left, right, precision=HIGH, preferred_element_type=jnp.float32)


def inner_left(left, right):
    return lax.dot_general(
        left, right, (((0,), (0,)), ((), ())), preferred_element_type=jnp.float32
    )


def inner_right(left, right):
    return lax.dot_general(
        left,
        right,
        (((left.ndim - 1,), (right.ndim - 1,)), ((), ())),
        preferred_element_type=jnp.float32,
    )


def unpack(grid, model_width, hidden_width, rank_cols):
    parts = grid.shape[0]
    shapes = [
        (model_width, 6 * model_width),
        (model_width, 3 * model_width),
        (model_width, model_width),
        (model_width, hidden_width),
        (hidden_width, model_width),
    ]
    result = []
    offset = 0
    for stream in range(2):
        pairs = []
        for fan, outer in shapes:
            a_len = fan // parts * rank_cols
            left_mat = grid[:, offset : offset + a_len].reshape(fan, rank_cols)
            offset += a_len
            b_len = rank_cols * (outer // parts)
            right_mat = grid[:, offset : offset + b_len].reshape(parts, rank_cols, outer // parts)
            right_mat = jnp.transpose(right_mat, (1, 0, 2)).reshape(rank_cols, outer)
            offset += b_len
            pairs.append((left_mat, right_mat))
        result.append(pairs)
    return result


def layer_norm(values):
    center = values - jnp.mean(values, axis=-1, keepdims=True)
    inverse = lax.rsqrt(jnp.mean(center * center, axis=-1, keepdims=True) + EPS)
    return (center * inverse, inverse)


def norm_back(grad_normed, normed, inverse, scale):
    grad_hat = grad_normed * (1.0 + scale)
    return inverse * (
        grad_hat
        - jnp.mean(grad_hat, axis=-1, keepdims=True)
        - normed * jnp.mean(grad_hat * normed, axis=-1, keepdims=True)
    )


def share_tokens(image_part, text_part):
    return (
        lax.all_gather(image_part, "tp", axis=1, tiled=True),
        lax.all_gather(text_part, "tp", axis=0, tiled=True),
    )


def return_sums(image_part, text_part):
    return (
        lax.psum_scatter(image_part, "tp", scatter_dimension=1, tiled=True),
        lax.psum_scatter(text_part, "tp", scatter_dimension=0, tiled=True),
    )


def share_grads(image_part, text_part):
    return (
        lax.all_gather(image_part, "tp", axis=1, tiled=True),
        lax.all_gather(text_part, "tp", axis=0, tiled=True),
    )


def return_grads(image_part, text_part):
    return (
        lax.psum_scatter(image_part, "tp", scatter_dimension=1, tiled=True),
        lax.psum_scatter(text_part, "tp", scatter_dimension=0, tiled=True),
    )


def rank_forward(image_part, text_part):
    return lax.psum((image_part, text_part), "tp")


def rank_backward(image_part, text_part):
    return (
        lax.psum(image_part.astype(jnp.bfloat16), "tp").astype(jnp.float32),
        lax.psum(text_part.astype(jnp.bfloat16), "tp").astype(jnp.float32),
    )


def slot_block(img_qkv, txt_qkv, member):
    return jnp.concatenate([img_qkv[member], txt_qkv], axis=0)


def slot_scores(slot_rows, allowed):
    scores = (
        jnp.einsum(
            "qhd,khd->hqk",
            slot_rows[:, :, 0],
            slot_rows[:, :, 1],
            preferred_element_type=jnp.float32,
        )
        * 0.125
    )
    return jnp.where(allowed[None, None, :], scores, -1e30)


def shards(
    image_tokens,
    text_tokens,
    conditioning,
    text_lengths,
    adapter_index,
    adapters,
    mod_weight,
    qkv_weight,
    out_weight,
    fc1_weight,
    fc2_weight,
    image_cot,
    text_cot,
):
    tp_rank = lax.axis_index("tp")
    tp_count = lax.axis_size("tp")
    fsdp_count = lax.axis_size("fsdp")
    slot_count, img_local, model_width = image_tokens.shape
    txt_local = text_tokens.shape[0]
    img_group = img_local * tp_count
    txt_group = txt_local * tp_count
    rank_cols = NAD * RANK
    frozen = (
        lax.all_gather(mod_weight, "fsdp", axis=1, tiled=True),
        lax.all_gather(qkv_weight, "fsdp", axis=1, tiled=True),
        lax.all_gather(out_weight, "fsdp", axis=2, tiled=True),
        lax.all_gather(fc1_weight, "fsdp", axis=1, tiled=True),
        lax.all_gather(fc2_weight, "fsdp", axis=2, tiled=True),
    )
    whole_flat = lax.all_gather(
        adapters.astype(jnp.bfloat16).reshape(-1), ("fsdp", "tp"), axis=0, tiled=True
    )
    full_grid = jnp.transpose(whole_flat.reshape(fsdp_count, tp_count, -1), (1, 0, 2)).reshape(
        tp_count, -1
    )
    pieces = unpack(full_grid, model_width, FF, rank_cols)

    def column_share(matrix):
        extent = matrix.shape[1] // tp_count
        return lax.dynamic_slice_in_dim(matrix, tp_rank * extent, extent, 1)

    def row_share(matrix):
        extent = matrix.shape[0] // tp_count
        return lax.dynamic_slice_in_dim(matrix, tp_rank * extent, extent, 0)

    seg_ends = jnp.cumsum(text_lengths[0])
    slot_ids = jnp.arange(slot_count)

    def owner_of(position):
        segment = jnp.sum((position[:, None] >= seg_ends[None, :]).astype(jnp.int32), axis=1)
        return (segment, (segment[:, None] == slot_ids[None, :]).astype(jnp.float32))

    seg_group, owner_group = owner_of(jnp.arange(txt_group))
    seg_local, owner_local = owner_of(tp_rank * txt_local + jnp.arange(txt_local))
    chosen = (adapter_index[:, None] == jnp.arange(NAD)[None, :]).astype(jnp.float32)
    seq_mask = jnp.repeat(chosen, RANK, axis=1)
    token_masks = [jnp.repeat(seq_mask, img_group, axis=0), exact(owner_group, seq_mask)]

    def spread(stream, values):
        if stream == 0:
            return values[:, None, :]
        return exact(owner_local, values)

    def collapse(stream, values):
        if stream == 0:
            return jnp.sum(values, axis=1)
        return exact(owner_local.T, values)

    def mine(stream, rows):
        if stream == 0:
            return lax.dynamic_slice_in_dim(
                rows.reshape(slot_count, img_group, rows.shape[-1]),
                tp_rank * img_local,
                img_local,
                1,
            )
        return lax.dynamic_slice_in_dim(rows, tp_rank * txt_local, txt_local, 0)

    def flatten(values):
        return values.reshape(slot_count * img_group, values.shape[-1])

    def fold(stream, values):
        if stream == 0:
            return values.reshape(slot_count, img_group, values.shape[-1])
        return values

    cond_act = jax.nn.silu(conditioning).astype(jnp.bfloat16)
    mod_mid = []
    mod_terms = []
    for stream in range(2):
        adapter_pair = pieces[stream][0]
        middle = (matmul(cond_act, adapter_pair[0]) * seq_mask).astype(jnp.bfloat16)
        mod_mid.append(middle)
        mod_terms.append(
            matmul(cond_act, frozen[0][stream]) + matmul(middle, column_share(adapter_pair[1]))
        )
    mods = lax.all_gather(jnp.stack(mod_terms), "tp", axis=2, tiled=True)

    def stretch(stream, index):
        return spread(stream, mods[stream][:, index * model_width : (index + 1) * model_width])

    inputs = [image_tokens.astype(jnp.float32), text_tokens.astype(jnp.float32)]
    normal_one = [layer_norm(inputs[stream]) for stream in range(2)]
    heads_in = [
        (normal_one[stream][0] * (1.0 + stretch(stream, 1)) + stretch(stream, 0)).astype(
            jnp.bfloat16
        )
        for stream in range(2)
    ]
    gathered = share_tokens(heads_in[0], heads_in[1])
    full_in = [flatten(gathered[0]), gathered[1]]
    qkv_mid = []
    qkv_rows = []
    for stream in range(2):
        adapter_pair = pieces[stream][1]
        middle = (matmul(full_in[stream], adapter_pair[0]) * token_masks[stream]).astype(
            jnp.bfloat16
        )
        qkv_mid.append(middle)
        qkv_rows.append(
            (
                matmul(full_in[stream], frozen[1][stream])
                + matmul(middle, column_share(adapter_pair[1]))
            ).astype(jnp.bfloat16)
        )
    head_count = qkv_rows[0].shape[1] // (3 * HD)
    img_qkv = qkv_rows[0].reshape(slot_count, img_group, head_count, 3, HD)
    txt_qkv = qkv_rows[1].reshape(txt_group, head_count, 3, HD)
    img_mixed = []
    txt_mixed = jnp.zeros((txt_group, head_count * HD), jnp.float32)
    saved_lse = []
    for member in range(slot_count):
        slot_rows = slot_block(img_qkv, txt_qkv, member)
        allowed = jnp.concatenate([jnp.ones((img_group,), bool), seg_group == member])
        scores = slot_scores(slot_rows, allowed)
        row_max = jnp.max(scores, axis=-1, keepdims=True)
        exponent = jnp.exp(scores - row_max)
        row_total = jnp.sum(exponent, axis=-1, keepdims=True)
        saved_lse.append(row_max + jnp.log(row_total))
        mixture = jnp.einsum(
            "hqk,khd->qhd",
            (exponent / row_total).astype(jnp.bfloat16),
            slot_rows[:, :, 2],
            preferred_element_type=jnp.float32,
        ).astype(jnp.bfloat16)
        mixture = mixture.reshape(mixture.shape[0], head_count * HD)
        img_mixed.append(mixture[:img_group])
        txt_mixed = txt_mixed + owner_group[:, member : member + 1] * mixture[img_group:].astype(
            jnp.float32
        )
    attended = [
        jnp.stack(img_mixed).reshape(slot_count * img_group, head_count * HD),
        txt_mixed.astype(jnp.bfloat16),
    ]
    branch_part = []
    rank_part = []
    for stream in range(2):
        branch_part.append(fold(stream, matmul(attended[stream], frozen[2][stream])))
        rank_part.append(matmul(attended[stream], row_share(pieces[stream][2][0])))
    rank_total = rank_forward(rank_part[0], rank_part[1])
    out_mid = [
        (rank_total[stream] * token_masks[stream]).astype(jnp.bfloat16) for stream in range(2)
    ]
    branch_total = return_sums(branch_part[0], branch_part[1])
    branch_out = [
        branch_total[stream] + matmul(mine(stream, out_mid[stream]), pieces[stream][2][1])
        for stream in range(2)
    ]
    after_attn = [inputs[stream] + stretch(stream, 2) * branch_out[stream] for stream in range(2)]
    normal_two = [layer_norm(after_attn[stream]) for stream in range(2)]
    mlp_local = [
        (normal_two[stream][0] * (1.0 + stretch(stream, 4)) + stretch(stream, 3)).astype(
            jnp.bfloat16
        )
        for stream in range(2)
    ]
    gathered = share_tokens(mlp_local[0], mlp_local[1])
    mlp_in = [flatten(gathered[0]), gathered[1]]
    fc1_mid = []
    pre_act = []
    activated = []
    feed_part = []
    rank_part = []
    for stream in range(2):
        adapter_pair = pieces[stream][3]
        middle = (matmul(mlp_in[stream], adapter_pair[0]) * token_masks[stream]).astype(
            jnp.bfloat16
        )
        fc1_mid.append(middle)
        hidden = matmul(mlp_in[stream], frozen[3][stream]) + matmul(
            middle, column_share(adapter_pair[1])
        )
        pre_act.append(hidden)
        active = jax.nn.gelu(hidden, approximate=True).astype(jnp.bfloat16)
        activated.append(active)
        feed_part.append(fold(stream, matmul(active, frozen[4][stream])))
        rank_part.append(matmul(active, row_share(pieces[stream][4][0])))
    rank_total = rank_forward(rank_part[0], rank_part[1])
    fc2_mid = [
        (rank_total[stream] * token_masks[stream]).astype(jnp.bfloat16) for stream in range(2)
    ]
    feed_total = return_sums(feed_part[0], feed_part[1])
    feed_out = [
        feed_total[stream] + matmul(mine(stream, fc2_mid[stream]), pieces[stream][4][1])
        for stream in range(2)
    ]
    results = [after_attn[stream] + stretch(stream, 5) * feed_out[stream] for stream in range(2)]
    frozen_back = (
        lax.all_gather(mod_weight, "fsdp", axis=1, tiled=True),
        lax.all_gather(qkv_weight, "fsdp", axis=1, tiled=True),
        lax.all_gather(out_weight, "fsdp", axis=2, tiled=True),
        lax.all_gather(fc1_weight, "fsdp", axis=1, tiled=True),
        lax.all_gather(fc2_weight, "fsdp", axis=2, tiled=True),
    )
    grad_a = [[None] * 5 for stream in range(2)]
    grad_b = [[None] * 5 for stream in range(2)]
    cots = [image_cot.astype(jnp.float32), text_cot.astype(jnp.float32)]
    grad_feed = [(stretch(stream, 5) * cots[stream]).astype(jnp.bfloat16) for stream in range(2)]
    gathered = share_grads(grad_feed[0], grad_feed[1])
    feed_full = [flatten(gathered[0]), gathered[1]]
    grad_pre = []
    back_part = []
    for stream in range(2):
        adapter_pair = pieces[stream][4]
        back_mid = (inner_right(feed_full[stream], adapter_pair[1]) * token_masks[stream]).astype(
            jnp.bfloat16
        )
        grad_a[stream][4] = inner_left(activated[stream], back_mid)
        grad_b[stream][4] = inner_left(fc2_mid[stream], column_share(feed_full[stream]))
        grad_act = inner_right(feed_full[stream], frozen_back[4][stream]) + inner_right(
            back_mid, row_share(adapter_pair[0])
        )
        gelu_pull = jax.vjp(lambda value: jax.nn.gelu(value, approximate=True), pre_act[stream])[1]
        grad_hidden = gelu_pull(grad_act)[0].astype(jnp.bfloat16)
        grad_pre.append(grad_hidden)
        back_part.append(inner_right(grad_hidden, column_share(pieces[stream][3][1])))
    back_total = rank_backward(back_part[0], back_part[1])
    norm_part = []
    fc1_back = []
    for stream in range(2):
        back_mid = (back_total[stream] * token_masks[stream]).astype(jnp.bfloat16)
        fc1_back.append(back_mid)
        grad_b[stream][3] = inner_left(fc1_mid[stream], grad_pre[stream])
        grad_a[stream][3] = inner_left(column_share(mlp_in[stream]), back_mid)
        norm_part.append(fold(stream, inner_right(grad_pre[stream], frozen_back[3][stream])))
    norm_total = return_grads(norm_part[0], norm_part[1])
    grad_after = []
    mod_parts = [[None] * 6 for stream in range(2)]
    for stream in range(2):
        grad_norm = norm_total[stream] + inner_right(
            mine(stream, fc1_back[stream]), pieces[stream][3][0]
        )
        grad_after.append(
            cots[stream]
            + norm_back(grad_norm, normal_two[stream][0], normal_two[stream][1], stretch(stream, 4))
        )
        mod_parts[stream][3] = collapse(stream, grad_norm)
        mod_parts[stream][4] = collapse(stream, grad_norm * normal_two[stream][0])
        mod_parts[stream][5] = collapse(stream, cots[stream] * feed_out[stream])
    grad_branch = [
        (stretch(stream, 2) * grad_after[stream]).astype(jnp.bfloat16) for stream in range(2)
    ]
    gathered = share_grads(grad_branch[0], grad_branch[1])
    branch_full = [flatten(gathered[0]), gathered[1]]
    grad_attended = []
    for stream in range(2):
        adapter_pair = pieces[stream][2]
        back_mid = (inner_right(branch_full[stream], adapter_pair[1]) * token_masks[stream]).astype(
            jnp.bfloat16
        )
        grad_a[stream][2] = inner_left(attended[stream], back_mid)
        grad_b[stream][2] = inner_left(out_mid[stream], column_share(branch_full[stream]))
        grad_attended.append(
            (
                inner_right(branch_full[stream], frozen_back[2][stream])
                + inner_right(back_mid, row_share(adapter_pair[0]))
            ).astype(jnp.bfloat16)
        )
    grad_img_att = grad_attended[0].reshape(slot_count, img_group, head_count, HD)
    grad_txt_att = grad_attended[1].astype(jnp.float32)
    img_back = []
    txt_back = jnp.zeros((txt_group, head_count, 3, HD), jnp.float32)
    for member in range(slot_count):
        slot_rows = slot_block(img_qkv, txt_qkv, member)
        allowed = jnp.concatenate([jnp.ones((img_group,), bool), seg_group == member])
        scores = slot_scores(slot_rows, allowed)
        attention = jnp.exp(scores - saved_lse[member])
        txt_grad_rows = (
            (owner_group[:, member : member + 1] * grad_txt_att)
            .astype(jnp.bfloat16)
            .reshape(txt_group, head_count, HD)
        )
        grad_rows_out = jnp.concatenate([grad_img_att[member], txt_grad_rows], axis=0)
        grad_values = jnp.einsum(
            "hqk,qhd->khd",
            attention.astype(jnp.bfloat16),
            grad_rows_out,
            preferred_element_type=jnp.float32,
        )
        grad_weights = jnp.einsum(
            "qhd,khd->hqk", grad_rows_out, slot_rows[:, :, 2], preferred_element_type=jnp.float32
        )
        row_delta = jnp.sum(attention * grad_weights, axis=-1, keepdims=True)
        grad_scores = (attention * (grad_weights - row_delta)).astype(jnp.bfloat16)
        grad_queries = (
            jnp.einsum(
                "hqk,khd->qhd", grad_scores, slot_rows[:, :, 1], preferred_element_type=jnp.float32
            )
            * 0.125
        )
        grad_keys = (
            jnp.einsum(
                "hqk,qhd->khd", grad_scores, slot_rows[:, :, 0], preferred_element_type=jnp.float32
            )
            * 0.125
        )
        grad_slot = jnp.stack([grad_queries, grad_keys, grad_values], axis=2)
        img_back.append(grad_slot[:img_group])
        txt_back = txt_back + grad_slot[img_group:]
    grad_qkv = [
        jnp.stack(img_back)
        .reshape(slot_count * img_group, 3 * head_count * HD)
        .astype(jnp.bfloat16),
        txt_back.reshape(txt_group, 3 * head_count * HD).astype(jnp.bfloat16),
    ]
    back_part = [
        inner_right(grad_qkv[stream], column_share(pieces[stream][1][1])) for stream in range(2)
    ]
    back_total = rank_backward(back_part[0], back_part[1])
    norm_part = []
    qkv_back = []
    for stream in range(2):
        back_mid = (back_total[stream] * token_masks[stream]).astype(jnp.bfloat16)
        qkv_back.append(back_mid)
        grad_b[stream][1] = inner_left(qkv_mid[stream], grad_qkv[stream])
        grad_a[stream][1] = inner_left(column_share(full_in[stream]), back_mid)
        norm_part.append(fold(stream, inner_right(grad_qkv[stream], frozen_back[1][stream])))
    norm_total = return_grads(norm_part[0], norm_part[1])
    grad_inputs = []
    for stream in range(2):
        grad_norm = norm_total[stream] + inner_right(
            mine(stream, qkv_back[stream]), pieces[stream][1][0]
        )
        grad_inputs.append(
            grad_after[stream]
            + norm_back(grad_norm, normal_one[stream][0], normal_one[stream][1], stretch(stream, 1))
        )
        mod_parts[stream][0] = collapse(stream, grad_norm)
        mod_parts[stream][1] = collapse(stream, grad_norm * normal_one[stream][0])
        mod_parts[stream][2] = collapse(stream, grad_after[stream] * branch_out[stream])
    mod_rows = jnp.stack([jnp.concatenate(mod_parts[stream], axis=1) for stream in range(2)])
    mod_share = lax.psum_scatter(
        mod_rows.astype(jnp.bfloat16), "tp", scatter_dimension=2, tiled=True
    )
    cond_part = jnp.zeros(conditioning.shape, jnp.float32)
    mod_back = []
    for stream in range(2):
        cond_part = cond_part + inner_right(mod_share[stream], frozen_back[0][stream])
        mod_back.append(inner_right(mod_share[stream], column_share(pieces[stream][0][1])))
        grad_b[stream][0] = inner_left(mod_mid[stream], mod_share[stream])
    cond_total, mod_rank = lax.psum((cond_part, jnp.stack(mod_back)), "tp")
    for stream in range(2):
        back_mid = (mod_rank[stream] * seq_mask).astype(jnp.bfloat16)
        cond_total = cond_total + inner_right(back_mid, pieces[stream][0][0])
        grad_a[stream][0] = inner_left(column_share(cond_act), back_mid)
    cond_grad = jax.vjp(jax.nn.silu, conditioning)[1](cond_total)[0]
    flat_pieces = []
    for stream in range(2):
        for index in range(5):
            flat_pieces.append(grad_a[stream][index].reshape(-1))
            flat_pieces.append(grad_b[stream][index].reshape(-1))
    own_row = jnp.concatenate(flat_pieces)
    adapter_grad = lax.psum_scatter(own_row, "fsdp", scatter_dimension=0, tiled=True).reshape(1, -1)
    return (
        results[0].astype(jnp.bfloat16),
        results[1].astype(jnp.bfloat16),
        grad_inputs[0],
        grad_inputs[1],
        cond_grad,
        adapter_grad,
    )


def solution(mesh):
    return jax.shard_map(
        shards,
        mesh=mesh,
        in_specs=(
            P("fsdp", "tp", None),
            P(("fsdp", "tp"), None),
            P("fsdp", None),
            P("fsdp", None),
            P("fsdp"),
            P("tp", "fsdp"),
            P(None, "fsdp", "tp"),
            P(None, "fsdp", "tp"),
            P(None, "tp", "fsdp"),
            P(None, "fsdp", "tp"),
            P(None, "tp", "fsdp"),
            P("fsdp", "tp", None),
            P(("fsdp", "tp"), None),
        ),
        out_specs=(
            P("fsdp", "tp", None),
            P(("fsdp", "tp"), None),
            P("fsdp", "tp", None),
            P(("fsdp", "tp"), None),
            P("fsdp", None),
            P("tp", "fsdp"),
        ),
        check_vma=False,
    )
```

profile of v0, /device:TPU:11, one launch (start us, length us, event | category | flops | bytes accessed | tf_op | source)
XLA Modules:
  0.0 3137.4 jit_solution(493509778878247268)
XLA Ops:
  13.3 77.0 %all-gather.12.cloned.1.call-done = bf16[2,1536,2304]{2,1,0:T(8,128)(2,1)} async-done(((bf16[2,192,2304]{2,1,0:T(8,128)(2,1)}), bf16[2,1536,2304]{2,1,0:T(8,128)(2,1)}) %all-gather.12.cloned.1.call-update) | async-done | bytes 14155792 | tf_op jit(solution)/shard_map/all_gather | solution.py:160
  98.4 200.9 %all-gather.30.cloned.1.call-done = bf16[1,9043968]{1,0:T(2,128)(2,1)} async-done(((bf16[1,282624]{1,0:T(2,128)(2,1)}), bf16[1,9043968]{1,0:T(2,128)(2,1)}) %all-gather.30.cloned.1.call-update) | async-done | bytes 18087952 | tf_op jit(solution)/shard_map/all_gather | solution.py:166
  299.2 382.8 %reduce = bf16[9043968]{0:T(1024)(128)(2,1)} reduce(bf16[1,9043968]{1,0:T(2,128)(2,1)} %all-gather.30.cloned.1.call-done, bf16[]{:T(256)} %constant.107), dimensions={0}, to_apply=%all-gather.reduce_sub_computation | reduce | bytes 36175872 | tf_op jit(solution)/shard_map/all_gather | solution.py:166
  682.0 17.1 reshape.420
  760.0 19.6 all_gather.55
  784.6 80.5 %all-gather.14.cloned.1.call-done = bf16[2,1024,1536]{2,1,0:T(8,128)(2,1)} async-done(((bf16[2,256,1536]{2,1,0:T(8,128)(2,1)}), bf16[2,1024,1536]{2,1,0:T(8,128)(2,1)}) %all-gather.14.cloned.1.call-update) | async-done | bytes 6291472 | tf_op jit(solution)/shard_map/all_gather | solution.py:82
  869.8 12.5 fusion.63
  888.6 13.8 fusion.331
  902.4 15.1 fusion.3
  917.6 16.3 fusion.94
  940.1 13.9 fusion.332
  954.0 14.5 fusion.2
  969.2 14.4 fusion.93
  1025.5 19.1 fusion.324
  1044.7 22.5 copy.243
  1068.8 194.5 %reduce-scatter.12.cloned.1.call-done = f32[2,256,1536]{2,1,0:T(8,128)} async-done(((f32[2,1024,1536]{2,1,0:T(8,128)}), f32[2,256,1536]{2,1,0:T(8,128)}) %reduce-scatter.12.cloned.1.call-update) | async-done | bytes 3145744 | tf_op jit(solution)/shard_map/reduce_scatter | solution.py:89
  1301.1 77.4 %all-gather.26.cloned.1.call-done = bf16[2,1024,1536]{2,1,0:T(8,128)(2,1)} async-done(((bf16[2,256,1536]{2,1,0:T(8,128)(2,1)}), bf16[2,1024,1536]{2,1,0:T(8,128)(2,1)}) %all-gather.26.cloned.1.call-update) | async-done | bytes 6291472 | tf_op jit(solution)/shard_map/all_gather | solution.py:96
  1383.3 15.7 fusion.48
  1410.1 12.8 all_gather.60
  1423.2 44.5 %all-gather.22.cloned.1.call-done = bf16[2,1536,1536]{2,1,0:T(8,128)(2,1)} async-done(((bf16[2,192,1536]{2,1,0:T(8,128)(2,1)}), bf16[2,1536,1536]{2,1,0:T(8,128)(2,1)}) %all-gather.22.cloned.1.call-update) | async-done | bytes 9437200 | tf_op jit(solution)/shard_map/all_gather | solution.py:163
  1473.6 108.5 %all-gather.20.cloned.1.call-done = bf16[2,1024,1536]{2,1,0:T(8,128)(2,1)} async-done(((bf16[2,256,1536]{2,1,0:T(8,128)(2,1)}), bf16[2,1024,1536]{2,1,0:T(8,128)(2,1)}) %all-gather.20.cloned.1.call-update) | async-done | bytes 6291472 | tf_op jit(solution)/shard_map/all_gather | solution.py:82
  1586.8 14.8 fusion.50
  1601.6 11.7 multiply_convert_fusion.2
  1613.3 13.2 fusion.22
  1639.6 16.1 fusion.40
  1655.7 16.1 fusion.46
  1671.9 22.5 copy.245
  1696.4 15.0 all_gather.63
  1733.3 211.5 %reduce-scatter.20.cloned.1.call-done = f32[2,256,1536]{2,1,0:T(8,128)} async-done(((f32[2,1024,1536]{2,1,0:T(8,128)}), f32[2,256,1536]{2,1,0:T(8,128)}) %reduce-scatter.20.cloned.1.call-update) | async-done | bytes 3145744 | tf_op jit(solution)/shard_map/reduce_scatter | solution.py:103
  1950.5 209.6 %reduce-scatter.14.cloned.1.call-done = f32[2,256,1536]{2,1,0:T(8,128)} async-done(((f32[2,1024,1536]{2,1,0:T(8,128)}), f32[2,256,1536]{2,1,0:T(8,128)}) %reduce-scatter.14.cloned.1.call-update) | async-done | bytes 3145744 | tf_op jit(solution)/shard_map/reduce_scatter | solution.py:89
  2173.8 15.6 psum.75
  2191.9 23.8 reduce-scatter.18.cloned.1.call-done
  2218.3 15.5 all_gather.64
  2237.3 97.2 %all-gather.28.cloned.1.call-done = bf16[2,1024,1536]{2,1,0:T(8,128)(2,1)} async-done(((bf16[2,256,1536]{2,1,0:T(8,128)(2,1)}), bf16[2,1024,1536]{2,1,0:T(8,128)(2,1)}) %all-gather.28.cloned.1.call-update) | async-done | bytes 6291472 | tf_op jit(solution)/shard_map/all_gather | solution.py:96
  2344.6 15.9 fusion.81
  2360.5 26.9 multiply_reduce_fusion.1
  2387.4 29.9 multiply_convert_fusion.1
  2417.3 12.9 fusion.88
  2440.9 16.1 fusion.84
  2457.0 26.7 multiply_reduce_fusion
  2483.7 29.8 multiply_convert_fusion
  2513.5 12.9 fusion.90
  2583.6 13.6 fusion.36
  2615.6 15.0 psum.77
  2643.9 200.3 %reduce-scatter.24.cloned.1.call-done = f32[2,256,1536]{2,1,0:T(8,128)} async-done(((f32[2,1024,1536]{2,1,0:T(8,128)}), f32[2,256,1536]{2,1,0:T(8,128)}) %reduce-scatter.24.cloned.1.call-update) | async-done | bytes 3145744 | tf_op jit(solution)/shard_map/reduce_scatter | solution.py:103
  2870.0 43.6 %reduce-scatter.28.cloned.1.call-done = bf16[2304,4]{1,0:T(8,128)(2,1)} async-done(((bf16[9216,4]{1,0:T(8,128)(2,1)}), bf16[2304,4]{1,0:T(8,128)(2,1)}) %reduce-scatter.28.cloned.1.call-update) | async-done | bytes 18448
  2943.1 14.7 all-reduce.3
  2999.2 128.7 %all-reduce.16.cloned.1.call-done = f32[2260992]{0:T(1024)} async-done(((f32[2260992]{0:T(1024)}), f32[2260992]{0:T(1024)}) %all-reduce.16.cloned.1.call-update) | async-done | bytes 9043984
  (714 shorter events, 476.3 us)
Async XLA Ops:
  7.2 83.1 %all-gather.12.cloned.1.call-start = ((), (), s32[]{:S(2)}) async-start(), calls=%async_computation.9 | async-start | bytes 15925248 | tf_op jit(solution)/shard_map/all_gather | solution.py:160
  7.9 291.3 %all-gather.30.cloned.1.call-start = ((), (), s32[]{:S(2)}) async-start(), calls=%async_computation.28 | async-start | bytes 37306368 | tf_op jit(solution)/shard_map/all_gather | solution.py:166
  11.4 769.0 %all-gather.16.cloned.1.call-start = ((), (), s32[]{:S(2)}) async-start(), calls=%async_computation.11 | async-start | bytes 7962624 | tf_op jit(solution)/shard_map/all_gather | solution.py:161
  12.1 852.9 %all-gather.14.cloned.1.call-start = ((), (), s32[]{:S(2)}) async-start(), calls=%async_computation.10 | async-start | bytes 7864320 | tf_op jit(solution)/shard_map/all_gather | solution.py:82
  12.5 727.7 %copy-start.165 = (f32[2,256]{1,0:T(2,128)}, f32[2,256]{1,0:T(2,128)S(1)}, u32[]{:S(2)}) copy-start(f32[2,256]{1,0:T(2,128)S(1)} %broadcast_multiply_fusion.5) | copy-start | bytes 6148
  13.1 727.1 %copy-start.172 = (f32[2,256]{1,0:T(2,128)}, f32[2,256]{1,0:T(2,128)S(1)}, u32[]{:S(2)}) copy-start(f32[2,256]{1,0:T(2,128)S(1)} %add_rsqrt_fusion.1) | copy-start | bytes 6148
  13.2 713.6 %copy-start.137 = (bf16[2,1536]{1,0:T(2,128)(2,1)}, bf16[2,1536]{1,0:T(2,128)(2,1)S(1)}, u32[]{:S(2)}) copy-start(bf16[2,1536]{1,0:T(2,128)(2,1)S(1)} %multiply_convert_fusion.12) | copy-start | bytes 18436
  13.3 851.7 %copy-start.138 = (f32[2,128]{1,0:T(2,128)}, f32[2,128]{1,0:T(2,128)S(1)}, u32[]{:S(2)}) copy-start(f32[2,128]{1,0:T(2,128)S(1)} %reshape.423) | copy-start | bytes 3076
  742.1 249.7 %all-gather.18.cloned.1.call-start = ((), (), s32[]{:S(2)}) async-start(), calls=%async_computation.12 | async-start | bytes 2654208 | tf_op jit(solution)/shard_map/all_gather | solution.py:162
  743.7 281.8 %all-gather.24.cloned.1.call-start = ((), (), s32[]{:S(2)}) async-start(), calls=%async_computation.16 | async-start | bytes 10616832 | tf_op jit(solution)/shard_map/all_gather | solution.py:164
  747.3 320.1 %all-reduce.20.cloned.1.call-start = ((), (), s32[]{:S(2)}) async-start(), calls=%async_computation.32 | async-start | bytes 2260992 | tf_op jit(solution)/shard_map/psum | solution.py:109
  991.7 271.6 %reduce-scatter.12.cloned.1.call-start = ((), (), s32[]{:S(2)}) async-start(), calls=%async_computation.13 | async-start | bytes 15728640 | tf_op jit(solution)/shard_map/reduce_scatter | solution.py:89
  1015.2 363.4 %all-gather.26.cloned.1.call-start = ((), (), s32[]{:S(2)}) async-start(), calls=%async_computation.20 | async-start | bytes 7864320 | tf_op jit(solution)/shard_map/all_gather | solution.py:96
  1018.7 387.0 %reduce-scatter.16.cloned.1.call-start = ((), (), s32[]{:S(2)}) async-start(), calls=%async_computation.18 | async-start | bytes 1228800 | tf_op jit(solution)/shard_map/reduce_scatter | solution.py:90
  1024.7 443.0 %all-gather.22.cloned.1.call-start = ((), (), s32[]{:S(2)}) async-start(), calls=%async_computation.15 | async-start | bytes 10616832 | tf_op jit(solution)/shard_map/all_gather | solution.py:163
  1025.5 556.6 %all-gather.20.cloned.1.call-start = ((), (), s32[]{:S(2)}) async-start(), calls=%async_computation.14 | async-start | bytes 7864320 | tf_op jit(solution)/shard_map/all_gather | solution.py:82
  1044.7 218.6 %copy-start.151 = (f32[2,1536]{1,0:T(2,128)S(1)}, f32[2,1536]{1,0:T(2,128)}, u32[]{:S(2)}) copy-start(f32[2,1536]{1,0:T(2,128)} %get-tuple-element.80) | copy-start | bytes 36868
  1067.2 196.1 %copy-start.10 = (bf16[2,256,1536]{2,1,0:T(8,128)(2,1)S(1)}, bf16[2,256,1536]{2,1,0:T(8,128)(2,1)}, u32[]{:S(2)}) copy-start(bf16[2,256,1536]{2,1,0:T(8,128)(2,1)} %param.13) | copy-start | bytes 4718596
  1068.8 198.8 %copy-start.75 = (bf16[2048,128]{1,0:T(8,128)(2,1)}, bf16[2048,128]{1,0:T(8,128)(2,1)S(1)}, u32[]{:S(2)}) copy-start(bf16[2048,128]{1,0:T(8,128)(2,1)S(1)} %fusion.139) | copy-start | bytes 1572868
  1271.1 458.4 %all-reduce.12.cloned.1.call-start = ((), (), s32[]{:S(2)}) async-start(), calls=%async_computation.22 | async-start | bytes 1048576 | tf_op jit(solution)/shard_map/psum | solution.py:114
  1301.1 108.0 %copy-start.87 = (f32[40,1536]{1,0:T(8,128)}, f32[40,1536]{1,0:T(8,128)S(1)}, u32[]{:S(2)}) copy-start(f32[40,1536]{1,0:T(8,128)S(1)} %convolution_add_fusion.15) | copy-start | bytes 737284
  1383.3 230.0 %copy-start.113 = (bf16[2048,128]{1,0:T(8,128)(2,1)}, bf16[2048,128]{1,0:T(8,128)(2,1)S(1)}, u32[]{:S(2)}) copy-start(bf16[2048,128]{1,0:T(8,128)(2,1)S(1)} %fusion.98) | copy-start | bytes 1572868
  1408.9 806.8 %copy-start.31 = (f32[40,1536]{1,0:T(8,128)}, f32[40,1536]{1,0:T(8,128)S(1)}, u32[]{:S(2)}) copy-start(f32[40,1536]{1,0:T(8,128)S(1)} %get-tuple-element.31) | copy-start | bytes 737284
  1408.9 806.8 %copy-start.182 = (f32[40]{0:T(128)}, f32[40]{0:T(128)S(1)}, u32[]{:S(2)}) copy-start(f32[40]{0:T(128)S(1)} %broadcast_multiply_fusion.10) | copy-start | bytes 484
  1409.1 806.5 %copy-start.190 = (f32[40]{0:T(128)}, f32[40]{0:T(128)S(1)}, u32[]{:S(2)}) copy-start(f32[40]{0:T(128)S(1)} %add_rsqrt_fusion.2) | copy-start | bytes 484
  1471.0 111.0 %copy-start.98 = (bf16[1536,128]{1,0:T(8,128)(2,1)S(1)}, bf16[1536,128]{1,0:T(8,128)(2,1)}, u32[]{:S(2)}) copy-start(bf16[1536,128]{1,0:T(8,128)(2,1)} %reshape.446) | copy-start | bytes 1179652
  1473.6 251.7 %copy-start.33 = (bf16[160,1536]{1,0:T(8,128)(2,1)}, bf16[160,1536]{1,0:T(8,128)(2,1)S(1)}, u32[]{:S(2)}) copy-start(bf16[160,1536]{1,0:T(8,128)(2,1)S(1)} %get-tuple-element.95) | copy-start | bytes 1474564
  1631.8 98.9 %all-reduce.18.cloned.1.call-start = ((), (), s32[]{:S(2)}) async-start(), calls=%async_computation.31 | async-start | bytes 2260992 | tf_op jit(solution)/shard_map/psum | solution.py:109
  1639.6 305.2 %reduce-scatter.20.cloned.1.call-start = ((), (), s32[]{:S(2)}) async-start(), calls=%async_computation.21 | async-start | bytes 15728640 | tf_op jit(solution)/shard_map/reduce_scatter | solution.py:103
  1655.7 504.4 %reduce-scatter.14.cloned.1.call-start = ((), (), s32[]{:S(2)}) async-start(), calls=%async_computation.17 | async-start | bytes 15728640 | tf_op jit(solution)/shard_map/reduce_scatter | solution.py:89
  1671.8 517.7 %reduce-scatter.22.cloned.1.call-start = ((), (), s32[]{:S(2)}) async-start(), calls=%async_computation.24 | async-start | bytes 1228800 | tf_op jit(solution)/shard_map/reduce_scatter | solution.py:104
  1722.9 492.8 %reduce-scatter.18.cloned.1.call-start = ((), (), s32[]{:S(2)}) async-start(), calls=%async_computation.19 | async-start | bytes 1228800 | tf_op jit(solution)/shard_map/reduce_scatter | solution.py:90
  1729.4 215.4 %copy-start.5 = (f32[2,256,1536]{2,1,0:T(8,128)S(1)}, f32[2,256,1536]{2,1,0:T(8,128)}, u32[]{:S(2)}) copy-start(f32[2,256,1536]{2,1,0:T(8,128)} %copy-done.4) | copy-start | bytes 9437188
  1729.4 215.4 %copy-start.126 = (f32[2,1536]{1,0:T(2,128)S(1)}, f32[2,1536]{1,0:T(2,128)}, u32[]{:S(2)}) copy-start(f32[2,1536]{1,0:T(2,128)} %get-tuple-element.77) | copy-start | bytes 36868
  1729.4 215.4 %copy-start.156 = (f32[2,256]{1,0:T(2,128)S(1)}, f32[2,256]{1,0:T(2,128)}, u32[]{:S(2)}) copy-start(f32[2,256]{1,0:T(2,128)} %copy-done.155) | copy-start | bytes 6148
  1729.4 215.4 %copy-start.163 = (f32[2,256]{1,0:T(2,128)S(1)}, f32[2,256]{1,0:T(2,128)}, u32[]{:S(2)}) copy-start(f32[2,256]{1,0:T(2,128)} %copy-done.162) | copy-start | bytes 6148
  1729.5 605.0 %all-gather.28.cloned.1.call-start = ((), (), s32[]{:S(2)}) async-start(), calls=%async_computation.23 | async-start | bytes 7864320 | tf_op jit(solution)/shard_map/all_gather | solution.py:96
  1944.8 215.3 %copy-start.136 = (f32[2,1536]{1,0:T(2,128)S(1)}, f32[2,1536]{1,0:T(2,128)}, u32[]{:S(2)}) copy-start(f32[2,1536]{1,0:T(2,128)} %get-tuple-element.75) | copy-start | bytes 36868
  2171.6 464.1 %all-reduce.14.cloned.1.call-start = ((), (), s32[]{:S(2)}) async-start(), calls=%async_computation.26 | async-start | bytes 1048576 | tf_op jit(solution)/shard_map/psum | solution.py:114
  2215.7 118.8 %copy-start.50 = (bf16[1,384,1536]{2,1,0:T(8,128)(2,1)S(1)}, bf16[1,384,1536]{2,1,0:T(8,128)(2,1)}, u32[]{:S(2)}) copy-start(bf16[1,384,1536]{2,1,0:T(8,128)(2,1)} %copy.242) | copy-start | bytes 3538948
  2562.5 75.3 %reduce-scatter.26.cloned.1.call-start = ((), (), s32[]{:S(2)}) async-start(), calls=%async_computation.27 | async-start | bytes 1228800 | tf_op jit(solution)/shard_map/reduce_scatter | solution.py:104
  2569.0 275.1 %reduce-scatter.24.cloned.1.call-start = ((), (), s32[]{:S(2)}) async-start(), calls=%async_computation.25 | async-start | bytes 15728640 | tf_op jit(solution)/shard_map/reduce_scatter | solution.py:103
  2597.3 316.3 %reduce-scatter.28.cloned.1.call-start = ((), (), s32[]{:S(2)}) async-start(), calls=%async_computation.29 | async-start | bytes 2949120
  2635.6 208.5 %copy-start.11 = (bf16[2,256,1536]{2,1,0:T(8,128)(2,1)S(1)}, bf16[2,256,1536]{2,1,0:T(8,128)(2,1)}, u32[]{:S(2)}) copy-start(bf16[2,256,1536]{2,1,0:T(8,128)(2,1)} %param.13) | copy-start | bytes 4718596
  2635.7 208.5 %copy-start.149 = (f32[2,1536]{1,0:T(2,128)S(1)}, f32[2,1536]{1,0:T(2,128)}, u32[]{:S(2)}) copy-start(f32[2,1536]{1,0:T(2,128)} %copy-done.148) | copy-start | bytes 36868
  2635.7 208.5 %copy-start.166 = (f32[2,256]{1,0:T(2,128)S(1)}, f32[2,256]{1,0:T(2,128)}, u32[]{:S(2)}) copy-start(f32[2,256]{1,0:T(2,128)} %copy-done.165) | copy-start | bytes 6148
  2635.7 208.4 %copy-start.173 = (f32[2,256]{1,0:T(2,128)S(1)}, f32[2,256]{1,0:T(2,128)}, u32[]{:S(2)}) copy-start(f32[2,256]{1,0:T(2,128)} %copy-done.172) | copy-start | bytes 6148
  2866.8 261.2 %all-reduce.16.cloned.1.call-start = ((), (), s32[]{:S(2)}) async-start(), calls=%async_computation.30 | async-start | bytes 18087936
  (181 other events, 2313.0 us)
Sparse Core Ops, SparseCore 0:
  9.9 80.3 all-gather.11
  93.7 205.5 all-gather.29
  301.1 48.9 all-gather.15
  742.2 122.8 all-gather.13
  866.8 30.3 all-gather.17
  898.9 58.8 all-gather.23
  991.8 57.3 all-reduce.19
  1051.6 211.7 reduce-scatter.11
  1264.9 113.5 all-gather.25
  1380.7 24.9 reduce-scatter.15
  1407.8 59.9 all-gather.21
  1469.8 112.1 all-gather.19
  1632.0 37.9 all-reduce.11
  1672.9 57.7 all-reduce.17
  1733.0 211.7 reduce-scatter.19
  1947.1 212.8 reduce-scatter.13
  2162.3 26.1 reduce-scatter.21
  2190.7 24.9 reduce-scatter.17
  2217.3 117.1 all-gather.27
  2562.6 36.9 all-reduce.13
  2602.6 26.2 reduce-scatter.25
  2631.3 212.7 reduce-scatter.23
  2866.9 46.6 reduce-scatter.27
  2989.8 138.1 all-reduce.15
where the time goes:
time: 3150 us; the launch traced here: 3140 us
  waiting for transfers between devices  1710 us (54%)
  other arithmetic  509 us (16%)
  matrix products  502 us (16%)
  local copies, waits for them, and re-layouts  279 us (9%)
  blocking collectives  119 us (4%)
    reduce_scatter x2, waiting for transfers between devices, return_grads(): lax.psum_scatter(image_part, 'tp', scatter_dimension=1, tiled=True)  412 us
    reduce_scatter x2, waiting for transfers between devices, return_sums(): lax.psum_scatter(image_part, 'tp', scatter_dimension=1, tiled=True)  404 us
    all_gather x1, other arithmetic, shards(): lax.all_gather(adapters.astype(jnp.bfloat16).reshape(-1), ('fsdp', 'tp'),...  383 us
    all_gather x1, waiting for transfers between devices, shards(): lax.all_gather(adapters.astype(jnp.bfloat16).reshape(-1), ('fsdp', 'tp'),...  201 us
    all_gather x2, waiting for transfers between devices, share_tokens(): lax.all_gather(image_part, 'tp', axis=1, tiled=True)  189 us
    unnamed x26, waiting for transfers between devices  175 us
    all_gather x2, waiting for transfers between devices, share_grads(): lax.all_gather(image_part, 'tp', axis=1, tiled=True)  175 us
    dot_general x30, matrix products, matmul(): return jnp.dot(left, right, preferred_element_type=jnp.float32)  134 us
  transfers between devices with their start and end apart: 24, of which 16 were waited for; matrix products, arithmetic and copies ran while one was open for 29% of the time, Pallas kernels for 0%

commit v1 on v0

v1 whole, which is shorter than its diff:
```python
import functools

import jax
import jax.numpy as jnp
from jax import lax
from jax.experimental import pallas as pl
from jax.experimental.pallas import tpu as pltpu
from jax.sharding import PartitionSpec as P

MESH = pl.DeviceIdType.MESH

def bits_of(count):
    return max(count.bit_length() - 1, 0)

def halves(width):
    tiles = width // 128
    first = (tiles + 1) // 2 * 128
    return [(0, first), (first, width - first)]

def gather_kernel(n_f, n_z, full_count, part_count, *refs):
    total = full_count + part_count
    ins, outs = refs[:total], refs[total:2 * total]
    z_send, z_recv, xy_send, xy_recv, core_send, core_recv, own_sem = refs[2 * total:]
    f = lax.axis_index("fsdp")
    z = lax.axis_index("tp")
    chip, core = f // 2, f % 2
    chips = n_f // 2
    nbits = bits_of(chips)
    partner = chip * 2 + (1 - core)

    def peer_of(mask):
        other = 0
        for bit in range(nbits):
            have = (chip // (1 << bit)) % 2
            want = 1 - have if (mask >> bit) & 1 else have
            other = other + want * (1 << bit)
        return other * 2 + core

    barrier = pltpu.get_barrier_semaphore()
    for bit in range(nbits):
        pl.semaphore_signal(barrier, inc=1, device_id=(peer_of(1 << bit), z), device_id_type=MESH)
    pl.semaphore_signal(barrier, inc=1, device_id=(partner, z), device_id_type=MESH)
    @pl.when(z > 0)
    def _():
        pl.semaphore_signal(barrier, inc=1, device_id=(f, z - 1), device_id_type=MESH)
    @pl.when(z < n_z - 1)
    def _():
        pl.semaphore_signal(barrier, inc=1, device_id=(f, z + 1), device_id_type=MESH)
    peers = nbits + 1 + (z > 0).astype(jnp.int32) + (z < n_z - 1).astype(jnp.int32)
    pl.semaphore_wait(barrier, peers)

    def width(m):
        return ins[m].shape[-1]

    def place(m, who, zz, off=0, w=None):
        w = width(m) if w is None else w
        if m < full_count:
            return outs[m].at[who, :, pl.ds(pl.multiple_of(zz * width(m) + off, 128), w)]
        if w == width(m):
            return outs[m].at[who]
        return outs[m].at[who, :, pl.ds(off, w)]

    def piece(m, off, w):
        return ins[m] if w == width(m) else ins[m].at[:, pl.ds(off, w)]

    def remote(src, dst, ssem, rsem, dev):
        return pltpu.make_async_remote_copy(src_ref=src, dst_ref=dst, send_sem=ssem, recv_sem=rsem, device_id=dev, device_id_type=MESH)

    def order_of(half):
        order = list(range(nbits))
        return order if half == 0 else order[::-1]

    def cuts(m):
        if width(m) >= 256:
            return list(enumerate(halves(width(m))))
        return [(m % 2, (0, width(m)))]

    def slot(m, zz):
        return zz if m < full_count else 0

    def xy_copy(m, zz, half, cut, mask, bit, own_piece=False):
        off, w = cut
        who = peer_of(mask)
        source = piece(m, off, w) if own_piece and mask == 0 else place(m, who, zz, off, w)
        return remote(source, place(m, who, zz, off, w),
                      xy_send.at[m, slot(m, zz), half, mask, bit], xy_recv.at[m, slot(m, zz), half, mask | (1 << bit)],
                      (peer_of(1 << bit), z))

    def xy_wait(m, zz, half, cut, mask):
        off, w = cut
        who = peer_of(mask)
        remote(place(m, who, zz, off, w), place(m, who, zz, off, w), xy_send.at[m, slot(m, zz), half, 0, 0],
               xy_recv.at[m, slot(m, zz), half, mask], (partner, z)).wait_recv()

    def core_copy(m, zz, half, cut, mask, own_piece=False):
        off, w = cut
        who = peer_of(mask)
        source = piece(m, off, w) if own_piece and mask == 0 else place(m, who, zz, off, w)
        return remote(source, place(m, who, zz, off, w),
                      core_send.at[m, slot(m, zz), half, mask], core_recv.at[m, slot(m, zz), half, mask], (partner, z))

    def core_wait_recv(m, zz, half, cut, mask):
        off, w = cut
        who = peer_of(mask) - core + (1 - core)
        remote(place(m, who, zz, off, w), place(m, who, zz, off, w),
               core_send.at[m, slot(m, zz), half, mask], core_recv.at[m, slot(m, zz), half, mask], (partner, z)).wait_recv()

    def own(m):
        return pltpu.make_async_copy(ins[m], place(m, f, z), own_sem.at[m])

    def z_copy(m, zz, up, own_piece=False):
        return remote(ins[m] if own_piece else place(m, f, zz), place(m, f, zz), z_send.at[m, zz, up], z_recv.at[m, zz], (f, z + 1 if up else z - 1))

    def launch(m, zz, own_piece=False):
        for half, cut in cuts(m):
            for bit in order_of(half):
                xy_copy(m, zz, half, cut, 0, bit, own_piece).start()
            core_copy(m, zz, half, cut, 0, own_piece).start()

    def masks_in_order(half):
        order = order_of(half)
        def rank(mask):
            return [1 if (mask >> b) & 1 else 0 for b in reversed(order)]
        return sorted(range(1, 1 << nbits), key=rank)

    def forward(m, zz):
        for half, cut in cuts(m):
            order = order_of(half)
            for mask in masks_in_order(half):
                last = max(i for i, b in enumerate(order) if (mask >> b) & 1)
                if last == nbits - 1:
                    continue
                xy_wait(m, zz, half, cut, mask)
                for b in order[last + 1:]:
                    xy_copy(m, zz, half, cut, mask, b).start()
                core_copy(m, zz, half, cut, mask).start()

    def finish(m, zz):
        for half, cut in cuts(m):
            order = order_of(half)
            for mask in masks_in_order(half):
                last = max(i for i, b in enumerate(order) if (mask >> b) & 1)
                if last == nbits - 1:
                    xy_wait(m, zz, half, cut, mask)
                    core_copy(m, zz, half, cut, mask).start()

    def drain(m, zz):
        for half, cut in cuts(m):
            order = order_of(half)
            for mask in [0] + masks_in_order(half):
                last = max([i for i, b in enumerate(order) if (mask >> b) & 1], default=-1)
                for b in order[last + 1:]:
                    xy_copy(m, zz, half, cut, mask, b).wait_send()
                core_copy(m, zz, half, cut, mask).wait_send()
                core_wait_recv(m, zz, half, cut, mask)

    for m in range(total):
        own(m).start()
    for m in range(total):
        if m < full_count:
            @pl.when(z < n_z - 1)
            def _():
                z_copy(m, z, 1, True).start()
            @pl.when(z > 0)
            def _():
                z_copy(m, z, 0, True).start()
        launch(m, z, True)
    for m in range(full_count, total):
        forward(m, z)
    for k in range(1, n_z):
        for m in range(full_count):
            @pl.when(z - k >= 0)
            def _():
                zz = z - k
                z_copy(m, zz, 1).wait_recv()
                @pl.when(z < n_z - 1)
                def _():
                    z_copy(m, zz, 1).start()
                launch(m, zz)
            @pl.when(z + k < n_z)
            def _():
                zz = z + k
                z_copy(m, zz, 0).wait_recv()
                @pl.when(z > 0)
                def _():
                    z_copy(m, zz, 0).start()
                launch(m, zz)
            for sign in ((-1, 1) if k > 1 else (1,)):
                zz = z + sign * (k - 1)
                @pl.when((zz >= 0) & (zz < n_z))
                def _():
                    forward(m, zz)
    for m in range(full_count):
        for sign in (-1, 1):
            zz = z + sign * (n_z - 1)
            @pl.when((zz >= 0) & (zz < n_z))
            def _():
                forward(m, zz)
    for m in range(total):
        if m < full_count:
            def body(zz, _):
                finish(m, zz)
                return 0
            lax.fori_loop(0, n_z, body, 0)
        else:
            finish(m, z)
    for m in range(total):
        own(m).wait()
        if m < full_count:
            def body(zz, _):
                drain(m, zz)
                @pl.when((zz <= z) & (z < n_z - 1))
                def _():
                    z_copy(m, zz, 1).wait_send()
                @pl.when((zz >= z) & (z > 0))
                def _():
                    z_copy(m, zz, 0).wait_send()
                return 0
            lax.fori_loop(0, n_z, body, 0)
        else:
            drain(m, z)

def gather(full, part, n_f, n_z, cid=1):
    arrays = list(full) + list(part)
    total = len(arrays)
    if n_f > 8:
        rows = [lax.all_gather(a, "fsdp", axis=0, tiled=True) for a in arrays]
        return [
            lax.all_gather(a, "tp", axis=1, tiled=True) if i < len(full) else a
            for i, a in enumerate(rows)
        ]
    chips = n_f // 2
    nbits = bits_of(chips)
    shapes = [jax.ShapeDtypeStruct((n_f,) + a.shape[:-1] + (a.shape[-1] * (n_z if i < len(full) else 1),), a.dtype) for i, a in enumerate(arrays)]
    dma = pltpu.SemaphoreType.DMA
    return pl.pallas_call(
        functools.partial(gather_kernel, n_f, n_z, len(full), len(part)),
        out_shape=shapes,
        in_specs=[pl.BlockSpec(memory_space=pl.ANY)] * total,
        out_specs=[pl.BlockSpec(memory_space=pl.ANY)] * total,
        scratch_shapes=[
            dma((total, n_z, 2)), dma((total, n_z)),
            dma((total, n_z, 2, chips, max(nbits, 1))), dma((total, n_z, 2, chips)),
            dma((total, n_z, 2, chips)), dma((total, n_z, 2, chips)), dma((total,)),
        ],
        compiler_params=pltpu.CompilerParams(collective_id=cid, has_side_effects=True),
        name="weight_gather",
    )(*arrays)

def dots(left, right, lc, rc):
    return lax.dot_general(left, right, (((lc,), (rc,)), ((), ())), preferred_element_type=jnp.float32)

def attend_kernel(hd, bq, img_ref, txt_ref, bias_ref, oi_ref, ot_ref, lse_ref):
    img_n, txt_n = img_ref.shape[0], txt_ref.shape[0]
    heads = img_ref.shape[1] // (3 * hd)
    bias = bias_ref[...]
    for h in range(heads):
        base = 3 * hd * h
        ki = img_ref[:, base + hd:base + 2 * hd]
        vi = img_ref[:, base + 2 * hd:base + 3 * hd]
        kt = txt_ref[:, base + hd:base + 2 * hd]
        vt = txt_ref[:, base + 2 * hd:base + 3 * hd]

        def block(q):
            q = q * jnp.bfloat16(0.125)
            si = dots(ki, q, 1, 1)
            st = dots(kt, q, 1, 1) + bias
            top = jnp.maximum(jnp.max(si, axis=0, keepdims=True), jnp.max(st, axis=0, keepdims=True))
            ei = jnp.exp(si - top)
            et = jnp.exp(st - top)
            total = jnp.sum(ei, axis=0, keepdims=True) + jnp.sum(et, axis=0, keepdims=True)
            o = dots(vi, ei.astype(jnp.bfloat16), 0, 0) + dots(vt, et.astype(jnp.bfloat16), 0, 0)
            return (o / total).T.astype(jnp.bfloat16), top + jnp.log(total)

        for i in range(img_n // bq):
            o, lse = block(img_ref[i * bq:(i + 1) * bq, base:base + hd])
            oi_ref[i * bq:(i + 1) * bq, h * hd:(h + 1) * hd] = o
            lse_ref[0, h:h + 1, i * bq:(i + 1) * bq] = lse
        o, lse = block(txt_ref[:, base:base + hd])
        ot_ref[:, h * hd:(h + 1) * hd] = o
        lse_ref[0, h:h + 1, img_n:img_n + txt_n] = lse

def attend(img, txt, bias, hd, bq=512):
    img_n, cols = img.shape
    txt_n = txt.shape[0]
    pairs = cols // (6 * hd)
    return pl.pallas_call(
        functools.partial(attend_kernel, hd, bq),
        grid=(pairs,),
        in_specs=[
            pl.BlockSpec((img_n, 6 * hd), lambda i: (0, i)),
            pl.BlockSpec((txt_n, 6 * hd), lambda i: (0, i)),
            pl.BlockSpec((txt_n, 1), lambda i: (0, 0)),
        ],
        out_specs=[
            pl.BlockSpec((img_n, 2 * hd), lambda i: (0, i)),
            pl.BlockSpec((txt_n, 2 * hd), lambda i: (0, i)),
            pl.BlockSpec((1, 2, img_n + txt_n), lambda i: (i, 0, 0)),
        ],
        out_shape=[
            jax.ShapeDtypeStruct((img_n, pairs * 2 * hd), jnp.bfloat16),
            jax.ShapeDtypeStruct((txt_n, pairs * 2 * hd), jnp.bfloat16),
            jax.ShapeDtypeStruct((pairs, 2, img_n + txt_n), jnp.float32),
        ],
        compiler_params=pltpu.CompilerParams(vmem_limit_bytes=48 * 1024 * 1024),
        name="attend",
    )(img, txt, bias)

def attend_back_kernel(hd, bq, img_ref, txt_ref, bias_ref, doi_ref, dot_ref, lse_ref, di_ref, dt_ref, acc_i, acc_t):
    img_n, txt_n = img_ref.shape[0], txt_ref.shape[0]
    heads = img_ref.shape[1] // (3 * hd)
    bias = bias_ref[...]
    for h in range(heads):
        base = 3 * hd * h
        ki = img_ref[:, base + hd:base + 2 * hd]
        vi = img_ref[:, base + 2 * hd:base + 3 * hd]
        kt = txt_ref[:, base + hd:base + 2 * hd]
        vt = txt_ref[:, base + 2 * hd:base + 3 * hd]

        def block(q, do, lse, first):
            q = q * jnp.bfloat16(0.125)
            pi = jnp.exp(dots(ki, q, 1, 1) - lse)
            pt = jnp.exp(dots(kt, q, 1, 1) + bias - lse)
            dwi = dots(vi, do, 1, 1)
            dwt = dots(vt, do, 1, 1)
            delta = jnp.sum(pi * dwi, axis=0, keepdims=True) + jnp.sum(pt * dwt, axis=0, keepdims=True)
            dsi = (pi * (dwi - delta)).astype(jnp.bfloat16)
            dst = (pt * (dwt - delta)).astype(jnp.bfloat16)
            dvi = dots(pi.astype(jnp.bfloat16), do, 1, 0)
            dvt = dots(pt.astype(jnp.bfloat16), do, 1, 0)
            dki = dots(dsi, q, 1, 0)
            dkt = dots(dst, q, 1, 0)
            if first:
                acc_i[0], acc_i[1], acc_t[0], acc_t[1] = dki, dvi, dkt, dvt
            else:
                acc_i[0] += dki
                acc_i[1] += dvi
                acc_t[0] += dkt
                acc_t[1] += dvt
            dq = dots(ki, dsi, 0, 0) + dots(kt, dst, 0, 0)
            return (dq.T * 0.125).astype(jnp.bfloat16)

        for i in range(img_n // bq):
            rows = slice(i * bq, (i + 1) * bq)
            di_ref[rows, base:base + hd] = block(
                img_ref[rows, base:base + hd], doi_ref[rows, h * hd:(h + 1) * hd], lse_ref[0, h:h + 1, rows], i == 0)
        dt_ref[:, base:base + hd] = block(
            txt_ref[:, base:base + hd], dot_ref[:, h * hd:(h + 1) * hd], lse_ref[0, h:h + 1, img_n:img_n + txt_n], False)
        di_ref[:, base + hd:base + 2 * hd] = acc_i[0].astype(jnp.bfloat16)
        di_ref[:, base + 2 * hd:base + 3 * hd] = acc_i[1].astype(jnp.bfloat16)
        dt_ref[:, base + hd:base + 2 * hd] = acc_t[0].astype(jnp.bfloat16)
        dt_ref[:, base + 2 * hd:base + 3 * hd] = acc_t[1].astype(jnp.bfloat16)

def attend_back(img, txt, bias, doi, dot, lse, hd, bq=512):
    img_n, cols = img.shape
    txt_n = txt.shape[0]
    pairs = cols // (6 * hd)
    wide = pl.BlockSpec((img_n, 6 * hd), lambda i: (0, i))
    wide_t = pl.BlockSpec((txt_n, 6 * hd), lambda i: (0, i))
    return pl.pallas_call(
        functools.partial(attend_back_kernel, hd, bq),
        grid=(pairs,),
        in_specs=[
            wide, wide_t,
            pl.BlockSpec((txt_n, 1), lambda i: (0, 0)),
            pl.BlockSpec((img_n, 2 * hd), lambda i: (0, i)),
            pl.BlockSpec((txt_n, 2 * hd), lambda i: (0, i)),
            pl.BlockSpec((1, 2, img_n + txt_n), lambda i: (i, 0, 0)),
        ],
        out_specs=[wide, wide_t],
        out_shape=[jax.ShapeDtypeStruct(img.shape, jnp.bfloat16), jax.ShapeDtypeStruct(txt.shape, jnp.bfloat16)],
        scratch_shapes=[pltpu.VMEM((2, img_n, hd), jnp.float32), pltpu.VMEM((2, txt_n, hd), jnp.float32)],
        compiler_params=pltpu.CompilerParams(vmem_limit_bytes=48 * 1024 * 1024),
        name="attend_back",
    )(img, txt, bias, doi, dot, lse)

HD = 64
FF = 6144
NAD = 8
RANK = 16
EPS = 1e-06
HIGH = lax.Precision.HIGHEST
F32 = jnp.float32
BF16 = jnp.bfloat16
BOTH = ("fsdp", "tp")


def matmul(left, right):
    return jnp.dot(left, right, preferred_element_type=F32)


def exact(left, right):
    return jnp.dot(left, right, precision=HIGH, preferred_element_type=F32)


def inner_left(left, right):
    return lax.dot_general(left, right, (((0,), (0,)), ((), ())), preferred_element_type=F32)


def inner_right(left, right):
    return lax.dot_general(
        left, right, (((left.ndim - 1,), (right.ndim - 1,)), ((), ())), preferred_element_type=F32
    )


def layer_norm(values):
    center = values - jnp.mean(values, axis=-1, keepdims=True)
    inverse = lax.rsqrt(jnp.mean(center * center, axis=-1, keepdims=True) + EPS)
    return (center * inverse, inverse)


def norm_back(grad_normed, normed, inverse, scale):
    grad_hat = grad_normed * (1.0 + scale)
    return inverse * (
        grad_hat
        - jnp.mean(grad_hat, axis=-1, keepdims=True)
        - normed * jnp.mean(grad_hat * normed, axis=-1, keepdims=True)
    )


def gelu(value):
    return jax.nn.gelu(value, approximate=True)


def gelu_back(value, grad):
    return jax.vjp(gelu, value)[1](grad)[0]


def shards(
    image_tokens,
    text_tokens,
    conditioning,
    text_lengths,
    adapter_index,
    adapters,
    mod_weight,
    qkv_weight,
    out_weight,
    fc1_weight,
    fc2_weight,
    image_cot,
    text_cot,
):
    n_f, n_z = lax.axis_size("fsdp"), lax.axis_size("tp")
    f, z = lax.axis_index("fsdp"), lax.axis_index("tp")
    core = f % 2
    slots, quarter, width = image_tokens.shape
    txt_local = text_tokens.shape[0]
    txt_group = txt_local * n_z
    img_half = 2 * quarter
    img_n = 2 * img_half
    cols = [6 * width, 3 * width, width, FF, width]
    fans = [width, width, width, width, FF]

    def round_pairs(r):
        pairs = []
        for fa in range(n_f):
            for t in range(n_z):
                there = (fa // 2 * 2 + t // 2) * n_z + 2 * (fa % 2) + (r ^ (t % 2))
                pairs.append((fa * n_z + t, there))
        return pairs

    low_bit = z % 2

    def pick(stack, bit):
        return lax.dynamic_index_in_dim(stack, bit, 0, keepdims=False)

    def flip(r):
        return low_bit if r == 0 else 1 - low_bit

    def to_chip(parts):
        got = [lax.ppermute(parts[r], BOTH, round_pairs(r)) for r in range(2)]
        return jnp.where(low_bit == 0, got[0], got[1]), jnp.where(low_bit == 0, got[1], got[0])

    def from_chip(pieces):
        got = []
        for r in range(2):
            mine = jnp.where(flip(r) == 0, pieces[0], pieces[1])
            got.append(lax.ppermute(mine, BOTH, [(b, a) for a, b in round_pairs(r)]))
        return jnp.where(low_bit == 0, got[0], got[1]), jnp.where(low_bit == 0, got[1], got[0])

    def reshard(values):
        return jnp.concatenate(to_chip([pick(values, flip(r)) for r in range(2)]), axis=0)

    def unshard(values):
        return jnp.stack(from_chip([values[:quarter], values[quarter:]]))

    def swap_core(values):
        return lax.ppermute(values, "fsdp", [(i, i ^ 1) for i in range(n_f)])

    def by_core(mine, other, axis):
        first = jnp.where(core == 0, mine, other)
        second = jnp.where(core == 0, other, mine)
        return jnp.concatenate([first, second], axis=axis)

    def to_heads(values):
        half = values.shape[1] // 2
        low, high = values[:, :half], values[:, half:]
        mine = jnp.where(core == 0, low, high)
        return by_core(mine, swap_core(jnp.where(core == 0, high, low)), 0)

    def to_tokens(values):
        low, high = values[:img_half], values[img_half:]
        mine = jnp.where(core == 0, low, high)
        return by_core(mine, swap_core(jnp.where(core == 0, high, low)), 1)

    out_t = jnp.swapaxes(out_weight, 1, 2)
    fc2_t = jnp.swapaxes(fc2_weight, 1, 2)
    local = [qkv_weight, out_t, fc1_weight, fc2_t]
    adapter_rows = adapters.astype(BF16).reshape(-1, 128)
    got = gather([w[0] for w in local], [w[1] for w in local] + [adapter_rows], n_f, n_z)
    got = [g.reshape(-1, g.shape[-1]) for g in got]
    img_w, txt_w, row = got[:4], got[4:8], got[8]
    x_img = reshard(image_tokens).astype(F32)
    g_img = reshard(image_cot).astype(F32)
    x_txt = text_tokens.astype(F32)
    g_txt = text_cot.astype(F32)

    seg_ends = jnp.cumsum(text_lengths[0])
    slot_ids = jnp.arange(slots)

    def owner_of(position):
        segment = jnp.sum((position[:, None] >= seg_ends[None, :]).astype(jnp.int32), axis=1)
        return (segment[:, None] == slot_ids[None, :]).astype(F32)

    owner_group = owner_of(jnp.arange(txt_group))
    owner_local = owner_of(z * txt_local + jnp.arange(txt_local))
    txt_mask = jnp.repeat(owner_group, RANK, axis=1)
    seq_mask = jnp.repeat(jnp.eye(slots, dtype=F32), RANK, axis=1)

    def by_group(mine, other):
        return by_core(mine, other, 0)

    column_picks = by_group(adapter_index, swap_core(adapter_index))
    column_count = 2 * slots
    one_hot = (
        jnp.arange(NAD * RANK)[:, None]
        == (column_picks[:, None] * RANK + jnp.arange(RANK)[None, :]).reshape(1, -1)
    ).astype(F32)
    own_picks = adapter_index
    own_hot = lax.dynamic_slice_in_dim(one_hot, core * slots * RANK, slots * RANK, 1)

    a_rows = [[None] * 5 for stream in range(2)]
    b_rows = [[None] * 5 for stream in range(2)]
    offset = 0
    for stream in range(2):
        for index in range(5):
            count = fans[index] // n_z
            a_rows[stream][index] = row[offset : offset + count]
            offset += count
            count = cols[index] // n_z
            b_rows[stream][index] = row[offset : offset + count]
            offset += count

    def b_pick(stream, index, pick_index):
        part = b_rows[stream][index]
        count = part.shape[0] // NAD
        return lax.dynamic_slice_in_dim(part, pick_index * count, count, 0).reshape(RANK, -1)

    def a_pick(rows, hot):
        return inner_right(hot.T.astype(BF16), rows).astype(BF16)

    img_a = a_pick(jnp.concatenate(a_rows[0], axis=0), one_hot)
    fan_share = sum(fans) // n_z
    img_a = img_a.reshape(column_count, RANK, fan_share)
    img_b = [
        jnp.concatenate([b_pick(0, index, column_picks[s]) for index in range(1, 5)], axis=1)
        for s in range(column_count)
    ]
    img_msg = jnp.concatenate([img_a, jnp.stack(img_b)], axis=2)
    txt_rows = jnp.concatenate(
        [a_rows[0][0], a_rows[1][0], a_rows[1][1], a_rows[1][3]], axis=0
    )
    txt_a = a_pick(txt_rows, own_hot).reshape(slots, RANK, -1)
    txt_b_own = [
        [b_pick(stream, index, own_picks[s]) for s in range(slots)]
        for stream, index in [(0, 0), (1, 0), (1, 1), (1, 2), (1, 3), (1, 4)]
    ]
    txt_b_own = [jnp.concatenate(parts, axis=0) for parts in txt_b_own]
    txt_a_own = a_pick(jnp.concatenate([a_rows[1][2], a_rows[1][4]], axis=0), own_hot)
    txt_msg = jnp.concatenate(
        [txt_a.reshape(slots * RANK, -1), txt_b_own[3], txt_b_own[5]], axis=1
    )
    img_got = lax.all_to_all(img_msg, "tp", 0, 0, tiled=False)
    txt_got = lax.all_gather(txt_msg, "tp", axis=0, tiled=False)

    def join(part):
        return jnp.swapaxes(part, 0, 1).reshape(part.shape[1], -1)

    img_pairs = []
    offset, b_offset = 0, fan_share
    for index in range(5):
        count = fans[index] // n_z
        a_full = join(img_got[:, :, offset : offset + count])
        offset += count
        if index == 0:
            img_pairs.append(None)
            continue
        count = cols[index] // n_z
        b_full = join(img_got[:, :, b_offset : b_offset + count])
        b_offset += count
        img_pairs.append((a_full, b_full))
    txt_full = []
    offset = 0
    for count in [width // n_z] * 6:
        txt_full.append(join(txt_got[:, :, offset : offset + count]))
        offset += count
    mod_a = [txt_full[0], txt_full[1]]
    mod_b = [txt_b_own[0], txt_b_own[1]]
    txt_pairs = [
        None,
        (txt_full[2], txt_b_own[2]),
        (txt_a_own[:, : width // n_z], txt_full[4]),
        (txt_full[3], txt_b_own[4]),
        (txt_a_own[:, width // n_z :], txt_full[5]),
    ]

    k_local = mod_weight.shape[1]
    cond_act = jax.nn.silu(conditioning).astype(BF16)
    cond_all = lax.all_gather(cond_act, "fsdp", axis=0, tiled=True)
    cond_slice = lax.dynamic_slice_in_dim(cond_all, f * k_local, k_local, 1)
    mod_part = jnp.stack([matmul(cond_slice, mod_weight[stream]) for stream in range(2)], axis=1)
    mod_part = lax.psum_scatter(mod_part, "fsdp", scatter_dimension=0, tiled=True)
    mod_mid = []
    mod_terms = []
    for stream in range(2):
        middle = (inner_right(cond_act, mod_a[stream]) * seq_mask).astype(BF16)
        mod_mid.append(middle)
        mod_terms.append(mod_part[:, stream] + matmul(middle, mod_b[stream]))
    mods = lax.all_gather(jnp.stack(mod_terms, axis=1), "tp", axis=2, tiled=True)
    img_mods = by_group(mods[:, 0], swap_core(mods[:, 0]))
    img_mod = lax.dynamic_slice_in_dim(img_mods, z, 1, 0)
    txt_mods = mods[:, 1]

    def stretch(stream, index):
        if stream == 0:
            return img_mod[:, index * width : (index + 1) * width]
        return exact(owner_local, txt_mods[:, index * width : (index + 1) * width])

    def collapse(stream, values):
        if stream == 0:
            return jnp.sum(values, axis=0, keepdims=True)
        return exact(owner_local.T, values)

    def share(values):
        return lax.all_gather(values, "tp", axis=0, tiled=True)

    def give(values):
        return lax.psum_scatter(values, "tp", scatter_dimension=0, tiled=True)

    def mine(values):
        return lax.dynamic_slice_in_dim(values, z * txt_local, txt_local, 0)

    def lanes(values):
        count = values.shape[1] // n_z
        return lax.dynamic_slice_in_dim(values, z * count, count, 1)

    inputs = [x_img, x_txt]
    cots = [g_img, g_txt]
    norm_one = [layer_norm(values) for values in inputs]
    heads_in = [
        (norm_one[s][0] * (1.0 + stretch(s, 1)) + stretch(s, 0)).astype(BF16) for s in range(2)
    ]

    def project(values, weight, pair, mask, flipped):
        middle = inner_right(values, pair[0])
        if mask is not None:
            middle = middle * mask
        middle = middle.astype(BF16)
        main = inner_right(values, weight) if flipped else matmul(values, weight)
        return middle, main + matmul(middle, pair[1])

    txt_in = share(heads_in[1])
    txt_qkv_mid, txt_qkv = project(txt_in, txt_w[0], txt_pairs[1], txt_mask, False)
    img_qkv_mid, img_qkv = project(heads_in[0], img_w[0], img_pairs[1], None, False)
    txt_qkv, img_qkv = txt_qkv.astype(BF16), img_qkv.astype(BF16)
    img_heads = to_heads(img_qkv)
    txt_heads = jnp.concatenate(to_chip([txt_qkv, txt_qkv]), axis=1)
    lengths = by_group(text_lengths[0:1], swap_core(text_lengths[0:1]))
    chip_lengths = jnp.cumsum(lax.dynamic_index_in_dim(lengths, z // slots, 0, keepdims=False))
    chip_slot = z % slots
    chip_segment = jnp.sum(
        (jnp.arange(txt_group)[:, None] >= chip_lengths[None, :]).astype(jnp.int32),
        axis=1,
        keepdims=True,
    )
    chip_owner = chip_segment == chip_slot
    bias = jnp.where(chip_owner, 0.0, -1e30).astype(F32)
    o_img, o_txt, lse = attend(img_heads, txt_heads, bias, HD)

    def txt_home(values):
        half = values.shape[1] // 2
        got = from_chip([values[:, :half], values[:, half:]])
        return jnp.where(owner_group[:, 0:1] > 0, got[0], got[1])

    attended = [to_tokens(o_img), txt_home(o_txt)]

    txt_rank = lax.psum(inner_right(attended[1], txt_pairs[2][0]), "tp")
    txt_out_mid = (txt_rank * txt_mask).astype(BF16)
    txt_branch = give(inner_right(attended[1], txt_w[1])) + matmul(
        mine(txt_out_mid), txt_pairs[2][1]
    )
    img_out_mid, img_branch = project(attended[0], img_w[1], img_pairs[2], None, True)
    branch = [img_branch, txt_branch]
    after = [inputs[s] + stretch(s, 2) * branch[s] for s in range(2)]
    norm_two = [layer_norm(values) for values in after]
    mlp_in = [
        (norm_two[s][0] * (1.0 + stretch(s, 4)) + stretch(s, 3)).astype(BF16) for s in range(2)
    ]

    txt_mlp = share(mlp_in[1])
    txt_fc1_mid, txt_pre = project(txt_mlp, txt_w[2], txt_pairs[3], txt_mask, False)
    txt_act = gelu(txt_pre).astype(BF16)
    txt_rank = lax.psum(inner_right(txt_act, txt_pairs[4][0]), "tp")
    txt_fc2_mid = (txt_rank * txt_mask).astype(BF16)
    txt_feed = give(inner_right(txt_act, txt_w[3])) + matmul(mine(txt_fc2_mid), txt_pairs[4][1])
    img_fc1_mid, img_pre = project(mlp_in[0], img_w[2], img_pairs[3], None, False)
    img_act = gelu(img_pre).astype(BF16)
    img_fc2_mid, img_feed = project(img_act, img_w[3], img_pairs[4], None, True)
    feed = [img_feed, txt_feed]
    results = [(after[s] + stretch(s, 5) * feed[s]).astype(BF16) for s in range(2)]
    image_out = unshard(results[0])

    grad_feed = [(stretch(s, 5) * cots[s]).astype(BF16) for s in range(2)]
    grads = [[None] * 5 for stream in range(2)]

    def project_back(grad, weight, pair, mask, flipped):
        middle = inner_right(grad, pair[1])
        if mask is not None:
            middle = middle * mask
        middle = middle.astype(BF16)
        main = matmul(grad, weight) if flipped else inner_right(grad, weight)
        return middle, main + matmul(middle, pair[0])

    img_back_mid, img_grad_act = project_back(grad_feed[0], img_w[3], img_pairs[4], None, True)
    grads[0][4] = (inner_left(img_back_mid, img_act), inner_left(img_fc2_mid, grad_feed[0]))
    img_grad_pre = gelu_back(img_pre, img_grad_act).astype(BF16)
    img_back_mid, img_grad_norm = project_back(img_grad_pre, img_w[2], img_pairs[3], None, False)
    grads[0][3] = (inner_left(img_back_mid, mlp_in[0]), inner_left(img_fc1_mid, img_grad_pre))

    txt_feed_full = share(grad_feed[1])
    txt_back_mid, txt_grad_act = project_back(txt_feed_full, txt_w[3], txt_pairs[4], txt_mask, True)
    grads[1][4] = (
        inner_left(txt_back_mid, txt_act),
        inner_left(txt_fc2_mid, lanes(txt_feed_full)),
    )
    txt_grad_pre = gelu_back(txt_pre, txt_grad_act).astype(BF16)
    txt_back_mid = lax.psum(inner_right(txt_grad_pre, txt_pairs[3][1]), "tp")
    txt_back_mid = (txt_back_mid * txt_mask).astype(BF16)
    grads[1][3] = (
        inner_left(txt_back_mid, lanes(txt_mlp)),
        inner_left(txt_fc1_mid, txt_grad_pre),
    )
    txt_grad_norm = give(inner_right(txt_grad_pre, txt_w[2])) + matmul(
        mine(txt_back_mid), txt_pairs[3][0]
    )
    grad_norm = [img_grad_norm, txt_grad_norm]
    mod_parts = [[None] * 6 for stream in range(2)]
    grad_after = []
    for s in range(2):
        grad_after.append(
            cots[s] + norm_back(grad_norm[s], norm_two[s][0], norm_two[s][1], stretch(s, 4))
        )
        mod_parts[s][3] = collapse(s, grad_norm[s])
        mod_parts[s][4] = collapse(s, grad_norm[s] * norm_two[s][0])
        mod_parts[s][5] = collapse(s, cots[s] * feed[s])
        mod_parts[s][2] = collapse(s, grad_after[s] * branch[s])
    grad_branch = [(stretch(s, 2) * grad_after[s]).astype(BF16) for s in range(2)]

    img_back_mid, img_grad_att = project_back(grad_branch[0], img_w[1], img_pairs[2], None, True)
    grads[0][2] = (inner_left(img_back_mid, attended[0]), inner_left(img_out_mid, grad_branch[0]))
    txt_branch_full = share(grad_branch[1])
    txt_back_mid, txt_grad_att = project_back(
        txt_branch_full, txt_w[1], txt_pairs[2], txt_mask, True
    )
    grads[1][2] = (
        inner_left(txt_back_mid, attended[1]),
        inner_left(txt_out_mid, lanes(txt_branch_full)),
    )
    txt_grad_att = txt_grad_att.astype(BF16)
    do_img = to_heads(img_grad_att.astype(BF16))
    do_txt = jnp.concatenate(to_chip([txt_grad_att, txt_grad_att]), axis=1)
    do_txt = jnp.where(chip_owner, do_txt, jnp.zeros_like(do_txt))
    d_img, d_txt = attend_back(img_heads, txt_heads, bias, do_img, do_txt, lse, HD)
    img_grad_qkv = to_tokens(d_img)
    txt_grad_qkv = txt_home(d_txt)

    img_back_mid, img_grad_norm = project_back(img_grad_qkv, img_w[0], img_pairs[1], None, False)
    grads[0][1] = (inner_left(img_back_mid, heads_in[0]), inner_left(img_qkv_mid, img_grad_qkv))
    txt_back_mid = lax.psum(inner_right(txt_grad_qkv, txt_pairs[1][1]), "tp")
    txt_back_mid = (txt_back_mid * txt_mask).astype(BF16)
    grads[1][1] = (
        inner_left(txt_back_mid, lanes(txt_in)),
        inner_left(txt_qkv_mid, txt_grad_qkv),
    )
    txt_grad_norm = give(inner_right(txt_grad_qkv, txt_w[0])) + matmul(
        mine(txt_back_mid), txt_pairs[1][0]
    )
    grad_norm = [img_grad_norm, txt_grad_norm]
    grad_inputs = []
    for s in range(2):
        grad_inputs.append(
            grad_after[s]
            + norm_back(grad_norm[s], norm_one[s][0], norm_one[s][1], stretch(s, 1))
        )
        mod_parts[s][0] = collapse(s, grad_norm[s])
        mod_parts[s][1] = collapse(s, grad_norm[s] * norm_one[s][0])
    image_grad = unshard(grad_inputs[0])

    img_dmod = jnp.concatenate(mod_parts[0], axis=1)
    img_dmod = (img_dmod + swap_core(img_dmod)).astype(BF16)
    img_dmods = lax.all_gather(img_dmod, "tp", axis=0, tiled=True)
    img_dmods = lax.dynamic_slice_in_dim(img_dmods, core * slots, slots, 0)
    img_dmods = lanes(img_dmods)
    txt_dmod = jnp.concatenate(mod_parts[1], axis=1)
    txt_dmods = lax.psum_scatter(txt_dmod, "tp", scatter_dimension=1, tiled=True).astype(BF16)
    dmods = jnp.stack([img_dmods, txt_dmods], axis=1)
    dmods_all = lax.all_gather(dmods, "fsdp", axis=0, tiled=True)
    cond_part = sum(inner_right(dmods_all[:, s], mod_weight[s]) for s in range(2))
    mod_back = [inner_right(dmods[:, s], mod_b[s]) for s in range(2)]
    cond_slices, mod_rank = lax.psum((cond_part, jnp.stack(mod_back)), "tp")
    cond_rows = lax.all_to_all(cond_slices, "fsdp", 0, 1, tiled=True)
    for s in range(2):
        back_mid = (mod_rank[s] * seq_mask).astype(BF16)
        cond_rows = cond_rows + matmul(back_mid, mod_a[s])
        grads[s][0] = (inner_left(back_mid, lanes(cond_act)), inner_left(mod_mid[s], dmods[:, s]))
    cond_grad = jax.vjp(jax.nn.silu, conditioning)[1](cond_rows)[0]

    def spread(values):
        return jnp.swapaxes(values.reshape(RANK, n_z, -1), 0, 1)

    img_parts = [spread(grads[0][index][side]) for side in range(2) for index in range(1, 5)]
    img_parts = lax.all_to_all(jnp.concatenate(img_parts, axis=2), "tp", 0, 0, tiled=False)
    img_parts = img_parts.reshape(column_count * RANK, -1)
    offset = 0
    img_rows = []
    for sizes in (fans, cols):
        for index in range(1, 5):
            count = sizes[index] // n_z
            img_rows.append(img_parts[:, offset : offset + count])
            offset += count
    flat = []
    for stream in range(2):
        for index in range(5):
            if stream == 0 and index > 0:
                part_a, part_b = img_rows[index - 1], img_rows[index + 3]
                hot = one_hot
            else:
                part_a, part_b = grads[stream][index]
                hot = own_hot
            flat.append(
                lax.dot_general(
                    part_a, hot, (((0,), (1,)), ((), ())),
                    precision=HIGH, preferred_element_type=F32,
                )
            )
            flat.append(exact(hot, part_b).reshape(-1, 128))
    total = jnp.concatenate(flat, axis=0).reshape(n_f, -1, 128)
    step = 1
    while step < n_f:
        bit = (f // step) % 2
        pairs = total.reshape((-1, 2) + total.shape[1:])
        keep = lax.dynamic_index_in_dim(pairs, bit, 1, keepdims=False)
        send = lax.dynamic_index_in_dim(pairs, 1 - bit, 1, keepdims=False)
        sent = lax.ppermute(send.astype(BF16), "fsdp", [(i, i ^ step) for i in range(n_f)])
        total = keep + sent.astype(F32)
        step *= 2
    adapter_grad = total.reshape(1, -1)
    return (image_out, results[1], image_grad, grad_inputs[1], cond_grad, adapter_grad)


def solution(mesh):
    return jax.shard_map(
        shards,
        mesh=mesh,
        in_specs=(
            P("fsdp", "tp", None),
            P(("fsdp", "tp"), None),
            P("fsdp", None),
            P("fsdp", None),
            P("fsdp"),
            P("tp", "fsdp"),
            P(None, "fsdp", "tp"),
            P(None, "fsdp", "tp"),
            P(None, "tp", "fsdp"),
            P(None, "fsdp", "tp"),
            P(None, "tp", "fsdp"),
            P("fsdp", "tp", None),
            P(("fsdp", "tp"), None),
        ),
        out_specs=(
            P("fsdp", "tp", None),
            P(("fsdp", "tp"), None),
            P("fsdp", "tp", None),
            P(("fsdp", "tp"), None),
            P("fsdp", None),
            P("tp", "fsdp"),
        ),
        check_vma=False,
    )
```

time: 3150 us -> 1360 us (0.43)
  waiting for transfers between devices: 1710 us -> 87.6 us
  Pallas kernels: 0 us -> 444 us
  other arithmetic: 509 us -> 72.3 us
  matrix products: 502 us -> 273 us
  local copies, waits for them, and re-layouts: 279 us -> 87.2 us
  blocking collectives: 119 us -> 257 us
  starting transfers between devices: 2.3 us -> 99.9 us
    reduce_scatter x8 -> x4, waiting for transfers between devices: 846 us -> 0.02 us  [give(): return lax.psum_scatter(values, 'tp', scatter_dimension=0, tiled=True)]
    all_gather x10 -> x0, waiting for transfers between devices: 686 us -> none  [the longest x1 201 us: shards(): lax.all_gather(adapters.astype(jnp.bfloat16).reshape(-1), ('fsdp', 'tp'),...]
    pallas_call x0 -> x3, Pallas kernels: none -> 444 us  [the longest x1 349 us: gather(): pl.pallas_call(functools.partial(gather_kernel, n_f, n_z, len(full), len(...]
    all_gather x1 -> x0, other arithmetic: 383 us -> none  [shards(): lax.all_gather(adapters.astype(jnp.bfloat16).reshape(-1), ('fsdp', 'tp'),...]
    dot_general x55 -> x62, matrix products: 333 us -> 149 us  [the longest x30 119 us: matmul(): return jnp.dot(left, right, preferred_element_type=F32)]
    unnamed x26 -> x8, waiting for transfers between devices: 175 us -> 0.1 us
    all_gather x5 -> x9, blocking collectives: 73.5 us -> 200 us  [the longest x1 77 us: shards(): img_dmods = lax.all_gather(img_dmod, 'tp', axis=0, tiled=True)]
    unnamed x444 -> x402, local copies, waits for them, and re-layouts: 131 us -> 39.5 us
  transfers between devices with their start and end apart: 24 -> 36, of which waited for: 16 -> 10; matrix products, arithmetic and copies ran while one was open for 29% -> 31% of each run, Pallas kernels for 0% -> 30%
where the time goes in v1:
time: 1360 us; the launch traced here: 1350 us
  Pallas kernels  444 us (33%)
  matrix products  273 us (20%)
  blocking collectives  257 us (19%)
  starting transfers between devices  99.9 us (7%)
  waiting for transfers between devices  87.6 us (6%)
  local copies, waits for them, and re-layouts  87.2 us (6%)
  other arithmetic  72.3 us (5%)
  between operations  30.5 us (2%)
    pallas_call x1, Pallas kernels, gather(): pl.pallas_call(functools.partial(gather_kernel, n_f, n_z, len(full), len(...  349 us
    dot_general x30, matrix products, matmul(): return jnp.dot(left, right, preferred_element_type=F32)  119 us
    dot_general x33, matrix products, inner_right(): lax.dot_general(left, right, (((left.ndim - 1,), (right.ndim - 1,)), ((),...  104 us
    all_gather x1, blocking collectives, shards(): img_dmods = lax.all_gather(img_dmod, 'tp', axis=0, tiled=True)  77 us
    ppermute x8, waiting for transfers between devices, from_chip(): got.append(lax.ppermute(mine, BOTH, [(b, a) for a, b in round_pairs(r)]))  73.5 us
    all_gather x4, blocking collectives, share(): return lax.all_gather(values, 'tp', axis=0, tiled=True)  66.4 us
    pallas_call x1, Pallas kernels, attend_back(): pl.pallas_call(functools.partial(attend_back_kernel, hd, bq), grid=(pairs...  58.6 us
    ppermute x8, starting transfers between devices, to_chip(): got = [lax.ppermute(parts[r], BOTH, round_pairs(r)) for r in range(2)]  43.7 us
  transfers between devices with their start and end apart: 36, of which 10 were waited for; matrix products, arithmetic and copies ran while one was open for 31% of the time, Pallas kernels for 30%

profile of v1, /device:TPU:11, one launch (start us, length us, event | category | flops | bytes accessed | tf_op | source)
XLA Modules:
  0.0 1351.0 jit_solution(4095549121535523821)
XLA Ops:
  8.8 9.5 all-gather.1
  23.4 4.3 collective-permute-start
  29.0 4.4 collective-permute-start.13
  40.7 13.5 convert_reduce_fusion.1
  59.1 348.7 %weight_gather.1 = (bf16[8,192,4608]{2,1,0:T(8,128)(2,1)}, bf16[8,192,1536]{2,1,0:T(8,128)(2,1)}, bf16[8,192,6144]{2,1,0:T(8,128)(2,1)}, bf16[8,192,6144]{2,1,0:...) custom-call(bf16[192,1152]{1,0:T(8,128)(2,1)} %get-tuple-element.120, ...), custom_call_target="tpu_custom_call" | custom-call | tf_op jit(solution)/shard_map/weight_gather/pallas_call | solution.py:236
  424.2 6.5 collective-permute-start.14
  444.0 15.1 %all-gather = bf16[128,2304]{1,0:T(8,128)(2,1)S(1)} all-gather(bf16[32,2304]{1,0:T(8,128)(2,1)S(1)} %maximum_maximum_fusion.1), channel_id=2, replica_groups=mesh['fsdp'=8,'tp'=4] {'tp'}, dimensions={0}, use_global_device_ids=true | all-gather | bytes 737280 | tf_op jit(solution)/shard_map/all_gather | solution.py:585
  464.6 5.3 all-to-all-start
  473.2 21.0 %all_gather.33 = f32[2,2,9216]{2,0,1:T(2,128)S(1)} all-gather(f32[2,2,2304]{2,0,1:T(2,128)S(1)} %pad_maximum_fusion.18), channel_id=1, replica_groups=mesh['fsdp'=8,'tp'=4] {'tp'}, dimensions={2}, use_global_device_ids=true | all-gather | bytes 184320 | tf_op jit(solution)/shard_map/all_gather | solution.py:630
  499.4 13.6 %all_gather.34 = bf16[160,1536]{1,0:T(8,128)(2,1)S(1)} all-gather(bf16[40,1536]{1,0:T(8,128)(2,1)S(1)} %fusion.27), channel_id=1, replica_groups=mesh['fsdp'=8,'tp'=4] {'tp'}, dimensions={0}, use_global_device_ids=true | all-gather | bytes 614400 | tf_op jit(solution)/shard_map/all_gather | solution.py:646
  514.0 12.6 all_gather.36
  528.6 4.2 fusion.229
  534.9 4.2 collective-permute-start.6
  540.0 5.0 collective-permute-start.5
  548.0 13.4 fusion.218
  563.9 5.1 add_convert_fusion
  577.7 6.3 fusion.226
  587.0 36.6 %attend.1 = (bf16[1024,768]{1,0:T(8,128)(2,1)S(1)}, bf16[160,768]{1,0:T(8,128)(2,1)S(1)}, f32[6,2,1184]{2,1,0:T(2,128)S(1)}) custom-call(bf16[1024,2304]{1,0:T(8,128)(2,1)} %pad_maximum_fusion.img_ref, bf16[160,2304]{1,0:T(8,128)(2,1)S(1)} %pad_maximum_fusion.13.txt_ref, f32[160,1]{1,0:T(8,128)S(1)} %copy.122.bias_ref), custom_call_target="tpu_custom_call" | custom-call | tf_op jit(solution)/shard_map/attend/pallas_call | solution.py:287
  636.5 11.6 psum.42
  655.2 6.8 fusion.208
  664.1 6.3 fusion.221
  670.4 26.1 %multiply_convert_fusion = (bf16[512,6144]{1,0:T(8,128)(2,1)}, f32[512,6144]{1,0:T(8,128)}) fusion(f32[512,6144]{1,0:T(8,128)} %fusion.221, bf16[512,1536]{1,0:T(8,128)(2,1)S(1)} %add_convert_fusion.2, bf16[1536,6144]{1,0:T(8,128)(2,1)} %bitcast.531), kind=kOutput, calls=%fused_computation.9 | convolution fusion | flops 9695133696 | bytes 51904512 | tf_op jit(solution)/shard_map/dot_general | solution.py:389
  696.6 4.5 convolution_convert_fusion.8
  703.4 22.4 %fusion.6 = bf16[512,6144]{1,0:T(8,128)(2,1)S(1)} fusion(f32[512,6144]{1,0:T(8,128)} %get-tuple-element.192, f32[512,6144]{1,0:T(8,128)} %fusion.226, bf16[1536,6144]{1,0:T(8,128)(2,1)} %bitcast.529, f32[1536]{0:T(1024)S(1)} %copy-done.154, bf16[256,1536]{1,0:T(8,128)(2,1)S(1)} %copy-done.73, bf16[256,1536]{1,0:T(8,128)(2,1)S(1)} %copy-done.70), kind=kOutput, calls=%fused_computation.8 | convolution fusion | flops 9734455296 | bytes 51910656 | tf_op jit(solution)/shard_map/dot_general | solution.py:389
  730.8 19.5 %multiply_reduce_fusion = (f32[1536]{0:T(1024)}, f32[512]{0:T(512)S(1)}, f32[512]{0:T(512)S(1)}, f32[1536]{0:T(1024)}, f32[512,1536]{1,0:T(8,128)}) fusion(f32[512,1536]{1,0:T(8,128)} %copy-done.13, f32[512]{0:T(512)S(1)} %add_rsqrt_fusion, f32[512]{0:T(512)S(1)} %broadcast_multiply_fusion.4, f32[1536]{0:T(1024)S(1)} %copy-done.130, ...), kind=kOutput, calls=%fused_computation.51 | convolution fusion | flops 9671536640 | bytes 34629632 | tf_op jit(solution)/shard_map/dot_general | solution.py:401
  750.3 18.9 %fusion.24 = (f32[1536]{0:T(1024)}, bf16[512,1536]{1,0:T(8,128)(2,1)S(1)}, f32[1536]{0:T(1024)}, f32[512,1536]{1,0:T(8,128)S(1)}) fusion(bf16[256,1536]{1,0:T(8,128)(2,1)} %copy-done.72, bf16[256,1536]{1,0:T(8,128)(2,1)} %copy-done.69, f32[512,1536]{1,0:T(8,128)} %copy-done.13, f32[1536]{0:T(1024)S(1)} %copy-done.154, f32[512,1536]{1,0:T(8,128)} %get-tuple-element.190, ...), kind=kOutput, calls=%fused_computation.49 | convolution fusion | flops 9679400960 | bytes 44072960 | tf_op jit(solution)/shard_map/dot_general | solution.py:401
  769.6 5.3 fusion.228
  799.6 28.7 %all_gather.35 = bf16[160,1536]{1,0:T(8,128)(2,1)S(1)} all-gather(bf16[40,1536]{1,0:T(8,128)(2,1)S(1)} %fusion.28), channel_id=1, replica_groups=mesh['fsdp'=8,'tp'=4] {'tp'}, dimensions={0}, use_global_device_ids=true | all-gather | bytes 614400 | tf_op jit(solution)/shard_map/all_gather | solution.py:646
  839.0 15.1 %psum.44 = f32[160,32]{0,1:T(8,128)S(1)} all-reduce(f32[160,32]{0,1:T(8,128)} %fusion.231), channel_id=1, replica_groups=mesh['fsdp'=8,'tp'=4] {'tp'}, use_global_device_ids=true, to_apply=%region_21.22 | all-reduce | flops 5120 | bytes 40960 | tf_op jit(solution)/shard_map/psum | solution.py:748
  862.2 5.0 fusion.225
  869.0 11.6 all_gather.37
  884.2 16.3 %collective-permute-start.17 = (bf16[160,384]{1,0:T(8,128)(2,1)S(1)}, bf16[160,384]{1,0:T(8,128)(2,1)S(1)}, u32[]{:S(2)}, u32[]{:S(2)}) collective-permute-start(bf16[160,384]{1,0:T(8,128)(2,1)S(1)} %fusion.37), channel_id=1, source_target_pairs={{0,1},{1,0},{2,5},{3,4},{4,3},{5,2},{6,7},{7,6},{8,9},{9,8},{10,13... | collective-permute-start | bytes 368648 | tf_op jit(solution)/shard_map/ppermute | solution.py:472
  908.4 58.6 %attend_back.1 = (bf16[1024,2304]{1,0:T(8,128)(2,1)}, bf16[160,2304]{1,0:T(8,128)(2,1)S(1)}) custom-call(bf16[1024,2304]{1,0:T(8,128)(2,1)} %pad_maximum_fusion.img_ref, bf16[160,2304]{1,0:T(8,128)(2,1)S(1)} %copy-done.1, f32[160,1]{1,0:T(8,128)S(1)} %copy.122.bias_ref, bf16[1024,768]{1,0:T(8,128)(2,1)S(1)} %pad_maximum_fusion.7.doi_ref, ...), custom_call_target="tpu_custom_call" | custom-call | tf_op jit(solution)/shard_map/attend_back/pallas_call | solution.py:360
  967.1 4.6 collective-permute-start.21
  974.7 9.1 collective-permute-done.21
  983.8 4.9 collective-permute-done.22
  988.9 4.3 fusion.233
  997.6 16.1 %all-reduce.2 = (f32[160,32]{0,1:T(8,128)S(1)}, f32[160,32]{0,1:T(8,128)S(1)}) all-reduce(f32[160,32]{0,1:T(8,128)S(1)} %copy-done.104, f32[160,32]{0,1:T(8,128)S(1)} %fusion.234), channel_id=1, replica_groups=mesh['fsdp'=8,'tp'=4] {'tp'}, use_global_device_ids=true, to_apply=%region_17.18 | all-reduce | flops 10240 | bytes 81920 | tf_op jit(solution)/shard_map/psum | solution.py:714
  1040.4 16.7 %fusion.21 = (f32[1536]{0:T(1024)S(1)}, f32[512]{0:T(512)}, f32[512]{0:T(512)}, f32[1536]{0:T(1024)S(1)}, f32[512,1536]{1,0:T(8,128)}) fusion(f32[512]{0:T(512)S(1)} %copy-done.138, f32[512]{0:T(512)S(1)} %copy-done.133, bf16[256,1536]{1,0:T(8,128)(2,1)S(1)} %copy-done.6, bf16[256,1536]{1,0:T(8,128)(2,1)S(1)} %copy-done.4, f32[1536]{0:T(1024)S(1)} %copy-done.114, ...), kind=kOutput, calls=%fused_computation.46 | convolution fusion | flops 7268200448 | bytes 26765312 | tf_op jit(solution)/shard_map/dot_general | solution.py:401
  1069.0 5.6 all-to-all-start.2
  1075.4 77.0 %all-gather.2 = bf16[4,1,9216]{2,1,0:T(2,128)(2,1)S(1)} all-gather(bf16[1,1,9216]{2,1,0:T(2,128)(2,1)S(1)} %convert_bitcast_fusion), channel_id=1, replica_groups=mesh['fsdp'=8,'tp'=4] {'tp'}, dimensions={0}, use_global_device_ids=true | all-gather | bytes 92160 | tf_op jit(solution)/shard_map/all_gather | solution.py:812
  1160.2 10.5 all_gather.39
  1182.6 14.4 %all-reduce.1 = (f32[8,2,192]{2,1,0:T(2,128)}, f32[2,2,32]{2,1,0:T(2,128)S(1)}) all-reduce(f32[8,2,192]{2,1,0:T(2,128)} %all_to_all.21, f32[2,2,32]{2,1,0:T(2,128)S(1)} %pad_maximum_fusion.20), channel_id=1, replica_groups=mesh['fsdp'=8,'tp'=4] {'tp'}, use_global_device_ids=true, to_apply=%region_37.38 | all-reduce | flops 3200 | bytes 25600 | tf_op jit(solution)/shard_map/psum | solution.py:821
  1258.2 4.9 all-to-all-start.1
  1267.1 4.3 collective-permute-start.19
  1272.2 10.2 all-to-all-done.1
  1286.5 19.8 %collective-permute-done.19 = f32[256,1536]{1,0:T(8,128)S(1)} collective-permute-done((f32[256,1536]{1,0:T(8,128)}, f32[256,1536]{1,0:T(8,128)S(1)}, u32[]{:S(2)}, u32[]{:S(2)}) %collective-permute-start.19) | collective-permute-done | bytes 1572896 | tf_op jit(solution)/shard_map/ppermute | solution.py:479
  1306.3 34.4 %collective-permute-done.20 = f32[256,1536]{1,0:T(8,128)S(1)} collective-permute-done((f32[256,1536]{1,0:T(8,128)}, f32[256,1536]{1,0:T(8,128)S(1)}, u32[]{:S(2)}, u32[]{:S(2)}) %collective-permute-start.20) | collective-permute-done | bytes 1572896 | tf_op jit(solution)/shard_map/ppermute | solution.py:479
  (752 shorter events, 297.4 us)
Async XLA Ops:
  7.2 463.8 %all-reduce.5.cloned.1.call-start = ((), (), s32[]{:S(2)}) async-start(), calls=%async_computation.13 | async-start | bytes 589824
  7.2 432.4 %collective-permute-start.7 = (s32[1,2]{1,0:T(1,128)}, s32[1,2]{1,0:T(1,128)}, u32[]{:S(2)}, u32[]{:S(2)}) collective-permute-start(s32[1,2]{1,0:T(1,128)} %param.16), channel_id=1, source_target_pairs={{0,4},{4,0},{8,12},{12,8},{16,20},{20,16},{24,28},{28,24},{1,5},{5... | collective-permute-start | bytes 32 | tf_op jit(solution)/shard_map/ppermute | solution.py:489
  8.0 416.2 %collective-permute-start.2 = (s32[2]{0:T(128)}, s32[2]{0:T(128)}, u32[]{:S(2)}, u32[]{:S(2)}) collective-permute-start(s32[2]{0:T(128)} %param.17), channel_id=1, source_target_pairs={{0,4},{4,0},{8,12},{12,8},{16,20},{20,16},{24,28},{28,24},{1,5},{5... | collective-permute-start | bytes 32 | tf_op jit(solution)/shard_map/ppermute | solution.py:489
  23.4 516.6 %collective-permute-start = (bf16[256,1536]{1,0:T(8,128)(2,1)}, bf16[256,1536]{1,0:T(8,128)(2,1)}, u32[]{:S(2)}, u32[]{:S(2)}) collective-permute-start(bf16[256,1536]{1,0:T(8,128)(2,1)} %get-tuple-element.113), channel_id=1, source_target_pairs={{0,0},{1,1},{2,4},{3,5},{4,2},{5,3},{6,6},{7,7},{8,8},{9,9},{10,12... | collective-permute-start | bytes 2359304 | tf_op jit(solution)/shard_map/ppermute | solution.py:472
  27.7 517.3 %collective-permute-start.1 = (bf16[256,1536]{1,0:T(8,128)(2,1)}, bf16[256,1536]{1,0:T(8,128)(2,1)}, u32[]{:S(2)}, u32[]{:S(2)}) collective-permute-start(bf16[256,1536]{1,0:T(8,128)(2,1)} %get-tuple-element.114), channel_id=1, source_target_pairs={{0,1},{1,0},{2,5},{3,4},{4,3},{5,2},{6,7},{7,6},{8,9},{9,8},{10,13... | collective-permute-start | bytes 2359304 | tf_op jit(solution)/shard_map/ppermute | solution.py:472
  29.0 542.1 %collective-permute-start.13 = (bf16[256,1536]{1,0:T(8,128)(2,1)}, bf16[256,1536]{1,0:T(8,128)(2,1)}, u32[]{:S(2)}, u32[]{:S(2)}) collective-permute-start(bf16[256,1536]{1,0:T(8,128)(2,1)} %get-tuple-element.105), channel_id=1, source_target_pairs={{0,0},{1,1},{2,4},{3,5},{4,2},{5,3},{6,6},{7,7},{8,8},{9,9},{10,12... | collective-permute-start | bytes 2359304 | tf_op jit(solution)/shard_map/ppermute | solution.py:472
  412.6 121.3 %copy-start.111 = (s32[40]{0:T(128)}, s32[40]{0:T(128)S(1)}, u32[]{:S(2)}) copy-start(s32[40]{0:T(128)S(1)} %fusion.174) | copy-start | bytes 484
  424.1 108.7 %copy-start.77 = (bf16[32,1152]{1,0:T(8,128)(2,1)}, bf16[32,1152]{1,0:T(8,128)(2,1)S(1)}, u32[]{:S(2)}) copy-start(bf16[32,1152]{1,0:T(8,128)(2,1)S(1)} %constant_dynamic-update-slice_fusion.8) | copy-start | bytes 221188
  424.2 147.0 %collective-permute-start.14 = (bf16[256,1536]{1,0:T(8,128)(2,1)}, bf16[256,1536]{1,0:T(8,128)(2,1)}, u32[]{:S(2)}, u32[]{:S(2)}) collective-permute-start(bf16[256,1536]{1,0:T(8,128)(2,1)} %get-tuple-element.106), channel_id=1, source_target_pairs={{0,1},{1,0},{2,5},{3,4},{4,3},{5,2},{6,7},{7,6},{8,9},{9,8},{10,13... | collective-permute-start | bytes 2359304 | tf_op jit(solution)/shard_map/ppermute | solution.py:472
  463.7 64.1 %copy-start.54 = (bf16[4,8,4,384]{3,1,2,0:T(8,128)(2,1)}, bf16[4,8,4,384]{3,1,2,0:T(8,128)(2,1)S(1)}, u32[]{:S(2)}) copy-start(bf16[4,8,4,384]{3,1,2,0:T(8,128)(2,1)S(1)} %copy.180) | copy-start | bytes 294916
  464.5 187.2 %copy-start.57 = (bf16[4,8,4,384]{3,1,2,0:T(8,128)(2,1)}, bf16[4,8,4,384]{3,1,2,0:T(8,128)(2,1)S(1)}, u32[]{:S(2)}) copy-start(bf16[4,8,4,384]{3,1,2,0:T(8,128)(2,1)S(1)} %copy.178) | copy-start | bytes 294916
  464.6 62.9 %copy-start.52 = (bf16[4,8,4,384]{3,1,2,0:T(8,128)(2,1)}, bf16[4,8,4,384]{3,1,2,0:T(8,128)(2,1)S(1)}, u32[]{:S(2)}) copy-start(bf16[4,8,4,384]{3,1,2,0:T(8,128)(2,1)S(1)} %copy.177) | copy-start | bytes 294916
  464.6 96.8 %all-to-all-start = ((bf16[4,16,6528]{2,1,0:T(8,128)(2,1)}), bf16[4,16,6528]{2,1,0:T(8,128)(2,1)}, u32[]{:S(2)}, u32[]{:S(2)}) async-start(bf16[4,16,6528]{2,1,0:T(8,128)(2,1)} %maximum_maximum_fusion), calls=%async_computation | async-start | bytes 1671168 | tf_op jit(solution)/shard_map/all_to_all | solution.py:584
  469.9 326.6 %reduce-scatter.9.cloned.1.call-start = ((), (), s32[]{:S(2)}) async-start(), calls=%async_computation.8 | async-start | bytes 1228800 | tf_op jit(solution)/shard_map/reduce_scatter | solution.py:649
  471.0 55.6 %copy-start.7 = (bf16[8,192,1152]{2,1,0:T(8,128)(2,1)S(1)}, bf16[8,192,1152]{2,1,0:T(8,128)(2,1)}, u32[]{:S(2)}) copy-start(bf16[8,192,1152]{2,1,0:T(8,128)(2,1)} %get-tuple-element.22) | copy-start | bytes 10616836
  495.6 39.2 %collective-permute-start.3 = (f32[2,9216]{1,0:T(2,128)S(1)}, f32[2,9216]{1,0:T(2,128)S(1)}, u32[]{:S(2)}, u32[]{:S(2)}) collective-permute-start(f32[2,9216]{1,0:T(2,128)S(1)} %get-tuple-element.165), channel_id=1, source_target_pairs={{0,4},{4,0},{8,12},{12,8},{16,20},{20,16},{24,28},{28,24},{1,5},{5... | collective-permute-start | bytes 221192 | tf_op jit(solution)/shard_map/ppermute | solution.py:489
  534.9 35.1 %collective-permute-start.6 = (bf16[160,1152]{1,0:T(8,128)(2,1)}, bf16[160,1152]{1,0:T(8,128)(2,1)}, u32[]{:S(2)}, u32[]{:S(2)}) collective-permute-start(bf16[160,1152]{1,0:T(8,128)(2,1)} %fusion.26), channel_id=1, source_target_pairs={{0,1},{1,0},{2,5},{3,4},{4,3},{5,2},{6,7},{7,6},{8,9},{9,8},{10,13... | collective-permute-start | bytes 1105928 | tf_op jit(solution)/shard_map/ppermute | solution.py:472
  540.0 30.0 %collective-permute-start.5 = (bf16[160,1152]{1,0:T(8,128)(2,1)}, bf16[160,1152]{1,0:T(8,128)(2,1)}, u32[]{:S(2)}, u32[]{:S(2)}) collective-permute-start(bf16[160,1152]{1,0:T(8,128)(2,1)} %fusion.26), channel_id=1, source_target_pairs={{0,0},{1,1},{2,4},{3,5},{4,2},{5,3},{6,6},{7,7},{8,8},{9,9},{10,12... | collective-permute-start | bytes 1105928 | tf_op jit(solution)/shard_map/ppermute | solution.py:472
  546.4 108.7 %copy-start.3 = (bf16[256,1536]{1,0:T(8,128)(2,1)}, bf16[256,1536]{1,0:T(8,128)(2,1)S(1)}, u32[]{:S(2)}) copy-start(bf16[256,1536]{1,0:T(8,128)(2,1)S(1)} %get-tuple-element.111) | copy-start | bytes 2359300
  546.4 108.7 %copy-start.5 = (bf16[256,1536]{1,0:T(8,128)(2,1)}, bf16[256,1536]{1,0:T(8,128)(2,1)S(1)}, u32[]{:S(2)}) copy-start(bf16[256,1536]{1,0:T(8,128)(2,1)S(1)} %get-tuple-element.112) | copy-start | bytes 2359300
  569.3 14.7 %collective-permute-start.4 = (bf16[512,2304]{1,0:T(8,128)(2,1)S(1)}, bf16[512,2304]{1,0:T(8,128)(2,1)S(1)}, u32[]{:S(2)}, u32[]{:S(2)}) collective-permute-start(bf16[512,2304]{1,0:T(8,128)(2,1)S(1)} %broadcast_select_fusion.6), channel_id=1, source_target_pairs={{0,4},{4,0},{8,12},{12,8},{16,20},{20,16},{24,28},{28,24},{1,5},{5... | collective-permute-start | bytes 7077896 | tf_op jit(solution)/shard_map/ppermute | solution.py:489
  623.7 7.8 collective-permute-start.11
  625.6 9.3 collective-permute-start.12
  629.6 23.0 %collective-permute-start.8 = (bf16[512,768]{1,0:T(8,128)(2,1)}, bf16[512,768]{1,0:T(8,128)(2,1)}, u32[]{:S(2)}, u32[]{:S(2)}) collective-permute-start(bf16[512,768]{1,0:T(8,128)(2,1)} %broadcast_select_fusion.15), channel_id=1, source_target_pairs={{0,4},{4,0},{8,12},{12,8},{16,20},{20,16},{24,28},{28,24},{1,5},{5... | collective-permute-start | bytes 2359304 | tf_op jit(solution)/shard_map/ppermute | solution.py:489
  651.6 215.8 %reduce-scatter.13.cloned.1.call-start = ((), (), s32[]{:S(2)}) async-start(), calls=%async_computation.10 | async-start | bytes 1228800 | tf_op jit(solution)/shard_map/reduce_scatter | solution.py:649
  777.1 18.1 %collective-permute-start.15 = (bf16[512,768]{1,0:T(8,128)(2,1)S(1)}, bf16[512,768]{1,0:T(8,128)(2,1)S(1)}, u32[]{:S(2)}, u32[]{:S(2)}) collective-permute-start(bf16[512,768]{1,0:T(8,128)(2,1)S(1)} %broadcast_select_fusion.11), channel_id=1, source_target_pairs={{0,4},{4,0},{8,12},{12,8},{16,20},{20,16},{24,28},{28,24},{1,5},{5... | collective-permute-start | bytes 2359304 | tf_op jit(solution)/shard_map/ppermute | solution.py:489
  781.5 462.5 %collective-permute-start.9 = (bf16[256,1536]{1,0:T(8,128)(2,1)}, bf16[256,1536]{1,0:T(8,128)(2,1)}, u32[]{:S(2)}, u32[]{:S(2)}) collective-permute-start(bf16[256,1536]{1,0:T(8,128)(2,1)} %get-tuple-element.109), channel_id=1, source_target_pairs={{0,0},{1,1},{4,2},{5,3},{2,4},{3,5},{6,6},{7,7},{8,8},{9,9},{12,10... | collective-permute-start | bytes 2359304 | tf_op jit(solution)/shard_map/ppermute | solution.py:479
  785.7 458.3 %collective-permute-start.10 = (bf16[256,1536]{1,0:T(8,128)(2,1)}, bf16[256,1536]{1,0:T(8,128)(2,1)}, u32[]{:S(2)}, u32[]{:S(2)}) collective-permute-start(bf16[256,1536]{1,0:T(8,128)(2,1)} %get-tuple-element.110), channel_id=1, source_target_pairs={{1,0},{0,1},{5,2},{4,3},{3,4},{2,5},{7,6},{6,7},{9,8},{8,9},{13,10... | collective-permute-start | bytes 2359304 | tf_op jit(solution)/shard_map/ppermute | solution.py:479
  836.3 182.7 %reduce-scatter.11.cloned.1.call-start = ((), (), s32[]{:S(2)}) async-start(), calls=%async_computation.9 | async-start | bytes 1228800 | tf_op jit(solution)/shard_map/reduce_scatter | solution.py:649
  867.3 153.6 %reduce-scatter.15.cloned.1.call-start = ((), (), s32[]{:S(2)}) async-start(), calls=%async_computation.11 | async-start | bytes 1228800 | tf_op jit(solution)/shard_map/reduce_scatter | solution.py:649
  868.9 156.5 %copy-start.29 = (f32[40,1536]{1,0:T(8,128)}, f32[40,1536]{1,0:T(8,128)S(1)}, u32[]{:S(2)}) copy-start(f32[40,1536]{1,0:T(8,128)S(1)} %get-tuple-element.60) | copy-start | bytes 737284
  884.2 21.3 %collective-permute-start.17 = (bf16[160,384]{1,0:T(8,128)(2,1)S(1)}, bf16[160,384]{1,0:T(8,128)(2,1)S(1)}, u32[]{:S(2)}, u32[]{:S(2)}) collective-permute-start(bf16[160,384]{1,0:T(8,128)(2,1)S(1)} %fusion.37), channel_id=1, source_target_pairs={{0,1},{1,0},{2,5},{3,4},{4,3},{5,2},{6,7},{7,6},{8,9},{9,8},{10,13... | collective-permute-start | bytes 368648 | tf_op jit(solution)/shard_map/ppermute | solution.py:472
  900.5 7.1 collective-permute-start.16
  908.3 65.6 %copy-start.36 = (bf16[160,384]{1,0:T(8,128)(2,1)S(1)}, bf16[160,384]{1,0:T(8,128)(2,1)}, u32[]{:S(2)}) copy-start(bf16[160,384]{1,0:T(8,128)(2,1)} %copy-done.35) | copy-start | bytes 368644
  908.4 80.4 %copy-start.161 = (pred[160]{0:T(512)(128)(4,1)S(1)}, pred[160]{0:T(512)(128)(4,1)}, u32[]{:S(2)}) copy-start(pred[160]{0:T(512)(128)(4,1)} %compare_reduce_fusion) | copy-start | bytes 484
  967.1 16.7 %collective-permute-start.21 = (bf16[160,1152]{1,0:T(8,128)(2,1)S(1)}, bf16[160,1152]{1,0:T(8,128)(2,1)S(1)}, u32[]{:S(2)}, u32[]{:S(2)}) collective-permute-start(bf16[160,1152]{1,0:T(8,128)(2,1)S(1)} %get-tuple-element.128), channel_id=1, source_target_pairs={{0,0},{1,1},{4,2},{5,3},{2,4},{3,5},{6,6},{7,7},{8,8},{9,9},{12,10... | collective-permute-start | bytes 1105928 | tf_op jit(solution)/shard_map/ppermute | solution.py:479
  971.7 17.0 %collective-permute-start.22 = (bf16[160,1152]{1,0:T(8,128)(2,1)S(1)}, bf16[160,1152]{1,0:T(8,128)(2,1)S(1)}, u32[]{:S(2)}, u32[]{:S(2)}) collective-permute-start(bf16[160,1152]{1,0:T(8,128)(2,1)S(1)} %get-tuple-element.129), channel_id=1, source_target_pairs={{1,0},{0,1},{5,2},{4,3},{3,4},{2,5},{7,6},{6,7},{9,8},{8,9},{13,10... | collective-permute-start | bytes 1105928 | tf_op jit(solution)/shard_map/ppermute | solution.py:479
  993.2 165.3 %reduce-scatter.17.cloned.1.call-start = ((), (), s32[]{:S(2)}) async-start(), calls=%async_computation.12 | async-start | bytes 5898240
  997.3 32.3 %collective-permute-start.18 = (bf16[512,2304]{1,0:T(8,128)(2,1)}, bf16[512,2304]{1,0:T(8,128)(2,1)}, u32[]{:S(2)}, u32[]{:S(2)}) collective-permute-start(bf16[512,2304]{1,0:T(8,128)(2,1)} %broadcast_select_fusion.2), channel_id=1, source_target_pairs={{0,4},{4,0},{8,12},{12,8},{16,20},{20,16},{24,28},{28,24},{1,5},{5... | collective-permute-start | bytes 7077896 | tf_op jit(solution)/shard_map/ppermute | solution.py:489
  1060.7 13.9 %collective-permute-start.23 = (f32[1,9216]{1,0:T(1,128)}, f32[1,9216]{1,0:T(1,128)}, u32[]{:S(2)}, u32[]{:S(2)}) collective-permute-start(f32[1,9216]{1,0:T(1,128)} %constant_dynamic-update-slice_fusion.12), channel_id=1, source_target_pairs={{0,4},{4,0},{8,12},{12,8},{16,20},{20,16},{24,28},{28,24},{1,5},{5... | collective-permute-start | bytes 110600 | tf_op jit(solution)/shard_map/ppermute | solution.py:489
  1064.8 87.8 %copy-start.164 = (bf16[2,32]{1,0:T(2,128)(2,1)S(1)}, bf16[2,32]{1,0:T(2,128)(2,1)}, u32[]{:S(2)}) copy-start(bf16[2,32]{1,0:T(2,128)(2,1)} %copy-done.163) | copy-start | bytes 388
  1069.0 133.7 %all-to-all-start.2 = ((f32[4,16,6144]{2,1,0:T(8,128)}), f32[4,16,6144]{2,1,0:T(8,128)S(1)}, u32[]{:S(2)}, u32[]{:S(2)}) async-start(f32[4,16,6144]{2,1,0:T(8,128)} %constant_dynamic-update-slice_fusion.18), calls=%async_computation.6 | async-start | bytes 3145728 | tf_op jit(solution)/shard_map/all_to_all | solution.py:833
  1240.0 8.3 collective-permute-start.24
  1255.0 28.3 %collective-permute-start.25 = (bf16[2,2208,128]{2,1,0:T(8,128)(2,1)}, bf16[2,2208,128]{2,1,0:T(8,128)(2,1)}, u32[]{:S(2)}, u32[]{:S(2)}) collective-permute-start(bf16[2,2208,128]{2,1,0:T(8,128)(2,1)} %fusion.38), channel_id=1, source_target_pairs={{0,8},{4,12},{8,0},{12,4},{16,24},{20,28},{24,16},{28,20},{1,9},{5... | collective-permute-start | bytes 3391496 | tf_op jit(solution)/shard_map/ppermute | solution.py:865
  1258.2 24.1 %all-to-all-start.1 = ((f32[8,2,192]{2,1,0:T(2,128)}), f32[8,2,192]{2,1,0:T(2,128)S(1)}, u32[]{:S(2)}, u32[]{:S(2)}) async-start(f32[8,2,192]{2,1,0:T(2,128)} %get-tuple-element.52), calls=%async_computation.5 | async-start | bytes 32768 | tf_op jit(solution)/shard_map/all_to_all | solution.py:822
  1267.1 39.1 %collective-permute-start.19 = (f32[256,1536]{1,0:T(8,128)}, f32[256,1536]{1,0:T(8,128)S(1)}, u32[]{:S(2)}, u32[]{:S(2)}) collective-permute-start(f32[256,1536]{1,0:T(8,128)} %get-tuple-element.97), channel_id=1, source_target_pairs={{0,0},{1,1},{4,2},{5,3},{2,4},{3,5},{6,6},{7,7},{8,8},{9,9},{12,10... | collective-permute-start | bytes 4718600 | tf_op jit(solution)/shard_map/ppermute | solution.py:479
  1271.4 69.3 %collective-permute-start.20 = (f32[256,1536]{1,0:T(8,128)}, f32[256,1536]{1,0:T(8,128)S(1)}, u32[]{:S(2)}, u32[]{:S(2)}) collective-permute-start(f32[256,1536]{1,0:T(8,128)} %get-tuple-element.98), channel_id=1, source_target_pairs={{1,0},{0,1},{5,2},{4,3},{3,4},{2,5},{7,6},{6,7},{9,8},{8,9},{13,10... | collective-permute-start | bytes 4718600 | tf_op jit(solution)/shard_map/ppermute | solution.py:479
  1285.6 57.2 %collective-permute-start.26 = (bf16[1,2208,128]{2,1,0:T(8,128)(2,1)S(1)}, bf16[1,2208,128]{2,1,0:T(8,128)(2,1)S(1)}, u32[]{:S(2)}, u32[]{:S(2)}) collective-permute-start(bf16[1,2208,128]{2,1,0:T(8,128)(2,1)S(1)} %dynamic-slice_convert_fusion.2), channel_id=1, source_target_pairs={{0,16},{4,20},{8,24},{12,28},{16,0},{20,4},{24,8},{28,12},{1,17},{... | collective-permute-start | bytes 1695752 | tf_op jit(solution)/shard_map/ppermute | solution.py:865
  (165 other events, 2068.8 us)
Sparse Core Ops, SparseCore 0:
  22.2 52.6 all-reduce.4
  651.7 27.6 reduce-scatter.8
  836.4 28.7 reduce-scatter.12
  867.9 34.7 reduce-scatter.10
  993.3 25.4 reduce-scatter.14
  1029.7 122.4 reduce-scatter.16

commit v2 on v1

--- a/solution.py
+++ b/solution.py
@@ -493,6 +493,27 @@
         second = jnp.where(core == 0, other, mine)
         return jnp.concatenate([first, second], axis=axis)
 
+    def z_swap(values, step):
+        return lax.ppermute(values, "tp", [(i, i ^ step) for i in range(n_z)])
+
+    def z_order(pieces):
+        stack = jnp.stack(pieces)
+        return [pick(stack, z ^ a) for a in range(n_z)]
+
+    def z_gather(values):
+        return z_order([values] + [z_swap(values, j) for j in range(1, n_z)])
+
+    def z_exchange(blocks):
+        return z_order([pick(blocks, z ^ j) if j == 0 else z_swap(pick(blocks, z ^ j), j) for j in range(n_z)])
+
+    def z_scatter(values):
+        count = values.shape[0] // n_z
+        mine = lax.dynamic_slice_in_dim(values, z * count, count, 0)
+        for j in range(1, n_z):
+            part = lax.dynamic_slice_in_dim(values, (z ^ j) * count, count, 0)
+            mine = mine + z_swap(part.astype(BF16), j).astype(F32)
+        return mine
+
     def to_heads(values):
         half = values.shape[1] // 2
         low, high = values[:, :half], values[:, half:]
@@ -526,6 +547,8 @@
     owner_group = owner_of(jnp.arange(txt_group))
     owner_local = owner_of(z * txt_local + jnp.arange(txt_local))
     txt_mask = jnp.repeat(owner_group, RANK, axis=1)
+    txt_mask_local = jnp.repeat(owner_local, RANK, axis=1)
+    rank_cols = slots * RANK
     seq_mask = jnp.repeat(jnp.eye(slots, dtype=F32), RANK, axis=1)
 
     def by_group(mine, other):
@@ -581,8 +604,8 @@
     txt_msg = jnp.concatenate(
         [txt_a.reshape(slots * RANK, -1), txt_b_own[3], txt_b_own[5]], axis=1
     )
-    img_got = lax.all_to_all(img_msg, "tp", 0, 0, tiled=False)
-    txt_got = lax.all_gather(txt_msg, "tp", axis=0, tiled=False)
+    img_got = jnp.stack(z_exchange(img_msg))
+    txt_got = jnp.stack(z_gather(txt_msg))
 
     def join(part):
         return jnp.swapaxes(part, 0, 1).reshape(part.shape[1], -1)
@@ -627,7 +650,7 @@
         middle = (inner_right(cond_act, mod_a[stream]) * seq_mask).astype(BF16)
         mod_mid.append(middle)
         mod_terms.append(mod_part[:, stream] + matmul(middle, mod_b[stream]))
-    mods = lax.all_gather(jnp.stack(mod_terms, axis=1), "tp", axis=2, tiled=True)
+    mods = jnp.concatenate(z_gather(jnp.stack(mod_terms, axis=1)), axis=2)
     img_mods = by_group(mods[:, 0], swap_core(mods[:, 0]))
     img_mod = lax.dynamic_slice_in_dim(img_mods, z, 1, 0)
     txt_mods = mods[:, 1]
@@ -643,13 +666,11 @@
         return exact(owner_local.T, values)
 
     def share(values):
-        return lax.all_gather(values, "tp", axis=0, tiled=True)
-
-    def give(values):
-        return lax.psum_scatter(values, "tp", scatter_dimension=0, tiled=True)
-
-    def mine(values):
-        return lax.dynamic_slice_in_dim(values, z * txt_local, txt_local, 0)
+        return jnp.concatenate(z_gather(values), axis=0)
+
+    def give(values, rank_part):
+        got = z_scatter(jnp.concatenate([values, rank_part], axis=1))
+        return got[:, :width], (got[:, width:] * txt_mask_local).astype(BF16)
 
     def lanes(values):
         count = values.shape[1] // n_z
@@ -695,11 +716,10 @@
 
     attended = [to_tokens(o_img), txt_home(o_txt)]
 
-    txt_rank = lax.psum(inner_right(attended[1], txt_pairs[2][0]), "tp")
-    txt_out_mid = (txt_rank * txt_mask).astype(BF16)
-    txt_branch = give(inner_right(attended[1], txt_w[1])) + matmul(
-        mine(txt_out_mid), txt_pairs[2][1]
-    )
+    txt_branch, txt_out_mid = give(
+        inner_right(attended[1], txt_w[1]), inner_right(attended[1], txt_pairs[2][0])
+    )
+    txt_branch = txt_branch + matmul(txt_out_mid, txt_pairs[2][1])
     img_out_mid, img_branch = project(attended[0], img_w[1], img_pairs[2], None, True)
     branch = [img_branch, txt_branch]
     after = [inputs[s] + stretch(s, 2) * branch[s] for s in range(2)]
@@ -708,12 +728,14 @@
         (norm_two[s][0] * (1.0 + stretch(s, 4)) + stretch(s, 3)).astype(BF16) for s in range(2)
     ]
 
-    txt_mlp = share(mlp_in[1])
+    txt_mlp = share(jnp.concatenate([mlp_in[1], txt_out_mid], axis=1))
+    txt_mlp, txt_out_mid = txt_mlp[:, :width], txt_mlp[:, width:]
     txt_fc1_mid, txt_pre = project(txt_mlp, txt_w[2], txt_pairs[3], txt_mask, False)
     txt_act = gelu(txt_pre).astype(BF16)
-    txt_rank = lax.psum(inner_right(txt_act, txt_pairs[4][0]), "tp")
-    txt_fc2_mid = (txt_rank * txt_mask).astype(BF16)
-    txt_feed = give(inner_right(txt_act, txt_w[3])) + matmul(mine(txt_fc2_mid), txt_pairs[4][1])
+    txt_feed, txt_fc2_mid = give(
+        inner_right(txt_act, txt_w[3]), inner_right(txt_act, txt_pairs[4][0])
+    )
+    txt_feed = txt_feed + matmul(txt_fc2_mid, txt_pairs[4][1])
     img_fc1_mid, img_pre = project(mlp_in[0], img_w[2], img_pairs[3], None, False)
     img_act = gelu(img_pre).astype(BF16)
     img_fc2_mid, img_feed = project(img_act, img_w[3], img_pairs[4], None, True)
@@ -740,20 +762,12 @@
 
     txt_feed_full = share(grad_feed[1])
     txt_back_mid, txt_grad_act = project_back(txt_feed_full, txt_w[3], txt_pairs[4], txt_mask, True)
-    grads[1][4] = (
-        inner_left(txt_back_mid, txt_act),
-        inner_left(txt_fc2_mid, lanes(txt_feed_full)),
-    )
+    txt_fc2_grad_a = inner_left(txt_back_mid, txt_act)
     txt_grad_pre = gelu_back(txt_pre, txt_grad_act).astype(BF16)
-    txt_back_mid = lax.psum(inner_right(txt_grad_pre, txt_pairs[3][1]), "tp")
-    txt_back_mid = (txt_back_mid * txt_mask).astype(BF16)
-    grads[1][3] = (
-        inner_left(txt_back_mid, lanes(txt_mlp)),
-        inner_left(txt_fc1_mid, txt_grad_pre),
-    )
-    txt_grad_norm = give(inner_right(txt_grad_pre, txt_w[2])) + matmul(
-        mine(txt_back_mid), txt_pairs[3][0]
-    )
+    txt_grad_norm, txt_fc1_back = give(
+        inner_right(txt_grad_pre, txt_w[2]), inner_right(txt_grad_pre, txt_pairs[3][1])
+    )
+    txt_grad_norm = txt_grad_norm + matmul(txt_fc1_back, txt_pairs[3][0])
     grad_norm = [img_grad_norm, txt_grad_norm]
     mod_parts = [[None] * 6 for stream in range(2)]
     grad_after = []
@@ -769,7 +783,15 @@
 
     img_back_mid, img_grad_att = project_back(grad_branch[0], img_w[1], img_pairs[2], None, True)
     grads[0][2] = (inner_left(img_back_mid, attended[0]), inner_left(img_out_mid, grad_branch[0]))
-    txt_branch_full = share(grad_branch[1])
+    shared = share(jnp.concatenate([grad_branch[1], txt_fc1_back, txt_fc2_mid], axis=1))
+    txt_branch_full = shared[:, :width]
+    txt_fc1_back = shared[:, width : width + rank_cols]
+    txt_fc2_mid = shared[:, width + rank_cols :]
+    grads[1][4] = (txt_fc2_grad_a, inner_left(txt_fc2_mid, lanes(txt_feed_full)))
+    grads[1][3] = (
+        inner_left(txt_fc1_back, lanes(txt_mlp)),
+        inner_left(txt_fc1_mid, txt_grad_pre),
+    )
     txt_back_mid, txt_grad_att = project_back(
         txt_branch_full, txt_w[1], txt_pairs[2], txt_mask, True
     )
@@ -787,14 +809,13 @@
 
     img_back_mid, img_grad_norm = project_back(img_grad_qkv, img_w[0], img_pairs[1], None, False)
     grads[0][1] = (inner_left(img_back_mid, heads_in[0]), inner_left(img_qkv_mid, img_grad_qkv))
-    txt_back_mid = lax.psum(inner_right(txt_grad_qkv, txt_pairs[1][1]), "tp")
-    txt_back_mid = (txt_back_mid * txt_mask).astype(BF16)
+    txt_grad_norm, txt_qkv_back = give(
+        inner_right(txt_grad_qkv, txt_w[0]), inner_right(txt_grad_qkv, txt_pairs[1][1])
+    )
+    txt_grad_norm = txt_grad_norm + matmul(txt_qkv_back, txt_pairs[1][0])
     grads[1][1] = (
-        inner_left(txt_back_mid, lanes(txt_in)),
+        inner_left(share(txt_qkv_back), lanes(txt_in)),
         inner_left(txt_qkv_mid, txt_grad_qkv),
-    )
-    txt_grad_norm = give(inner_right(txt_grad_qkv, txt_w[0])) + matmul(
-        mine(txt_back_mid), txt_pairs[1][0]
     )
     grad_norm = [img_grad_norm, txt_grad_norm]
     grad_inputs = []
@@ -805,21 +826,27 @@
         )
         mod_parts[s][0] = collapse(s, grad_norm[s])
         mod_parts[s][1] = collapse(s, grad_norm[s] * norm_one[s][0])
-    image_grad = unshard(grad_inputs[0])
+    image_grad = unshard(grad_inputs[0].astype(BF16)).astype(F32)
 
     img_dmod = jnp.concatenate(mod_parts[0], axis=1)
     img_dmod = (img_dmod + swap_core(img_dmod)).astype(BF16)
-    img_dmods = lax.all_gather(img_dmod, "tp", axis=0, tiled=True)
+    def lane_blocks(values):
+        return jnp.swapaxes(values.reshape(values.shape[0], n_z, -1), 0, 1)
+
+    img_dmods = jnp.concatenate(z_exchange(lane_blocks(img_dmod)), axis=0)
     img_dmods = lax.dynamic_slice_in_dim(img_dmods, core * slots, slots, 0)
-    img_dmods = lanes(img_dmods)
     txt_dmod = jnp.concatenate(mod_parts[1], axis=1)
-    txt_dmods = lax.psum_scatter(txt_dmod, "tp", scatter_dimension=1, tiled=True).astype(BF16)
+    txt_dmods = sum(z_exchange(lane_blocks(txt_dmod))).astype(BF16)
     dmods = jnp.stack([img_dmods, txt_dmods], axis=1)
     dmods_all = lax.all_gather(dmods, "fsdp", axis=0, tiled=True)
     cond_part = sum(inner_right(dmods_all[:, s], mod_weight[s]) for s in range(2))
     mod_back = [inner_right(dmods[:, s], mod_b[s]) for s in range(2)]
-    cond_slices, mod_rank = lax.psum((cond_part, jnp.stack(mod_back)), "tp")
-    cond_rows = lax.all_to_all(cond_slices, "fsdp", 0, 1, tiled=True)
+    cond_part = cond_part.reshape(-1, width // n_f)
+    joined = jnp.concatenate([cond_part.reshape(-1), jnp.stack(mod_back).reshape(-1)])
+    joined = sum(z_gather(joined))
+    cond_slices = joined[: cond_part.size].reshape(n_f, -1, width // n_f)
+    mod_rank = joined[cond_part.size :].reshape(2, slots, -1)
+    cond_rows = lax.all_to_all(cond_slices, "fsdp", 0, 2, tiled=True)[0]
     for s in range(2):
         back_mid = (mod_rank[s] * seq_mask).astype(BF16)
         cond_rows = cond_rows + matmul(back_mid, mod_a[s])
@@ -829,21 +856,21 @@
     def spread(values):
         return jnp.swapaxes(values.reshape(RANK, n_z, -1), 0, 1)
 
-    img_parts = [spread(grads[0][index][side]) for side in range(2) for index in range(1, 5)]
-    img_parts = lax.all_to_all(jnp.concatenate(img_parts, axis=2), "tp", 0, 0, tiled=False)
-    img_parts = img_parts.reshape(column_count * RANK, -1)
-    offset = 0
-    img_rows = []
-    for sizes in (fans, cols):
-        for index in range(1, 5):
-            count = sizes[index] // n_z
-            img_rows.append(img_parts[:, offset : offset + count])
-            offset += count
+    img_rows = {}
+    for group in ((2, 3, 4), (1,)):
+        parts = [spread(grads[0][index][side]) for side in range(2) for index in group]
+        parts = jnp.concatenate(z_exchange(jnp.concatenate(parts, axis=2)), axis=0)
+        offset = 0
+        for side, sizes in enumerate((fans, cols)):
+            for index in group:
+                count = sizes[index] // n_z
+                img_rows[side, index] = parts[:, offset : offset + count]
+                offset += count
     flat = []
     for stream in range(2):
         for index in range(5):
             if stream == 0 and index > 0:
-                part_a, part_b = img_rows[index - 1], img_rows[index + 3]
+                part_a, part_b = img_rows[0, index], img_rows[1, index]
                 hot = one_hot
             else:
                 part_a, part_b = grads[stream][index]

time: 1360 us -> 1220 us (0.90)
  blocking collectives: 257 us -> 19 us
  waiting for transfers between devices: 87.6 us -> 170 us
  matrix products: 273 us -> 241 us
  starting transfers between devices: 99.9 us -> 125 us
  local copies, waits for them, and re-layouts: 87.2 us -> 110 us
    all_gather x7 -> x0, blocking collectives: 180 us -> none  [the longest x1 77 us: shards(): img_dmods = lax.all_gather(img_dmod, 'tp', axis=0, tiled=True)]
    ppermute x0 -> x51, waiting for transfers between devices: none -> 107 us  [z_swap(): return lax.ppermute(values, 'tp', [(i, i ^ step) for i in range(n_z)])]
    ppermute x0 -> x51, starting transfers between devices: none -> 57.6 us  [z_swap(): return lax.ppermute(values, 'tp', [(i, i ^ step) for i in range(n_z)])]
    psum x4 -> x0, blocking collectives: 57.3 us -> none  [the longest x1 16.1 us: shards(): txt_rank = lax.psum(inner_right(txt_act, txt_pairs[4][0]), 'tp')]
    ppermute x8, waiting for transfers between devices: 73.5 us -> 32.6 us  [from_chip(): got.append(lax.ppermute(mine, BOTH, [(b, a) for a, b in round_pairs(r)]))]
    ppermute x8, starting transfers between devices: 43.7 us -> 23.8 us  [to_chip(): got = [lax.ppermute(parts[r], BOTH, round_pairs(r)) for r in range(2)]]
    dot_general x33, matrix products: 104 us -> 88.8 us  [inner_right(): lax.dot_general(left, right, (((left.ndim - 1,), (right.ndim - 1,)), ((),...]
    dot_general x30, matrix products: 119 us -> 105 us  [matmul(): return jnp.dot(left, right, preferred_element_type=F32)]
  transfers between devices with their start and end apart: 36 -> 80, of which waited for: 10 -> 35; matrix products, arithmetic and copies ran while one was open for 31% -> 23% of each run, Pallas kernels for 30% -> 33%
where the time goes in v2:
time: 1220 us; the launch traced here: 1210 us
  Pallas kernels  439 us (36%)
  matrix products  241 us (20%)
  waiting for transfers between devices  170 us (14%)
  starting transfers between devices  125 us (10%)
  local copies, waits for them, and re-layouts  110 us (9%)
  other arithmetic  73.6 us (6%)
  between operations  31.9 us (3%)
  blocking collectives  19 us (2%)
    pallas_call x1, Pallas kernels, gather(): pl.pallas_call(functools.partial(gather_kernel, n_f, n_z, len(full), len(...  344 us
    ppermute x51, waiting for transfers between devices, z_swap(): return lax.ppermute(values, 'tp', [(i, i ^ step) for i in range(n_z)])  107 us
    dot_general x30, matrix products, matmul(): return jnp.dot(left, right, preferred_element_type=F32)  105 us
    dot_general x33, matrix products, inner_right(): lax.dot_general(left, right, (((left.ndim - 1,), (right.ndim - 1,)), ((),...  88.8 us
    pallas_call x1, Pallas kernels, attend_back(): pl.pallas_call(functools.partial(attend_back_kernel, hd, bq), grid=(pairs...  58.6 us
    ppermute x51, starting transfers between devices, z_swap(): return lax.ppermute(values, 'tp', [(i, i ^ step) for i in range(n_z)])  57.6 us
    pallas_call x1, Pallas kernels, attend(): pl.pallas_call(functools.partial(attend_kernel, hd, bq), grid=(pairs,), i...  36.6 us
    ppermute x8, waiting for transfers between devices, from_chip(): got.append(lax.ppermute(mine, BOTH, [(b, a) for a, b in round_pairs(r)]))  32.6 us
  transfers between devices with their start and end apart: 80, of which 35 were waited for; matrix products, arithmetic and copies ran while one was open for 23% of the time, Pallas kernels for 33%

profile of v2, /device:TPU:11, one launch (start us, length us, event | category | flops | bytes accessed | tf_op | source)
XLA Modules:
  0.0 1210.4 jit_solution(605530398531175161)
XLA Ops:
  8.7 9.1 all-gather
  23.0 4.4 collective-permute-start
  27.5 3.7 collective-permute-start.19
  38.3 12.5 %convert_reduce_fusion.1 = bf16[282624]{0:T(1024)(128)(2,1)} fusion(f32[1,282624]{1,0:T(1,128)S(1)} %copy-done.85), kind=kLoop, calls=%fused_computation.138 | loop fusion | flops 282624 | bytes 1695744 | tf_op jit(solution)/shard_map/convert_element_type | solution.py:531
  50.8 343.9 %weight_gather.1 = (bf16[8,192,4608]{2,1,0:T(8,128)(2,1)}, bf16[8,192,1536]{2,1,0:T(8,128)(2,1)}, bf16[8,192,6144]{2,1,0:T(8,128)(2,1)}, bf16[8,192,6144]{2,1,0:...) custom-call(bf16[192,1152]{1,0:T(8,128)(2,1)} %get-tuple-element.137, ...), custom_call_target="tpu_custom_call" | custom-call | tf_op jit(solution)/shard_map/weight_gather/pallas_call | solution.py:236
  435.7 7.5 collective-permute-start.4
  454.9 4.7 collective-permute-done.5
  478.2 11.2 collective-permute-done.12
  489.4 4.9 collective-permute-start.9
  503.9 5.0 collective-permute-start.34
  509.0 5.4 collective-permute-start.35
  514.4 5.8 collective-permute-done.39
  525.2 11.0 fusion.345
  548.3 9.9 collective-permute-done.17
  558.2 5.0 collective-permute-done.18
  569.2 36.6 %attend.1 = (bf16[1024,768]{1,0:T(8,128)(2,1)S(1)}, bf16[160,768]{1,0:T(8,128)(2,1)S(1)}, f32[6,2,1184]{2,1,0:T(2,128)S(1)}) custom-call(bf16[1024,2304]{1,0:T(8,128)(2,1)} %pad_maximum_fusion.img_ref, bf16[160,2304]{1,0:T(8,128)(2,1)S(1)} %pad_maximum_fusion.16.txt_ref, f32[160,1]{1,0:T(8,128)S(1)} %copy.129.bias_ref), custom_call_target="tpu_custom_call" | custom-call | tf_op jit(solution)/shard_map/attend/pallas_call | solution.py:287
  619.3 6.3 fusion.354
  625.7 5.7 collective-permute-done.27
  640.9 8.6 collective-permute-done.30
  669.8 9.1 collective-permute-done.33
  680.5 5.4 collective-permute-done.42
  697.0 8.8 collective-permute-done.45
  725.5 6.8 fusion.336
  734.4 6.5 fusion.348
  740.8 25.7 %multiply_convert_fusion = (bf16[512,6144]{1,0:T(8,128)(2,1)}, f32[512,6144]{1,0:T(8,128)}) fusion(f32[512,6144]{1,0:T(8,128)} %fusion.348, bf16[512,1536]{1,0:T(8,128)(2,1)S(1)} %add_convert_fusion.2, bf16[1536,6144]{1,0:T(8,128)(2,1)} %bitcast.664), kind=kOutput, calls=%fused_computation.9 | convolution fusion | flops 9695133696 | bytes 51904512 | tf_op jit(solution)/shard_map/dot_general | solution.py:389
  766.5 4.5 convolution_convert_fusion.8
  773.3 22.5 %fusion.6 = bf16[512,6144]{1,0:T(8,128)(2,1)S(1)} fusion(f32[512,6144]{1,0:T(8,128)} %get-tuple-element.271, f32[512,6144]{1,0:T(8,128)} %fusion.354, bf16[1536,6144]{1,0:T(8,128)(2,1)} %bitcast.662, f32[1536]{0:T(1024)S(1)} %copy-done.211, bf16[256,1536]{1,0:T(8,128)(2,1)S(1)} %copy-done.111, bf16[256,1536]{1,0:T(8,128)(2,1)S(1)} %copy-done.108), kind=kOutput, calls=%fused_computation.8 | convolution fusion | flops 9734455296 | bytes 51910656 | tf_op jit(solution)/shard_map/dot_general | solution.py:389
  800.6 19.5 %multiply_reduce_fusion = (f32[1536]{0:T(1024)}, f32[512]{0:T(512)S(1)}, f32[512]{0:T(512)S(1)}, f32[1536]{0:T(1024)}, f32[512,1536]{1,0:T(8,128)}) fusion(f32[512,1536]{1,0:T(8,128)} %copy-done.16, f32[512]{0:T(512)S(1)} %add_rsqrt_fusion, f32[512]{0:T(512)S(1)} %broadcast_multiply_fusion.4, f32[1536]{0:T(1024)S(1)} %copy-done.191, ...), kind=kOutput, calls=%fused_computation.51 | convolution fusion | flops 9671536640 | bytes 34629632 | tf_op jit(solution)/shard_map/dot_general | solution.py:401
  820.1 19.6 %fusion.25 = (f32[1536]{0:T(1024)}, bf16[512,1536]{1,0:T(8,128)(2,1)}, f32[1536]{0:T(1024)}, f32[512,1536]{1,0:T(8,128)S(1)}) fusion(bf16[256,1536]{1,0:T(8,128)(2,1)} %get-tuple-element.101, bf16[256,1536]{1,0:T(8,128)(2,1)S(1)} %copy-done.108, f32[512,1536]{1,0:T(8,128)} %copy-done.16, f32[1536]{0:T(1024)S(1)} %copy-done.211, ...), kind=kOutput, calls=%fused_computation.50 | convolution fusion | flops 9679400960 | bytes 44072960 | tf_op jit(solution)/shard_map/dot_general | solution.py:401
  841.4 5.3 fusion.356
  868.2 3.8 constant_dynamic-slice_fusion.11
  877.2 6.0 collective-permute-start.21
  886.3 16.9 %collective-permute-done.70 = f32[16,4608]{1,0:T(8,128)S(1)} collective-permute-done((f32[16,4608]{1,0:T(8,128)S(1)}, f32[16,4608]{1,0:T(8,128)S(1)}, u32[]{:S(2)}, u32[]{:S(2)}) %collective-permute-start.70) | collective-permute-done | bytes 294944 | tf_op jit(solution)/shard_map/ppermute | solution.py:497
  903.4 6.8 collective-permute-done.71
  920.7 58.6 %attend_back.1 = (bf16[1024,2304]{1,0:T(8,128)(2,1)}, bf16[160,2304]{1,0:T(8,128)(2,1)S(1)}) custom-call(bf16[1024,2304]{1,0:T(8,128)(2,1)} %pad_maximum_fusion.img_ref, bf16[160,2304]{1,0:T(8,128)(2,1)S(1)} %copy-done.1, f32[160,1]{1,0:T(8,128)S(1)} %copy-done.3, bf16[1024,768]{1,0:T(8,128)(2,1)S(1)} %pad_maximum_fusion.6.doi_ref, ...), custom_call_target="tpu_custom_call" | custom-call | tf_op jit(solution)/shard_map/attend_back/pallas_call | solution.py:360
  984.2 4.2 broadcast_select_fusion.2
  988.3 3.7 collective-permute-done.51
  992.0 8.9 collective-permute-done.52
  1010.6 6.9 collective-permute-done.55
  1047.8 17.1 %fusion.22 = (f32[1536]{0:T(1024)S(1)}, f32[512]{0:T(512)}, f32[512]{0:T(512)}, f32[1536]{0:T(1024)S(1)}, f32[512,1536]{1,0:T(8,128)}) fusion(f32[512]{0:T(512)S(1)} %copy-done.194, f32[512]{0:T(512)S(1)} %copy-done.187, bf16[256,1536]{1,0:T(8,128)(2,1)S(1)} %copy-done.8, bf16[256,1536]{1,0:T(8,128)(2,1)S(1)} %copy-done.6, f32[1536]{0:T(1024)S(1)} %copy-done.169, ...), kind=kOutput, calls=%fused_computation.47 | convolution fusion | flops 7268200448 | bytes 26765312 | tf_op jit(solution)/shard_map/dot_general | solution.py:401
  1079.8 9.8 all_gather.7
  1108.6 3.8 collective-permute-done.68
  1137.9 3.9 fusion.30
  1156.4 4.4 all-to-all-start
  1160.9 4.2 collective-permute-start.49
  1165.5 15.1 %all-to-all-done = f32[8,2,192]{2,1,0:T(2,128)S(1)} async-done(((f32[8,2,192]{2,1,0:T(2,128)}), f32[8,2,192]{2,1,0:T(2,128)S(1)}, u32[]{:S(2)}, u32[]{:S(2)}) %all-to-all-start) | async-done | bytes 12320 | tf_op jit(solution)/shard_map/all_to_all | solution.py:849
  1184.5 6.4 collective-permute-done.49
  1190.9 9.5 collective-permute-done.50
  (1044 shorter events, 353.9 us)
Async XLA Ops:
  7.2 453.1 %all-reduce.3.cloned.1.call-start = ((), (), s32[]{:S(2)}) async-start(), calls=%async_computation.1 | async-start | bytes 589824
  7.2 422.2 %collective-permute-start.2 = (s32[2]{0:T(128)}, s32[2]{0:T(128)}, u32[]{:S(2)}, u32[]{:S(2)}) collective-permute-start(s32[2]{0:T(128)} %param.17), channel_id=1, source_target_pairs={{0,4},{4,0},{8,12},{12,8},{16,20},{20,16},{24,28},{28,24},{1,5},{5... | collective-permute-start | bytes 32 | tf_op jit(solution)/shard_map/ppermute | solution.py:489
  23.0 498.6 %collective-permute-start = (bf16[256,1536]{1,0:T(8,128)(2,1)}, bf16[256,1536]{1,0:T(8,128)(2,1)}, u32[]{:S(2)}, u32[]{:S(2)}) collective-permute-start(bf16[256,1536]{1,0:T(8,128)(2,1)} %get-tuple-element.110), channel_id=1, source_target_pairs={{0,0},{1,1},{2,4},{3,5},{4,2},{5,3},{6,6},{7,7},{8,8},{9,9},{10,12... | collective-permute-start | bytes 2359304 | tf_op jit(solution)/shard_map/ppermute | solution.py:472
  27.4 494.2 %collective-permute-start.1 = (bf16[256,1536]{1,0:T(8,128)(2,1)}, bf16[256,1536]{1,0:T(8,128)(2,1)}, u32[]{:S(2)}, u32[]{:S(2)}) collective-permute-start(bf16[256,1536]{1,0:T(8,128)(2,1)} %get-tuple-element.111), channel_id=1, source_target_pairs={{0,1},{1,0},{2,5},{3,4},{4,3},{5,2},{6,7},{7,6},{8,9},{9,8},{10,13... | collective-permute-start | bytes 2359304 | tf_op jit(solution)/shard_map/ppermute | solution.py:472
  27.5 424.1 %collective-permute-start.19 = (s32[1,2]{1,0:T(1,128)}, s32[1,2]{1,0:T(1,128)}, u32[]{:S(2)}, u32[]{:S(2)}) collective-permute-start(s32[1,2]{1,0:T(1,128)} %param.16), channel_id=1, source_target_pairs={{0,4},{4,0},{8,12},{12,8},{16,20},{20,16},{24,28},{28,24},{1,5},{5... | collective-permute-start | bytes 32 | tf_op jit(solution)/shard_map/ppermute | solution.py:489
  435.7 19.2 %collective-permute-start.3 = (bf16[32,2304]{1,0:T(8,128)(2,1)S(1)}, bf16[32,2304]{1,0:T(8,128)(2,1)S(1)}, u32[]{:S(2)}, u32[]{:S(2)}) collective-permute-start(bf16[32,2304]{1,0:T(8,128)(2,1)S(1)} %maximum_maximum_fusion.1), channel_id=1, source_target_pairs={{0,1},{1,0},{2,3},{3,2},{4,5},{5,4},{6,7},{7,6},{8,9},{9,8},{10,11... | collective-permute-start | bytes 442376 | tf_op jit(solution)/shard_map/ppermute | solution.py:497
  435.7 19.2 %collective-permute-start.4 = (bf16[32,2304]{1,0:T(8,128)(2,1)S(1)}, bf16[32,2304]{1,0:T(8,128)(2,1)S(1)}, u32[]{:S(2)}, u32[]{:S(2)}) collective-permute-start(bf16[32,2304]{1,0:T(8,128)(2,1)S(1)} %maximum_maximum_fusion.1), channel_id=1, source_target_pairs={{0,2},{1,3},{2,0},{3,1},{4,6},{5,7},{6,4},{7,5},{8,10},{9,11},{10,... | collective-permute-start | bytes 442376 | tf_op jit(solution)/shard_map/ppermute | solution.py:497
  469.5 19.9 %collective-permute-start.12 = (bf16[16,6528]{1,0:T(8,128)(2,1)S(1)}, bf16[16,6528]{1,0:T(8,128)(2,1)S(1)}, u32[]{:S(2)}, u32[]{:S(2)}) collective-permute-start(bf16[16,6528]{1,0:T(8,128)(2,1)S(1)} %get-tuple-element.149), channel_id=1, source_target_pairs={{0,3},{1,2},{2,1},{3,0},{4,7},{5,6},{6,5},{7,4},{8,11},{9,10},{10,... | collective-permute-start | bytes 626696 | tf_op jit(solution)/shard_map/ppermute | solution.py:497
  474.1 24.9 %collective-permute-start.14 = (bf16[40,1536]{1,0:T(8,128)(2,1)S(1)}, bf16[40,1536]{1,0:T(8,128)(2,1)S(1)}, u32[]{:S(2)}, u32[]{:S(2)}) collective-permute-start(bf16[40,1536]{1,0:T(8,128)(2,1)S(1)} %fusion.28), channel_id=1, source_target_pairs={{0,1},{1,0},{2,3},{3,2},{4,5},{5,4},{6,7},{7,6},{8,9},{9,8},{10,11... | collective-permute-start | bytes 368648 | tf_op jit(solution)/shard_map/ppermute | solution.py:497
  476.8 22.2 %collective-permute-start.15 = (bf16[40,1536]{1,0:T(8,128)(2,1)S(1)}, bf16[40,1536]{1,0:T(8,128)(2,1)S(1)}, u32[]{:S(2)}, u32[]{:S(2)}) collective-permute-start(bf16[40,1536]{1,0:T(8,128)(2,1)S(1)} %fusion.28), channel_id=1, source_target_pairs={{0,2},{1,3},{2,0},{3,1},{4,6},{5,7},{6,4},{7,5},{8,10},{9,11},{10,... | collective-permute-start | bytes 368648 | tf_op jit(solution)/shard_map/ppermute | solution.py:497
  489.4 8.7 collective-permute-start.9
  499.0 10.0 collective-permute-start.38
  503.1 17.1 %collective-permute-start.39 = (bf16[40,1536]{1,0:T(8,128)(2,1)S(1)}, bf16[40,1536]{1,0:T(8,128)(2,1)S(1)}, u32[]{:S(2)}, u32[]{:S(2)}) collective-permute-start(bf16[40,1536]{1,0:T(8,128)(2,1)S(1)} %get-tuple-element.274), channel_id=1, source_target_pairs={{0,3},{1,2},{2,1},{3,0},{4,7},{5,6},{6,5},{7,4},{8,11},{9,10},{10,... | collective-permute-start | bytes 368648 | tf_op jit(solution)/shard_map/ppermute | solution.py:497
  503.9 59.4 %collective-permute-start.34 = (bf16[256,1536]{1,0:T(8,128)(2,1)S(1)}, bf16[256,1536]{1,0:T(8,128)(2,1)S(1)}, u32[]{:S(2)}, u32[]{:S(2)}) collective-permute-start(bf16[256,1536]{1,0:T(8,128)(2,1)S(1)} %copy-done.102), channel_id=1, source_target_pairs={{0,0},{1,1},{2,4},{3,5},{4,2},{5,3},{6,6},{7,7},{8,8},{9,9},{10,12... | collective-permute-start | bytes 2359304 | tf_op jit(solution)/shard_map/ppermute | solution.py:472
  509.0 54.4 %collective-permute-start.35 = (bf16[256,1536]{1,0:T(8,128)(2,1)S(1)}, bf16[256,1536]{1,0:T(8,128)(2,1)}, u32[]{:S(2)}, u32[]{:S(2)}) collective-permute-start(bf16[256,1536]{1,0:T(8,128)(2,1)S(1)} %copy-done.101), channel_id=1, source_target_pairs={{0,1},{1,0},{2,5},{3,4},{4,3},{5,2},{6,7},{7,6},{8,9},{9,8},{10,13... | collective-permute-start | bytes 2359304 | tf_op jit(solution)/shard_map/ppermute | solution.py:472
  537.9 28.1 %collective-permute-start.13 = (bf16[512,2304]{1,0:T(8,128)(2,1)S(1)}, bf16[512,2304]{1,0:T(8,128)(2,1)S(1)}, u32[]{:S(2)}, u32[]{:S(2)}) collective-permute-start(bf16[512,2304]{1,0:T(8,128)(2,1)S(1)} %broadcast_select_fusion.6), channel_id=1, source_target_pairs={{0,4},{4,0},{8,12},{12,8},{16,20},{20,16},{24,28},{28,24},{1,5},{5... | collective-permute-start | bytes 7077896 | tf_op jit(solution)/shard_map/ppermute | solution.py:489
  540.5 17.7 %collective-permute-start.17 = (bf16[160,1152]{1,0:T(8,128)(2,1)S(1)}, bf16[160,1152]{1,0:T(8,128)(2,1)S(1)}, u32[]{:S(2)}, u32[]{:S(2)}) collective-permute-start(bf16[160,1152]{1,0:T(8,128)(2,1)S(1)} %fusion.27), channel_id=1, source_target_pairs={{0,0},{1,1},{2,4},{3,5},{4,2},{5,3},{6,6},{7,7},{8,8},{9,9},{10,12... | collective-permute-start | bytes 1105928 | tf_op jit(solution)/shard_map/ppermute | solution.py:472
  543.3 19.9 %collective-permute-start.18 = (bf16[160,1152]{1,0:T(8,128)(2,1)S(1)}, bf16[160,1152]{1,0:T(8,128)(2,1)S(1)}, u32[]{:S(2)}, u32[]{:S(2)}) collective-permute-start(bf16[160,1152]{1,0:T(8,128)(2,1)S(1)} %fusion.27), channel_id=1, source_target_pairs={{0,1},{1,0},{2,5},{3,4},{4,3},{5,2},{6,7},{7,6},{8,9},{9,8},{10,13... | collective-permute-start | bytes 1105928 | tf_op jit(solution)/shard_map/ppermute | solution.py:472
  615.4 10.2 collective-permute-start.25
  618.0 13.4 %collective-permute-start.27 = (bf16[40,1568]{1,0:T(8,128)(2,1)S(1)}, bf16[40,1568]{1,0:T(8,128)(2,1)S(1)}, u32[]{:S(2)}, u32[]{:S(2)}) collective-permute-start(bf16[40,1568]{1,0:T(8,128)(2,1)S(1)} %get-tuple-element.135), channel_id=1, source_target_pairs={{0,3},{1,2},{2,1},{3,0},{4,7},{5,6},{6,5},{7,4},{8,11},{9,10},{10,... | collective-permute-start | bytes 376328 | tf_op jit(solution)/shard_map/ppermute | solution.py:497
  635.7 13.8 %collective-permute-start.30 = (bf16[40,1568]{1,0:T(8,128)(2,1)S(1)}, bf16[40,1568]{1,0:T(8,128)(2,1)S(1)}, u32[]{:S(2)}, u32[]{:S(2)}) collective-permute-start(bf16[40,1568]{1,0:T(8,128)(2,1)S(1)} %get-tuple-element.224), channel_id=1, source_target_pairs={{0,3},{1,2},{2,1},{3,0},{4,7},{5,6},{6,5},{7,4},{8,11},{9,10},{10,... | collective-permute-start | bytes 376328 | tf_op jit(solution)/shard_map/ppermute | solution.py:497
  638.6 83.4 %collective-permute-start.20 = (bf16[512,768]{1,0:T(8,128)(2,1)}, bf16[512,768]{1,0:T(8,128)(2,1)}, u32[]{:S(2)}, u32[]{:S(2)}) collective-permute-start(bf16[512,768]{1,0:T(8,128)(2,1)} %broadcast_select_fusion.16), channel_id=1, source_target_pairs={{0,4},{4,0},{8,12},{12,8},{16,20},{20,16},{24,28},{28,24},{1,5},{5... | collective-permute-start | bytes 2359304 | tf_op jit(solution)/shard_map/ppermute | solution.py:489
  660.5 18.3 %collective-permute-start.33 = (bf16[40,1568]{1,0:T(8,128)(2,1)}, bf16[40,1568]{1,0:T(8,128)(2,1)}, u32[]{:S(2)}, u32[]{:S(2)}) collective-permute-start(bf16[40,1568]{1,0:T(8,128)(2,1)} %get-tuple-element.132), channel_id=1, source_target_pairs={{0,3},{1,2},{2,1},{3,0},{4,7},{5,6},{6,5},{7,4},{8,11},{9,10},{10,... | collective-permute-start | bytes 376328 | tf_op jit(solution)/shard_map/ppermute | solution.py:497
  663.5 16.6 %collective-permute-start.40 = (bf16[40,1568]{1,0:T(8,128)(2,1)}, bf16[40,1568]{1,0:T(8,128)(2,1)}, u32[]{:S(2)}, u32[]{:S(2)}) collective-permute-start(bf16[40,1568]{1,0:T(8,128)(2,1)} %get-tuple-element.127), channel_id=1, source_target_pairs={{0,1},{1,0},{2,3},{3,2},{4,5},{5,4},{6,7},{7,6},{8,9},{9,8},{10,11... | collective-permute-start | bytes 376328 | tf_op jit(solution)/shard_map/ppermute | solution.py:497
  668.0 12.5 %collective-permute-start.41 = (bf16[40,1568]{1,0:T(8,128)(2,1)}, bf16[40,1568]{1,0:T(8,128)(2,1)S(1)}, u32[]{:S(2)}, u32[]{:S(2)}) collective-permute-start(bf16[40,1568]{1,0:T(8,128)(2,1)} %get-tuple-element.128), channel_id=1, source_target_pairs={{0,2},{1,3},{2,0},{3,1},{4,6},{5,7},{6,4},{7,5},{8,10},{9,11},{10,... | collective-permute-start | bytes 376328 | tf_op jit(solution)/shard_map/ppermute | solution.py:497
  668.3 17.5 %collective-permute-start.42 = (bf16[40,1568]{1,0:T(8,128)(2,1)}, bf16[40,1568]{1,0:T(8,128)(2,1)S(1)}, u32[]{:S(2)}, u32[]{:S(2)}) collective-permute-start(bf16[40,1568]{1,0:T(8,128)(2,1)} %get-tuple-element.129), channel_id=1, source_target_pairs={{0,3},{1,2},{2,1},{3,0},{4,7},{5,6},{6,5},{7,4},{8,11},{9,10},{10,... | collective-permute-start | bytes 376328 | tf_op jit(solution)/shard_map/ppermute | solution.py:497
  692.0 13.7 %collective-permute-start.45 = (bf16[40,1600]{1,0:T(8,128)(2,1)S(1)}, bf16[40,1600]{1,0:T(8,128)(2,1)S(1)}, u32[]{:S(2)}, u32[]{:S(2)}) collective-permute-start(bf16[40,1600]{1,0:T(8,128)(2,1)S(1)} %concatenate.177), channel_id=1, source_target_pairs={{0,3},{1,2},{2,1},{3,0},{4,7},{5,6},{6,5},{7,4},{8,11},{9,10},{10,... | collective-permute-start | bytes 384008 | tf_op jit(solution)/shard_map/ppermute | solution.py:497
  708.4 12.5 %collective-permute-start.46 = (bf16[160,384]{1,0:T(8,128)(2,1)}, bf16[160,384]{1,0:T(8,128)(2,1)}, u32[]{:S(2)}, u32[]{:S(2)}) collective-permute-start(bf16[160,384]{1,0:T(8,128)(2,1)} %fusion.38), channel_id=1, source_target_pairs={{0,0},{1,1},{2,4},{3,5},{4,2},{5,3},{6,6},{7,7},{8,8},{9,9},{10,12... | collective-permute-start | bytes 368648 | tf_op jit(solution)/shard_map/ppermute | solution.py:472
  711.2 9.6 collective-permute-start.47
  854.9 64.2 %collective-permute-start.36 = (bf16[512,768]{1,0:T(8,128)(2,1)}, bf16[512,768]{1,0:T(8,128)(2,1)}, u32[]{:S(2)}, u32[]{:S(2)}) collective-permute-start(bf16[512,768]{1,0:T(8,128)(2,1)} %broadcast_select_fusion.12), channel_id=1, source_target_pairs={{0,4},{4,0},{8,12},{12,8},{16,20},{20,16},{24,28},{28,24},{1,5},{5... | collective-permute-start | bytes 2359304 | tf_op jit(solution)/shard_map/ppermute | solution.py:489
  872.0 14.1 %collective-permute-start.69 = (f32[16,4608]{1,0:T(8,128)S(1)}, f32[16,4608]{1,0:T(8,128)S(1)}, u32[]{:S(2)}, u32[]{:S(2)}) collective-permute-start(f32[16,4608]{1,0:T(8,128)S(1)} %bitcast.608), channel_id=1, source_target_pairs={{0,1},{1,0},{2,3},{3,2},{4,5},{5,4},{6,7},{7,6},{8,9},{9,8},{10,11... | collective-permute-start | bytes 884744 | tf_op jit(solution)/shard_map/ppermute | solution.py:497
  874.4 28.8 %collective-permute-start.70 = (f32[16,4608]{1,0:T(8,128)S(1)}, f32[16,4608]{1,0:T(8,128)S(1)}, u32[]{:S(2)}, u32[]{:S(2)}) collective-permute-start(f32[16,4608]{1,0:T(8,128)S(1)} %bitcast.609), channel_id=1, source_target_pairs={{0,2},{1,3},{2,0},{3,1},{4,6},{5,7},{6,4},{7,5},{8,10},{9,11},{10,... | collective-permute-start | bytes 884744 | tf_op jit(solution)/shard_map/ppermute | solution.py:497
  875.7 34.5 %collective-permute-start.71 = (f32[16,4608]{1,0:T(8,128)S(1)}, f32[16,4608]{1,0:T(8,128)S(1)}, u32[]{:S(2)}, u32[]{:S(2)}) collective-permute-start(f32[16,4608]{1,0:T(8,128)S(1)} %bitcast.610), channel_id=1, source_target_pairs={{0,3},{1,2},{2,1},{3,0},{4,7},{5,6},{6,5},{7,4},{8,11},{9,10},{10,... | collective-permute-start | bytes 884744 | tf_op jit(solution)/shard_map/ppermute | solution.py:497
  877.2 266.4 %collective-permute-start.21 = (bf16[256,1536]{1,0:T(8,128)(2,1)}, bf16[256,1536]{1,0:T(8,128)(2,1)}, u32[]{:S(2)}, u32[]{:S(2)}) collective-permute-start(bf16[256,1536]{1,0:T(8,128)(2,1)} %get-tuple-element.106), channel_id=1, source_target_pairs={{0,0},{1,1},{4,2},{5,3},{2,4},{3,5},{6,6},{7,7},{8,8},{9,9},{12,10... | collective-permute-start | bytes 2359304 | tf_op jit(solution)/shard_map/ppermute | solution.py:479
  979.4 12.6 %collective-permute-start.51 = (bf16[160,1152]{1,0:T(8,128)(2,1)S(1)}, bf16[160,1152]{1,0:T(8,128)(2,1)S(1)}, u32[]{:S(2)}, u32[]{:S(2)}) collective-permute-start(bf16[160,1152]{1,0:T(8,128)(2,1)S(1)} %get-tuple-element.152), channel_id=1, source_target_pairs={{0,0},{1,1},{4,2},{5,3},{2,4},{3,5},{6,6},{7,7},{8,8},{9,9},{12,10... | collective-permute-start | bytes 1105928 | tf_op jit(solution)/shard_map/ppermute | solution.py:479
  981.5 19.4 %collective-permute-start.52 = (bf16[160,1152]{1,0:T(8,128)(2,1)S(1)}, bf16[160,1152]{1,0:T(8,128)(2,1)S(1)}, u32[]{:S(2)}, u32[]{:S(2)}) collective-permute-start(bf16[160,1152]{1,0:T(8,128)(2,1)S(1)} %get-tuple-element.153), channel_id=1, source_target_pairs={{1,0},{0,1},{5,2},{4,3},{3,4},{2,5},{7,6},{6,7},{9,8},{8,9},{13,10... | collective-permute-start | bytes 1105928 | tf_op jit(solution)/shard_map/ppermute | solution.py:479
  988.3 49.9 %collective-permute-start.48 = (bf16[512,2304]{1,0:T(8,128)(2,1)}, bf16[512,2304]{1,0:T(8,128)(2,1)}, u32[]{:S(2)}, u32[]{:S(2)}) collective-permute-start(bf16[512,2304]{1,0:T(8,128)(2,1)} %broadcast_select_fusion.2), channel_id=1, source_target_pairs={{0,4},{4,0},{8,12},{12,8},{16,20},{20,16},{24,28},{28,24},{1,5},{5... | collective-permute-start | bytes 7077896 | tf_op jit(solution)/shard_map/ppermute | solution.py:489
  1003.8 13.7 %collective-permute-start.55 = (bf16[40,1568]{1,0:T(8,128)(2,1)}, bf16[40,1568]{1,0:T(8,128)(2,1)}, u32[]{:S(2)}, u32[]{:S(2)}) collective-permute-start(bf16[40,1568]{1,0:T(8,128)(2,1)} %get-tuple-element.126), channel_id=1, source_target_pairs={{0,3},{1,2},{2,1},{3,0},{4,7},{5,6},{6,5},{7,4},{8,11},{9,10},{10,... | collective-permute-start | bytes 376328 | tf_op jit(solution)/shard_map/ppermute | solution.py:497
  1018.6 8.5 collective-permute-start.72
  1018.7 9.5 collective-permute-start.73
  1019.6 8.7 collective-permute-start.74
  1032.0 111.7 %collective-permute-start.22 = (bf16[256,1536]{1,0:T(8,128)(2,1)}, bf16[256,1536]{1,0:T(8,128)(2,1)}, u32[]{:S(2)}, u32[]{:S(2)}) collective-permute-start(bf16[256,1536]{1,0:T(8,128)(2,1)} %get-tuple-element.107), channel_id=1, source_target_pairs={{1,0},{0,1},{5,2},{4,3},{3,4},{2,5},{7,6},{6,7},{9,8},{8,9},{13,10... | collective-permute-start | bytes 2359304 | tf_op jit(solution)/shard_map/ppermute | solution.py:479
  1103.7 8.7 collective-permute-start.68
  1152.6 28.9 %collective-permute-start.76 = (bf16[2,2208,128]{2,1,0:T(8,128)(2,1)}, bf16[2,2208,128]{2,1,0:T(8,128)(2,1)}, u32[]{:S(2)}, u32[]{:S(2)}) collective-permute-start(bf16[2,2208,128]{2,1,0:T(8,128)(2,1)} %fusion.39), channel_id=1, source_target_pairs={{0,8},{4,12},{8,0},{12,4},{16,24},{20,28},{24,16},{28,20},{1,9},{5... | collective-permute-start | bytes 3391496 | tf_op jit(solution)/shard_map/ppermute | solution.py:892
  1156.4 24.1 %all-to-all-start = ((f32[8,2,192]{2,1,0:T(2,128)}), f32[8,2,192]{2,1,0:T(2,128)S(1)}, u32[]{:S(2)}, u32[]{:S(2)}) async-start(f32[8,2,192]{2,1,0:T(2,128)} %reshape.643), calls=%async_computation | async-start | bytes 32768 | tf_op jit(solution)/shard_map/all_to_all | solution.py:849
  1160.9 29.9 %collective-permute-start.49 = (bf16[256,1536]{1,0:T(8,128)(2,1)S(1)}, bf16[256,1536]{1,0:T(8,128)(2,1)S(1)}, u32[]{:S(2)}, u32[]{:S(2)}) collective-permute-start(bf16[256,1536]{1,0:T(8,128)(2,1)S(1)} %get-tuple-element.98), channel_id=1, source_target_pairs={{0,0},{1,1},{4,2},{5,3},{2,4},{3,5},{6,6},{7,7},{8,8},{9,9},{12,10... | collective-permute-start | bytes 2359304 | tf_op jit(solution)/shard_map/ppermute | solution.py:479
  1165.1 35.2 %collective-permute-start.50 = (bf16[256,1536]{1,0:T(8,128)(2,1)S(1)}, bf16[256,1536]{1,0:T(8,128)(2,1)S(1)}, u32[]{:S(2)}, u32[]{:S(2)}) collective-permute-start(bf16[256,1536]{1,0:T(8,128)(2,1)S(1)} %get-tuple-element.99), channel_id=1, source_target_pairs={{1,0},{0,1},{5,2},{4,3},{3,4},{2,5},{7,6},{6,7},{9,8},{8,9},{13,10... | collective-permute-start | bytes 2359304 | tf_op jit(solution)/shard_map/ppermute | solution.py:479
  1183.7 18.6 %collective-permute-start.77 = (bf16[1,2208,128]{2,1,0:T(8,128)(2,1)S(1)}, bf16[1,2208,128]{2,1,0:T(8,128)(2,1)S(1)}, u32[]{:S(2)}, u32[]{:S(2)}) collective-permute-start(bf16[1,2208,128]{2,1,0:T(8,128)(2,1)S(1)} %dynamic-slice_convert_fusion.2), channel_id=1, source_target_pairs={{0,16},{4,20},{8,24},{12,28},{16,0},{20,4},{24,8},{28,12},{1,17},{... | collective-permute-start | bytes 1695752 | tf_op jit(solution)/shard_map/ppermute | solution.py:892
  (272 other events, 4631.7 us)
Sparse Core Ops, SparseCore 0:
  21.8 53.0 all-reduce.2

commit v3 on v2

--- a/solution.py
+++ b/solution.py
@@ -251,15 +251,15 @@
     return lax.dot_general(left, right, (((lc,), (rc,)), ((), ())), preferred_element_type=jnp.float32)
 
 def attend_kernel(hd, bq, img_ref, txt_ref, bias_ref, oi_ref, ot_ref, lse_ref):
-    img_n, txt_n = img_ref.shape[0], txt_ref.shape[0]
+    img_n, txt_n = img_ref.shape[0], txt_ref.shape[1]
     heads = img_ref.shape[1] // (3 * hd)
     bias = bias_ref[...]
     for h in range(heads):
         base = 3 * hd * h
         ki = img_ref[:, base + hd:base + 2 * hd]
         vi = img_ref[:, base + 2 * hd:base + 3 * hd]
-        kt = txt_ref[:, base + hd:base + 2 * hd]
-        vt = txt_ref[:, base + 2 * hd:base + 3 * hd]
+        kt = txt_ref[0, :, base + hd:base + 2 * hd]
+        vt = txt_ref[0, :, base + 2 * hd:base + 3 * hd]
 
         def block(q):
             q = q * jnp.bfloat16(0.125)
@@ -276,30 +276,31 @@
             o, lse = block(img_ref[i * bq:(i + 1) * bq, base:base + hd])
             oi_ref[i * bq:(i + 1) * bq, h * hd:(h + 1) * hd] = o
             lse_ref[0, h:h + 1, i * bq:(i + 1) * bq] = lse
-        o, lse = block(txt_ref[:, base:base + hd])
-        ot_ref[:, h * hd:(h + 1) * hd] = o
+        o, lse = block(txt_ref[0, :, base:base + hd])
+        ot_ref[0, :, h * hd:(h + 1) * hd] = o
         lse_ref[0, h:h + 1, img_n:img_n + txt_n] = lse
 
 def attend(img, txt, bias, hd, bq=512):
     img_n, cols = img.shape
-    txt_n = txt.shape[0]
+    parts, txt_n, _ = txt.shape
     pairs = cols // (6 * hd)
+    per = pairs // parts
     return pl.pallas_call(
         functools.partial(attend_kernel, hd, bq),
         grid=(pairs,),
         in_specs=[
             pl.BlockSpec((img_n, 6 * hd), lambda i: (0, i)),
-            pl.BlockSpec((txt_n, 6 * hd), lambda i: (0, i)),
+            pl.BlockSpec((1, txt_n, 6 * hd), lambda i: (i // per, 0, i % per)),
             pl.BlockSpec((txt_n, 1), lambda i: (0, 0)),
         ],
         out_specs=[
             pl.BlockSpec((img_n, 2 * hd), lambda i: (0, i)),
-            pl.BlockSpec((txt_n, 2 * hd), lambda i: (0, i)),
+            pl.BlockSpec((1, txt_n, 2 * hd), lambda i: (i // per, 0, i % per)),
             pl.BlockSpec((1, 2, img_n + txt_n), lambda i: (i, 0, 0)),
         ],
         out_shape=[
             jax.ShapeDtypeStruct((img_n, pairs * 2 * hd), jnp.bfloat16),
-            jax.ShapeDtypeStruct((txt_n, pairs * 2 * hd), jnp.bfloat16),
+            jax.ShapeDtypeStruct((parts, txt_n, per * 2 * hd), jnp.bfloat16),
             jax.ShapeDtypeStruct((pairs, 2, img_n + txt_n), jnp.float32),
         ],
         compiler_params=pltpu.CompilerParams(vmem_limit_bytes=48 * 1024 * 1024),
@@ -307,15 +308,15 @@
     )(img, txt, bias)
 
 def attend_back_kernel(hd, bq, img_ref, txt_ref, bias_ref, doi_ref, dot_ref, lse_ref, di_ref, dt_ref, acc_i, acc_t):
-    img_n, txt_n = img_ref.shape[0], txt_ref.shape[0]
+    img_n, txt_n = img_ref.shape[0], txt_ref.shape[1]
     heads = img_ref.shape[1] // (3 * hd)
     bias = bias_ref[...]
     for h in range(heads):
         base = 3 * hd * h
         ki = img_ref[:, base + hd:base + 2 * hd]
         vi = img_ref[:, base + 2 * hd:base + 3 * hd]
-        kt = txt_ref[:, base + hd:base + 2 * hd]
-        vt = txt_ref[:, base + 2 * hd:base + 3 * hd]
+        kt = txt_ref[0, :, base + hd:base + 2 * hd]
+        vt = txt_ref[0, :, base + 2 * hd:base + 3 * hd]
 
         def block(q, do, lse, first):
             q = q * jnp.bfloat16(0.125)
@@ -344,19 +345,21 @@
             rows = slice(i * bq, (i + 1) * bq)
             di_ref[rows, base:base + hd] = block(
                 img_ref[rows, base:base + hd], doi_ref[rows, h * hd:(h + 1) * hd], lse_ref[0, h:h + 1, rows], i == 0)
-        dt_ref[:, base:base + hd] = block(
-            txt_ref[:, base:base + hd], dot_ref[:, h * hd:(h + 1) * hd], lse_ref[0, h:h + 1, img_n:img_n + txt_n], False)
+        grad = jnp.where(bias < 0, 0.0, dot_ref[0, :, h * hd:(h + 1) * hd].astype(jnp.float32)).astype(jnp.bfloat16)
+        dt_ref[0, :, base:base + hd] = block(
+            txt_ref[0, :, base:base + hd], grad, lse_ref[0, h:h + 1, img_n:img_n + txt_n], False)
         di_ref[:, base + hd:base + 2 * hd] = acc_i[0].astype(jnp.bfloat16)
         di_ref[:, base + 2 * hd:base + 3 * hd] = acc_i[1].astype(jnp.bfloat16)
-        dt_ref[:, base + hd:base + 2 * hd] = acc_t[0].astype(jnp.bfloat16)
-        dt_ref[:, base + 2 * hd:base + 3 * hd] = acc_t[1].astype(jnp.bfloat16)
+        dt_ref[0, :, base + hd:base + 2 * hd] = acc_t[0].astype(jnp.bfloat16)
+        dt_ref[0, :, base + 2 * hd:base + 3 * hd] = acc_t[1].astype(jnp.bfloat16)
 
 def attend_back(img, txt, bias, doi, dot, lse, hd, bq=512):
     img_n, cols = img.shape
-    txt_n = txt.shape[0]
+    parts, txt_n, _ = txt.shape
     pairs = cols // (6 * hd)
+    per = pairs // parts
     wide = pl.BlockSpec((img_n, 6 * hd), lambda i: (0, i))
-    wide_t = pl.BlockSpec((txt_n, 6 * hd), lambda i: (0, i))
+    wide_t = pl.BlockSpec((1, txt_n, 6 * hd), lambda i: (i // per, 0, i % per))
     return pl.pallas_call(
         functools.partial(attend_back_kernel, hd, bq),
         grid=(pairs,),
@@ -364,7 +367,7 @@
             wide, wide_t,
             pl.BlockSpec((txt_n, 1), lambda i: (0, 0)),
             pl.BlockSpec((img_n, 2 * hd), lambda i: (0, i)),
-            pl.BlockSpec((txt_n, 2 * hd), lambda i: (0, i)),
+            pl.BlockSpec((1, txt_n, 2 * hd), lambda i: (i // per, 0, i % per)),
             pl.BlockSpec((1, 2, img_n + txt_n), lambda i: (i, 0, 0)),
         ],
         out_specs=[wide, wide_t],
@@ -373,6 +376,446 @@
         compiler_params=pltpu.CompilerParams(vmem_limit_bytes=48 * 1024 * 1024),
         name="attend_back",
     )(img, txt, bias, doi, dot, lse)
+
+ROWS = 64
+
+
+def mm(left, right):
+    return dots(left, right, 1, 0)
+
+
+def mm_t(left, right):
+    return dots(left, right, 1, 1)
+
+
+def t_mm(left, right):
+    return dots(left, right, 0, 0)
+
+
+def gelu_parts(u):
+    scale = 0.7978845608028654
+    square = u * u
+    tanh = jnp.tanh(scale * (u + 0.044715 * u * square))
+    half = 0.5 * (1.0 + tanh)
+    slope = half + 0.5 * u * (1.0 - tanh * tanh) * (scale * (1.0 + 3 * 0.044715 * square))
+    return u * half, slope
+
+
+def norm_rows(v):
+    center = v - jnp.mean(v, axis=-1, keepdims=True)
+    inverse = lax.rsqrt(jnp.mean(center * center, axis=-1, keepdims=True) + 1e-06)
+    return center * inverse, inverse
+
+
+def block_fwd_kernel(tiles, o_ref, x_ref, g_ref, mod_ref, wo_ref, ao_ref, bo_ref, a1_ref, b1_ref, w1_ref, a2_ref, w2_ref, b2_ref,
+                     a_out, x1_out, h2_out, u_out, y_out, to_out, t1_out, t2_out, gate_out, m_acc, t2_acc):
+    step = pl.program_id(0)
+    rows = o_ref.shape[0]
+    width = o_ref.shape[1]
+
+    @pl.when(step == 0)
+    def _():
+        to = mm_t(o_ref[...], ao_ref[...]).astype(jnp.bfloat16)
+        to_out[...] = to
+
+        def cols(n, _):
+            sl = pl.ds(pl.multiple_of(n * 256, 256), 256)
+            a_out[:, sl] = mm_t(o_ref[...], wo_ref[sl, :]) + mm(to_out[...], bo_ref[:, sl])
+            return 0
+
+        lax.fori_loop(0, width // 256, cols, 0)
+
+        def norm(r, _):
+            sl = pl.ds(pl.multiple_of(r * ROWS, ROWS), ROWS)
+            x1 = x_ref[sl, :].astype(jnp.float32) + mod_ref[2:3, :] * a_out[sl, :]
+            x1_out[sl, :] = x1
+            xh, _inv = norm_rows(x1)
+            h2_out[sl, :] = (xh * (1.0 + mod_ref[4:5, :]) + mod_ref[3:4, :]).astype(jnp.bfloat16)
+            return 0
+
+        lax.fori_loop(0, rows // ROWS, norm, 0)
+        t1_out[...] = mm_t(h2_out[...], a1_ref[...]).astype(jnp.bfloat16)
+        m_acc[...] = jnp.zeros_like(m_acc)
+        t2_acc[...] = jnp.zeros_like(t2_acc)
+
+    u = mm(h2_out[...], w1_ref[...]) + mm(t1_out[...], b1_ref[...])
+    u_out[...] = u
+    f = gelu_parts(u)[0].astype(jnp.bfloat16)
+    m_acc[...] += mm_t(f, w2_ref[...])
+    t2_acc[...] += mm_t(f, a2_ref[...])
+
+    @pl.when(step == tiles - 1)
+    def _():
+        t2_out[...] = t2_acc[...].astype(jnp.bfloat16)
+        gate_out[...] = jnp.zeros_like(gate_out)
+
+        def last(r, _):
+            sl = pl.ds(pl.multiple_of(r * ROWS, ROWS), ROWS)
+            m = m_acc[sl, :] + mm(t2_out[sl, :], b2_ref[...])
+            y_out[sl, :] = (x1_out[sl, :] + mod_ref[5:6, :] * m).astype(jnp.bfloat16)
+            gm = g_ref[sl, :].astype(jnp.float32) * m
+            gate_out[...] += sum(gm[8 * i:8 * i + 8, :] for i in range(ROWS // 8))
+            return 0
+
+        lax.fori_loop(0, rows // ROWS, last, 0)
+
+
+def block_fwd(o, x, g, mod, wo, pair_o, pair_1, w1, pair_2, w2, tn=512):
+    rows, width = o.shape
+    hidden = w1.shape[1]
+    tiles = hidden // tn
+    rank = pair_o[0].shape[0]
+    whole = lambda shape: pl.BlockSpec(shape, lambda n: (0,) * len(shape))
+    once = lambda shape: pl.BlockSpec(shape, lambda n: (0,) * len(shape), pipeline_mode=pl.Buffered(1))
+    tile = lambda height: pl.BlockSpec((height, tn), lambda n: (0, n))
+    f32, bf16 = jnp.float32, jnp.bfloat16
+    act = (rows, width)
+    return pl.pallas_call(
+        functools.partial(block_fwd_kernel, tiles),
+        grid=(tiles,),
+        in_specs=[once(act), once(act), once(act), once(mod.shape), once((width, width)), once((rank, width)), once((rank, width)),
+                  once((rank, width)), tile(rank), tile(width), tile(rank), tile(width), once((rank, width))],
+        out_specs=[whole(act), whole(act), whole(act), tile(rows), whole(act), whole((rows, rank)), whole((rows, rank)),
+                   whole((rows, rank)), whole((8, width))],
+        out_shape=[jax.ShapeDtypeStruct(act, f32), jax.ShapeDtypeStruct(act, f32), jax.ShapeDtypeStruct(act, bf16),
+                   jax.ShapeDtypeStruct((rows, hidden), f32), jax.ShapeDtypeStruct(act, bf16)]
+        + [jax.ShapeDtypeStruct((rows, rank), bf16)] * 3 + [jax.ShapeDtypeStruct((8, width), f32)],
+        scratch_shapes=[pltpu.VMEM(act, f32), pltpu.VMEM((rows, rank), f32)],
+        compiler_params=pltpu.CompilerParams(vmem_limit_bytes=58 * 1024 * 1024),
+        cost_estimate=pl.CostEstimate(flops=2 * rows * width * (width + 2 * hidden), bytes_accessed=4 * width * hidden, transcendentals=0),
+        name="block_forward",
+    )(o, x, g, mod, wo, *pair_o, pair_1[0], pair_1[1], w1, pair_2[0], w2, pair_2[1])
+
+
+def block_back_kernel(tiles, g_ref, x1_ref, a_ref, h2_ref, o_ref, mod_ref, u_ref, w2_ref, a2_ref, b2_ref, w1_ref, a1_ref, b1_ref,
+                      wo_ref, ao_ref, bo_ref, to_ref, t1_ref, t2_ref,
+                      dx1_out, do_out, sums_out, ga2_out, gb1_out, ga1_out, gb2_out, gao_out, gbo_out,
+                      dm_ref, dt2_ref, dh_acc, dt1_acc, da_ref):
+    step = pl.program_id(0)
+    rows, width = g_ref.shape
+    bf16 = jnp.bfloat16
+
+    @pl.when(step == 0)
+    def _():
+        def start(r, _):
+            sl = pl.ds(pl.multiple_of(r * ROWS, ROWS), ROWS)
+            dm_ref[sl, :] = (mod_ref[5:6, :] * g_ref[sl, :].astype(jnp.float32)).astype(bf16)
+            return 0
+
+        lax.fori_loop(0, rows // ROWS, start, 0)
+        dt2_ref[...] = mm_t(dm_ref[...], b2_ref[...]).astype(bf16)
+        gb2_out[...] = t_mm(t2_ref[...], dm_ref[...])
+        dh_acc[...] = jnp.zeros_like(dh_acc)
+        dt1_acc[...] = jnp.zeros_like(dt1_acc)
+
+    act, slope = gelu_parts(u_ref[...])
+    df = mm(dm_ref[...], w2_ref[...]) + mm(dt2_ref[...], a2_ref[...])
+    ga2_out[...] = t_mm(dt2_ref[...], act.astype(bf16))
+    du = (df * slope).astype(bf16)
+    gb1_out[...] = t_mm(t1_ref[...], du)
+    dh_acc[...] += mm_t(du, w1_ref[...])
+    dt1_acc[...] += mm_t(du, b1_ref[...])
+
+    @pl.when(step == tiles - 1)
+    def _():
+        dt1 = dt1_acc[...].astype(bf16)
+        dt2_ref[...] = dt1
+        ga1_out[...] = t_mm(dt1, h2_ref[...])
+        sums_out[...] = jnp.zeros_like(sums_out)
+
+        def last(r, _):
+            sl = pl.ds(pl.multiple_of(r * ROWS, ROWS), ROWS)
+            dh = dh_acc[sl, :] + mm(dt2_ref[sl, :], a1_ref[...])
+            xh, inverse = norm_rows(x1_ref[sl, :])
+            dz = dh * (1.0 + mod_ref[4:5, :])
+            dx1 = g_ref[sl, :].astype(jnp.float32) + inverse * (
+                dz - jnp.mean(dz, axis=-1, keepdims=True) - xh * jnp.mean(dz * xh, axis=-1, keepdims=True))
+            dx1_out[sl, :] = dx1
+            da_ref[sl, :] = (mod_ref[2:3, :] * dx1).astype(bf16)
+            fold = lambda v: sum(v[8 * i:8 * i + 8, :] for i in range(ROWS // 8))
+            sums_out[0:8, :] += fold(dx1 * a_ref[sl, :])
+            sums_out[8:16, :] += fold(dh)
+            sums_out[16:24, :] += fold(dh * xh)
+            return 0
+
+        lax.fori_loop(0, rows // ROWS, last, 0)
+        dto = mm_t(da_ref[...], bo_ref[...]).astype(bf16)
+        dt2_ref[...] = dto
+        gao_out[...] = t_mm(dto, o_ref[...])
+        gbo_out[...] = t_mm(to_ref[...], da_ref[...])
+
+        def cols(n, _):
+            sl = pl.ds(pl.multiple_of(n * 256, 256), 256)
+            do_out[:, sl] = (mm(da_ref[...], wo_ref[:, sl]) + mm(dt2_ref[...], ao_ref[:, sl])).astype(bf16)
+            return 0
+
+        lax.fori_loop(0, width // 256, cols, 0)
+
+
+def block_back(g, x1, a, h2, o, mod, u, w2, pair_2, w1, pair_1, wo, pair_o, mids, tn=512):
+    rows, width = o.shape
+    hidden = w1.shape[1]
+    tiles = hidden // tn
+    rank = pair_o[0].shape[0]
+    whole = lambda shape: pl.BlockSpec(shape, lambda n: (0,) * len(shape))
+    once = lambda shape: pl.BlockSpec(shape, lambda n: (0,) * len(shape), pipeline_mode=pl.Buffered(1))
+    tile = lambda height: pl.BlockSpec((height, tn), lambda n: (0, n))
+    f32, bf16 = jnp.float32, jnp.bfloat16
+    act = (rows, width)
+    side = (rank, width)
+    thin = (rows, rank)
+    return pl.pallas_call(
+        functools.partial(block_back_kernel, tiles),
+        grid=(tiles,),
+        in_specs=[once(act)] * 5 + [once(mod.shape), tile(rows), tile(width), tile(rank), once(side), tile(width), once(side), tile(rank),
+                  once((width, width)), once(side), once(side)] + [once(thin)] * 3,
+        out_specs=[whole(act), whole(act), whole((24, width)), tile(rank), tile(rank)] + [whole(side)] * 4,
+        out_shape=[jax.ShapeDtypeStruct(act, f32), jax.ShapeDtypeStruct(act, bf16), jax.ShapeDtypeStruct((24, width), f32)]
+        + [jax.ShapeDtypeStruct((rank, hidden), f32)] * 2 + [jax.ShapeDtypeStruct(side, f32)] * 4,
+        scratch_shapes=[pltpu.VMEM(act, bf16), pltpu.VMEM(thin, bf16), pltpu.VMEM(act, f32), pltpu.VMEM(thin, f32), pltpu.VMEM(act, bf16)],
+        compiler_params=pltpu.CompilerParams(vmem_limit_bytes=58 * 1024 * 1024),
+        cost_estimate=pl.CostEstimate(flops=2 * rows * width * (width + 2 * hidden), bytes_accessed=4 * width * hidden, transcendentals=0),
+        name="block_backward",
+    )(g, x1, a, h2, o, mod, u, w2, pair_2[0], pair_2[1], w1, pair_1[0], pair_1[1], wo, *pair_o, *mids)
+
+
+def column_peers(n_z):
+    f, z = lax.axis_index("fsdp"), lax.axis_index("tp")
+    core = f % 2
+    base = f - core
+    peers = [(f, (z + j) % n_z) for j in range(1, n_z)]
+    peers += [(base + 1 - core, (z + j) % n_z) for j in range(n_z)]
+    return f, z, core, base, peers
+
+
+def meet(peers):
+    barrier = pltpu.get_barrier_semaphore()
+    for peer in peers:
+        pl.semaphore_signal(barrier, inc=1, device_id=peer, device_id_type=MESH)
+    pl.semaphore_wait(barrier, len(peers))
+
+
+def push(src, dst, send, recv, peer):
+    return pltpu.make_async_remote_copy(
+        src_ref=src, dst_ref=dst, send_sem=send, recv_sem=recv, device_id=peer, device_id_type=MESH)
+
+
+class ZRing:
+    def __init__(self, f, z, n_z):
+        self.f, self.z, self.n_z = f, z, n_z
+
+    def start(self, source_of, buf, send, recv):
+        for j in range(1, self.n_z):
+            to = (self.z + j) % self.n_z
+            push(source_of(to), buf.at[self.z], send.at[j], recv.at[self.z], (self.f, to)).start()
+
+    def wait(self, buf, send, recv):
+        for j in range(1, self.n_z):
+            came = (self.z + j) % self.n_z
+            push(buf.at[came], buf.at[came], send.at[j], recv.at[came], (self.f, came)).wait_recv()
+
+    def drain(self, source_of, buf, send, recv):
+        for j in range(1, self.n_z):
+            to = (self.z + j) % self.n_z
+            push(source_of(to), buf.at[self.z], send.at[j], recv.at[self.z], (self.f, to)).wait_send()
+
+
+def text_mid_kernel(n_z, o_ref, x_ref, g_ref, mod_ref, owner_ref, own_ref, mask_ref, lmask_ref, wo_ref, w1_ref, w2_ref,
+                    ao_ref, bo_ref, a1_ref, b1_ref, a2_ref, b2_ref,
+                    y_out, dx1_out, do_out, sums_out, gao_out, gbo_out, ga1_out, gb1_out, ga2_out, gb2_out,
+                    o_got, part_ref, out_buf, in_buf, ag_ref, da_ref, dm_ref, u_ref, f_ref, att_ref, do_buf, x1_ref, br_ref, t_ref,
+                    o_send, o_recv, rs_send, rs_recv, ag_send, ag_recv, dm_send, dm_recv, do_send, do_recv):
+    f, z, core, base, peers = column_peers(n_z)
+    ring = ZRing(f, z, n_z)
+    bf16, f32 = jnp.bfloat16, jnp.float32
+    pad, width = x_ref.shape
+    rank = ao_ref.shape[0]
+    share = ao_ref.shape[1]
+    meet(peers)
+
+    def modulation(row):
+        return jnp.where(own_ref[...] > 0, mod_ref[row:row + 1, :], mod_ref[8 + row:9 + row, :])
+
+    home = [(base + z // 2, 2 * core + i) for i in range(2)]
+    for i in range(2):
+        here = (z // 2 == core) & (2 * core + i == z)
+
+        @pl.when(here)
+        def _():
+            copy = pltpu.make_async_copy(o_ref.at[i], o_got.at[z % 2], o_recv.at[z % 2])
+            copy.start()
+            copy.wait()
+
+        @pl.when(jnp.logical_not(here))
+        def _():
+            push(o_ref.at[i], o_got.at[z % 2], o_send.at[i], o_recv.at[z % 2], home[i]).start()
+
+    dm_ref[z, :, :] = (modulation(5) * g_ref[...].astype(f32)).astype(bf16)
+    ring.start(lambda to: dm_ref.at[z], dm_ref, dm_send, dm_recv)
+
+    for s in range(2):
+        here = (z // 2 == core) & (2 * core + s == z)
+
+        @pl.when(jnp.logical_not(here))
+        def _():
+            push(o_got.at[s], o_got.at[s], o_send.at[s], o_recv.at[s], home[s]).wait_recv()
+
+    owner = owner_ref[...]
+    att_ref[...] = jnp.where(
+        owner > 0, o_got[0].astype(f32), jnp.where(owner < 0, o_got[1].astype(f32), 0.0)).astype(bf16)
+
+    def scatter(turn, main, rank_part):
+        full = jnp.concatenate([main, rank_part], axis=1)
+        full = full.reshape(n_z, pad, full.shape[1])
+        part_ref[...] = full
+        out_buf[...] = full.astype(bf16)
+        ring.start(lambda to: out_buf.at[to], in_buf.at[turn], rs_send.at[turn], rs_recv.at[turn])
+
+    def collect(turn):
+        ring.wait(in_buf.at[turn], rs_send.at[turn], rs_recv.at[turn])
+        total = part_ref[z]
+        for j in range(1, n_z):
+            total = total + in_buf[turn, (z + j) % n_z].astype(f32)
+        ring.drain(lambda to: out_buf.at[to], in_buf.at[turn], rs_send.at[turn], rs_recv.at[turn])
+        return total[:, :width], (total[:, width:] * lmask_ref[...]).astype(bf16)
+
+    def spread(turn, ref, *parts):
+        offset = 0
+        for part in parts:
+            ref[z, :, offset:offset + part.shape[1]] = part
+            offset += part.shape[1]
+        ring.start(lambda to: ref.at[z], ref, ag_send.at[turn], ag_recv.at[turn])
+
+    def spread_end(turn, ref):
+        ring.wait(ref, ag_send.at[turn], ag_recv.at[turn])
+        ring.drain(lambda to: ref.at[z], ref, ag_send.at[turn], ag_recv.at[turn])
+
+    def gathered(ref, start, count):
+        return ref[:, :, start:start + count].reshape(n_z * pad, count)
+
+    def own_lanes(ref):
+        at = pl.ds(pl.multiple_of(z * share, 128), share)
+        return ref[:, :, at].reshape(n_z * pad, share)
+
+    mask = mask_ref[...]
+    att = att_ref[...]
+    scatter(0, mm_t(att, wo_ref[...]), mm_t(att, ao_ref[...]))
+    branch, to_mine = collect(0)
+    branch = branch + mm(to_mine, bo_ref[...])
+    br_ref[...] = branch
+    x1 = x_ref[...].astype(f32) + modulation(2) * branch
+    x1_ref[...] = x1
+    xh, _inv = norm_rows(x1)
+    h2 = (xh * (1.0 + modulation(4)) + modulation(3)).astype(bf16)
+    spread(0, ag_ref, h2, to_mine)
+    spread_end(0, ag_ref)
+    h2_all = gathered(ag_ref, 0, width)
+    to_all = gathered(ag_ref, width, rank)
+    t1 = (mm_t(h2_all, a1_ref[...]) * mask).astype(bf16)
+    u = mm(h2_all, w1_ref[...]) + mm(t1, b1_ref[...])
+    u_ref[...] = u
+    act = gelu_parts(u)[0].astype(bf16)
+    f_ref[...] = act
+    scatter(1, mm_t(act, w2_ref[...]), mm_t(act, a2_ref[...]))
+    t_ref[0] = to_all
+    t_ref[1] = t1
+    feed, t2_mine = collect(1)
+    feed = feed + mm(t2_mine, b2_ref[...])
+    y_out[...] = (x1_ref[...] + modulation(5) * feed).astype(bf16)
+
+    def collapse(place, values):
+        for s in range(2):
+            sums_out[2 * place + s:2 * place + s + 1, :] = jnp.sum(
+                jnp.where(own_ref[...] == (1.0 if s == 0 else -1.0), values, 0.0), axis=0, keepdims=True)
+
+    collapse(3, g_ref[...].astype(f32) * feed)
+
+    ring.wait(dm_ref, dm_send, dm_recv)
+    ring.drain(lambda to: dm_ref.at[z], dm_ref, dm_send, dm_recv)
+    dm_all = dm_ref[...].reshape(n_z * pad, width)
+    dt2 = (mm_t(dm_all, b2_ref[...]) * mask).astype(bf16)
+    df = mm(dm_all, w2_ref[...]) + mm(dt2, a2_ref[...])
+    ga2_out[...] = t_mm(dt2, f_ref[...])
+    du = (df * gelu_parts(u_ref[...])[1]).astype(bf16)
+    scatter(2, mm_t(du, w1_ref[...]), mm_t(du, b1_ref[...]))
+    gb1_out[...] = t_mm(t_ref[1], du)
+    dh, dt1_mine = collect(2)
+    dh = dh + mm(dt1_mine, a1_ref[...])
+    xh, inverse = norm_rows(x1_ref[...])
+    dz = dh * (1.0 + modulation(4))
+    dx1 = g_ref[...].astype(f32) + inverse * (
+        dz - jnp.mean(dz, axis=-1, keepdims=True) - xh * jnp.mean(dz * xh, axis=-1, keepdims=True))
+    spread(1, da_ref, (modulation(2) * dx1).astype(bf16), dt1_mine, t2_mine)
+    dx1_out[...] = dx1
+    collapse(0, dx1 * br_ref[...])
+    collapse(1, dh)
+    collapse(2, dh * xh)
+    spread_end(1, da_ref)
+    da_all = gathered(da_ref, 0, width)
+    dt1 = gathered(da_ref, width, rank)
+    t2 = gathered(da_ref, width + rank, rank)
+    dto = (mm_t(da_all, bo_ref[...]) * mask).astype(bf16)
+    do_buf[...] = (mm(da_all, wo_ref[...]) + mm(dto, ao_ref[...])).astype(bf16)
+    for s in range(2):
+        here = (z // 2 == core) & (2 * core + s == z)
+
+        @pl.when(here)
+        def _():
+            copy = pltpu.make_async_copy(do_buf, do_out.at[z % 2], do_recv.at[z % 2])
+            copy.start()
+            copy.wait()
+
+        @pl.when(jnp.logical_not(here))
+        def _():
+            push(do_buf, do_out.at[z % 2], do_send.at[s], do_recv.at[z % 2], (base + z // 2, 2 * core + s)).start()
+
+    gao_out[...] = t_mm(dto, att_ref[...])
+    gbo_out[...] = t_mm(t_ref[0], own_lanes(da_ref))
+    gb2_out[...] = t_mm(t2, own_lanes(dm_ref))
+    ga1_out[...] = t_mm(dt1, own_lanes(ag_ref))
+    for i in range(2):
+        here = (z // 2 == core) & (2 * core + i == z)
+
+        @pl.when(jnp.logical_not(here))
+        def _():
+            push(do_out.at[i], do_out.at[i], do_send.at[i], do_recv.at[i], home[i]).wait_recv()
+            push(do_buf, do_out.at[i], do_send.at[i], do_recv.at[i], home[i]).wait_send()
+            push(o_ref.at[i], o_got.at[z % 2], o_send.at[i], o_recv.at[z % 2], home[i]).wait_send()
+
+
+def text_mid(o, x, g, mod, owner, own, mask, lmask, wo, w1, w2, pair_o, pair_1, pair_2, n_z, cid):
+    pad, width = x.shape
+    rank, share = pair_o[0].shape
+    total = n_z * pad
+    hidden = w1.shape[1]
+    wide = width + rank
+    f32, bf16 = jnp.float32, jnp.bfloat16
+    shape = jax.ShapeDtypeStruct
+    vmem = pltpu.VMEM
+    dma = pltpu.SemaphoreType.DMA
+    args = (o, x, g, mod, owner, own, mask, lmask, wo, w1, w2, *pair_o, *pair_1, *pair_2)
+    out_shape = [
+        shape((pad, width), bf16), shape((pad, width), f32), shape((2, total, share), bf16), shape((8, width), f32),
+        shape((rank, share), f32), shape((rank, share), f32), shape((rank, share), f32), shape((rank, hidden), f32),
+        shape((rank, hidden), f32), shape((rank, share), f32),
+    ]
+    return pl.pallas_call(
+        functools.partial(text_mid_kernel, n_z),
+        out_shape=out_shape,
+        in_specs=[pl.BlockSpec(memory_space=vmem)] * len(args),
+        out_specs=[pl.BlockSpec(memory_space=vmem)] * len(out_shape),
+        scratch_shapes=[
+            vmem((2, total, share), bf16), vmem((n_z, pad, wide), f32), vmem((n_z, pad, wide), bf16),
+            vmem((3, n_z, pad, wide), bf16), vmem((n_z, pad, wide), bf16), vmem((n_z, pad, wide + rank), bf16),
+            vmem((n_z, pad, width), bf16),
+            vmem((total, hidden), f32), vmem((total, hidden), bf16), vmem((total, share), bf16),
+            vmem((total, share), bf16), vmem((pad, width), f32), vmem((pad, width), f32), vmem((2, total, rank), bf16),
+            dma((2,)), dma((2,)), dma((3, n_z)), dma((3, n_z)), dma((2, n_z)), dma((2, n_z)), dma((n_z,)), dma((n_z,)),
+            dma((2,)), dma((2,)),
+        ],
+        compiler_params=pltpu.CompilerParams(collective_id=cid, has_side_effects=True, vmem_limit_bytes=50 * 1024 * 1024),
+        name="text_block",
+    )(*args)
 
 HD = 64
 FF = 6144
@@ -532,10 +975,15 @@
     got = gather([w[0] for w in local], [w[1] for w in local] + [adapter_rows], n_f, n_z)
     got = [g.reshape(-1, g.shape[-1]) for g in got]
     img_w, txt_w, row = got[:4], got[4:8], got[8]
-    x_img = reshard(image_tokens).astype(F32)
-    g_img = reshard(image_cot).astype(F32)
-    x_txt = text_tokens.astype(F32)
-    g_txt = text_cot.astype(F32)
+    x_img = reshard(image_tokens)
+    g_img = reshard(image_cot)
+    txt_pad = (txt_local + 15) // 16 * 16
+
+    def padded(values):
+        return jnp.pad(values, ((0, txt_pad - txt_local), (0, 0)))
+
+    x_txt_low, g_txt_low = padded(text_tokens), padded(text_cot)
+    x_txt = x_txt_low.astype(F32)
 
     seg_ends = jnp.cumsum(text_lengths[0])
     slot_ids = jnp.arange(slots)
@@ -544,8 +992,16 @@
         segment = jnp.sum((position[:, None] >= seg_ends[None, :]).astype(jnp.int32), axis=1)
         return (segment[:, None] == slot_ids[None, :]).astype(F32)
 
-    owner_group = owner_of(jnp.arange(txt_group))
-    owner_local = owner_of(z * txt_local + jnp.arange(txt_local))
+    def real(owner):
+        place = jnp.arange(owner.shape[0]) % txt_pad
+        return jnp.where((place < txt_local)[:, None], owner, 0.0)
+
+    def position(rows):
+        return rows // txt_pad * txt_local + rows % txt_pad
+
+    txt_rows = jnp.arange(n_z * txt_pad)
+    owner_group = real(owner_of(position(txt_rows)))
+    owner_local = real(owner_of(z * txt_local + jnp.arange(txt_pad)))
     txt_mask = jnp.repeat(owner_group, RANK, axis=1)
     txt_mask_local = jnp.repeat(owner_local, RANK, axis=1)
     rank_cols = slots * RANK
@@ -591,10 +1047,10 @@
         for s in range(column_count)
     ]
     img_msg = jnp.concatenate([img_a, jnp.stack(img_b)], axis=2)
-    txt_rows = jnp.concatenate(
+    txt_a_rows = jnp.concatenate(
         [a_rows[0][0], a_rows[1][0], a_rows[1][1], a_rows[1][3]], axis=0
     )
-    txt_a = a_pick(txt_rows, own_hot).reshape(slots, RANK, -1)
+    txt_a = a_pick(txt_a_rows, own_hot).reshape(slots, RANK, -1)
     txt_b_own = [
         [b_pick(stream, index, own_picks[s]) for s in range(slots)]
         for stream, index in [(0, 0), (1, 0), (1, 1), (1, 2), (1, 3), (1, 4)]
@@ -676,8 +1132,7 @@
         count = values.shape[1] // n_z
         return lax.dynamic_slice_in_dim(values, z * count, count, 1)
 
-    inputs = [x_img, x_txt]
-    cots = [g_img, g_txt]
+    inputs = [x_img.astype(F32), x_txt]
     norm_one = [layer_norm(values) for values in inputs]
     heads_in = [
         (norm_one[s][0] * (1.0 + stretch(s, 1)) + stretch(s, 0)).astype(BF16) for s in range(2)
@@ -696,54 +1151,52 @@
     img_qkv_mid, img_qkv = project(heads_in[0], img_w[0], img_pairs[1], None, False)
     txt_qkv, img_qkv = txt_qkv.astype(BF16), img_qkv.astype(BF16)
     img_heads = to_heads(img_qkv)
-    txt_heads = jnp.concatenate(to_chip([txt_qkv, txt_qkv]), axis=1)
+    txt_heads = jnp.stack(to_chip([txt_qkv, txt_qkv]))
     lengths = by_group(text_lengths[0:1], swap_core(text_lengths[0:1]))
     chip_lengths = jnp.cumsum(lax.dynamic_index_in_dim(lengths, z // slots, 0, keepdims=False))
     chip_slot = z % slots
     chip_segment = jnp.sum(
-        (jnp.arange(txt_group)[:, None] >= chip_lengths[None, :]).astype(jnp.int32),
+        (position(txt_rows)[:, None] >= chip_lengths[None, :]).astype(jnp.int32),
         axis=1,
         keepdims=True,
     )
-    chip_owner = chip_segment == chip_slot
+    chip_owner = (chip_segment == chip_slot) & (txt_rows % txt_pad < txt_local)[:, None]
     bias = jnp.where(chip_owner, 0.0, -1e30).astype(F32)
     o_img, o_txt, lse = attend(img_heads, txt_heads, bias, HD)
 
     def txt_home(values):
-        half = values.shape[1] // 2
-        got = from_chip([values[:, :half], values[:, half:]])
-        return jnp.where(owner_group[:, 0:1] > 0, got[0], got[1])
-
-    attended = [to_tokens(o_img), txt_home(o_txt)]
-
-    txt_branch, txt_out_mid = give(
-        inner_right(attended[1], txt_w[1]), inner_right(attended[1], txt_pairs[2][0])
+        got = from_chip([values[0], values[1]])
+        return jnp.where(owner_group[:, 0:1] > 0, got[0], jnp.where(owner_group[:, 1:2] > 0, got[1], 0))
+
+    attended = to_tokens(o_img)
+    thick = 128
+
+    def thicker(part):
+        return jnp.concatenate([part, jnp.zeros((thick - part.shape[0], part.shape[1]), part.dtype)], axis=0)
+
+    def sign(owner):
+        return owner[:, 0:1] - owner[:, 1:2]
+
+    def lanes_pad(mask):
+        return jnp.pad(mask, ((0, 0), (0, thick - mask.shape[1])))
+
+    txt_mod = jnp.pad(txt_mods.reshape(slots, 6, width), ((0, 0), (0, 2), (0, 0))).reshape(-1, width)
+    thick_pairs = [None] + [tuple(thicker(part) for part in txt_pairs[index]) for index in range(1, 5)]
+    (txt_result, txt_grad_after, do_txt, txt_sums, *txt_sides) = text_mid(
+        o_txt, x_txt_low, g_txt_low, txt_mod, sign(owner_group), sign(owner_local), lanes_pad(txt_mask),
+        lanes_pad(txt_mask_local), txt_w[1], txt_w[2], txt_w[3], thick_pairs[2], thick_pairs[3], thick_pairs[4],
+        n_z, 2,
     )
-    txt_branch = txt_branch + matmul(txt_out_mid, txt_pairs[2][1])
-    img_out_mid, img_branch = project(attended[0], img_w[1], img_pairs[2], None, True)
-    branch = [img_branch, txt_branch]
-    after = [inputs[s] + stretch(s, 2) * branch[s] for s in range(2)]
-    norm_two = [layer_norm(values) for values in after]
-    mlp_in = [
-        (norm_two[s][0] * (1.0 + stretch(s, 4)) + stretch(s, 3)).astype(BF16) for s in range(2)
-    ]
-
-    txt_mlp = share(jnp.concatenate([mlp_in[1], txt_out_mid], axis=1))
-    txt_mlp, txt_out_mid = txt_mlp[:, :width], txt_mlp[:, width:]
-    txt_fc1_mid, txt_pre = project(txt_mlp, txt_w[2], txt_pairs[3], txt_mask, False)
-    txt_act = gelu(txt_pre).astype(BF16)
-    txt_feed, txt_fc2_mid = give(
-        inner_right(txt_act, txt_w[3]), inner_right(txt_act, txt_pairs[4][0])
+    txt_sides = [part[:rank_cols] for part in txt_sides]
+    txt_sums = txt_sums.reshape(4, slots, width)
+
+    img_rows_mod = jnp.concatenate([img_mod.reshape(6, width), jnp.zeros((2, width), F32)], axis=0)
+    (img_branch, img_after, img_mlp, img_pre, img_result, *img_mids, img_gate) = block_fwd(
+        attended, x_img, g_img, img_rows_mod, img_w[1], img_pairs[2], img_pairs[3], img_w[2],
+        img_pairs[4], img_w[3],
     )
-    txt_feed = txt_feed + matmul(txt_fc2_mid, txt_pairs[4][1])
-    img_fc1_mid, img_pre = project(mlp_in[0], img_w[2], img_pairs[3], None, False)
-    img_act = gelu(img_pre).astype(BF16)
-    img_fc2_mid, img_feed = project(img_act, img_w[3], img_pairs[4], None, True)
-    feed = [img_feed, txt_feed]
-    results = [(after[s] + stretch(s, 5) * feed[s]).astype(BF16) for s in range(2)]
-    image_out = unshard(results[0])
-
-    grad_feed = [(stretch(s, 5) * cots[s]).astype(BF16) for s in range(2)]
+    image_out = unshard(img_result)
+
     grads = [[None] * 5 for stream in range(2)]
 
     def project_back(grad, weight, pair, mask, flipped):
@@ -754,55 +1207,25 @@
         main = matmul(grad, weight) if flipped else inner_right(grad, weight)
         return middle, main + matmul(middle, pair[0])
 
-    img_back_mid, img_grad_act = project_back(grad_feed[0], img_w[3], img_pairs[4], None, True)
-    grads[0][4] = (inner_left(img_back_mid, img_act), inner_left(img_fc2_mid, grad_feed[0]))
-    img_grad_pre = gelu_back(img_pre, img_grad_act).astype(BF16)
-    img_back_mid, img_grad_norm = project_back(img_grad_pre, img_w[2], img_pairs[3], None, False)
-    grads[0][3] = (inner_left(img_back_mid, mlp_in[0]), inner_left(img_fc1_mid, img_grad_pre))
-
-    txt_feed_full = share(grad_feed[1])
-    txt_back_mid, txt_grad_act = project_back(txt_feed_full, txt_w[3], txt_pairs[4], txt_mask, True)
-    txt_fc2_grad_a = inner_left(txt_back_mid, txt_act)
-    txt_grad_pre = gelu_back(txt_pre, txt_grad_act).astype(BF16)
-    txt_grad_norm, txt_fc1_back = give(
-        inner_right(txt_grad_pre, txt_w[2]), inner_right(txt_grad_pre, txt_pairs[3][1])
+    (img_grad_after, img_grad_att, img_sums, *sides) = block_back(
+        g_img, img_after, img_branch, img_mlp, attended, img_rows_mod, img_pre, img_w[3],
+        img_pairs[4], img_w[2], img_pairs[3], img_w[1], img_pairs[2], img_mids,
     )
-    txt_grad_norm = txt_grad_norm + matmul(txt_fc1_back, txt_pairs[3][0])
-    grad_norm = [img_grad_norm, txt_grad_norm]
+    grads[0][4] = (sides[0], sides[3])
+    grads[0][3] = (sides[2], sides[1])
+    grads[0][2] = (sides[4], sides[5])
     mod_parts = [[None] * 6 for stream in range(2)]
-    grad_after = []
-    for s in range(2):
-        grad_after.append(
-            cots[s] + norm_back(grad_norm[s], norm_two[s][0], norm_two[s][1], stretch(s, 4))
-        )
-        mod_parts[s][3] = collapse(s, grad_norm[s])
-        mod_parts[s][4] = collapse(s, grad_norm[s] * norm_two[s][0])
-        mod_parts[s][5] = collapse(s, cots[s] * feed[s])
-        mod_parts[s][2] = collapse(s, grad_after[s] * branch[s])
-    grad_branch = [(stretch(s, 2) * grad_after[s]).astype(BF16) for s in range(2)]
-
-    img_back_mid, img_grad_att = project_back(grad_branch[0], img_w[1], img_pairs[2], None, True)
-    grads[0][2] = (inner_left(img_back_mid, attended[0]), inner_left(img_out_mid, grad_branch[0]))
-    shared = share(jnp.concatenate([grad_branch[1], txt_fc1_back, txt_fc2_mid], axis=1))
-    txt_branch_full = shared[:, :width]
-    txt_fc1_back = shared[:, width : width + rank_cols]
-    txt_fc2_mid = shared[:, width + rank_cols :]
-    grads[1][4] = (txt_fc2_grad_a, inner_left(txt_fc2_mid, lanes(txt_feed_full)))
-    grads[1][3] = (
-        inner_left(txt_fc1_back, lanes(txt_mlp)),
-        inner_left(txt_fc1_mid, txt_grad_pre),
-    )
-    txt_back_mid, txt_grad_att = project_back(
-        txt_branch_full, txt_w[1], txt_pairs[2], txt_mask, True
-    )
-    grads[1][2] = (
-        inner_left(txt_back_mid, attended[1]),
-        inner_left(txt_out_mid, lanes(txt_branch_full)),
-    )
-    txt_grad_att = txt_grad_att.astype(BF16)
-    do_img = to_heads(img_grad_att.astype(BF16))
-    do_txt = jnp.concatenate(to_chip([txt_grad_att, txt_grad_att]), axis=1)
-    do_txt = jnp.where(chip_owner, do_txt, jnp.zeros_like(do_txt))
+    for place in range(4):
+        mod_parts[1][2 + place] = txt_sums[place]
+    grads[1][2] = (txt_sides[0], txt_sides[1])
+    grads[1][3] = (txt_sides[2], txt_sides[3])
+    grads[1][4] = (txt_sides[4], txt_sides[5])
+    img_sums = jnp.sum(jnp.concatenate([img_sums, img_gate]).reshape(4, 8, width), axis=1)
+    for place in range(4):
+        mod_parts[0][2 + place] = img_sums[place : place + 1]
+    grad_after = [img_grad_after, txt_grad_after]
+
+    do_img = to_heads(img_grad_att)
     d_img, d_txt = attend_back(img_heads, txt_heads, bias, do_img, do_txt, lse, HD)
     img_grad_qkv = to_tokens(d_img)
     txt_grad_qkv = txt_home(d_txt)
@@ -893,7 +1316,9 @@
         total = keep + sent.astype(F32)
         step *= 2
     adapter_grad = total.reshape(1, -1)
-    return (image_out, results[1], image_grad, grad_inputs[1], cond_grad, adapter_grad)
+    return (
+        image_out, txt_result[:txt_local], image_grad, grad_inputs[1][:txt_local], cond_grad, adapter_grad
+    )
 
 
 def solution(mesh):

time: 1220 us -> 1200 us (0.984)
  Pallas kernels: 439 us -> 665 us
  matrix products: 241 us -> 88.8 us
  waiting for transfers between devices: 170 us -> 122 us
  starting transfers between devices: 125 us -> 87.5 us
    pallas_call x0 -> x3, Pallas kernels: none -> 220 us  [the longest x1 121 us: text_mid(): pl.pallas_call(functools.partial(text_mid_kernel, n_z), out_shape=out_sha...]
    dot_general x30 -> x12, matrix products: 105 us -> 24.9 us  [matmul(): return jnp.dot(left, right, preferred_element_type=F32)]
    dot_general x33 -> x15, matrix products: 88.8 us -> 28.5 us  [inner_right(): lax.dot_general(left, right, (((left.ndim - 1,), (right.ndim - 1,)), ((),...]
    ppermute x51 -> x33, waiting for transfers between devices: 107 us -> 62.3 us  [z_swap(): return lax.ppermute(values, 'tp', [(i, i ^ step) for i in range(n_z)])]
    ppermute x51 -> x33, starting transfers between devices: 57.6 us -> 38.1 us  [z_swap(): return lax.ppermute(values, 'tp', [(i, i ^ step) for i in range(n_z)])]
    ppermute x8 -> x6, waiting for transfers between devices: 32.6 us -> 30.9 us  [from_chip(): got.append(lax.ppermute(mine, BOTH, [(b, a) for a, b in round_pairs(r)]))]
    unnamed x529 -> x347, local copies, waits for them, and re-layouts: 30.7 us -> 30.3 us
  transfers between devices with their start and end apart: 80 -> 58, of which waited for: 35 -> 19; matrix products, arithmetic and copies ran while one was open for 23% -> 20% of each run, Pallas kernels for 33% -> 44%
where the time goes in v3:
time: 1200 us; the launch traced here: 1190 us
  Pallas kernels  665 us (55%)
  waiting for transfers between devices  122 us (10%)
  local copies, waits for them, and re-layouts  100 us (8%)
  matrix products  88.8 us (7%)
  starting transfers between devices  87.5 us (7%)
  other arithmetic  77.9 us (6%)
  between operations  31.2 us (3%)
  blocking collectives  19.3 us (2%)
    pallas_call x1, Pallas kernels, gather(): pl.pallas_call(functools.partial(gather_kernel, n_f, n_z, len(full), len(...  346 us
    pallas_call x1, Pallas kernels, text_mid(): pl.pallas_call(functools.partial(text_mid_kernel, n_z), out_shape=out_sha...  121 us
    ppermute x33, waiting for transfers between devices, z_swap(): return lax.ppermute(values, 'tp', [(i, i ^ step) for i in range(n_z)])  62.3 us
    pallas_call x1, Pallas kernels, attend_back(): pl.pallas_call(functools.partial(attend_back_kernel, hd, bq), grid=(pairs...  61.5 us
    pallas_call x1, Pallas kernels, block_back(): pl.pallas_call(functools.partial(block_back_kernel, tiles), grid=(tiles,)...  53.5 us
    pallas_call x1, Pallas kernels, block_fwd(): pl.pallas_call(functools.partial(block_fwd_kernel, tiles), grid=(tiles,),...  45.5 us
    ppermute x33, starting transfers between devices, z_swap(): return lax.ppermute(values, 'tp', [(i, i ^ step) for i in range(n_z)])  38.1 us
    pallas_call x1, Pallas kernels, attend(): pl.pallas_call(functools.partial(attend_kernel, hd, bq), grid=(pairs,), i...  37.7 us
  transfers between devices with their start and end apart: 58, of which 19 were waited for; matrix products, arithmetic and copies ran while one was open for 20% of the time, Pallas kernels for 44%

profile of v3, /device:TPU:11, one launch (start us, length us, event | category | flops | bytes accessed | tf_op | source)
XLA Modules:
  0.0 1192.2 jit_solution(6165307171567399101)
XLA Ops:
  8.8 9.4 all-gather
  23.3 4.4 collective-permute-start
  36.1 13.6 %convert_reduce_fusion.1 = bf16[282624]{0:T(1024)(128)(2,1)} fusion(f32[1,282624]{1,0:T(1,128)} %param.18), kind=kLoop, calls=%fused_computation.84 | loop fusion | flops 282624 | bytes 1695744 | tf_op jit(solution)/shard_map/convert_element_type | solution.py:974
  53.3 346.0 %weight_gather.1 = (bf16[8,192,4608]{2,1,0:T(8,128)(2,1)}, bf16[8,192,1536]{2,1,0:T(8,128)(2,1)}, bf16[8,192,6144]{2,1,0:T(8,128)(2,1)}, bf16[8,192,6144]{2,1,0:...) custom-call(bf16[192,1152]{1,0:T(8,128)(2,1)} %get-tuple-element.169, ...), custom_call_target="tpu_custom_call" | custom-call | tf_op jit(solution)/shard_map/weight_gather/pallas_call | solution.py:236
  432.2 6.2 collective-permute-start.4
  446.8 5.9 collective-permute-done.5
  464.0 2.3 collective-permute-start.11
  468.8 8.3 collective-permute-done.12
  477.3 6.5 collective-permute-done.11
  483.8 3.1 collective-permute-start.15
  486.9 5.6 collective-permute-start.9
  496.3 4.3 collective-permute-start.21
  507.1 10.2 fusion.227
  521.7 4.6 collective-permute-start.13
  527.6 3.6 collective-permute-start.17
  537.3 13.0 %collective-permute-done.18 = bf16[192,1152]{1,0:T(8,128)(2,1)S(1)} collective-permute-done((bf16[192,1152]{1,0:T(8,128)(2,1)S(1)}, bf16[192,1152]{1,0:T(8,128)(2,1)S(1)}, u32[]{:S(2)}, u32[]{:S(2)}) %collective-permute-start.18) | collective-permute-done | bytes 442400 | tf_op jit(solution)/shard_map/ppermute | solution.py:915
  558.2 2.5 pad_maximum_fusion.img_ref
  560.7 37.7 %attend.1 = (bf16[1024,768]{1,0:T(8,128)(2,1)S(1)}, bf16[2,192,384]{2,1,0:T(8,128)(2,1)S(1)}, f32[6,2,1216]{2,1,0:T(2,128)S(1)}) custom-call(bf16[1024,2304]{1,0:T(8,128)(2,1)} %pad_maximum_fusion.img_ref, bf16[2,192,1152]{2,1,0:T(8,128)(2,1)S(1)} %pad_maximum_fusion.14.txt_ref, f32[192,1]{1,0:T(8,128)S(1)} %fusion.119.bias_ref), custom_call_target="tpu_custom_call" | custom-call | tf_op jit(solution)/shard_map/attend/pallas_call | solution.py:288
  601.4 121.1 %text_block.1 = (bf16[48,1536]{1,0:T(8,128)(2,1)S(1)}, f32[48,1536]{1,0:T(8,128)S(1)}, bf16[2,192,384]{2,1,0:T(8,128)(2,1)S(1)}, f32[8,1536]{1,0:T(8,128)S(1)}, ...) custom-call(bf16[2,192,384]{2,1,0:T(8,128)(2,1)S(1)} %get-tuple-elem, ...), custom_call_target="tpu_custom_call" | custom-call | tf_op jit(solution)/shard_map/text_block/pallas_call | solution.py:802
  737.0 45.5 %block_forward.1 = (f32[512,1536]{1,0:T(8,128)}, f32[512,1536]{1,0:T(8,128)}, bf16[512,1536]{1,0:T(8,128)(2,1)}, f32[512,6144]{1,0:T(8,128)}, bf16[512,1536]{1,0...) custom-call(bf16[512,1536]{1,0:T(8,128)(2,1)} %pad_maximum_fusion.3., ...), custom_call_target="tpu_custom_call" | custom-call | flops 21743271936 | bytes 37748736 | tf_op jit(solution)/shard_map/block_forward/pallas_call | solution.py:473
  782.4 53.5 %block_backward.1 = (f32[512,1536]{1,0:T(8,128)}, bf16[512,1536]{1,0:T(8,128)(2,1)}, f32[24,1536]{1,0:T(8,128)}, f32[16,6144]{1,0:T(8,128)}, f32[16,6144]{1,0:T(...) custom-call(bf16[512,1536]{1,0:T(8,128)(2,1)} %get-tuple-element.285.g_ref, ...), custom_call_target="tpu_custom_call" | custom-call | flops 21743271936 | bytes 37748736 | tf_op jit(solution)/shard_map/block_backward/pallas_call | solution.py:567
  847.9 2.6 collective-permute-start.49
  851.7 4.2 collective-permute-start.23
  857.9 3.6 collective-permute-done.48
  861.7 22.5 %collective-permute-done.49 = f32[16,4608]{1,0:T(8,128)S(1)} collective-permute-done((f32[16,4608]{1,0:T(8,128)S(1)}, f32[16,4608]{1,0:T(8,128)S(1)}, u32[]{:S(2)}, u32[]{:S(2)}) %collective-permute-start.49) | collective-permute-done | bytes 294944 | tf_op jit(solution)/shard_map/ppermute | solution.py:940
  893.2 61.5 %attend_back.1 = (bf16[1024,2304]{1,0:T(8,128)(2,1)}, bf16[2,192,1152]{2,1,0:T(8,128)(2,1)S(1)}) custom-call(bf16[1024,2304]{1,0:T(8,128)(2,1)} %pad_maximum_fusion.img_ref, bf16[2,192,1152]{2,1,0:T(8,128)(2,1)S(1)} %pad_maximum_fusion.14.txt_ref, f32[192,1]{1,0:T(8,128)S(1)} %fusion.119.bias_ref, bf16[1024,768]{1,0:T(8,128)(2,1)S(1)} %pad_maximum_fusion.6.doi_ref, ...), custom_call_target="tpu_custom_call" | custom-call | tf_op jit(solution)/shard_map/attend_back/pallas_call | solution.py:363
  957.9 4.2 broadcast_select_fusion.2
  962.1 4.7 collective-permute-done.29
  966.8 11.3 collective-permute-done.30
  981.0 2.6 collective-permute-start.33
  988.3 8.4 collective-permute-done.33
  1009.1 3.4 collective-permute-start.24
  1015.9 3.5 broadcast_select_fusion.1
  1025.5 16.6 %fusion.15 = (f32[1536]{0:T(1024)S(1)}, f32[512]{0:T(512)}, f32[512]{0:T(512)}, f32[1536]{0:T(1024)S(1)}, f32[512,1536]{1,0:T(8,128)}) fusion(f32[512]{0:T(512)S(1)} %copy-done.117, f32[512]{0:T(512)S(1)} %copy-done.114, bf16[256,1536]{1,0:T(8,128)(2,1)S(1)} %copy-done.26, bf16[256,1536]{1,0:T(8,128)(2,1)S(1)} %copy-done.23, f32[1536]{0:T(1024)S(1)} %copy-done.101, ...), kind=kOutput, calls=%fused_computation.28 | convolution fusion | flops 7268200448 | bytes 26765312 | tf_op jit(solution)/shard_map/dot_general | solution.py:844
  1049.1 4.3 collective-permute-start.36
  1058.7 9.9 all_gather.7
  1072.0 2.5 collective-permute-start.42
  1078.4 3.1 collective-permute-start.45
  1085.3 2.4 collective-permute-done.45
  1102.6 2.8 convolution_dynamic-update-slice_fusion.1
  1115.6 2.7 convolution_dynamic-update-slice_fusion
  1119.0 3.9 fusion.19
  1128.6 3.5 bitcast_add_fusion
  1137.6 4.2 all-to-all-start
  1141.9 4.3 collective-permute-start.27
  1147.7 13.9 %all-to-all-done = f32[8,2,192]{2,1,0:T(2,128)S(1)} async-done(((f32[8,2,192]{2,1,0:T(2,128)}), f32[8,2,192]{2,1,0:T(2,128)S(1)}, u32[]{:S(2)}, u32[]{:S(2)}) %all-to-all-start) | async-done | bytes 12320 | tf_op jit(solution)/shard_map/all_to_all | solution.py:1272
  1167.2 4.7 collective-permute-done.27
  1171.8 10.2 collective-permute-done.28
  (755 shorter events, 232.2 us)
Async XLA Ops:
  7.2 447.2 %all-reduce.14.cloned.1.call-start = ((), (), s32[]{:S(2)}) async-start(), calls=%async_computation.1 | async-start | bytes 589824
  7.2 432.5 %collective-permute-start.19 = (s32[1,2]{1,0:T(1,128)}, s32[1,2]{1,0:T(1,128)}, u32[]{:S(2)}, u32[]{:S(2)}) collective-permute-start(s32[1,2]{1,0:T(1,128)} %param.16), channel_id=1, source_target_pairs={{0,4},{4,0},{8,12},{12,8},{16,20},{20,16},{24,28},{28,24},{1,5},{5... | collective-permute-start | bytes 32 | tf_op jit(solution)/shard_map/ppermute | solution.py:932
  8.0 413.6 %collective-permute-start.2 = (s32[2]{0:T(128)}, s32[2]{0:T(128)S(1)}, u32[]{:S(2)}, u32[]{:S(2)}) collective-permute-start(s32[2]{0:T(128)} %param.17), channel_id=1, source_target_pairs={{0,4},{4,0},{8,12},{12,8},{16,20},{20,16},{24,28},{28,24},{1,5},{5... | collective-permute-start | bytes 32 | tf_op jit(solution)/shard_map/ppermute | solution.py:932
  23.3 480.2 %collective-permute-start = (bf16[256,1536]{1,0:T(8,128)(2,1)}, bf16[256,1536]{1,0:T(8,128)(2,1)}, u32[]{:S(2)}, u32[]{:S(2)}) collective-permute-start(bf16[256,1536]{1,0:T(8,128)(2,1)} %get-tuple-element.147), channel_id=1, source_target_pairs={{0,0},{1,1},{2,4},{3,5},{4,2},{5,3},{6,6},{7,7},{8,8},{9,9},{10,12... | collective-permute-start | bytes 2359304 | tf_op jit(solution)/shard_map/ppermute | solution.py:915
  27.7 475.8 %collective-permute-start.1 = (bf16[256,1536]{1,0:T(8,128)(2,1)}, bf16[256,1536]{1,0:T(8,128)(2,1)}, u32[]{:S(2)}, u32[]{:S(2)}) collective-permute-start(bf16[256,1536]{1,0:T(8,128)(2,1)} %get-tuple-element.148), channel_id=1, source_target_pairs={{0,1},{1,0},{2,5},{3,4},{4,3},{5,2},{6,7},{7,6},{8,9},{9,8},{10,13... | collective-permute-start | bytes 2359304 | tf_op jit(solution)/shard_map/ppermute | solution.py:915
  432.2 14.5 %collective-permute-start.4 = (bf16[32,2304]{1,0:T(8,128)(2,1)}, bf16[32,2304]{1,0:T(8,128)(2,1)S(1)}, u32[]{:S(2)}, u32[]{:S(2)}) collective-permute-start(bf16[32,2304]{1,0:T(8,128)(2,1)} %maximum_maximum_fusion.2), channel_id=1, source_target_pairs={{0,2},{1,3},{2,0},{3,1},{4,6},{5,7},{6,4},{7,5},{8,10},{9,11},{10,... | collective-permute-start | bytes 442376 | tf_op jit(solution)/shard_map/ppermute | solution.py:940
  438.5 8.3 collective-permute-start.3
  439.7 13.0 %collective-permute-start.5 = (bf16[32,2304]{1,0:T(8,128)(2,1)}, bf16[32,2304]{1,0:T(8,128)(2,1)}, u32[]{:S(2)}, u32[]{:S(2)}) collective-permute-start(bf16[32,2304]{1,0:T(8,128)(2,1)} %maximum_maximum_fusion.2), channel_id=1, source_target_pairs={{0,3},{1,2},{2,1},{3,0},{4,7},{5,6},{6,5},{7,4},{8,11},{9,10},{10,... | collective-permute-start | bytes 442376 | tf_op jit(solution)/shard_map/ppermute | solution.py:940
  456.5 7.4 collective-permute-start.6
  458.4 7.9 collective-permute-start.8
  463.3 13.8 %collective-permute-start.12 = (bf16[16,6528]{1,0:T(8,128)(2,1)S(1)}, bf16[16,6528]{1,0:T(8,128)(2,1)S(1)}, u32[]{:S(2)}, u32[]{:S(2)}) collective-permute-start(bf16[16,6528]{1,0:T(8,128)(2,1)S(1)} %get-tuple-element.181), channel_id=1, source_target_pairs={{0,3},{1,2},{2,1},{3,0},{4,7},{5,6},{6,5},{7,4},{8,11},{9,10},{10,... | collective-permute-start | bytes 626696 | tf_op jit(solution)/shard_map/ppermute | solution.py:940
  464.0 19.9 %collective-permute-start.11 = (bf16[16,6528]{1,0:T(8,128)(2,1)S(1)}, bf16[16,6528]{1,0:T(8,128)(2,1)S(1)}, u32[]{:S(2)}, u32[]{:S(2)}) collective-permute-start(bf16[16,6528]{1,0:T(8,128)(2,1)S(1)} %get-tuple-element.182), channel_id=1, source_target_pairs={{0,2},{1,3},{2,0},{3,1},{4,6},{5,7},{6,4},{7,5},{8,10},{9,11},{10,... | collective-permute-start | bytes 626696 | tf_op jit(solution)/shard_map/ppermute | solution.py:940
  466.3 20.7 %collective-permute-start.10 = (bf16[16,6528]{1,0:T(8,128)(2,1)S(1)}, bf16[16,6528]{1,0:T(8,128)(2,1)}, u32[]{:S(2)}, u32[]{:S(2)}) collective-permute-start(bf16[16,6528]{1,0:T(8,128)(2,1)S(1)} %get-tuple-element.183), channel_id=1, source_target_pairs={{0,1},{1,0},{2,3},{3,2},{4,5},{5,4},{6,7},{7,6},{8,9},{9,8},{10,11... | collective-permute-start | bytes 626696 | tf_op jit(solution)/shard_map/ppermute | solution.py:940
  477.1 19.1 %collective-permute-start.16 = (bf16[48,1536]{1,0:T(8,128)(2,1)S(1)}, bf16[48,1536]{1,0:T(8,128)(2,1)}, u32[]{:S(2)}, u32[]{:S(2)}) collective-permute-start(bf16[48,1536]{1,0:T(8,128)(2,1)S(1)} %fusion.18), channel_id=1, source_target_pairs={{0,3},{1,2},{2,1},{3,0},{4,7},{5,6},{6,5},{7,4},{8,11},{9,10},{10,... | collective-permute-start | bytes 442376 | tf_op jit(solution)/shard_map/ppermute | solution.py:940
  483.8 16.7 %collective-permute-start.15 = (bf16[48,1536]{1,0:T(8,128)(2,1)S(1)}, bf16[48,1536]{1,0:T(8,128)(2,1)}, u32[]{:S(2)}, u32[]{:S(2)}) collective-permute-start(bf16[48,1536]{1,0:T(8,128)(2,1)S(1)} %fusion.18), channel_id=1, source_target_pairs={{0,2},{1,3},{2,0},{3,1},{4,6},{5,7},{6,4},{7,5},{8,10},{9,11},{10,... | collective-permute-start | bytes 442376 | tf_op jit(solution)/shard_map/ppermute | solution.py:940
  486.9 7.0 collective-permute-start.9
  494.0 7.4 collective-permute-start.14
  496.3 58.3 %collective-permute-start.21 = (bf16[256,1536]{1,0:T(8,128)(2,1)}, bf16[256,1536]{1,0:T(8,128)(2,1)}, u32[]{:S(2)}, u32[]{:S(2)}) collective-permute-start(bf16[256,1536]{1,0:T(8,128)(2,1)} %get-tuple-element.143), channel_id=1, source_target_pairs={{0,0},{1,1},{2,4},{3,5},{4,2},{5,3},{6,6},{7,7},{8,8},{9,9},{10,12... | collective-permute-start | bytes 2359304 | tf_op jit(solution)/shard_map/ppermute | solution.py:915
  500.6 54.0 %collective-permute-start.22 = (bf16[256,1536]{1,0:T(8,128)(2,1)}, bf16[256,1536]{1,0:T(8,128)(2,1)}, u32[]{:S(2)}, u32[]{:S(2)}) collective-permute-start(bf16[256,1536]{1,0:T(8,128)(2,1)} %get-tuple-element.144), channel_id=1, source_target_pairs={{0,1},{1,0},{2,5},{3,4},{4,3},{5,2},{6,7},{7,6},{8,9},{9,8},{10,13... | collective-permute-start | bytes 2359304 | tf_op jit(solution)/shard_map/ppermute | solution.py:915
  521.7 34.3 %collective-permute-start.13 = (bf16[512,2304]{1,0:T(8,128)(2,1)}, bf16[512,2304]{1,0:T(8,128)(2,1)}, u32[]{:S(2)}, u32[]{:S(2)}) collective-permute-start(bf16[512,2304]{1,0:T(8,128)(2,1)} %broadcast_select_fusion.6), channel_id=1, source_target_pairs={{0,4},{4,0},{8,12},{12,8},{16,20},{20,16},{24,28},{28,24},{1,5},{5... | collective-permute-start | bytes 7077896 | tf_op jit(solution)/shard_map/ppermute | solution.py:932
  526.9 23.3 %collective-permute-start.18 = (bf16[192,1152]{1,0:T(8,128)(2,1)S(1)}, bf16[192,1152]{1,0:T(8,128)(2,1)S(1)}, u32[]{:S(2)}, u32[]{:S(2)}) collective-permute-start(bf16[192,1152]{1,0:T(8,128)(2,1)S(1)} %fusion.17), channel_id=1, source_target_pairs={{0,1},{1,0},{2,5},{3,4},{4,3},{5,2},{6,7},{7,6},{8,9},{9,8},{10,13... | collective-permute-start | bytes 1327112 | tf_op jit(solution)/shard_map/ppermute | solution.py:915
  527.6 25.6 %collective-permute-start.17 = (bf16[192,1152]{1,0:T(8,128)(2,1)S(1)}, bf16[192,1152]{1,0:T(8,128)(2,1)}, u32[]{:S(2)}, u32[]{:S(2)}) collective-permute-start(bf16[192,1152]{1,0:T(8,128)(2,1)S(1)} %fusion.17), channel_id=1, source_target_pairs={{0,0},{1,1},{2,4},{3,5},{4,2},{5,3},{6,6},{7,7},{8,8},{9,9},{10,12... | collective-permute-start | bytes 1327112 | tf_op jit(solution)/shard_map/ppermute | solution.py:915
  599.4 135.1 %collective-permute-start.20 = (bf16[512,768]{1,0:T(8,128)(2,1)}, bf16[512,768]{1,0:T(8,128)(2,1)}, u32[]{:S(2)}, u32[]{:S(2)}) collective-permute-start(bf16[512,768]{1,0:T(8,128)(2,1)} %broadcast_select_fusion.16), channel_id=1, source_target_pairs={{0,4},{4,0},{8,12},{12,8},{16,20},{20,16},{24,28},{28,24},{1,5},{5... | collective-permute-start | bytes 2359304 | tf_op jit(solution)/shard_map/ppermute | solution.py:932
  844.5 46.7 %collective-permute-start.25 = (bf16[512,768]{1,0:T(8,128)(2,1)}, bf16[512,768]{1,0:T(8,128)(2,1)}, u32[]{:S(2)}, u32[]{:S(2)}) collective-permute-start(bf16[512,768]{1,0:T(8,128)(2,1)} %broadcast_select_fusion.12), channel_id=1, source_target_pairs={{0,4},{4,0},{8,12},{12,8},{16,20},{20,16},{24,28},{28,24},{1,5},{5... | collective-permute-start | bytes 2359304 | tf_op jit(solution)/shard_map/ppermute | solution.py:932
  847.8 9.9 collective-permute-start.47
  847.8 13.7 %collective-permute-start.48 = (f32[16,4608]{1,0:T(8,128)S(1)}, f32[16,4608]{1,0:T(8,128)S(1)}, u32[]{:S(2)}, u32[]{:S(2)}) collective-permute-start(f32[16,4608]{1,0:T(8,128)S(1)} %bitcast.480), channel_id=1, source_target_pairs={{0,2},{1,3},{2,0},{3,1},{4,6},{5,7},{6,4},{7,5},{8,10},{9,11},{10,... | collective-permute-start | bytes 884744 | tf_op jit(solution)/shard_map/ppermute | solution.py:940
  847.9 36.3 %collective-permute-start.49 = (f32[16,4608]{1,0:T(8,128)S(1)}, f32[16,4608]{1,0:T(8,128)S(1)}, u32[]{:S(2)}, u32[]{:S(2)}) collective-permute-start(f32[16,4608]{1,0:T(8,128)S(1)} %bitcast.479), channel_id=1, source_target_pairs={{0,3},{1,2},{2,1},{3,0},{4,7},{5,6},{6,5},{7,4},{8,11},{9,10},{10,... | collective-permute-start | bytes 884744 | tf_op jit(solution)/shard_map/ppermute | solution.py:940
  851.7 273.1 %collective-permute-start.23 = (bf16[256,1536]{1,0:T(8,128)(2,1)}, bf16[256,1536]{1,0:T(8,128)(2,1)}, u32[]{:S(2)}, u32[]{:S(2)}) collective-permute-start(bf16[256,1536]{1,0:T(8,128)(2,1)} %get-tuple-element.139), channel_id=1, source_target_pairs={{0,0},{1,1},{4,2},{5,3},{2,4},{3,5},{6,6},{7,7},{8,8},{9,9},{12,10... | collective-permute-start | bytes 2359304 | tf_op jit(solution)/shard_map/ppermute | solution.py:922
  954.7 12.1 %collective-permute-start.29 = (bf16[192,1152]{1,0:T(8,128)(2,1)S(1)}, bf16[192,1152]{1,0:T(8,128)(2,1)S(1)}, u32[]{:S(2)}, u32[]{:S(2)}) collective-permute-start(bf16[192,1152]{1,0:T(8,128)(2,1)S(1)} %get-tuple-element.164), channel_id=1, source_target_pairs={{0,0},{1,1},{4,2},{5,3},{2,4},{3,5},{6,6},{7,7},{8,8},{9,9},{12,10... | collective-permute-start | bytes 1327112 | tf_op jit(solution)/shard_map/ppermute | solution.py:922
  956.8 21.4 %collective-permute-start.30 = (bf16[192,1152]{1,0:T(8,128)(2,1)S(1)}, bf16[192,1152]{1,0:T(8,128)(2,1)S(1)}, u32[]{:S(2)}, u32[]{:S(2)}) collective-permute-start(bf16[192,1152]{1,0:T(8,128)(2,1)S(1)} %get-tuple-element.165), channel_id=1, source_target_pairs={{1,0},{0,1},{5,2},{4,3},{3,4},{2,5},{7,6},{6,7},{9,8},{8,9},{13,10... | collective-permute-start | bytes 1327112 | tf_op jit(solution)/shard_map/ppermute | solution.py:922
  962.1 53.8 %collective-permute-start.26 = (bf16[512,2304]{1,0:T(8,128)(2,1)}, bf16[512,2304]{1,0:T(8,128)(2,1)}, u32[]{:S(2)}, u32[]{:S(2)}) collective-permute-start(bf16[512,2304]{1,0:T(8,128)(2,1)} %broadcast_select_fusion.2), channel_id=1, source_target_pairs={{0,4},{4,0},{8,12},{12,8},{16,20},{20,16},{24,28},{28,24},{1,5},{5... | collective-permute-start | bytes 7077896 | tf_op jit(solution)/shard_map/ppermute | solution.py:932
  981.0 7.2 collective-permute-start.32
  981.0 15.6 %collective-permute-start.33 = (bf16[48,1568]{1,0:T(8,128)(2,1)S(1)}, bf16[48,1568]{1,0:T(8,128)(2,1)S(1)}, u32[]{:S(2)}, u32[]{:S(2)}) collective-permute-start(bf16[48,1568]{1,0:T(8,128)(2,1)S(1)} %get-tuple-element.151), channel_id=1, source_target_pairs={{0,3},{1,2},{2,1},{3,0},{4,7},{5,6},{6,5},{7,4},{8,11},{9,10},{10,... | collective-permute-start | bytes 451592 | tf_op jit(solution)/shard_map/ppermute | solution.py:940
  996.8 7.5 collective-permute-start.52
  996.9 7.5 collective-permute-start.51
  997.7 8.0 collective-permute-start.50
  1004.4 8.2 collective-permute-start.39
  1005.6 6.9 collective-permute-start.40
  1009.1 115.7 %collective-permute-start.24 = (bf16[256,1536]{1,0:T(8,128)(2,1)}, bf16[256,1536]{1,0:T(8,128)(2,1)}, u32[]{:S(2)}, u32[]{:S(2)}) collective-permute-start(bf16[256,1536]{1,0:T(8,128)(2,1)} %get-tuple-element.140), channel_id=1, source_target_pairs={{1,0},{0,1},{5,2},{4,3},{3,4},{2,5},{7,6},{6,7},{9,8},{8,9},{13,10... | collective-permute-start | bytes 2359304 | tf_op jit(solution)/shard_map/ppermute | solution.py:922
  1048.9 6.8 collective-permute-start.37
  1074.5 7.1 collective-permute-start.41
  1078.0 7.3 collective-permute-start.46
  1078.4 9.4 collective-permute-start.45
  1133.3 30.9 %collective-permute-start.54 = (bf16[2,2208,128]{2,1,0:T(8,128)(2,1)}, bf16[2,2208,128]{2,1,0:T(8,128)(2,1)}, u32[]{:S(2)}, u32[]{:S(2)}) collective-permute-start(bf16[2,2208,128]{2,1,0:T(8,128)(2,1)} %fusion.22), channel_id=1, source_target_pairs={{0,8},{4,12},{8,0},{12,4},{16,24},{20,28},{24,16},{28,20},{1,9},{5... | collective-permute-start | bytes 3391496 | tf_op jit(solution)/shard_map/ppermute | solution.py:1315
  1137.6 24.1 %all-to-all-start = ((f32[8,2,192]{2,1,0:T(2,128)}), f32[8,2,192]{2,1,0:T(2,128)S(1)}, u32[]{:S(2)}, u32[]{:S(2)}) async-start(f32[8,2,192]{2,1,0:T(2,128)} %reshape.672), calls=%async_computation | async-start | bytes 32768 | tf_op jit(solution)/shard_map/all_to_all | solution.py:1272
  1141.9 29.9 %collective-permute-start.27 = (bf16[256,1536]{1,0:T(8,128)(2,1)S(1)}, bf16[256,1536]{1,0:T(8,128)(2,1)S(1)}, u32[]{:S(2)}, u32[]{:S(2)}) collective-permute-start(bf16[256,1536]{1,0:T(8,128)(2,1)S(1)} %get-tuple-element.135), channel_id=1, source_target_pairs={{0,0},{1,1},{4,2},{5,3},{2,4},{3,5},{6,6},{7,7},{8,8},{9,9},{12,10... | collective-permute-start | bytes 2359304 | tf_op jit(solution)/shard_map/ppermute | solution.py:922
  1146.2 35.8 %collective-permute-start.28 = (bf16[256,1536]{1,0:T(8,128)(2,1)S(1)}, bf16[256,1536]{1,0:T(8,128)(2,1)S(1)}, u32[]{:S(2)}, u32[]{:S(2)}) collective-permute-start(bf16[256,1536]{1,0:T(8,128)(2,1)S(1)} %get-tuple-element.136), channel_id=1, source_target_pairs={{1,0},{0,1},{5,2},{4,3},{3,4},{2,5},{7,6},{6,7},{9,8},{8,9},{13,10... | collective-permute-start | bytes 2359304 | tf_op jit(solution)/shard_map/ppermute | solution.py:922
  1166.4 17.6 %collective-permute-start.55 = (bf16[1,2208,128]{2,1,0:T(8,128)(2,1)S(1)}, bf16[1,2208,128]{2,1,0:T(8,128)(2,1)S(1)}, u32[]{:S(2)}, u32[]{:S(2)}) collective-permute-start(bf16[1,2208,128]{2,1,0:T(8,128)(2,1)S(1)} %dynamic-slice_convert_fusion.2), channel_id=1, source_target_pairs={{0,16},{4,20},{8,24},{12,28},{16,0},{20,4},{24,8},{28,12},{1,17},{... | collective-permute-start | bytes 1695752 | tf_op jit(solution)/shard_map/ppermute | solution.py:1315
  (158 other events, 1480.4 us)
Sparse Core Ops, SparseCore 0:
  22.1 53.0 all-reduce.13

commit v4 on v3

--- a/solution.py
+++ b/solution.py
@@ -817,6 +817,292 @@
         name="text_block",
     )(*args)
 
+
+def flip_bits(chip, mask, nbits):
+    other = 0
+    for bit in range(nbits):
+        have = (chip // (1 << bit)) % 2
+        other = other + (1 - have if (mask >> bit) & 1 else have) * (1 << bit)
+    return other
+
+
+def tail_kernel(n_f, n_z, fans, cols, *refs):
+    it = iter(refs)
+    take = lambda count: [next(it) for _ in range(count)]
+    grad_ref, = take(1)
+    img_a, img_b, txt_a, txt_b = take(4), take(4), take(4), take(4)
+    hot4_ref, hot2_ref, dmod_ref, wmod_ref, bmod_ref, tmod_ref, cond_ref, smask_ref = take(8)
+    grad_out, cond_out, rank_out, shard_out = take(4)
+    zmsg, zgot, dense, snd1, rcv1, snd2, rcv2, dgot, own_dm, all_dm, cpart, cgot, zsum, zall, dts = take(15)
+    (g_send, g_recv, z_send, z_recv, c_send, c_recv, s_send, s_recv, d_send, d_recv, f_send, f_recv, p_send, p_recv,
+     q_send, q_recv, t_send, t_recv) = take(18)
+    f32, bf16 = jnp.float32, jnp.bfloat16
+    f, z, core, base, column = column_peers(n_z)
+    chip = f // 2
+    chips = n_f // 2
+    nbits = bits_of(chips)
+    partner = base + 1 - core
+    around = [((f + j) % n_f, z) for j in range(1, n_f)]
+    others = [(flip_bits(chip, mask, nbits) * 2 + side, z) for mask in range(1, chips) for side in range(2)]
+    meet(column + others)
+    ring = ZRing(f, z, n_z)
+    blk = shard_out.shape[0]
+    hidden_rank = hot2_ref.shape[0]
+
+    def dmod_copy(index, peer):
+        return push(dmod_ref.at[peer[1]], dgot.at[core * n_z + z], d_send.at[index], d_recv.at[core * n_z + z], peer)
+
+    for index, peer in enumerate(column):
+        dmod_copy(index, peer).start()
+    dgot[core * n_z + z] = dmod_ref[z]
+
+    offset = 0
+    spans = []
+    for part, sizes in ((img_a, fans), (img_b, cols)):
+        for index in range(4):
+            count = sizes[index + 1] // n_z
+            for t in range(n_z):
+                zmsg[t, :, offset:offset + count] = part[index][:, t * count:(t + 1) * count].astype(bf16)
+            spans.append((offset, count))
+            offset += count
+    ring.start(lambda to: zmsg.at[to], zgot, z_send, z_recv)
+    zgot[z] = zmsg[z]
+
+    for index, peer in enumerate(column):
+        place = peer[0] % 2 * n_z + peer[1]
+        push(dgot.at[place], dgot.at[place], d_send.at[index], d_recv.at[place], peer).wait_recv()
+    rows = []
+    for slot in range(2):
+        rows.append(dgot[2 * core + slot, 0] + dgot[n_z + 2 * core + slot, 0])
+    for slot in range(2):
+        total = dgot[core * n_z, 1 + slot]
+        for t in range(1, n_z):
+            total = total + dgot[core * n_z + t, 1 + slot]
+        rows.append(total)
+    chunk = dmod_ref.shape[-1]
+    own_dm[...] = jnp.zeros_like(own_dm)
+    for r, total in enumerate(rows):
+        for j in range(own_dm.shape[1] // chunk):
+            own_dm[r:r + 1, j * chunk:(j + 1) * chunk] = total[j:j + 1, :].astype(bf16).astype(f32)
+    for j in range(1, n_f):
+        push(own_dm, all_dm.at[f], f_send.at[j], f_recv.at[f], around[j - 1]).start()
+    all_dm[f] = own_dm[...]
+    dm_low = own_dm[...].astype(bf16)
+    tmod = [tmod_ref[s].astype(bf16) for s in range(2)]
+    gb_mod = [t_mm(tmod[s], dm_low) for s in range(2)]
+    rank_img = mm_t(dm_low, bmod_ref[0])
+    rank_txt = mm_t(dm_low, bmod_ref[1])
+    row = lax.broadcasted_iota(jnp.int32, rank_img.shape, 0)
+    rank_part = jnp.where(row < 2, rank_img, rank_txt)
+
+    hot2 = hot2_ref[...]
+    starts = []
+    offset = 0
+    for stream in range(2):
+        for index in range(5):
+            starts.append((stream, index, offset, offset + fans[index] // n_z))
+            offset += fans[index] // n_z + cols[index] // n_z
+
+    def put_a(at, part, hot):
+        dense[at:at + part.shape[1], :] = dots(part, hot, 0, 0)
+
+    def put_b(at, part, hot):
+        full = dots(hot, part, 0, 0)
+        blocks = part.shape[1] // 128
+        for j in range(blocks):
+            dense[pl.ds(at + j, 128, stride=blocks), :] = full[:, j * 128:(j + 1) * 128]
+
+    for stream, index, at_a, at_b in starts:
+        if index == 0:
+            dense[at_a:at_b, :] = jnp.zeros((at_b - at_a, 128), f32)
+            put_b(at_b, gb_mod[stream].astype(bf16), hot2)
+        elif stream == 1:
+            put_a(at_a, txt_a[index - 1][...].astype(bf16), hot2)
+            put_b(at_b, txt_b[index - 1][...].astype(bf16), hot2)
+
+    ring.wait(zgot, z_send, z_recv)
+    hot4 = hot4_ref[...]
+    for stream, index, at_a, at_b in starts:
+        if stream == 0 and index > 0:
+            for at, put, (begin, count) in ((at_a, put_a, spans[index - 1]), (at_b, put_b, spans[index + 3])):
+                part = zgot[:, :, begin:begin + count].reshape(hot4.shape[0], count)
+                put(at, part, hot4)
+
+    home = [(base + z // 2, 2 * core + i) for i in range(2)]
+
+    def is_here(i):
+        return (z // 2 == core) & (2 * core + i == z)
+
+    for i in range(2):
+        @pl.when(is_here(i))
+        def _():
+            pltpu.make_async_copy(grad_ref.at[i], grad_out.at[z % 2], g_recv.at[z % 2]).start()
+
+        @pl.when(jnp.logical_not(is_here(i)))
+        def _():
+            push(grad_ref.at[i], grad_out.at[z % 2], g_send.at[i], g_recv.at[z % 2], home[i]).start()
+
+    def block(number):
+        return pl.ds(pl.multiple_of(number * blk, 16), blk)
+
+    for p in range(chips):
+        snd1[p] = dense[block(2 * p + 1 - core), :].astype(bf16)
+        push(snd1.at[p], rcv1.at[p], c_send.at[p], c_recv.at[p], (partner, z)).start()
+
+    for j in range(1, n_f):
+        came = (f - j + n_f) % n_f
+        push(own_dm, all_dm.at[came], f_send.at[j], f_recv.at[came], (came, z)).wait_recv()
+    everyone = all_dm[...].reshape(n_f * 8, own_dm.shape[1]).astype(bf16)
+    part = mm_t(everyone, wmod_ref[0]) + pltpu.roll(mm_t(everyone, wmod_ref[1]), n_f * 8 - 2, 0)
+    k_local = part.shape[1]
+    cpart[...] = jnp.zeros_like(cpart)
+    cpart[:, :, :k_local] = part.reshape(n_f, 8, k_local)
+    for j in range(1, n_f):
+        to = (f + j) % n_f
+        push(cpart.at[to], cgot.at[f], p_send.at[j], p_recv.at[f], (to, z)).start()
+    cgot[f] = cpart[f]
+
+    for p in range(chips):
+        push(snd1.at[p], rcv1.at[p], c_send.at[p], c_recv.at[p], (partner, z)).wait_recv()
+
+    def mine_of(p):
+        return block(2 * p + core)
+
+    for p in range(chips):
+        dense[mine_of(p), :] += rcv1[p].astype(f32)
+
+    half = blk // 2
+    orders = [list(range(nbits)), list(range(nbits))[::-1]]
+
+    def masks_at(side, turn):
+        left = orders[side][turn:]
+        return [sum(1 << b for i, b in enumerate(left) if (m >> i) & 1) for m in range(1 << len(left))]
+
+    def rs_copy(side, turn, index):
+        slot = turn * 2 + index
+        peer = flip_bits(chip, 1 << orders[side][turn], nbits) * 2 + core
+        return push(snd2.at[side, slot], rcv2.at[side, slot], s_send.at[side, slot], s_recv.at[side, slot], (peer, z))
+
+    def half_of(number, side):
+        return pl.ds(pl.multiple_of((2 * number + core) * blk + side * half, 16), half)
+
+    def rs_start(turn):
+        for side in range(2):
+            bit = 1 << orders[side][turn]
+            for index, mask in enumerate(masks_at(side, turn + 1)):
+                number = flip_bits(chip, bit | mask, nbits)
+                snd2[side, turn * 2 + index] = dense[half_of(number, side), :].astype(bf16)
+                rs_copy(side, turn, index).start()
+
+    def rs_end(turn):
+        for side in range(2):
+            for index, mask in enumerate(masks_at(side, turn + 1)):
+                number = flip_bits(chip, mask, nbits)
+                rs_copy(side, turn, index).wait_recv()
+                dense[half_of(number, side), :] += rcv2[side, turn * 2 + index].astype(f32)
+
+    rs_start(0)
+
+    for j in range(1, n_f):
+        came = (f - j + n_f) % n_f
+        push(cpart.at[came], cgot.at[came], p_send.at[j], p_recv.at[came], (came, z)).wait_recv()
+    zsum[:n_f] = cgot[...]
+    zsum[n_f] = jnp.zeros(zsum.shape[1:], f32)
+    zsum[n_f, :, :hidden_rank] = rank_part
+    zall[z] = zsum[...]
+    ring.start(lambda to: zsum, zall, q_send, q_recv)
+    ring.wait(zall, q_send, q_recv)
+    total = zall[0]
+    for t in range(1, n_z):
+        total = total + zall[t]
+    cond_out[...] = total[:n_f]
+    dt = (total[n_f][:, :hidden_rank] * smask_ref[...]).astype(bf16)
+    rank_out[...] = dt.astype(f32)
+    wide = mm(dt, hot2)
+    dts[f] = wide
+    for j in range(1, n_f):
+        push(dts.at[f], dts.at[f], t_send.at[j], t_recv.at[f], around[j - 1]).start()
+
+    rs_end(0)
+    if nbits > 1:
+        rs_start(1)
+    for j in range(1, n_f):
+        came = (f - j + n_f) % n_f
+        push(dts.at[came], dts.at[came], t_send.at[j], t_recv.at[came], (came, z)).wait_recv()
+    all_dt = dts[...].reshape(n_f * 8, 128)
+    row = lax.broadcasted_iota(jnp.int32, all_dt.shape, 0) % 8
+    act = cond_ref[...].reshape(n_f * 8, cond_ref.shape[-1]).astype(bf16)
+    mod_a = [
+        dots(act, jnp.where(row < 2, all_dt, 0.0).astype(bf16), 0, 0),
+        dots(act, pltpu.roll(jnp.where((row >= 2) & (row < 4), all_dt, 0.0), n_f * 8 - 2, 0).astype(bf16), 0, 0),
+    ]
+    if nbits > 1:
+        rs_end(1)
+    shard_out[...] = dense[block(f), :]
+    for stream in range(2):
+        first = starts[5 * stream][2]
+        own = jnp.where(f == first // blk, 1.0, 0.0)
+        count = mod_a[stream].shape[0]
+        shard_out[:count, :] += own * mod_a[stream]
+
+    ring.drain(lambda to: zmsg.at[to], zgot, z_send, z_recv)
+    ring.drain(lambda to: zsum, zall, q_send, q_recv)
+    for index, peer in enumerate(column):
+        dmod_copy(index, peer).wait_send()
+    for j in range(1, n_f):
+        to = (f + j) % n_f
+        push(own_dm, all_dm.at[f], f_send.at[j], f_recv.at[f], (to, z)).wait_send()
+        push(cpart.at[to], cgot.at[f], p_send.at[j], p_recv.at[f], (to, z)).wait_send()
+        push(dts.at[f], dts.at[f], t_send.at[j], t_recv.at[f], (to, z)).wait_send()
+    for p in range(chips):
+        push(snd1.at[p], rcv1.at[p], c_send.at[p], c_recv.at[p], (partner, z)).wait_send()
+    for turn in range(nbits):
+        for side in range(2):
+            for index in range(len(masks_at(side, turn + 1))):
+                rs_copy(side, turn, index).wait_send()
+    for i in range(2):
+        @pl.when(is_here(i))
+        def _():
+            pltpu.make_async_copy(grad_ref.at[i], grad_out.at[z % 2], g_recv.at[z % 2]).wait()
+
+        @pl.when(jnp.logical_not(is_here(i)))
+        def _():
+            push(grad_out.at[i], grad_out.at[i], g_send.at[i], g_recv.at[i], home[i]).wait_recv()
+            push(grad_ref.at[i], grad_out.at[z % 2], g_send.at[i], g_recv.at[z % 2], home[i]).wait_send()
+
+
+def tail(grad, img_a, img_b, txt_a, txt_b, hot4, hot2, dmod, wmod, bmod, tmod, cond, smask, n_f, n_z, fans, cols, cid):
+    f32, bf16 = jnp.float32, jnp.bfloat16
+    vmem, dma = pltpu.VMEM, pltpu.SemaphoreType.DMA
+    shape = jax.ShapeDtypeStruct
+    args = (grad, *img_a, *img_b, *txt_a, *txt_b, hot4, hot2, dmod, wmod, bmod, tmod, cond, smask)
+    lanes = (sum(fans[1:]) + sum(cols[1:])) // n_z
+    rows = 2 * (sum(fans) + sum(cols)) // n_z
+    blk = rows // n_f
+    chips = n_f // 2
+    cut = cols[0] // n_z
+    rank = hot2.shape[0]
+    inside = pl.BlockSpec(memory_space=vmem)
+    return pl.pallas_call(
+        functools.partial(tail_kernel, n_f, n_z, tuple(fans), tuple(cols)),
+        out_shape=[shape(grad.shape, bf16), shape((n_f, 8, 256), f32), shape((8, rank), f32), shape((blk, 128), f32)],
+        in_specs=[pl.BlockSpec(memory_space=pl.ANY)] + [inside] * (len(args) - 1),
+        out_specs=[pl.BlockSpec(memory_space=pl.ANY)] + [inside] * 3,
+        scratch_shapes=[
+            vmem((n_z, RANK, lanes), bf16), vmem((n_z, RANK, lanes), bf16), vmem((rows, 128), f32),
+            vmem((chips, blk, 128), bf16), vmem((chips, blk, 128), bf16),
+            vmem((2, 4, blk // 2, 128), bf16), vmem((2, 4, blk // 2, 128), bf16),
+            vmem((2 * n_z,) + dmod.shape[1:], f32), vmem((8, cut), f32), vmem((n_f, 8, cut), f32),
+            vmem((n_f, 8, 256), f32), vmem((n_f, 8, 256), f32), vmem((n_f + 1, 8, 256), f32),
+            vmem((n_z, n_f + 1, 8, 256), f32), vmem((n_f, 8, 128), f32),
+            dma((2,)), dma((2,)), dma((n_z,)), dma((n_z,)), dma((chips,)), dma((chips,)), dma((2, 4)), dma((2, 4)),
+            dma((2 * n_z,)), dma((2 * n_z,)), dma((n_f,)), dma((n_f,)), dma((n_f,)), dma((n_f,)), dma((n_z,)), dma((n_z,)),
+            dma((n_f,)), dma((n_f,)),
+        ],
+        compiler_params=pltpu.CompilerParams(collective_id=cid, has_side_effects=True, vmem_limit_bytes=56 * 1024 * 1024),
+        name="gradient_exchange",
+    )(*args)
+
 HD = 64
 FF = 6144
 NAD = 8
@@ -1249,16 +1535,39 @@
         )
         mod_parts[s][0] = collapse(s, grad_norm[s])
         mod_parts[s][1] = collapse(s, grad_norm[s] * norm_one[s][0])
+    img_dmod = jnp.concatenate(mod_parts[0], axis=1)
+    txt_dmod = jnp.concatenate(mod_parts[1], axis=1)
+    if n_f == 8:
+        cut = width // n_z
+        dmod = jnp.concatenate([img_dmod, txt_dmod]).reshape(1 + slots, n_z, -1, cut)
+        dmod = jnp.pad(jnp.swapaxes(dmod, 0, 1), ((0, 0), (0, 0), (0, 8 - dmod.shape[2]), (0, 0)))
+        tmod = jnp.stack([jnp.pad(mod_mid[s].astype(F32), ((2 * s, 6 - 2 * s), (0, 0))) for s in range(2)])
+        cond_own = jnp.pad(lanes(cond_all).astype(F32).reshape(n_f, slots, -1), ((0, 0), (0, 6), (0, 0)))
+        sides_of = lambda stream, side: [grads[stream][index][side] for index in range(1, 5)]
+        image_low, cond_slices, mod_rank, shard = tail(
+            grad_inputs[0].astype(BF16).reshape(2, quarter, width),
+            sides_of(0, 0), sides_of(0, 1), sides_of(1, 0), sides_of(1, 1),
+            one_hot.T.astype(BF16), own_hot.T.astype(BF16), dmod, mod_weight, jnp.stack(mod_b), tmod, cond_own,
+            jnp.pad(jnp.concatenate([seq_mask, seq_mask]), ((0, 4), (0, 0))),
+            n_f, n_z, fans, cols, 3,
+        )
+        image_grad = image_low.astype(F32)
+        cond_rows = jnp.swapaxes(cond_slices[:, :slots, :k_local], 0, 1).reshape(slots, width)
+        for s in range(2):
+            cond_rows = cond_rows + matmul(mod_rank[2 * s : 2 * s + 2].astype(BF16), mod_a[s])
+        cond_grad = jax.vjp(jax.nn.silu, conditioning)[1](cond_rows)[0]
+        adapter_grad = shard.reshape(1, -1)
+        return (
+            image_out, txt_result[:txt_local], image_grad, grad_inputs[1][:txt_local], cond_grad, adapter_grad
+        )
     image_grad = unshard(grad_inputs[0].astype(BF16)).astype(F32)
 
-    img_dmod = jnp.concatenate(mod_parts[0], axis=1)
     img_dmod = (img_dmod + swap_core(img_dmod)).astype(BF16)
     def lane_blocks(values):
         return jnp.swapaxes(values.reshape(values.shape[0], n_z, -1), 0, 1)
 
     img_dmods = jnp.concatenate(z_exchange(lane_blocks(img_dmod)), axis=0)
     img_dmods = lax.dynamic_slice_in_dim(img_dmods, core * slots, slots, 0)
-    txt_dmod = jnp.concatenate(mod_parts[1], axis=1)
     txt_dmods = sum(z_exchange(lane_blocks(txt_dmod))).astype(BF16)
     dmods = jnp.stack([img_dmods, txt_dmods], axis=1)
     dmods_all = lax.all_gather(dmods, "fsdp", axis=0, tiled=True)

time: 1200 us -> 1090 us (0.908)
  Pallas kernels: 665 us -> 743 us
  waiting for transfers between devices: 122 us -> 65.7 us
  local copies, waits for them, and re-layouts: 100 us -> 50.4 us
  matrix products: 88.8 us -> 51 us
  starting transfers between devices: 87.5 us -> 55.7 us
    pallas_call x0 -> x1, Pallas kernels: none -> 76.8 us  [tail(): pl.pallas_call(functools.partial(tail_kernel, n_f, n_z, tuple(fans), tupl...]
    ppermute x33 -> x18, waiting for transfers between devices: 62.3 us -> 34.9 us  [z_swap(): return lax.ppermute(values, 'tp', [(i, i ^ step) for i in range(n_z)])]
    unnamed x347 -> x179, local copies, waits for them, and re-layouts: 30.3 us -> 8.95 us
    reshape x22 -> x4, local copies, waits for them, and re-layouts: 20.9 us -> 0.19 us  [the longest x2 0.1 us: shards(): jnp.concatenate([img_dmod, txt_dmod]).reshape(1 + slots, n_z, -1, cut)]
    dot_general x10 -> x0, matrix products: 17.1 us -> none  [shards(): lax.dot_general(part_a, hot, (((0,), (1,)), ((), ())), precision=HIGH, pr...]
    ppermute x6 -> x4, waiting for transfers between devices: 30.9 us -> 14.3 us  [from_chip(): got.append(lax.ppermute(mine, BOTH, [(b, a) for a, b in round_pairs(r)]))]
    ppermute x33 -> x18, starting transfers between devices: 38.1 us -> 23 us  [z_swap(): return lax.ppermute(values, 'tp', [(i, i ^ step) for i in range(n_z)])]
    all_to_all x1 -> x0, waiting for transfers between devices: 13.9 us -> none  [shards(): cond_rows = lax.all_to_all(cond_slices, 'fsdp', 0, 2, tiled=True)[0]]
  transfers between devices with their start and end apart: 58 -> 36, of which waited for: 19 -> 13; matrix products, arithmetic and copies ran while one was open for 20% -> 12% of each run, Pallas kernels for 44% -> 53%
where the time goes in v4:
time: 1090 us; the launch traced here: 1080 us
  Pallas kernels  743 us (68%)
  other arithmetic  70.9 us (7%)
  waiting for transfers between devices  65.7 us (6%)
  starting transfers between devices  55.7 us (5%)
  matrix products  51 us (5%)
  local copies, waits for them, and re-layouts  50.4 us (5%)
  between operations  29.8 us (3%)
    pallas_call x1, Pallas kernels, gather(): pl.pallas_call(functools.partial(gather_kernel, n_f, n_z, len(full), len(...  346 us
    pallas_call x1, Pallas kernels, text_mid(): pl.pallas_call(functools.partial(text_mid_kernel, n_z), out_shape=out_sha...  122 us
    pallas_call x1, Pallas kernels, tail(): pl.pallas_call(functools.partial(tail_kernel, n_f, n_z, tuple(fans), tupl...  76.8 us
    pallas_call x1, Pallas kernels, attend_back(): pl.pallas_call(functools.partial(attend_back_kernel, hd, bq), grid=(pairs...  61.5 us
    pallas_call x1, Pallas kernels, block_back(): pl.pallas_call(functools.partial(block_back_kernel, tiles), grid=(tiles,)...  53.7 us
    pallas_call x1, Pallas kernels, block_fwd(): pl.pallas_call(functools.partial(block_fwd_kernel, tiles), grid=(tiles,),...  45.5 us
    pallas_call x1, Pallas kernels, attend(): pl.pallas_call(functools.partial(attend_kernel, hd, bq), grid=(pairs,), i...  37.6 us
    ppermute x18, waiting for transfers between devices, z_swap(): return lax.ppermute(values, 'tp', [(i, i ^ step) for i in range(n_z)])  34.9 us
  transfers between devices with their start and end apart: 36, of which 13 were waited for; matrix products, arithmetic and copies ran while one was open for 12% of the time, Pallas kernels for 53%

profile of v4, /device:TPU:11, one launch (start us, length us, event | category | flops | bytes accessed | tf_op | source)
XLA Modules:
  0.0 1076.0 jit_solution(17607646899575915699)
XLA Ops:
  8.8 9.4 all-gather
  23.3 4.4 collective-permute-start
  37.1 13.5 %convert_reduce_fusion.1 = bf16[282624]{0:T(1024)(128)(2,1)} fusion(f32[1,282624]{1,0:T(1,128)} %param.18), kind=kLoop, calls=%fused_computation.63 | loop fusion | flops 282624 | bytes 1695744 | tf_op jit(solution)/shard_map/convert_element_type | solution.py:1260
  50.6 2.1 slice_bitcast_fusion.4
  54.2 346.0 %weight_gather.1 = (bf16[8,192,4608]{2,1,0:T(8,128)(2,1)}, bf16[8,192,1536]{2,1,0:T(8,128)(2,1)}, bf16[8,192,6144]{2,1,0:T(8,128)(2,1)}, bf16[8,192,6144]{2,1,0:...) custom-call(bf16[192,1152]{1,0:T(8,128)(2,1)} %get-tuple-element.163, ...), custom_call_target="tpu_custom_call" | custom-call | tf_op jit(solution)/shard_map/weight_gather/pallas_call | solution.py:236
  400.3 2.0 fusion.122
  402.3 2.1 fusion.123
  404.5 2.2 fusion.121
  419.5 2.3 fusion.120
  438.2 6.2 collective-permute-start.4
  453.8 4.8 collective-permute-done.5
  463.2 1.8 collective-permute-start.6
  471.7 12.4 %collective-permute-done.12 = bf16[16,6528]{1,0:T(8,128)(2,1)S(1)} collective-permute-done((bf16[16,6528]{1,0:T(8,128)(2,1)S(1)}, bf16[16,6528]{1,0:T(8,128)(2,1)S(1)}, u32[]{:S(2)}, u32[]{:S(2)}) %collective-permute-start.12) | collective-permute-done | bytes 208928 | tf_op jit(solution)/shard_map/ppermute | solution.py:1226
  485.4 3.9 collective-permute-done.11
  489.3 3.1 collective-permute-start.15
  497.3 5.0 collective-permute-start.21
  506.9 10.2 fusion.129
  520.3 1.9 copy-done
  522.1 4.7 collective-permute-start.13
  529.5 4.9 collective-permute-start.17
  539.1 12.0 %collective-permute-done.18 = bf16[192,1152]{1,0:T(8,128)(2,1)} collective-permute-done((bf16[192,1152]{1,0:T(8,128)(2,1)S(1)}, bf16[192,1152]{1,0:T(8,128)(2,1)}, u32[]{:S(2)}, u32[]{:S(2)}) %collective-permute-start.18) | collective-permute-done | bytes 442400 | tf_op jit(solution)/shard_map/ppermute | solution.py:1201
  551.1 4.0 collective-permute-done.17
  556.4 3.5 broadcast_select_fusion.5
  559.9 2.4 pad_maximum_fusion.img_ref
  562.4 37.6 %attend.1 = (bf16[1024,768]{1,0:T(8,128)(2,1)S(1)}, bf16[2,192,384]{2,1,0:T(8,128)(2,1)S(1)}, f32[6,2,1216]{2,1,0:T(2,128)S(1)}) custom-call(bf16[1024,2304]{1,0:T(8,128)(2,1)} %pad_maximum_fusion.img_ref, bf16[2,192,1152]{2,1,0:T(8,128)(2,1)S(1)} %pad_maximum_fusion.12.txt_ref, f32[192,1]{1,0:T(8,128)S(1)} %fusion.63.bias_ref), custom_call_target="tpu_custom_call" | custom-call | tf_op jit(solution)/shard_map/attend/pallas_call | solution.py:288
  601.7 1.9 pad_maximum_fusion.2
  605.0 45.5 %block_forward.1 = (f32[512,1536]{1,0:T(8,128)}, f32[512,1536]{1,0:T(8,128)}, bf16[512,1536]{1,0:T(8,128)(2,1)}, f32[512,6144]{1,0:T(8,128)}, bf16[512,1536]{1,0...) custom-call(bf16[512,1536]{1,0:T(8,128)(2,1)} %pad_maximum_fusion.3., ...), custom_call_target="tpu_custom_call" | custom-call | flops 21743271936 | bytes 37748736 | tf_op jit(solution)/shard_map/block_forward/pallas_call | solution.py:473
  650.5 53.7 %block_backward.1 = (f32[512,1536]{1,0:T(8,128)}, bf16[512,1536]{1,0:T(8,128)(2,1)}, f32[24,1536]{1,0:T(8,128)}, f32[16,6144]{1,0:T(8,128)}, f32[16,6144]{1,0:T(...) custom-call(bf16[512,1536]{1,0:T(8,128)(2,1)} %get-tuple-element.255.g_ref, ...), custom_call_target="tpu_custom_call" | custom-call | flops 21743271936 | bytes 37748736 | tf_op jit(solution)/shard_map/block_backward/pallas_call | solution.py:567
  704.2 2.4 broadcast_select_fusion.11
  708.7 121.8 %text_block.1 = (bf16[48,1536]{1,0:T(8,128)(2,1)S(1)}, f32[48,1536]{1,0:T(8,128)S(1)}, bf16[2,192,384]{2,1,0:T(8,128)(2,1)S(1)}, f32[8,1536]{1,0:T(8,128)S(1)}, ...) custom-call(bf16[2,192,384]{2,1,0:T(8,128)(2,1)S(1)} %get-tuple-elem, ...), custom_call_target="tpu_custom_call" | custom-call | tf_op jit(solution)/shard_map/text_block/pallas_call | solution.py:802
  837.0 2.3 collective-permute-start.23
  842.0 61.5 %attend_back.1 = (bf16[1024,2304]{1,0:T(8,128)(2,1)}, bf16[2,192,1152]{2,1,0:T(8,128)(2,1)S(1)}) custom-call(bf16[1024,2304]{1,0:T(8,128)(2,1)} %pad_maximum_fusion.img_ref, bf16[2,192,1152]{2,1,0:T(8,128)(2,1)S(1)} %pad_maximum_fusion.12.txt_ref, f32[192,1]{1,0:T(8,128)S(1)} %fusion.63.bias_ref, bf16[1024,768]{1,0:T(8,128)(2,1)S(1)} %pad_maximum_fusion.6.doi_ref, ...), custom_call_target="tpu_custom_call" | custom-call | tf_op jit(solution)/shard_map/attend_back/pallas_call | solution.py:363
  903.5 3.7 collective-permute-start.27
  907.2 2.7 collective-permute-start.28
  909.9 2.6 broadcast_select_fusion.2
  914.0 7.7 collective-permute-done.27
  921.8 6.5 collective-permute-done.28
  930.4 2.6 collective-permute-start.31
  935.1 2.0 collective-permute-done.30
  937.1 9.0 collective-permute-done.31
  947.1 1.8 collective-permute-start.32
  951.3 1.8 fusion.56.refs_9_
  953.1 3.5 broadcast_select_fusion.1
  961.2 2.3 fusion.131
  963.4 16.1 %fusion.15 = (f32[1536]{0:T(1024)S(1)}, f32[512]{0:T(512)S(1)}, f32[512]{0:T(512)S(1)}, f32[1536]{0:T(1024)S(1)}, f32[512,1536]{1,0:T(8,128)}) fusion(f32[512]{0:T(512)S(1)} %copy-done.60, f32[512]{0:T(512)S(1)} %broadcast_multiply_fusion.2, bf16[256,1536]{1,0:T(8,128)(2,1)S(1)} %copy-done.5, bf16[256,1536]{1,0:T(8,128)(2,1)S(1)} %copy-done.2, ...), kind=kOutput, calls=%fused_computation.26 | convolution fusion | flops 7268200448 | bytes 26765312 | tf_op jit(solution)/shard_map/dot_general | solution.py:1130
  980.5 4.6 fusion.14
  985.1 76.8 %gradient_exchange.1 = (bf16[2,256,1536]{2,1,0:T(8,128)(2,1)}, f32[8,8,256]{2,1,0:T(8,128)}, f32[8,32]{1,0:T(8,128)}, f32[2208,128]{1,0:T(8,128)}) custom-call(bf16[2,256,1536]{2,1,0:T(8,128)(2,1)} %bitcast.286, f32[16,1536]{1,0:T(8,128)} %fusion.132.refs_1_, f32[16,1536]{1,0:T(8,128)} %get-tuple-element.77.refs_2_, f32[16,1536]{1,0:T(8,128)} %get-tuple-element.78.refs_3_, ...), custom_call_target="tpu_custom_call" | custom-call | tf_op jit(solution)/shard_map/gradient_exchange/pallas_call | solution.py:1086
  1064.5 3.5 convert_element_type.177
  (466 shorter events, 107.5 us)
Async XLA Ops:
  7.2 453.8 %all-reduce.19.cloned.1.call-start = ((), (), s32[]{:S(2)}) async-start(), calls=%async_computation | async-start | bytes 589824
  7.2 438.4 %collective-permute-start.19 = (s32[1,2]{1,0:T(1,128)}, s32[1,2]{1,0:T(1,128)}, u32[]{:S(2)}, u32[]{:S(2)}) collective-permute-start(s32[1,2]{1,0:T(1,128)} %param.16), channel_id=1, source_target_pairs={{0,4},{4,0},{8,12},{12,8},{16,20},{20,16},{24,28},{28,24},{1,5},{5... | collective-permute-start | bytes 32 | tf_op jit(solution)/shard_map/ppermute | solution.py:1218
  8.0 416.3 %collective-permute-start.2 = (s32[2]{0:T(128)}, s32[2]{0:T(128)}, u32[]{:S(2)}, u32[]{:S(2)}) collective-permute-start(s32[2]{0:T(128)} %param.17), channel_id=1, source_target_pairs={{0,4},{4,0},{8,12},{12,8},{16,20},{20,16},{24,28},{28,24},{1,5},{5... | collective-permute-start | bytes 32 | tf_op jit(solution)/shard_map/ppermute | solution.py:1218
  22.0 30.7 %copy-start.23 = (bf16[2,1536,192]{1,2,0:T(8,128)(2,1)S(1)}, bf16[2,1536,192]{1,2,0:T(8,128)(2,1)}, u32[]{:S(2)}) copy-start(bf16[2,1536,192]{1,2,0:T(8,128)(2,1)} %param.23) | copy-start | bytes 3538948
  23.3 480.0 %collective-permute-start = (bf16[256,1536]{1,0:T(8,128)(2,1)}, bf16[256,1536]{1,0:T(8,128)(2,1)}, u32[]{:S(2)}, u32[]{:S(2)}) collective-permute-start(bf16[256,1536]{1,0:T(8,128)(2,1)} %get-tuple-element.149), channel_id=1, source_target_pairs={{0,0},{1,1},{2,4},{3,5},{4,2},{5,3},{6,6},{7,7},{8,8},{9,9},{10,12... | collective-permute-start | bytes 2359304 | tf_op jit(solution)/shard_map/ppermute | solution.py:1201
  27.7 475.6 %collective-permute-start.1 = (bf16[256,1536]{1,0:T(8,128)(2,1)}, bf16[256,1536]{1,0:T(8,128)(2,1)}, u32[]{:S(2)}, u32[]{:S(2)}) collective-permute-start(bf16[256,1536]{1,0:T(8,128)(2,1)} %get-tuple-element.150), channel_id=1, source_target_pairs={{0,1},{1,0},{2,5},{3,4},{4,3},{5,2},{6,7},{7,6},{8,9},{9,8},{10,13... | collective-permute-start | bytes 2359304 | tf_op jit(solution)/shard_map/ppermute | solution.py:1201
  27.9 443.3 %copy-start.61 = (pred[48]{0:T(512)(128)(4,1)}, pred[48]{0:T(512)(128)(4,1)S(1)}, u32[]{:S(2)}) copy-start(pred[48]{0:T(512)(128)(4,1)S(1)} %iota_compare_fusion.9) | copy-start | bytes 148
  423.4 104.8 %copy-start.33 = (bf16[32,1152]{1,0:T(8,128)(2,1)}, bf16[32,1152]{1,0:T(8,128)(2,1)S(1)}, u32[]{:S(2)}) copy-start(bf16[32,1152]{1,0:T(8,128)(2,1)S(1)} %constant_dynamic-update-slice_fusion.5) | copy-start | bytes 221188
  438.2 15.6 %collective-permute-start.4 = (bf16[32,2304]{1,0:T(8,128)(2,1)}, bf16[32,2304]{1,0:T(8,128)(2,1)}, u32[]{:S(2)}, u32[]{:S(2)}) collective-permute-start(bf16[32,2304]{1,0:T(8,128)(2,1)} %maximum_maximum_fusion.2), channel_id=1, source_target_pairs={{0,2},{1,3},{2,0},{3,1},{4,6},{5,7},{6,4},{7,5},{8,10},{9,11},{10,... | collective-permute-start | bytes 442376 | tf_op jit(solution)/shard_map/ppermute | solution.py:1226
  444.4 9.4 collective-permute-start.3
  445.6 13.0 %collective-permute-start.5 = (bf16[32,2304]{1,0:T(8,128)(2,1)}, bf16[32,2304]{1,0:T(8,128)(2,1)}, u32[]{:S(2)}, u32[]{:S(2)}) collective-permute-start(bf16[32,2304]{1,0:T(8,128)(2,1)} %maximum_maximum_fusion.2), channel_id=1, source_target_pairs={{0,3},{1,2},{2,1},{3,0},{4,7},{5,6},{6,5},{7,4},{8,11},{9,10},{10,... | collective-permute-start | bytes 442376 | tf_op jit(solution)/shard_map/ppermute | solution.py:1226
  460.7 33.1 %copy-start.37 = (bf16[4,4,8,384]{3,2,0,1:T(8,128)(2,1)}, bf16[4,4,8,384]{3,2,0,1:T(8,128)(2,1)S(1)}, u32[]{:S(2)}) copy-start(bf16[4,4,8,384]{3,2,0,1:T(8,128)(2,1)S(1)} %copy.149) | copy-start | bytes 294916
  463.1 3.8 collective-permute-start.7
  463.2 4.4 collective-permute-start.6
  465.0 3.9 collective-permute-start.8
  465.8 61.1 %copy-start.28 = (bf16[4,4,8,384]{3,2,0,1:T(8,128)(2,1)}, bf16[4,4,8,384]{3,2,0,1:T(8,128)(2,1)S(1)}, u32[]{:S(2)}) copy-start(bf16[4,4,8,384]{3,2,0,1:T(8,128)(2,1)S(1)} %copy.153) | copy-start | bytes 294916
  466.9 17.1 %collective-permute-start.12 = (bf16[16,6528]{1,0:T(8,128)(2,1)S(1)}, bf16[16,6528]{1,0:T(8,128)(2,1)S(1)}, u32[]{:S(2)}, u32[]{:S(2)}) collective-permute-start(bf16[16,6528]{1,0:T(8,128)(2,1)S(1)} %get-tuple-element.175), channel_id=1, source_target_pairs={{0,3},{1,2},{2,1},{3,0},{4,7},{5,6},{6,5},{7,4},{8,11},{9,10},{10,... | collective-permute-start | bytes 626696 | tf_op jit(solution)/shard_map/ppermute | solution.py:1226
  467.5 21.8 %collective-permute-start.11 = (bf16[16,6528]{1,0:T(8,128)(2,1)S(1)}, bf16[16,6528]{1,0:T(8,128)(2,1)S(1)}, u32[]{:S(2)}, u32[]{:S(2)}) collective-permute-start(bf16[16,6528]{1,0:T(8,128)(2,1)S(1)} %get-tuple-element.176), channel_id=1, source_target_pairs={{0,2},{1,3},{2,0},{3,1},{4,6},{5,7},{6,4},{7,5},{8,10},{9,11},{10,... | collective-permute-start | bytes 626696 | tf_op jit(solution)/shard_map/ppermute | solution.py:1226
  468.9 23.5 %collective-permute-start.10 = (bf16[16,6528]{1,0:T(8,128)(2,1)S(1)}, bf16[16,6528]{1,0:T(8,128)(2,1)S(1)}, u32[]{:S(2)}, u32[]{:S(2)}) collective-permute-start(bf16[16,6528]{1,0:T(8,128)(2,1)S(1)} %get-tuple-element.177), channel_id=1, source_target_pairs={{0,1},{1,0},{2,3},{3,2},{4,5},{5,4},{6,7},{7,6},{8,9},{9,8},{10,11... | collective-permute-start | bytes 626696 | tf_op jit(solution)/shard_map/ppermute | solution.py:1226
  484.0 13.2 %collective-permute-start.16 = (bf16[48,1536]{1,0:T(8,128)(2,1)S(1)}, bf16[48,1536]{1,0:T(8,128)(2,1)}, u32[]{:S(2)}, u32[]{:S(2)}) collective-permute-start(bf16[48,1536]{1,0:T(8,128)(2,1)S(1)} %fusion.18), channel_id=1, source_target_pairs={{0,3},{1,2},{2,1},{3,0},{4,7},{5,6},{6,5},{7,4},{8,11},{9,10},{10,... | collective-permute-start | bytes 442376 | tf_op jit(solution)/shard_map/ppermute | solution.py:1226
  489.3 12.9 %collective-permute-start.15 = (bf16[48,1536]{1,0:T(8,128)(2,1)S(1)}, bf16[48,1536]{1,0:T(8,128)(2,1)S(1)}, u32[]{:S(2)}, u32[]{:S(2)}) collective-permute-start(bf16[48,1536]{1,0:T(8,128)(2,1)S(1)} %fusion.18), channel_id=1, source_target_pairs={{0,2},{1,3},{2,0},{3,1},{4,6},{5,7},{6,4},{7,5},{8,10},{9,11},{10,... | collective-permute-start | bytes 442376 | tf_op jit(solution)/shard_map/ppermute | solution.py:1226
  492.4 2.3 collective-permute-start.9
  494.7 7.6 collective-permute-start.14
  497.3 102.9 %collective-permute-start.21 = (bf16[256,1536]{1,0:T(8,128)(2,1)}, bf16[256,1536]{1,0:T(8,128)(2,1)}, u32[]{:S(2)}, u32[]{:S(2)}) collective-permute-start(bf16[256,1536]{1,0:T(8,128)(2,1)} %get-tuple-element.145), channel_id=1, source_target_pairs={{0,0},{1,1},{2,4},{3,5},{4,2},{5,3},{6,6},{7,7},{8,8},{9,9},{10,12... | collective-permute-start | bytes 2359304 | tf_op jit(solution)/shard_map/ppermute | solution.py:1201
  502.2 97.9 %collective-permute-start.22 = (bf16[256,1536]{1,0:T(8,128)(2,1)}, bf16[256,1536]{1,0:T(8,128)(2,1)}, u32[]{:S(2)}, u32[]{:S(2)}) collective-permute-start(bf16[256,1536]{1,0:T(8,128)(2,1)} %get-tuple-element.146), channel_id=1, source_target_pairs={{0,1},{1,0},{2,5},{3,4},{4,3},{5,2},{6,7},{7,6},{8,9},{9,8},{10,13... | collective-permute-start | bytes 2359304 | tf_op jit(solution)/shard_map/ppermute | solution.py:1201
  504.8 96.8 %copy-start.1 = (bf16[256,1536]{1,0:T(8,128)(2,1)}, bf16[256,1536]{1,0:T(8,128)(2,1)S(1)}, u32[]{:S(2)}) copy-start(bf16[256,1536]{1,0:T(8,128)(2,1)S(1)} %get-tuple-element.147) | copy-start | bytes 2359300
  522.1 34.3 %collective-permute-start.13 = (bf16[512,2304]{1,0:T(8,128)(2,1)}, bf16[512,2304]{1,0:T(8,128)(2,1)}, u32[]{:S(2)}, u32[]{:S(2)}) collective-permute-start(bf16[512,2304]{1,0:T(8,128)(2,1)} %broadcast_select_fusion.6), channel_id=1, source_target_pairs={{0,4},{4,0},{8,12},{12,8},{16,20},{20,16},{24,28},{28,24},{1,5},{5... | collective-permute-start | bytes 7077896 | tf_op jit(solution)/shard_map/ppermute | solution.py:1218
  528.5 22.5 %collective-permute-start.18 = (bf16[192,1152]{1,0:T(8,128)(2,1)S(1)}, bf16[192,1152]{1,0:T(8,128)(2,1)}, u32[]{:S(2)}, u32[]{:S(2)}) collective-permute-start(bf16[192,1152]{1,0:T(8,128)(2,1)S(1)} %fusion.17), channel_id=1, source_target_pairs={{0,1},{1,0},{2,5},{3,4},{4,3},{5,2},{6,7},{7,6},{8,9},{9,8},{10,13... | collective-permute-start | bytes 1327112 | tf_op jit(solution)/shard_map/ppermute | solution.py:1201
  529.5 25.5 %collective-permute-start.17 = (bf16[192,1152]{1,0:T(8,128)(2,1)S(1)}, bf16[192,1152]{1,0:T(8,128)(2,1)}, u32[]{:S(2)}, u32[]{:S(2)}) collective-permute-start(bf16[192,1152]{1,0:T(8,128)(2,1)S(1)} %fusion.17), channel_id=1, source_target_pairs={{0,0},{1,1},{2,4},{3,5},{4,2},{5,3},{6,6},{7,7},{8,8},{9,9},{10,12... | collective-permute-start | bytes 1327112 | tf_op jit(solution)/shard_map/ppermute | solution.py:1201
  600.1 3.5 collective-permute-start.20
  650.5 57.2 %copy-start.40 = (bf16[4,4,8,384]{3,2,1,0:T(8,128)(2,1)S(1)}, bf16[4,4,8,384]{3,2,1,0:T(8,128)(2,1)}, u32[]{:S(2)}) copy-start(bf16[4,4,8,384]{3,2,1,0:T(8,128)(2,1)} %get-tuple-element.178) | copy-start | bytes 294916
  650.5 57.2 %copy-start.39 = (bf16[4,4,8,384]{3,2,1,0:T(8,128)(2,1)S(1)}, bf16[4,4,8,384]{3,2,1,0:T(8,128)(2,1)}, u32[]{:S(2)}) copy-start(bf16[4,4,8,384]{3,2,1,0:T(8,128)(2,1)} %get-tuple-element.179) | copy-start | bytes 294916
  706.6 133.9 %collective-permute-start.25 = (bf16[512,768]{1,0:T(8,128)(2,1)}, bf16[512,768]{1,0:T(8,128)(2,1)}, u32[]{:S(2)}, u32[]{:S(2)}) collective-permute-start(bf16[512,768]{1,0:T(8,128)(2,1)} %broadcast_select_fusion.11), channel_id=1, source_target_pairs={{0,4},{4,0},{8,12},{12,8},{16,20},{20,16},{24,28},{28,24},{1,5},{5... | collective-permute-start | bytes 2359304 | tf_op jit(solution)/shard_map/ppermute | solution.py:1218
  708.6 128.2 %copy-start.22 = (bf16[512,1536]{1,0:T(8,128)(2,1)S(1)}, bf16[512,1536]{1,0:T(8,128)(2,1)}, u32[]{:S(2)}) copy-start(bf16[512,1536]{1,0:T(8,128)(2,1)} %get-tuple-element.59) | copy-start | bytes 4718596
  837.0 75.6 %collective-permute-start.23 = (bf16[256,1536]{1,0:T(8,128)(2,1)S(1)}, bf16[256,1536]{1,0:T(8,128)(2,1)S(1)}, u32[]{:S(2)}, u32[]{:S(2)}) collective-permute-start(bf16[256,1536]{1,0:T(8,128)(2,1)S(1)} %get-tuple-element.141), channel_id=1, source_target_pairs={{0,0},{1,1},{4,2},{5,3},{2,4},{3,5},{6,6},{7,7},{8,8},{9,9},{12,10... | collective-permute-start | bytes 2359304 | tf_op jit(solution)/shard_map/ppermute | solution.py:1208
  839.3 73.3 %collective-permute-start.24 = (bf16[256,1536]{1,0:T(8,128)(2,1)S(1)}, bf16[256,1536]{1,0:T(8,128)(2,1)S(1)}, u32[]{:S(2)}, u32[]{:S(2)}) collective-permute-start(bf16[256,1536]{1,0:T(8,128)(2,1)S(1)} %get-tuple-element.142), channel_id=1, source_target_pairs={{1,0},{0,1},{5,2},{4,3},{3,4},{2,5},{7,6},{6,7},{9,8},{8,9},{13,10... | collective-permute-start | bytes 2359304 | tf_op jit(solution)/shard_map/ppermute | solution.py:1208
  903.5 18.3 %collective-permute-start.27 = (bf16[192,1152]{1,0:T(8,128)(2,1)S(1)}, bf16[192,1152]{1,0:T(8,128)(2,1)S(1)}, u32[]{:S(2)}, u32[]{:S(2)}) collective-permute-start(bf16[192,1152]{1,0:T(8,128)(2,1)S(1)} %get-tuple-element.158), channel_id=1, source_target_pairs={{0,0},{1,1},{4,2},{5,3},{2,4},{3,5},{6,6},{7,7},{8,8},{9,9},{12,10... | collective-permute-start | bytes 1327112 | tf_op jit(solution)/shard_map/ppermute | solution.py:1208
  907.2 21.1 %collective-permute-start.28 = (bf16[192,1152]{1,0:T(8,128)(2,1)S(1)}, bf16[192,1152]{1,0:T(8,128)(2,1)S(1)}, u32[]{:S(2)}, u32[]{:S(2)}) collective-permute-start(bf16[192,1152]{1,0:T(8,128)(2,1)S(1)} %get-tuple-element.159), channel_id=1, source_target_pairs={{1,0},{0,1},{5,2},{4,3},{3,4},{2,5},{7,6},{6,7},{9,8},{8,9},{13,10... | collective-permute-start | bytes 1327112 | tf_op jit(solution)/shard_map/ppermute | solution.py:1208
  912.5 40.6 %collective-permute-start.26 = (bf16[512,2304]{1,0:T(8,128)(2,1)S(1)}, bf16[512,2304]{1,0:T(8,128)(2,1)}, u32[]{:S(2)}, u32[]{:S(2)}) collective-permute-start(bf16[512,2304]{1,0:T(8,128)(2,1)S(1)} %broadcast_select_fusion.2), channel_id=1, source_target_pairs={{0,4},{4,0},{8,12},{12,8},{16,20},{20,16},{24,28},{28,24},{1,5},{5... | collective-permute-start | bytes 7077896 | tf_op jit(solution)/shard_map/ppermute | solution.py:1218
  930.3 4.8 collective-permute-start.29
  930.3 6.8 collective-permute-start.30
  930.4 15.7 %collective-permute-start.31 = (bf16[48,1568]{1,0:T(8,128)(2,1)S(1)}, bf16[48,1568]{1,0:T(8,128)(2,1)S(1)}, u32[]{:S(2)}, u32[]{:S(2)}) collective-permute-start(bf16[48,1568]{1,0:T(8,128)(2,1)S(1)} %get-tuple-element.153), channel_id=1, source_target_pairs={{0,3},{1,2},{2,1},{3,0},{4,7},{5,6},{6,5},{7,4},{8,11},{9,10},{10,... | collective-permute-start | bytes 451592 | tf_op jit(solution)/shard_map/ppermute | solution.py:1226
  946.2 4.7 collective-permute-start.34
  946.3 4.7 collective-permute-start.33
  947.1 3.8 collective-permute-start.32
  985.1 78.6 %copy-start.38 = (bf16[4,4,8,384]{3,2,0,1:T(8,128)(2,1)S(1)}, bf16[4,4,8,384]{3,2,0,1:T(8,128)(2,1)}, u32[]{:S(2)}) copy-start(bf16[4,4,8,384]{3,2,0,1:T(8,128)(2,1)} %copy-done.37) | copy-start | bytes 294916
  985.1 78.7 %copy-start.51 = (bf16[4,4,8,384]{3,2,0,1:T(8,128)(2,1)S(1)}, bf16[4,4,8,384]{3,2,0,1:T(8,128)(2,1)}, u32[]{:S(2)}) copy-start(bf16[4,4,8,384]{3,2,0,1:T(8,128)(2,1)} %copy-done.50) | copy-start | bytes 294916
  985.1 78.7 %copy-start.58 = (f32[2,1536]{1,0:T(2,128)S(1)}, f32[2,1536]{1,0:T(2,128)}, u32[]{:S(2)}) copy-start(f32[2,1536]{1,0:T(2,128)} %param.15) | copy-start | bytes 36868
  (68 other events, 724.7 us)
Sparse Core Ops, SparseCore 0:
  22.1 52.8 all-reduce.18

commit v5 on v4

--- a/solution.py
+++ b/solution.py
@@ -1103,6 +1103,602 @@
         name="gradient_exchange",
     )(*args)
 
+FULL = 4
+PART = 4
+
+
+def front_kernel(n_f, n_z, fans, cols, *refs):
+    it = iter(refs)
+    take = lambda count: [next(it) for _ in range(count)]
+    ins = take(FULL + PART + 1)
+    (x_ref, g_ref, picks_ref, hot2_ref, cblk_ref, clane_ref, c8_ref, smask_ref, wmod_ref, xt_ref, own_ref, tmask_ref) = take(12)
+    outs = take(FULL + PART)
+    x_out, g_out, imod_out, tmod_out = take(4)
+    img_a, img_b, txt_a, txt_b = take(4), take(4), take(4), take(4)
+    moda_out, modb_out, midm_out, cond_out = take(4)
+    h_out, mid_out, heads_out, th_out, tmid_out, theads_out = take(6)
+    (row_ref, fl_ref, img_msg, img_got, txt_msg, txt_got, cgot, mpart, mgot, own_mod, mod_got, wtile, wtxt, stage, tq_ref) = take(15)
+    (z_send, z_recv, xy_send, xy_recv, core_send, core_recv, own_sem, x_send, x_recv, g_send, g_recv, c_send, c_recv, l_send,
+     l_recv, m_send, m_recv, i_send, i_recv, t_send, t_recv, d_send, d_recv, a_send, a_recv, w_sem, tw_sem, h_send, h_recv,
+     h_sem, q_send, q_recv) = take(32)
+    f32, bf16 = jnp.float32, jnp.bfloat16
+    f, z, core, base, column = column_peers(n_z)
+    chip = f // 2
+    chips = n_f // 2
+    nbits = bits_of(chips)
+    partner = base + 1 - core
+    others = [(flip_bits(chip, mask, nbits) * 2 + side, z) for mask in range(1, chips) for side in range(2)]
+    meet(column + others)
+    ring = ZRing(f, z, n_z)
+    total = FULL + PART + 1
+    adapters = total - 1
+    blk = ins[adapters].shape[0]
+    width = x_ref.shape[2]
+    rank2 = hot2_ref.shape[0]
+
+    def peer_of(mask):
+        return flip_bits(chip, mask, nbits) * 2 + core
+
+    def wide_of(m):
+        return ins[m].shape[-1]
+
+    def cuts(m):
+        if m == adapters:
+            return [(0, (0, blk // 2)), (1, (blk // 2, blk // 2))]
+        return list(enumerate(halves(wide_of(m))))
+
+    def place(m, who, zz, cut):
+        off, w = cut
+        if m == adapters:
+            return row_ref.at[pl.ds(pl.multiple_of(who * blk + off, 16), w), :]
+        if m < FULL:
+            return outs[m].at[who, :, pl.ds(pl.multiple_of(zz * wide_of(m) + off, 128), w)]
+        return outs[m].at[who, :, pl.ds(off, w)]
+
+    def piece(m, cut):
+        off, w = cut
+        if m == adapters:
+            return ins[m].at[pl.ds(off, w), :]
+        return ins[m].at[:, pl.ds(off, w)]
+
+    def whole_place(m, who, zz):
+        return place(m, who, zz, (0, blk if m == adapters else wide_of(m)))
+
+    def slot(m, zz):
+        return zz if m < FULL else 0
+
+    def order_of(half):
+        order = list(range(nbits))
+        return order if half == 0 else order[::-1]
+
+    def xy_copy(m, zz, half, cut, mask, bit, own_piece=False):
+        where = place(m, peer_of(mask), zz, cut)
+        return push(piece(m, cut) if own_piece else where, where, xy_send.at[m, slot(m, zz), half, mask, bit],
+                    xy_recv.at[m, slot(m, zz), half, mask | (1 << bit)], (peer_of(1 << bit), z))
+
+    def xy_wait(m, zz, half, cut, mask):
+        where = place(m, peer_of(mask), zz, cut)
+        push(where, where, xy_send.at[m, slot(m, zz), half, 0, 0], xy_recv.at[m, slot(m, zz), half, mask], (partner, z)).wait_recv()
+
+    def core_copy(m, zz, half, cut, mask, own_piece=False):
+        where = place(m, peer_of(mask), zz, cut)
+        return push(piece(m, cut) if own_piece else where, where, core_send.at[m, slot(m, zz), half, mask],
+                    core_recv.at[m, slot(m, zz), half, mask], (partner, z))
+
+    def core_wait(m, zz, half, cut, mask):
+        where = place(m, peer_of(mask) - core + (1 - core), zz, cut)
+        push(where, where, core_send.at[m, slot(m, zz), half, mask], core_recv.at[m, slot(m, zz), half, mask], (partner, z)).wait_recv()
+
+    def own_copy(m):
+        return pltpu.make_async_copy(ins[m], whole_place(m, f, z), own_sem.at[m])
+
+    def z_copy(m, zz, up, own_piece=False):
+        where = whole_place(m, f, zz)
+        return push(ins[m] if own_piece else where, where, z_send.at[m, zz, up], z_recv.at[m, zz], (f, z + 1 if up else z - 1))
+
+    def last_of(order, mask):
+        return max([i for i, b in enumerate(order) if (mask >> b) & 1], default=-1)
+
+    def masks_in_order(half):
+        order = order_of(half)
+        return sorted(range(1, 1 << nbits), key=lambda mask: [1 if (mask >> b) & 1 else 0 for b in reversed(order)])
+
+    def launch(m, zz, own_piece=False):
+        for half, cut in cuts(m):
+            for bit in order_of(half):
+                xy_copy(m, zz, half, cut, 0, bit, own_piece).start()
+            core_copy(m, zz, half, cut, 0, own_piece).start()
+
+    def launch_own(m):
+        if m < FULL:
+            @pl.when(z < n_z - 1)
+            def _():
+                z_copy(m, z, 1, True).start()
+
+            @pl.when(z > 0)
+            def _():
+                z_copy(m, z, 0, True).start()
+        launch(m, z, True)
+        own_copy(m).start()
+
+    def forward(m, zz):
+        for half, cut in cuts(m):
+            order = order_of(half)
+            for mask in masks_in_order(half):
+                if last_of(order, mask) < nbits - 1:
+                    xy_wait(m, zz, half, cut, mask)
+                    for b in order[last_of(order, mask) + 1:]:
+                        xy_copy(m, zz, half, cut, mask, b).start()
+                    core_copy(m, zz, half, cut, mask).start()
+
+    def finish(m, zz):
+        for half, cut in cuts(m):
+            order = order_of(half)
+            for mask in masks_in_order(half):
+                if last_of(order, mask) == nbits - 1:
+                    xy_wait(m, zz, half, cut, mask)
+                    core_copy(m, zz, half, cut, mask).start()
+
+    def settle(m, zz):
+        for half, cut in cuts(m):
+            for mask in range(1 << nbits):
+                core_wait(m, zz, half, cut, mask)
+
+    def drain(m, zz):
+        for half, cut in cuts(m):
+            order = order_of(half)
+            for mask in range(1 << nbits):
+                for b in order[last_of(order, mask) + 1:]:
+                    xy_copy(m, zz, half, cut, mask, b).wait_send()
+                core_copy(m, zz, half, cut, mask).wait_send()
+
+    def at_distance(k, body):
+        for sign in ((-1, 1) if k else (1,)):
+            zz = z + sign * k
+
+            @pl.when((zz >= 0) & (zz < n_z))
+            def _():
+                body(zz)
+
+    def arrive(m, k):
+        @pl.when(z - k >= 0)
+        def _():
+            zz = z - k
+            z_copy(m, zz, 1).wait_recv()
+
+            @pl.when(z < n_z - 1)
+            def _():
+                z_copy(m, zz, 1).start()
+
+            launch(m, zz)
+
+        @pl.when(z + k < n_z)
+        def _():
+            zz = z + k
+            z_copy(m, zz, 0).wait_recv()
+
+            @pl.when(z > 0)
+            def _():
+                z_copy(m, zz, 0).start()
+
+            launch(m, zz)
+
+    def every_z(m, body):
+        if m < FULL:
+            def step(zz, _):
+                body(m, zz)
+                return 0
+
+            lax.fori_loop(0, n_z, step, 0)
+        else:
+            body(m, z)
+
+    there = [(base + z // 2, 2 * core + s) for s in range(2)]
+
+    def is_here(s):
+        return (z // 2 == core) & (2 * core + s == z)
+
+    def token_push(src, dst, send, recv, s):
+        return push(src.at[s], dst.at[z % 2], send.at[s], recv.at[z % 2], there[s])
+
+    def tokens_start(src, dst, send, recv):
+        for s in range(2):
+            @pl.when(is_here(s))
+            def _():
+                pltpu.make_async_copy(src.at[s], dst.at[z % 2], recv.at[z % 2]).start()
+
+            @pl.when(jnp.logical_not(is_here(s)))
+            def _():
+                token_push(src, dst, send, recv, s).start()
+
+    def tokens_wait(src, dst, send, recv):
+        for i in range(2):
+            @pl.when(is_here(i))
+            def _():
+                pltpu.make_async_copy(src.at[i], dst.at[z % 2], recv.at[z % 2]).wait()
+
+            @pl.when(jnp.logical_not(is_here(i)))
+            def _():
+                push(dst.at[i], dst.at[i], send.at[i], recv.at[i], there[i]).wait_recv()
+
+    def tokens_drain(src, dst, send, recv):
+        for s in range(2):
+            @pl.when(jnp.logical_not(is_here(s)))
+            def _():
+                token_push(src, dst, send, recv, s).wait_send()
+
+    def around(src_of, dst, send, recv):
+        return [push(src_of((f + j) % n_f), dst.at[f], send.at[j], recv.at[f], ((f + j) % n_f, z)) for j in range(1, n_f)]
+
+    def around_wait(dst, send, recv):
+        for j in range(1, n_f):
+            came = (f - j + n_f) % n_f
+            push(dst.at[came], dst.at[came], send.at[j], recv.at[came], (came, z)).wait_recv()
+
+    cond_sends = around(lambda to: cblk_ref.at[to], cgot, c_send, c_recv)
+    lane_sends = around(lambda to: clane_ref, cond_out, l_send, l_recv)
+    mod_sends = around(lambda to: mpart.at[to], mgot, m_send, m_recv)
+
+    for copy in cond_sends + lane_sends:
+        copy.start()
+    launch_own(adapters)
+    tokens_start(x_ref, x_out, x_send, x_recv)
+    launch_own(FULL)
+    launch_own(0)
+    cgot[f] = cblk_ref[f]
+    cond_out[f] = clane_ref[...]
+
+    around_wait(cgot, c_send, c_recv)
+    k_local = wmod_ref.shape[1]
+    everyone = cgot[...].reshape(n_f * 8, cgot.shape[2])[:, :k_local].astype(bf16)
+    mpart[...] = (mm(everyone, wmod_ref[0]) + pltpu.roll(mm(everyone, wmod_ref[1]), 2, 0)).reshape(mpart.shape)
+    for copy in mod_sends:
+        copy.start()
+    mgot[f] = mpart[f]
+
+    forward(adapters, z)
+    forward(FULL, z)
+    for m in (1, 2, 3):
+        launch_own(m)
+    for m in (FULL + 1, FULL + 2, FULL + 3):
+        launch_own(m)
+    for k in range(1, n_z):
+        arrive(0, k)
+        at_distance(k - 1, lambda zz: forward(0, zz))
+    for m in (1, 2, 3):
+        arrive(m, 1)
+        at_distance(0, lambda zz: forward(m, zz))
+    at_distance(n_z - 1, lambda zz: forward(0, zz))
+    for m in (FULL + 1, FULL + 2, FULL + 3):
+        forward(m, z)
+
+    finish(adapters, z)
+    settle(adapters, z)
+    own_copy(adapters).wait()
+    hot2 = hot2_ref[...]
+    starts = {}
+    offset = 0
+    for stream in range(2):
+        for index in range(5):
+            starts[stream, index] = (offset, offset + fans[index] // n_z)
+            offset += fans[index] // n_z + cols[index] // n_z
+
+    def pick_a(stream, index):
+        at = starts[stream, index][0]
+        return mm_t(hot2, row_ref[at:at + fans[index] // n_z, :]).astype(bf16)
+
+    def pick_b(stream, index, s, put):
+        at = starts[stream, index][1]
+        count = cols[index] // n_z // NAD
+        flat = row_ref[at:at + count, :].astype(f32) * picks_ref[s * NAD:s * NAD + 1, :]
+        for k in range(1, NAD):
+            begin = at + k * count
+            flat = flat + row_ref[begin:begin + count, :].astype(f32) * picks_ref[s * NAD + k:s * NAD + k + 1, :]
+        fl_ref[:count, :] = flat
+        blocks = count // RANK
+        for j in range(blocks):
+            put(j * 128, fl_ref[pl.ds(j, RANK, stride=blocks), :].astype(bf16))
+
+    spans_a, spans_b = [], []
+    offset = 0
+    for index in range(1, 5):
+        count = fans[index] // n_z
+        picked = pick_a(0, index)
+        for s in range(2):
+            img_msg[s, :, offset:offset + count] = picked[s * RANK:(s + 1) * RANK]
+        spans_a.append((offset, count))
+        offset += count
+    for index in range(1, 5):
+        count = cols[index] // n_z
+        for s in range(2):
+            def put(at, value, s=s, offset=offset):
+                img_msg[s, :, offset + at:offset + at + 128] = value
+            pick_b(0, index, s, put)
+        spans_b.append((offset, count))
+        offset += count
+
+    def img_push(s, side):
+        return push(img_msg.at[s], img_got.at[z], i_send.at[s, side], i_recv.at[z], (base + side, 2 * core + s))
+
+    for s in range(2):
+        for side in range(2):
+            self_here = (side == core) & (2 * core + s == z)
+
+            @pl.when(self_here)
+            def _():
+                img_got[z] = img_msg[s]
+
+            @pl.when(jnp.logical_not(self_here))
+            def _():
+                img_push(s, side).start()
+
+    share = width // n_z
+    for place_at, (stream, index) in enumerate([(0, 0), (1, 0), (1, 1), (1, 3)]):
+        txt_msg[:, place_at * share:(place_at + 1) * share] = pick_a(stream, index)
+    for place_at, index in ((4, 2), (5, 4)):
+        for s in range(2):
+            def put(at, value, s=s, place_at=place_at):
+                txt_msg[s * RANK:(s + 1) * RANK, place_at * share + at:place_at * share + at + 128] = value
+            pick_b(1, index, s, put)
+    txt_got[z] = txt_msg[...]
+    ring.start(lambda to: txt_msg, txt_got, t_send, t_recv)
+    for ref in txt_a + txt_b:
+        ref[...] = jnp.zeros_like(ref)
+    for index in (2, 4):
+        txt_a[index - 1][:rank2, :] = pick_a(1, index)
+    for ref, stream, index in ((txt_b[0], 1, 1), (txt_b[2], 1, 3), (modb_out.at[0], 0, 0), (modb_out.at[1], 1, 0)):
+        for s in range(2):
+            def put(at, value, ref=ref, s=s):
+                ref[s * RANK:(s + 1) * RANK, at:at + 128] = value
+            pick_b(stream, index, s, put)
+
+    for m in (1, 2, 3):
+        arrive(m, 2)
+        at_distance(1, lambda zz: forward(m, zz))
+
+    ring.wait(txt_got, t_send, t_recv)
+    for t in range(n_z):
+        lanes = slice(t * share, (t + 1) * share)
+        got = lambda number: txt_got[t, :, number * share:(number + 1) * share]
+        moda_out[0, :, lanes] = got(0)
+        moda_out[1, :, lanes] = got(1)
+        txt_a[0][:rank2, lanes] = got(2)
+        txt_a[2][:rank2, lanes] = got(3)
+        txt_b[1][:rank2, lanes] = got(4)
+        txt_b[3][:rank2, lanes] = got(5)
+    around_wait(mgot, m_send, m_recv)
+    mod_sum = mgot[0]
+    for j in range(1, n_f):
+        mod_sum = mod_sum + mgot[j]
+    c8 = c8_ref[...].astype(bf16)
+    thin = mm_t(c8, moda_out[0])
+    row = lax.broadcasted_iota(jnp.int32, thin.shape, 0)
+    middle = (jnp.where(row < 2, thin, mm_t(c8, moda_out[1])) * smask_ref[...]).astype(bf16)
+    low = jnp.where(row < 2, middle.astype(f32), 0.0)
+    high = jnp.where((row >= 2) & (row < 4), middle.astype(f32), 0.0)
+    midm_out[0] = low
+    midm_out[1] = high
+    own_mod[...] = mod_sum + mm(low.astype(bf16), modb_out[0]) + mm(high.astype(bf16), modb_out[1])
+
+    def mod_push(index, peer):
+        return push(own_mod, mod_got.at[core * n_z + z], d_send.at[index], d_recv.at[core * n_z + z], peer)
+
+    for index, peer in enumerate(column):
+        mod_push(index, peer).start()
+    mod_got[core * n_z + z] = own_mod[...]
+
+    for t in range(n_z):
+        @pl.when(jnp.logical_not((z // 2 == core) & (t == z)))
+        def _():
+            push(img_got.at[t], img_got.at[t], i_send.at[0, 0], i_recv.at[t], (base + z // 2, t)).wait_recv()
+    for t in range(n_z):
+        for refs_of, spans in ((img_a, spans_a), (img_b, spans_b)):
+            for ref, (begin, count) in zip(refs_of, spans):
+                ref[:, t * count:(t + 1) * count] = img_got[t, :, begin:begin + count]
+
+    for index, peer in enumerate(column):
+        place_at = peer[0] % 2 * n_z + peer[1]
+        push(mod_got.at[place_at], mod_got.at[place_at], d_send.at[index], d_recv.at[place_at], peer).wait_recv()
+    step = width // 2
+    per = own_mod.shape[1] // step
+    imod_out[...] = jnp.zeros_like(imod_out)
+    tmod_out[...] = jnp.zeros_like(tmod_out)
+    for q in range(12):
+        t, lanes = q // per, slice(q % per * step, (q % per + 1) * step)
+        into = slice(q % 2 * step, (q % 2 + 1) * step)
+        here = mod_got[z // 2 * n_z + t]
+        imod_out[q // 2:q // 2 + 1, into] = jnp.where(z % 2 == 0, here[0:1, lanes], here[1:2, lanes])
+        ours = mod_got[core * n_z + t]
+        for s in range(2):
+            tmod_out[8 * s + q // 2:8 * s + q // 2 + 1, into] = ours[2 + s:3 + s, lanes]
+
+    own = own_ref[...]
+    pick = lambda r: jnp.where(own > 0, tmod_out[r:r + 1, :], tmod_out[8 + r:9 + r, :])
+    hat, _inv = norm_rows(xt_ref[...].astype(f32))
+    th_out[z] = (hat * (1.0 + pick(1)) + pick(0)).astype(bf16)
+    ring.start(lambda to: th_out.at[z], th_out, a_send, a_recv)
+    tokens_wait(x_ref, x_out, x_send, x_recv)
+    quarter = x_ref.shape[1]
+    for i in range(2):
+        def norm(r, _):
+            sl = pl.ds(pl.multiple_of(r * ROWS, ROWS), ROWS)
+            hat, _inv = norm_rows(x_out[i, sl, :].astype(f32))
+            h_out[pl.ds(pl.multiple_of(i * quarter + r * ROWS, ROWS), ROWS), :] = (
+                hat * (1.0 + imod_out[1:2, :]) + imod_out[0:1, :]).astype(bf16)
+            return 0
+
+        lax.fori_loop(0, quarter // ROWS, norm, 0)
+    tokens_start(g_ref, g_out, g_send, g_recv)
+
+    for m in (1, 2, 3):
+        arrive(m, 3)
+        at_distance(2, lambda zz: forward(m, zz))
+
+    finish(FULL, z)
+    settle(FULL, z)
+    own_copy(FULL).wait()
+    load = pltpu.make_async_copy(outs[FULL], wtxt, tw_sem)
+    load.start()
+    ring.wait(th_out, a_send, a_recv)
+    pad = xt_ref.shape[0]
+    h_txt = th_out[...].reshape(n_z * pad, width)
+    tmid = (mm_t(h_txt, txt_a[0][...]) * tmask_ref[...]).astype(bf16)
+    tmid_out[...] = tmid
+    load.wait()
+    tq_ref[...] = (mm(h_txt, wtxt[...].reshape(width, wtxt.shape[2])) + mm(tmid, txt_b[0][...])).astype(bf16)
+    for s in range(2):
+        @pl.when(is_here(s))
+        def _():
+            copy = pltpu.make_async_copy(tq_ref, theads_out.at[z % 2], q_recv.at[z % 2])
+            copy.start()
+            copy.wait()
+
+        @pl.when(jnp.logical_not(is_here(s)))
+        def _():
+            push(tq_ref, theads_out.at[z % 2], q_send.at[s], q_recv.at[z % 2], there[s]).start()
+
+    every_z(0, finish)
+    every_z(0, settle)
+    own_copy(0).wait()
+    mid = mm_t(h_out[...], img_a[0][...]).astype(bf16)
+    mid_out[...] = mid
+    tn = wtile.shape[3]
+    per_half = stage.shape[2] // tn
+
+    def tile_of(n):
+        side = 1 - core if n < per_half else core
+        return side, side * per_half + n % per_half
+
+    def tile_load(n):
+        at = pl.ds(pl.multiple_of(tile_of(n)[1] * tn, 128), tn)
+        return pltpu.make_async_copy(outs[0].at[:, :, at], wtile.at[n % 2], w_sem.at[n % 2])
+
+    def heads_push():
+        return push(stage.at[0], heads_out.at[core], h_send, h_recv, (partner, z))
+
+    tile_load(0).start()
+    for n in range(2 * per_half):
+        if n + 1 < 2 * per_half:
+            tile_load(n + 1).start()
+        tile_load(n).wait()
+        at = pl.ds(pl.multiple_of(tile_of(n)[1] * tn, 128), tn)
+        lanes = slice(n % per_half * tn, (n % per_half + 1) * tn)
+        stage[n // per_half, :, lanes] = (
+            mm(h_out[...], wtile[n % 2].reshape(width, tn)) + mm(mid, img_b[0][:, at])).astype(bf16)
+        if n == per_half - 1:
+            heads_push().start()
+    keep = pltpu.make_async_copy(stage.at[1], heads_out.at[core], h_sem)
+    keep.start()
+
+    for m in (1, 2, 3):
+        at_distance(n_z - 1, lambda zz: forward(m, zz))
+    for m in range(total - 1):
+        if m not in (0, FULL):
+            every_z(m, finish)
+    for m in range(total - 1):
+        if m not in (0, FULL):
+            every_z(m, settle)
+            own_copy(m).wait()
+    for m in range(total):
+        every_z(m, drain)
+        if m < FULL:
+            def sent(zz, _):
+                @pl.when((zz <= z) & (z < n_z - 1))
+                def _():
+                    z_copy(m, zz, 1).wait_send()
+
+                @pl.when((zz >= z) & (z > 0))
+                def _():
+                    z_copy(m, zz, 0).wait_send()
+
+                return 0
+
+            lax.fori_loop(0, n_z, sent, 0)
+    for copy in cond_sends + lane_sends + mod_sends:
+        copy.wait_send()
+    around_wait(cond_out, l_send, l_recv)
+    ring.drain(lambda to: txt_msg, txt_got, t_send, t_recv)
+    ring.drain(lambda to: th_out.at[z], th_out, a_send, a_recv)
+    for index, peer in enumerate(column):
+        mod_push(index, peer).wait_send()
+    for s in range(2):
+        for side in range(2):
+            @pl.when(jnp.logical_not((side == core) & (2 * core + s == z)))
+            def _():
+                img_push(s, side).wait_send()
+    tokens_wait(g_ref, g_out, g_send, g_recv)
+    tokens_drain(x_ref, x_out, x_send, x_recv)
+    tokens_drain(g_ref, g_out, g_send, g_recv)
+    keep.wait()
+    heads_push().wait_send()
+    push(stage.at[0], heads_out.at[1 - core], h_send, h_recv, (partner, z)).wait_recv()
+    for s in range(2):
+        @pl.when(jnp.logical_not(is_here(s)))
+        def _():
+            push(theads_out.at[s], theads_out.at[s], q_send.at[s], q_recv.at[s], there[s]).wait_recv()
+            push(tq_ref, theads_out.at[z % 2], q_send.at[s], q_recv.at[z % 2], there[s]).wait_send()
+
+
+def front(full, part, adapter_rows, x, g, picks, hot2, cond, wmod, x_txt, own, tmask, smask, n_f, n_z, fans, cols, cid):
+    f32, bf16 = jnp.float32, jnp.bfloat16
+    vmem, dma = pltpu.VMEM, pltpu.SemaphoreType.DMA
+    shape = jax.ShapeDtypeStruct
+    slots, width = cond.shape
+    k_local = wmod.shape[1]
+    z = lax.axis_index("tp")
+    blocks = jnp.pad(jnp.swapaxes(cond.reshape(slots, n_f, k_local), 0, 1), ((0, 0), (0, 6), (0, 256 - k_local)))
+    cond8 = jnp.concatenate([cond, cond, jnp.zeros((4, width), f32)])
+    lane = jnp.pad(lax.dynamic_slice_in_dim(cond, z * (width // n_z), width // n_z, 1), ((0, 6), (0, 0)))
+    chosen = (picks[:, None] == jnp.arange(NAD)[None, :]).astype(f32).reshape(-1, 1)
+    smalls = (jnp.broadcast_to(chosen, (slots * NAD, 128)), hot2, blocks, lane, cond8, smask, wmod, x_txt, own, tmask)
+    args = (*full, *part, adapter_rows, x, g, *smalls)
+    any_spec, in_vmem = pl.BlockSpec(memory_space=pl.ANY), pl.BlockSpec(memory_space=vmem)
+    rows = 2 * (sum(fans) + sum(cols)) // n_z
+    chips = n_f // 2
+    nbits = bits_of(chips)
+    total = len(full) + len(part) + 1
+    pad = x_txt.shape[0]
+    img_rows = 2 * x.shape[1]
+    cut = cols[0] // n_z
+    qkv_part = cols[1] // n_z
+    thick = tmask.shape[1]
+    rank2 = hot2.shape[0]
+    own_a = [fans[1], fans[2] // n_z, fans[3], fans[4] // n_z]
+    own_b = [cols[1] // n_z, cols[2], cols[3] // n_z, cols[4]]
+    lanes = (sum(fans[1:]) + sum(cols[1:])) // n_z
+    share = width // n_z
+    outs = [shape((n_f,) + a.shape[:-1] + (a.shape[-1] * (n_z if i < len(full) else 1),), a.dtype) for i, a in enumerate(full + part)]
+    in_hbm = len(outs)
+    outs += [shape(x.shape, bf16), shape(g.shape, bf16), shape((8, width), f32), shape((16, width), f32)]
+    outs += [shape((RANK, n), bf16) for n in fans[1:]] + [shape((RANK, n), bf16) for n in cols[1:]]
+    outs += [shape((thick, n), bf16) for n in own_a] + [shape((thick, n), bf16) for n in own_b]
+    outs += [shape((2, rank2, width), bf16), shape((2, rank2, cut), bf16), shape((2, 8, rank2), f32), shape((n_f, 8, share), f32)]
+    outs += [shape((img_rows, width), bf16), shape((img_rows, RANK), bf16), shape((2, img_rows, cols[1] // 2), bf16),
+             shape((n_z, pad, width), bf16), shape((n_z * pad, thick), bf16), shape((2, n_z * pad, qkv_part), bf16)]
+    specs = [any_spec] * in_hbm + [in_vmem, any_spec] + [in_vmem] * (len(outs) - in_hbm - 2)
+    specs[len(outs) - 4] = any_spec
+    specs[len(outs) - 1] = any_spec
+    return pl.pallas_call(
+        functools.partial(front_kernel, n_f, n_z, tuple(fans), tuple(cols)),
+        out_shape=outs,
+        in_specs=[any_spec] * (total + 2) + [in_vmem] * len(smalls),
+        out_specs=specs,
+        scratch_shapes=[
+            vmem((rows, 128), bf16), vmem((cut // NAD, 128), f32), vmem((2, RANK, lanes), bf16), vmem((n_z, RANK, lanes), bf16),
+            vmem((rank2, 6 * share), bf16), vmem((n_z, rank2, 6 * share), bf16), vmem((n_f, 8, 256), f32),
+            vmem((n_f, 8, cut), f32), vmem((n_f, 8, cut), f32), vmem((8, cut), f32), vmem((2 * n_z, 8, cut), f32),
+            vmem((2, n_f, k_local, 768), bf16), vmem((n_f, k_local, qkv_part), bf16), vmem((2, img_rows, cols[1] // 2), bf16),
+            vmem((n_z * pad, qkv_part), bf16),
+            dma((total, n_z, 2)), dma((total, n_z)), dma((total, n_z, 2, chips, nbits)), dma((total, n_z, 2, chips)),
+            dma((total, n_z, 2, chips)), dma((total, n_z, 2, chips)), dma((total,)),
+            dma((2,)), dma((2,)), dma((2,)), dma((2,)), dma((n_f,)), dma((n_f,)), dma((n_f,)), dma((n_f,)), dma((n_f,)), dma((n_f,)),
+            dma((2, 2)), dma((n_z,)), dma((n_z,)), dma((n_z,)), dma((2 * n_z,)), dma((2 * n_z,)), dma((n_z,)), dma((n_z,)),
+            dma((2,)), dma, dma, dma, dma, dma((2,)), dma((2,)),
+        ],
+        compiler_params=pltpu.CompilerParams(collective_id=cid, has_side_effects=True, vmem_limit_bytes=58 * 1024 * 1024),
+        name="front",
+    )(*args)
+
 HD = 64
 FF = 6144
 NAD = 8
@@ -1258,11 +1854,6 @@
     fc2_t = jnp.swapaxes(fc2_weight, 1, 2)
     local = [qkv_weight, out_t, fc1_weight, fc2_t]
     adapter_rows = adapters.astype(BF16).reshape(-1, 128)
-    got = gather([w[0] for w in local], [w[1] for w in local] + [adapter_rows], n_f, n_z)
-    got = [g.reshape(-1, g.shape[-1]) for g in got]
-    img_w, txt_w, row = got[:4], got[4:8], got[8]
-    x_img = reshard(image_tokens)
-    g_img = reshard(image_cot)
     txt_pad = (txt_local + 15) // 16 * 16
 
     def padded(values):
@@ -1302,101 +1893,6 @@
         jnp.arange(NAD * RANK)[:, None]
         == (column_picks[:, None] * RANK + jnp.arange(RANK)[None, :]).reshape(1, -1)
     ).astype(F32)
-    own_picks = adapter_index
-    own_hot = lax.dynamic_slice_in_dim(one_hot, core * slots * RANK, slots * RANK, 1)
-
-    a_rows = [[None] * 5 for stream in range(2)]
-    b_rows = [[None] * 5 for stream in range(2)]
-    offset = 0
-    for stream in range(2):
-        for index in range(5):
-            count = fans[index] // n_z
-            a_rows[stream][index] = row[offset : offset + count]
-            offset += count
-            count = cols[index] // n_z
-            b_rows[stream][index] = row[offset : offset + count]
-            offset += count
-
-    def b_pick(stream, index, pick_index):
-        part = b_rows[stream][index]
-        count = part.shape[0] // NAD
-        return lax.dynamic_slice_in_dim(part, pick_index * count, count, 0).reshape(RANK, -1)
-
-    def a_pick(rows, hot):
-        return inner_right(hot.T.astype(BF16), rows).astype(BF16)
-
-    img_a = a_pick(jnp.concatenate(a_rows[0], axis=0), one_hot)
-    fan_share = sum(fans) // n_z
-    img_a = img_a.reshape(column_count, RANK, fan_share)
-    img_b = [
-        jnp.concatenate([b_pick(0, index, column_picks[s]) for index in range(1, 5)], axis=1)
-        for s in range(column_count)
-    ]
-    img_msg = jnp.concatenate([img_a, jnp.stack(img_b)], axis=2)
-    txt_a_rows = jnp.concatenate(
-        [a_rows[0][0], a_rows[1][0], a_rows[1][1], a_rows[1][3]], axis=0
-    )
-    txt_a = a_pick(txt_a_rows, own_hot).reshape(slots, RANK, -1)
-    txt_b_own = [
-        [b_pick(stream, index, own_picks[s]) for s in range(slots)]
-        for stream, index in [(0, 0), (1, 0), (1, 1), (1, 2), (1, 3), (1, 4)]
-    ]
-    txt_b_own = [jnp.concatenate(parts, axis=0) for parts in txt_b_own]
-    txt_a_own = a_pick(jnp.concatenate([a_rows[1][2], a_rows[1][4]], axis=0), own_hot)
-    txt_msg = jnp.concatenate(
-        [txt_a.reshape(slots * RANK, -1), txt_b_own[3], txt_b_own[5]], axis=1
-    )
-    img_got = jnp.stack(z_exchange(img_msg))
-    txt_got = jnp.stack(z_gather(txt_msg))
-
-    def join(part):
-        return jnp.swapaxes(part, 0, 1).reshape(part.shape[1], -1)
-
-    img_pairs = []
-    offset, b_offset = 0, fan_share
-    for index in range(5):
-        count = fans[index] // n_z
-        a_full = join(img_got[:, :, offset : offset + count])
-        offset += count
-        if index == 0:
-            img_pairs.append(None)
-            continue
-        count = cols[index] // n_z
-        b_full = join(img_got[:, :, b_offset : b_offset + count])
-        b_offset += count
-        img_pairs.append((a_full, b_full))
-    txt_full = []
-    offset = 0
-    for count in [width // n_z] * 6:
-        txt_full.append(join(txt_got[:, :, offset : offset + count]))
-        offset += count
-    mod_a = [txt_full[0], txt_full[1]]
-    mod_b = [txt_b_own[0], txt_b_own[1]]
-    txt_pairs = [
-        None,
-        (txt_full[2], txt_b_own[2]),
-        (txt_a_own[:, : width // n_z], txt_full[4]),
-        (txt_full[3], txt_b_own[4]),
-        (txt_a_own[:, width // n_z :], txt_full[5]),
-    ]
-
-    k_local = mod_weight.shape[1]
-    cond_act = jax.nn.silu(conditioning).astype(BF16)
-    cond_all = lax.all_gather(cond_act, "fsdp", axis=0, tiled=True)
-    cond_slice = lax.dynamic_slice_in_dim(cond_all, f * k_local, k_local, 1)
-    mod_part = jnp.stack([matmul(cond_slice, mod_weight[stream]) for stream in range(2)], axis=1)
-    mod_part = lax.psum_scatter(mod_part, "fsdp", scatter_dimension=0, tiled=True)
-    mod_mid = []
-    mod_terms = []
-    for stream in range(2):
-        middle = (inner_right(cond_act, mod_a[stream]) * seq_mask).astype(BF16)
-        mod_mid.append(middle)
-        mod_terms.append(mod_part[:, stream] + matmul(middle, mod_b[stream]))
-    mods = jnp.concatenate(z_gather(jnp.stack(mod_terms, axis=1)), axis=2)
-    img_mods = by_group(mods[:, 0], swap_core(mods[:, 0]))
-    img_mod = lax.dynamic_slice_in_dim(img_mods, z, 1, 0)
-    txt_mods = mods[:, 1]
-
     def stretch(stream, index):
         if stream == 0:
             return img_mod[:, index * width : (index + 1) * width]
@@ -1417,12 +1913,6 @@
     def lanes(values):
         count = values.shape[1] // n_z
         return lax.dynamic_slice_in_dim(values, z * count, count, 1)
-
-    inputs = [x_img.astype(F32), x_txt]
-    norm_one = [layer_norm(values) for values in inputs]
-    heads_in = [
-        (norm_one[s][0] * (1.0 + stretch(s, 1)) + stretch(s, 0)).astype(BF16) for s in range(2)
-    ]
 
     def project(values, weight, pair, mask, flipped):
         middle = inner_right(values, pair[0])
@@ -1432,12 +1922,162 @@
         main = inner_right(values, weight) if flipped else matmul(values, weight)
         return middle, main + matmul(middle, pair[1])
 
-    txt_in = share(heads_in[1])
-    txt_qkv_mid, txt_qkv = project(txt_in, txt_w[0], txt_pairs[1], txt_mask, False)
-    img_qkv_mid, img_qkv = project(heads_in[0], img_w[0], img_pairs[1], None, False)
-    txt_qkv, img_qkv = txt_qkv.astype(BF16), img_qkv.astype(BF16)
-    img_heads = to_heads(img_qkv)
-    txt_heads = jnp.stack(to_chip([txt_qkv, txt_qkv]))
+    own_hot = (
+        jnp.arange(NAD * RANK)[:, None]
+        == (adapter_index[:, None] * RANK + jnp.arange(RANK)[None, :]).reshape(1, -1)
+    ).astype(F32)
+    k_local = mod_weight.shape[1]
+    cond_act = jax.nn.silu(conditioning).astype(BF16)
+    thick = 128
+
+    def thicker(part):
+        return jnp.concatenate([part, jnp.zeros((thick - part.shape[0], part.shape[1]), part.dtype)], axis=0)
+
+    def sign(owner):
+        return owner[:, 0:1] - owner[:, 1:2]
+
+    def lanes_pad(mask):
+        return jnp.pad(mask, ((0, 0), (0, thick - mask.shape[1])))
+
+    if n_f == 8:
+        slot_mask = jnp.pad(jnp.concatenate([seq_mask, seq_mask]), ((0, 4), (0, 0)))
+        made = front(
+            [w[0] for w in local], [w[1] for w in local], adapter_rows, image_tokens, image_cot,
+            adapter_index, own_hot.T.astype(BF16), cond_act.astype(F32), mod_weight, x_txt_low,
+            sign(owner_local), lanes_pad(txt_mask), slot_mask, n_f, n_z, fans, cols, 1,
+        )
+        made = iter(made)
+        take = lambda count: [next(made) for _ in range(count)]
+        img_w = [w.reshape(-1, w.shape[-1]) for w in take(4)]
+        txt_w = [w.reshape(-1, w.shape[-1]) for w in take(4)]
+        x_img, g_img = [v.reshape(-1, width) for v in take(2)]
+        img_rows_mod, txt_mod = take(2)
+        img_pairs = [None] + list(zip(take(4), take(4)))
+        thick_pairs = [None] + list(zip(take(4), take(4)))
+        mod_a, mod_b, tmod, cond_own = take(4)
+        img_in, img_qkv_mid, img_heads, txt_in, txt_qkv_mid, txt_heads = take(6)
+        img_heads = img_heads.reshape(img_n, -1)
+        txt_in = txt_in.reshape(-1, width)
+        txt_qkv_mid = txt_qkv_mid[:, :rank_cols]
+        txt_pairs = [None, tuple(part[:rank_cols] for part in thick_pairs[1])]
+        img_mod = img_rows_mod[:6].reshape(1, -1)
+        txt_mods = txt_mod.reshape(slots, 8, width)[:, :6].reshape(slots, -1)
+    else:
+        got = gather([w[0] for w in local], [w[1] for w in local] + [adapter_rows], n_f, n_z)
+        got = [g.reshape(-1, g.shape[-1]) for g in got]
+        img_w, txt_w, row = got[:4], got[4:8], got[8]
+        x_img = reshard(image_tokens)
+        g_img = reshard(image_cot)
+        own_picks = adapter_index
+
+        a_rows = [[None] * 5 for stream in range(2)]
+        b_rows = [[None] * 5 for stream in range(2)]
+        offset = 0
+        for stream in range(2):
+            for index in range(5):
+                count = fans[index] // n_z
+                a_rows[stream][index] = row[offset : offset + count]
+                offset += count
+                count = cols[index] // n_z
+                b_rows[stream][index] = row[offset : offset + count]
+                offset += count
+
+        def b_pick(stream, index, pick_index):
+            part = b_rows[stream][index]
+            count = part.shape[0] // NAD
+            return lax.dynamic_slice_in_dim(part, pick_index * count, count, 0).reshape(RANK, -1)
+
+        def a_pick(rows, hot):
+            return inner_right(hot.T.astype(BF16), rows).astype(BF16)
+
+        img_a = a_pick(jnp.concatenate(a_rows[0], axis=0), one_hot)
+        fan_share = sum(fans) // n_z
+        img_a = img_a.reshape(column_count, RANK, fan_share)
+        img_b = [
+            jnp.concatenate([b_pick(0, index, column_picks[s]) for index in range(1, 5)], axis=1)
+            for s in range(column_count)
+        ]
+        img_msg = jnp.concatenate([img_a, jnp.stack(img_b)], axis=2)
+        txt_a_rows = jnp.concatenate(
+            [a_rows[0][0], a_rows[1][0], a_rows[1][1], a_rows[1][3]], axis=0
+        )
+        txt_a = a_pick(txt_a_rows, own_hot).reshape(slots, RANK, -1)
+        txt_b_own = [
+            [b_pick(stream, index, own_picks[s]) for s in range(slots)]
+            for stream, index in [(0, 0), (1, 0), (1, 1), (1, 2), (1, 3), (1, 4)]
+        ]
+        txt_b_own = [jnp.concatenate(parts, axis=0) for parts in txt_b_own]
+        txt_a_own = a_pick(jnp.concatenate([a_rows[1][2], a_rows[1][4]], axis=0), own_hot)
+        txt_msg = jnp.concatenate(
+            [txt_a.reshape(slots * RANK, -1), txt_b_own[3], txt_b_own[5]], axis=1
+        )
+        img_got = jnp.stack(z_exchange(img_msg))
+        txt_got = jnp.stack(z_gather(txt_msg))
+
+        def join(part):
+            return jnp.swapaxes(part, 0, 1).reshape(part.shape[1], -1)
+
+        img_pairs = []
+        offset, b_offset = 0, fan_share
+        for index in range(5):
+            count = fans[index] // n_z
+            a_full = join(img_got[:, :, offset : offset + count])
+            offset += count
+            if index == 0:
+                img_pairs.append(None)
+                continue
+            count = cols[index] // n_z
+            b_full = join(img_got[:, :, b_offset : b_offset + count])
+            b_offset += count
+            img_pairs.append((a_full, b_full))
+        txt_full = []
+        offset = 0
+        for count in [width // n_z] * 6:
+            txt_full.append(join(txt_got[:, :, offset : offset + count]))
+            offset += count
+        mod_a = [txt_full[0], txt_full[1]]
+        mod_b = [txt_b_own[0], txt_b_own[1]]
+        txt_pairs = [
+            None,
+            (txt_full[2], txt_b_own[2]),
+            (txt_a_own[:, : width // n_z], txt_full[4]),
+            (txt_full[3], txt_b_own[4]),
+            (txt_a_own[:, width // n_z :], txt_full[5]),
+        ]
+
+        cond_all = lax.all_gather(cond_act, "fsdp", axis=0, tiled=True)
+        cond_slice = lax.dynamic_slice_in_dim(cond_all, f * k_local, k_local, 1)
+        mod_part = jnp.stack([matmul(cond_slice, mod_weight[stream]) for stream in range(2)], axis=1)
+        mod_part = lax.psum_scatter(mod_part, "fsdp", scatter_dimension=0, tiled=True)
+        mod_mid = []
+        mod_terms = []
+        for stream in range(2):
+            middle = (inner_right(cond_act, mod_a[stream]) * seq_mask).astype(BF16)
+            mod_mid.append(middle)
+            mod_terms.append(mod_part[:, stream] + matmul(middle, mod_b[stream]))
+        mods = jnp.concatenate(z_gather(jnp.stack(mod_terms, axis=1)), axis=2)
+        img_mods = by_group(mods[:, 0], swap_core(mods[:, 0]))
+        img_mod = lax.dynamic_slice_in_dim(img_mods, z, 1, 0)
+        txt_mods = mods[:, 1]
+
+        img_rows_mod = jnp.concatenate([img_mod.reshape(6, width), jnp.zeros((2, width), F32)], axis=0)
+        txt_mod = jnp.pad(txt_mods.reshape(slots, 6, width), ((0, 0), (0, 2), (0, 0))).reshape(-1, width)
+        thick_pairs = [None] + [tuple(thicker(part) for part in txt_pairs[index]) for index in range(1, 5)]
+        norm_first = [layer_norm(v.astype(F32)) for v in (x_img, x_txt)]
+        heads_in = [
+            (norm_first[s][0] * (1.0 + stretch(s, 1)) + stretch(s, 0)).astype(BF16) for s in range(2)
+        ]
+
+        txt_in = share(heads_in[1])
+        txt_qkv_mid, txt_qkv = project(txt_in, txt_w[0], txt_pairs[1], txt_mask, False)
+        img_qkv_mid, img_qkv = project(heads_in[0], img_w[0], img_pairs[1], None, False)
+        txt_qkv, img_qkv = txt_qkv.astype(BF16), img_qkv.astype(BF16)
+        img_heads = to_heads(img_qkv)
+        txt_heads = jnp.stack(to_chip([txt_qkv, txt_qkv]))
+        img_in = heads_in[0]
+
+    inputs = [x_img.astype(F32), x_txt]
+    norm_one = [layer_norm(values) for values in inputs]
     lengths = by_group(text_lengths[0:1], swap_core(text_lengths[0:1]))
     chip_lengths = jnp.cumsum(lax.dynamic_index_in_dim(lengths, z // slots, 0, keepdims=False))
     chip_slot = z % slots
@@ -1455,19 +2095,6 @@
         return jnp.where(owner_group[:, 0:1] > 0, got[0], jnp.where(owner_group[:, 1:2] > 0, got[1], 0))
 
     attended = to_tokens(o_img)
-    thick = 128
-
-    def thicker(part):
-        return jnp.concatenate([part, jnp.zeros((thick - part.shape[0], part.shape[1]), part.dtype)], axis=0)
-
-    def sign(owner):
-        return owner[:, 0:1] - owner[:, 1:2]
-
-    def lanes_pad(mask):
-        return jnp.pad(mask, ((0, 0), (0, thick - mask.shape[1])))
-
-    txt_mod = jnp.pad(txt_mods.reshape(slots, 6, width), ((0, 0), (0, 2), (0, 0))).reshape(-1, width)
-    thick_pairs = [None] + [tuple(thicker(part) for part in txt_pairs[index]) for index in range(1, 5)]
     (txt_result, txt_grad_after, do_txt, txt_sums, *txt_sides) = text_mid(
         o_txt, x_txt_low, g_txt_low, txt_mod, sign(owner_group), sign(owner_local), lanes_pad(txt_mask),
         lanes_pad(txt_mask_local), txt_w[1], txt_w[2], txt_w[3], thick_pairs[2], thick_pairs[3], thick_pairs[4],
@@ -1476,7 +2103,6 @@
     txt_sides = [part[:rank_cols] for part in txt_sides]
     txt_sums = txt_sums.reshape(4, slots, width)
 
-    img_rows_mod = jnp.concatenate([img_mod.reshape(6, width), jnp.zeros((2, width), F32)], axis=0)
     (img_branch, img_after, img_mlp, img_pre, img_result, *img_mids, img_gate) = block_fwd(
         attended, x_img, g_img, img_rows_mod, img_w[1], img_pairs[2], img_pairs[3], img_w[2],
         img_pairs[4], img_w[3],
@@ -1517,7 +2143,7 @@
     txt_grad_qkv = txt_home(d_txt)
 
     img_back_mid, img_grad_norm = project_back(img_grad_qkv, img_w[0], img_pairs[1], None, False)
-    grads[0][1] = (inner_left(img_back_mid, heads_in[0]), inner_left(img_qkv_mid, img_grad_qkv))
+    grads[0][1] = (inner_left(img_back_mid, img_in), inner_left(img_qkv_mid, img_grad_qkv))
     txt_grad_norm, txt_qkv_back = give(
         inner_right(txt_grad_qkv, txt_w[0]), inner_right(txt_grad_qkv, txt_pairs[1][1])
     )
@@ -1541,14 +2167,12 @@
         cut = width // n_z
         dmod = jnp.concatenate([img_dmod, txt_dmod]).reshape(1 + slots, n_z, -1, cut)
         dmod = jnp.pad(jnp.swapaxes(dmod, 0, 1), ((0, 0), (0, 0), (0, 8 - dmod.shape[2]), (0, 0)))
-        tmod = jnp.stack([jnp.pad(mod_mid[s].astype(F32), ((2 * s, 6 - 2 * s), (0, 0))) for s in range(2)])
-        cond_own = jnp.pad(lanes(cond_all).astype(F32).reshape(n_f, slots, -1), ((0, 0), (0, 6), (0, 0)))
         sides_of = lambda stream, side: [grads[stream][index][side] for index in range(1, 5)]
         image_low, cond_slices, mod_rank, shard = tail(
             grad_inputs[0].astype(BF16).reshape(2, quarter, width),
             sides_of(0, 0), sides_of(0, 1), sides_of(1, 0), sides_of(1, 1),
-            one_hot.T.astype(BF16), own_hot.T.astype(BF16), dmod, mod_weight, jnp.stack(mod_b), tmod, cond_own,
-            jnp.pad(jnp.concatenate([seq_mask, seq_mask]), ((0, 4), (0, 0))),
+            one_hot.T.astype(BF16), own_hot.T.astype(BF16), dmod, mod_weight, mod_b, tmod, cond_own,
+            slot_mask,
             n_f, n_z, fans, cols, 3,
         )
         image_grad = image_low.astype(F32)

time: 1090 us -> 924 us (0.85)
  starting transfers between devices: 55.7 us -> 16.9 us
  waiting for transfers between devices: 65.7 us -> 27.9 us
  local copies, waits for them, and re-layouts: 50.4 us -> 20.7 us
  between operations: 29.8 us -> 1.68 us
  other arithmetic: 70.9 us -> 49.9 us
  matrix products: 51 us -> 30.2 us
  Pallas kernels: 743 us -> 763 us
    ppermute x18 -> x6, waiting for transfers between devices: 34.9 us -> 12.2 us  [z_swap(): return lax.ppermute(values, 'tp', [(i, i ^ step) for i in range(n_z)])]
    pallas_call x1, Pallas kernels: 346 us -> 368 us  [front(): pl.pallas_call(functools.partial(front_kernel, n_f, n_z, tuple(fans), tup...]
    ppermute x18 -> x6, starting transfers between devices: 23 us -> 5.4 us  [z_swap(): return lax.ppermute(values, 'tp', [(i, i ^ step) for i in range(n_z)])]
    dot_general x12 -> x4, matrix products: 21.3 us -> 4.17 us  [matmul(): return jnp.dot(left, right, preferred_element_type=F32)]
    ppermute x6 -> x0, waiting for transfers between devices: 16 us -> none  [to_chip(): got = [lax.ppermute(parts[r], BOTH, round_pairs(r)) for r in range(2)]]
    ppermute x6 -> x0, starting transfers between devices: 15.4 us -> none  [to_chip(): got = [lax.ppermute(parts[r], BOTH, round_pairs(r)) for r in range(2)]]
    dot_general x11 -> x4, matrix products: 23 us -> 19.6 us  [inner_right(): lax.dot_general(left, right, (((left.ndim - 1,), (right.ndim - 1,)), ((),...]
  transfers between devices with their start and end apart: 36 -> 15, of which waited for: 13 -> 6; matrix products, arithmetic and copies ran while one was open for 12% -> 6% of each run, Pallas kernels for 53% -> 20%
where the time goes in v5:
time: 924 us; the launch traced here: 910 us
  Pallas kernels  763 us (83%)
  other arithmetic  49.9 us (5%)
  matrix products  30.2 us (3%)
  waiting for transfers between devices  27.9 us (3%)
  local copies, waits for them, and re-layouts  20.7 us (2%)
  starting transfers between devices  16.9 us (2%)
    pallas_call x1, Pallas kernels, front(): pl.pallas_call(functools.partial(front_kernel, n_f, n_z, tuple(fans), tup...  368 us
    pallas_call x1, Pallas kernels, text_mid(): pl.pallas_call(functools.partial(text_mid_kernel, n_z), out_shape=out_sha...  119 us
    pallas_call x1, Pallas kernels, tail(): pl.pallas_call(functools.partial(tail_kernel, n_f, n_z, tuple(fans), tupl...  77.4 us
    pallas_call x1, Pallas kernels, attend_back(): pl.pallas_call(functools.partial(attend_back_kernel, hd, bq), grid=(pairs...  61.5 us
    pallas_call x1, Pallas kernels, block_back(): pl.pallas_call(functools.partial(block_back_kernel, tiles), grid=(tiles,)...  53.7 us
    pallas_call x1, Pallas kernels, block_fwd(): pl.pallas_call(functools.partial(block_fwd_kernel, tiles), grid=(tiles,),...  45.8 us
    pallas_call x1, Pallas kernels, attend(): pl.pallas_call(functools.partial(attend_kernel, hd, bq), grid=(pairs,), i...  37.6 us
    dot_general x4, matrix products, inner_right(): lax.dot_general(left, right, (((left.ndim - 1,), (right.ndim - 1,)), ((),...  19.6 us
  transfers between devices with their start and end apart: 15, of which 6 were waited for; matrix products, arithmetic and copies ran while one was open for 6% of the time, Pallas kernels for 20%

profile of v5, /device:TPU:11, one launch (start us, length us, event | category | flops | bytes accessed | tf_op | source)
XLA Modules:
  0.0 910.4 jit_solution(1028993248025309625)
XLA Ops:
  4.1 1.0 convert_reduce_fusion.2
  5.2 1.1 fusion.18
  10.1 1.6 pad.35.refs_18_.x_ref
  12.6 1.7 slice_bitcast_fusion.6
  14.3 13.5 %convert_reduce_fusion.1 = bf16[282624]{0:T(1024)(128)(2,1)} fusion(f32[1,282624]{1,0:T(1,128)} %param.18), kind=kLoop, calls=%fused_computation.34 | loop fusion | flops 282624 | bytes 1695744 | tf_op jit(solution)/shard_map/convert_element_type | solution.py:1856
  27.8 1.0 slice_bitcast_fusion.4
  28.8 1.5 slice_bitcast_fusion
  33.3 368.2 %front.1 = (bf16[8,192,4608]{2,1,0:T(8,128)(2,1)}, bf16[8,192,1536]{2,1,0:T(8,128)(2,1)}, bf16[8,192,6144]{2,1,0:T(8,128)(2,1)}, bf16[8,192,6144]{2,1,0:T(8,128)...) custom-call(bf16[192,1152]{1,0:T(8,128)(2,1)} %get-tuple-element.186, ...), custom_call_target="tpu_custom_call" | custom-call | tf_op jit(solution)/shard_map/front/pallas_call | solution.py:1681
  401.6 1.8 convert_reduce_fusion
  403.4 2.0 fusion.1
  405.4 37.6 %attend.1 = (bf16[1024,768]{1,0:T(8,128)(2,1)S(1)}, bf16[2,192,384]{2,1,0:T(8,128)(2,1)S(1)}, f32[6,2,1216]{2,1,0:T(2,128)S(1)}) custom-call(bf16[1024,2304]{1,0:T(8,128)(2,1)} %bitcast.110, bf16[2,192,1152]{2,1,0:T(8,128)(2,1)S(1)} %copy-done, f32[192,1]{1,0:T(8,128)S(1)} %fusion.38.bias_ref), custom_call_target="tpu_custom_call" | custom-call | tf_op jit(solution)/shard_map/attend/pallas_call | solution.py:288
  443.8 1.7 collective-permute-done.1
  445.6 1.3 pad_maximum_fusion.1.o_ref
  446.9 45.8 %block_forward.1 = (f32[512,1536]{1,0:T(8,128)}, f32[512,1536]{1,0:T(8,128)}, bf16[512,1536]{1,0:T(8,128)(2,1)}, f32[512,6144]{1,0:T(8,128)}, bf16[512,1536]{1,0...) custom-call(bf16[512,1536]{1,0:T(8,128)(2,1)} %pad_maximum_fusion.1., ...), custom_call_target="tpu_custom_call" | custom-call | flops 21743271936 | bytes 37748736 | tf_op jit(solution)/shard_map/block_forward/pallas_call | solution.py:473
  492.7 53.7 %block_backward.1 = (f32[512,1536]{1,0:T(8,128)}, bf16[512,1536]{1,0:T(8,128)(2,1)}, f32[24,1536]{1,0:T(8,128)}, f32[16,6144]{1,0:T(8,128)}, f32[16,6144]{1,0:T(...) custom-call(bf16[512,1536]{1,0:T(8,128)(2,1)} %bitcast.156, ...), custom_call_target="tpu_custom_call" | custom-call | flops 21743271936 | bytes 37748736 | tf_op jit(solution)/shard_map/block_backward/pallas_call | solution.py:567
  546.4 2.3 broadcast_select_fusion.7
  549.3 118.9 %text_block.1 = (bf16[48,1536]{1,0:T(8,128)(2,1)S(1)}, f32[48,1536]{1,0:T(8,128)S(1)}, bf16[2,192,384]{2,1,0:T(8,128)(2,1)S(1)}, f32[8,1536]{1,0:T(8,128)S(1)}, ...) custom-call(bf16[2,192,384]{2,1,0:T(8,128)(2,1)S(1)} %get-tuple-elem, ...), custom_call_target="tpu_custom_call" | custom-call | tf_op jit(solution)/shard_map/text_block/pallas_call | solution.py:802
  671.4 1.6 slice.195.refs_12_
  673.0 1.6 slice.198.refs_15_
  675.4 2.2 collective-permute-start.2
  677.5 1.1 collective-permute-start.3
  678.7 1.3 broadcast_select_fusion.6
  680.1 61.5 %attend_back.1 = (bf16[1024,2304]{1,0:T(8,128)(2,1)}, bf16[2,192,1152]{2,1,0:T(8,128)(2,1)S(1)}) custom-call(bf16[1024,2304]{1,0:T(8,128)(2,1)} %bitcast.111, bf16[2,192,1152]{2,1,0:T(8,128)(2,1)S(1)} %copy-done, f32[192,1]{1,0:T(8,128)S(1)} %fusion.38.bias_ref, bf16[1024,768]{1,0:T(8,128)(2,1)S(1)} %pad_maximum_fusion.3.doi_ref, ...), custom_call_target="tpu_custom_call" | custom-call | tf_op jit(solution)/shard_map/attend_back/pallas_call | solution.py:363
  741.7 4.0 collective-permute-start.6
  745.7 2.7 collective-permute-start.7
  748.3 2.6 broadcast_select_fusion.2
  751.2 1.3 pad_maximum_fusion.2
  752.5 7.5 collective-permute-done.6
  759.9 6.5 collective-permute-done.7
  766.7 1.3 fusion.90
  768.0 1.2 fusion.39
  769.4 2.6 collective-permute-start.10
  772.9 1.2 collective-permute-done.8
  774.1 2.0 collective-permute-done.9
  776.1 9.0 collective-permute-done.10
  786.1 1.8 collective-permute-start.11
  787.9 1.1 slice_add_fusion
  791.7 1.8 fusion.23.refs_9_
  793.4 3.5 broadcast_select_fusion.1
  797.0 1.3 fusion.5
  799.1 1.5 fusion.3.refs_5_
  800.6 1.0 fusion.89.refs_1_
  801.5 2.3 fusion.88
  803.8 15.8 %multiply_reduce_fusion = (f32[1536]{0:T(1024)S(1)}, f32[512]{0:T(512)S(1)}, f32[512]{0:T(512)S(1)}, f32[1536]{0:T(1024)S(1)}, f32[512,1536]{1,0:T(8,128)}) fusion(f32[512]{0:T(512)S(1)} %bitcast.139, f32[512]{0:T(512)S(1)} %bitcast.137, bf16[2,256,1536]{2,1,0:T(8,128)(2,1)S(1)} %copy-done.9, f32[1536]{0:T(1024)S(1)} %fusion.66, f32[512,1536]{1,0:T(8,128)} %fusion.88, ...), kind=kOutput, calls=%fused_computation.6 | convolution fusion | flops 7265841152 | bytes 26765312 | tf_op jit(solution)/shard_map/dot_general | solution.py:1726
  820.6 5.1 add_convert_fusion
  825.7 77.4 %gradient_exchange.1 = (bf16[2,256,1536]{2,1,0:T(8,128)(2,1)}, f32[8,8,256]{2,1,0:T(8,128)}, f32[8,32]{1,0:T(8,128)}, f32[2208,128]{1,0:T(8,128)}) custom-call(bf16[2,256,1536]{2,1,0:T(8,128)(2,1)} %bitcast.113, f32[16,1536]{1,0:T(8,128)} %fusion.89.refs_1_, f32[16,1536]{1,0:T(8,128)} %get-tuple-element.125.refs_2_, f32[16,1536]{1,0:T(8,128)} %get-tuple-element.126.refs_3_, ...), custom_call_target="tpu_custom_call" | custom-call | tf_op jit(solution)/shard_map/gradient_exchange/pallas_call | solution.py:1086
  905.7 3.5 convert_element_type.141
  909.2 1.0 copy.89
  (195 shorter events, 26.2 us)
Async XLA Ops:
  0.6 27.1 %copy-start.20 = (bf16[2,192,1152]{2,1,0:T(8,128)(2,1)S(1)}, bf16[2,192,1152]{2,1,0:T(8,128)(2,1)}, u32[]{:S(2)}) copy-start(bf16[2,192,1152]{2,1,0:T(8,128)(2,1)} %param.20) | copy-start | bytes 2654212
  0.6 28.2 %copy-start.17 = (bf16[2,1536,192]{1,2,0:T(8,128)(2,1)S(1)}, bf16[2,1536,192]{1,2,0:T(8,128)(2,1)}, u32[]{:S(2)}) copy-start(bf16[2,1536,192]{1,2,0:T(8,128)(2,1)} %param.23) | copy-start | bytes 3538948
  0.7 28.2 %copy-start.18 = (bf16[2,192,1536]{2,1,0:T(8,128)(2,1)S(1)}, bf16[2,192,1536]{2,1,0:T(8,128)(2,1)}, u32[]{:S(2)}) copy-start(bf16[2,192,1536]{2,1,0:T(8,128)(2,1)} %param.22) | copy-start | bytes 3538948
  0.7 29.6 %collective-permute-start = (s32[1,2]{1,0:T(1,128)}, s32[1,2]{1,0:T(1,128)S(1)}, u32[]{:S(2)}, u32[]{:S(2)}) collective-permute-start(s32[1,2]{1,0:T(1,128)} %param.16), channel_id=1, source_target_pairs={{0,4},{4,0},{8,12},{12,8},{16,20},{20,16},{24,28},{28,24},{1,5},{5... | collective-permute-start | bytes 32 | tf_op jit(solution)/shard_map/ppermute | solution.py:1814
  1.4 29.2 %collective-permute-start.14 = (s32[2]{0:T(128)}, s32[2]{0:T(128)S(1)}, u32[]{:S(2)}, u32[]{:S(2)}) collective-permute-start(s32[2]{0:T(128)} %param.17), channel_id=1, source_target_pairs={{0,4},{4,0},{8,12},{12,8},{16,20},{20,16},{24,28},{28,24},{1,5},{5... | collective-permute-start | bytes 32 | tf_op jit(solution)/shard_map/ppermute | solution.py:1814
  27.8 2.5 copy-start.28
  27.8 2.8 copy-start.29
  401.6 3.8 copy-start.24
  401.6 3.8 copy-start
  405.4 38.3 %copy-start.6 = (f32[16,1536]{1,0:T(8,128)S(1)}, f32[16,1536]{1,0:T(8,128)}, u32[]{:S(2)}) copy-start(f32[16,1536]{1,0:T(8,128)} %get-tuple-element.98.mod_ref) | copy-start | bytes 294916
  443.1 2.4 collective-permute-start.1
  492.7 56.6 %copy-start.1 = (bf16[48,1536]{1,0:T(8,128)(2,1)S(1)}, bf16[48,1536]{1,0:T(8,128)(2,1)}, u32[]{:S(2)}) copy-start(bf16[48,1536]{1,0:T(8,128)(2,1)} %pad.35.refs_18_.x_ref) | copy-start | bytes 442372
  492.7 56.6 %copy-start.2 = (f32[192,128]{1,0:T(8,128)S(1)}, f32[192,128]{1,0:T(8,128)}, u32[]{:S(2)}) copy-start(f32[192,128]{1,0:T(8,128)} %pad.36.refs_20_.mask_ref) | copy-start | bytes 294916
  492.7 56.6 %copy-start.3 = (bf16[128,1536]{1,0:T(8,128)(2,1)S(1)}, bf16[128,1536]{1,0:T(8,128)(2,1)}, u32[]{:S(2)}) copy-start(bf16[128,1536]{1,0:T(8,128)(2,1)} %get-tuple-element.104.a1_ref) | copy-start | bytes 1179652
  492.7 56.6 %copy-start.4 = (bf16[128,1536]{1,0:T(8,128)(2,1)S(1)}, bf16[128,1536]{1,0:T(8,128)(2,1)}, u32[]{:S(2)}) copy-start(bf16[128,1536]{1,0:T(8,128)(2,1)} %get-tuple-element.103.bo_ref) | copy-start | bytes 1179652
  492.7 56.6 %copy-start.5 = (bf16[128,1536]{1,0:T(8,128)(2,1)S(1)}, bf16[128,1536]{1,0:T(8,128)(2,1)}, u32[]{:S(2)}) copy-start(bf16[128,1536]{1,0:T(8,128)(2,1)} %get-tuple-element.105.b1_ref) | copy-start | bytes 1179652
  492.7 56.6 %copy-start.7 = (f32[48,1]{1,0:T(8,128)S(1)}, f32[48,1]{1,0:T(8,128)}, u32[]{:S(2)}) copy-start(f32[48,1]{1,0:T(8,128)} %slice_subtract_fusion.2.refs_19_.own_ref) | copy-start | bytes 580
  492.7 56.6 %copy-start.8 = (bf16[128,384]{1,0:T(8,128)(2,1)S(1)}, bf16[128,384]{1,0:T(8,128)(2,1)}, u32[]{:S(2)}) copy-start(bf16[128,384]{1,0:T(8,128)(2,1)} %get-tuple-element.102.ao_ref) | copy-start | bytes 294916
  548.8 130.0 %collective-permute-start.4 = (bf16[512,768]{1,0:T(8,128)(2,1)}, bf16[512,768]{1,0:T(8,128)(2,1)}, u32[]{:S(2)}, u32[]{:S(2)}) collective-permute-start(bf16[512,768]{1,0:T(8,128)(2,1)} %broadcast_select_fusion.7), channel_id=1, source_target_pairs={{0,4},{4,0},{8,12},{12,8},{16,20},{20,16},{24,28},{28,24},{1,5},{5... | collective-permute-start | bytes 2359304 | tf_op jit(solution)/shard_map/ppermute | solution.py:1814
  549.3 126.0 %copy-start.16 = (bf16[512,1536]{1,0:T(8,128)(2,1)S(1)}, bf16[512,1536]{1,0:T(8,128)(2,1)}, u32[]{:S(2)}) copy-start(bf16[512,1536]{1,0:T(8,128)(2,1)} %get-tuple-element.96) | copy-start | bytes 4718596
  668.2 10.5 %copy-start.21 = (f32[24,1536]{1,0:T(8,128)S(1)}, f32[24,1536]{1,0:T(8,128)}, u32[]{:S(2)}) copy-start(f32[24,1536]{1,0:T(8,128)} %get-tuple-element.143) | copy-start | bytes 442372
  668.2 10.4 %copy-start.23 = (f32[8,1536]{1,0:T(8,128)S(1)}, f32[8,1536]{1,0:T(8,128)}, u32[]{:S(2)}) copy-start(f32[8,1536]{1,0:T(8,128)} %get-tuple-element.144) | copy-start | bytes 147460
  668.2 10.5 %copy-start.10 = (bf16[512,1536]{1,0:T(8,128)(2,1)S(1)}, bf16[512,1536]{1,0:T(8,128)(2,1)}, u32[]{:S(2)}) copy-start(bf16[512,1536]{1,0:T(8,128)(2,1)} %get-tuple-element.117) | copy-start | bytes 4718596
  675.4 75.7 %collective-permute-start.2 = (bf16[256,1536]{1,0:T(8,128)(2,1)S(1)}, bf16[256,1536]{1,0:T(8,128)(2,1)S(1)}, u32[]{:S(2)}, u32[]{:S(2)}) collective-permute-start(bf16[256,1536]{1,0:T(8,128)(2,1)S(1)} %get-tuple-element.174), channel_id=1, source_target_pairs={{0,0},{1,1},{4,2},{5,3},{2,4},{3,5},{6,6},{7,7},{8,8},{9,9},{12,10... | collective-permute-start | bytes 2359304 | tf_op jit(solution)/shard_map/ppermute | solution.py:1804
  677.5 73.5 %collective-permute-start.3 = (bf16[256,1536]{1,0:T(8,128)(2,1)S(1)}, bf16[256,1536]{1,0:T(8,128)(2,1)S(1)}, u32[]{:S(2)}, u32[]{:S(2)}) collective-permute-start(bf16[256,1536]{1,0:T(8,128)(2,1)S(1)} %get-tuple-element.175), channel_id=1, source_target_pairs={{1,0},{0,1},{5,2},{4,3},{3,4},{2,5},{7,6},{6,7},{9,8},{8,9},{13,10... | collective-permute-start | bytes 2359304 | tf_op jit(solution)/shard_map/ppermute | solution.py:1804
  741.7 18.3 %collective-permute-start.6 = (bf16[192,1152]{1,0:T(8,128)(2,1)S(1)}, bf16[192,1152]{1,0:T(8,128)(2,1)S(1)}, u32[]{:S(2)}, u32[]{:S(2)}) collective-permute-start(bf16[192,1152]{1,0:T(8,128)(2,1)S(1)} %get-tuple-element.183), channel_id=1, source_target_pairs={{0,0},{1,1},{4,2},{5,3},{2,4},{3,5},{6,6},{7,7},{8,8},{9,9},{12,10... | collective-permute-start | bytes 1327112 | tf_op jit(solution)/shard_map/ppermute | solution.py:1804
  745.7 20.8 %collective-permute-start.7 = (bf16[192,1152]{1,0:T(8,128)(2,1)S(1)}, bf16[192,1152]{1,0:T(8,128)(2,1)S(1)}, u32[]{:S(2)}, u32[]{:S(2)}) collective-permute-start(bf16[192,1152]{1,0:T(8,128)(2,1)S(1)} %get-tuple-element.184), channel_id=1, source_target_pairs={{1,0},{0,1},{5,2},{4,3},{3,4},{2,5},{7,6},{6,7},{9,8},{8,9},{13,10... | collective-permute-start | bytes 1327112 | tf_op jit(solution)/shard_map/ppermute | solution.py:1804
  751.0 15.7 %copy-start.11 = (bf16[8,192,1152]{2,1,0:T(8,128)(2,1)S(1)}, bf16[8,192,1152]{2,1,0:T(8,128)(2,1)}, u32[]{:S(2)}) copy-start(bf16[8,192,1152]{2,1,0:T(8,128)(2,1)} %get-tuple-element.133) | copy-start | bytes 10616836
  751.0 42.4 %collective-permute-start.5 = (bf16[512,2304]{1,0:T(8,128)(2,1)S(1)}, bf16[512,2304]{1,0:T(8,128)(2,1)}, u32[]{:S(2)}, u32[]{:S(2)}) collective-permute-start(bf16[512,2304]{1,0:T(8,128)(2,1)S(1)} %broadcast_select_fusion.2), channel_id=1, source_target_pairs={{0,4},{4,0},{8,12},{12,8},{16,20},{20,16},{24,28},{28,24},{1,5},{5... | collective-permute-start | bytes 7077896 | tf_op jit(solution)/shard_map/ppermute | solution.py:1814
  766.7 5.3 copy-start.22
  768.0 21.3 %copy-start.12 = (bf16[40,1536]{1,0:T(8,128)(2,1)S(1)}, bf16[40,1536]{1,0:T(8,128)(2,1)}, u32[]{:S(2)}) copy-start(bf16[40,1536]{1,0:T(8,128)(2,1)} %param.14) | copy-start | bytes 368644
  769.3 4.8 collective-permute-start.8
  769.3 6.8 collective-permute-start.9
  769.4 15.7 %collective-permute-start.10 = (bf16[48,1568]{1,0:T(8,128)(2,1)S(1)}, bf16[48,1568]{1,0:T(8,128)(2,1)S(1)}, u32[]{:S(2)}, u32[]{:S(2)}) collective-permute-start(bf16[48,1568]{1,0:T(8,128)(2,1)S(1)} %get-tuple-element.178), channel_id=1, source_target_pairs={{0,3},{1,2},{2,1},{3,0},{4,7},{5,6},{6,5},{7,4},{8,11},{9,10},{10,... | collective-permute-start | bytes 451592 | tf_op jit(solution)/shard_map/ppermute | solution.py:1822
  785.2 6.0 collective-permute-start.13
  785.3 6.0 collective-permute-start.12
  786.1 5.1 collective-permute-start.11
  793.4 3.6 copy-start.30
  796.9 1.4 copy-start.13
  797.0 2.1 copy-start.14
  797.0 2.1 copy-start.31
  799.1 1.5 copy-start.15
  799.1 2.4 copy-start.26
  800.6 3.2 copy-start.9
  825.7 79.2 %copy-start.25 = (bf16[2,32,1536]{2,1,0:T(8,128)(2,1)S(1)}, bf16[2,32,1536]{2,1,0:T(8,128)(2,1)}, u32[]{:S(2)}) copy-start(bf16[2,32,1536]{2,1,0:T(8,128)(2,1)} %get-tuple-element.154) | copy-start | bytes 589828
  825.7 79.3 %copy-start.27 = (f32[2,1536]{1,0:T(2,128)S(1)}, f32[2,1536]{1,0:T(2,128)}, u32[]{:S(2)}) copy-start(f32[2,1536]{1,0:T(2,128)} %param.15) | copy-start | bytes 36868
  903.1 6.1 copy-start.19

commit v6 on v5

--- a/solution.py
+++ b/solution.py
@@ -407,11 +407,128 @@
     return center * inverse, inverse
 
 
-def block_fwd_kernel(tiles, o_ref, x_ref, g_ref, mod_ref, wo_ref, ao_ref, bo_ref, a1_ref, b1_ref, w1_ref, a2_ref, w2_ref, b2_ref,
-                     a_out, x1_out, h2_out, u_out, y_out, to_out, t1_out, t2_out, gate_out, m_acc, t2_acc):
+def column_peers(n_z):
+    f, z = lax.axis_index("fsdp"), lax.axis_index("tp")
+    core = f % 2
+    base = f - core
+    peers = [(f, (z + j) % n_z) for j in range(1, n_z)]
+    peers += [(base + 1 - core, (z + j) % n_z) for j in range(n_z)]
+    return f, z, core, base, peers
+
+
+def meet(peers):
+    barrier = pltpu.get_barrier_semaphore()
+    for peer in peers:
+        pl.semaphore_signal(barrier, inc=1, device_id=peer, device_id_type=MESH)
+    pl.semaphore_wait(barrier, len(peers))
+
+
+def push(src, dst, send, recv, peer):
+    return pltpu.make_async_remote_copy(
+        src_ref=src, dst_ref=dst, send_sem=send, recv_sem=recv, device_id=peer, device_id_type=MESH)
+
+
+class ZRing:
+    def __init__(self, f, z, n_z):
+        self.f, self.z, self.n_z = f, z, n_z
+
+    def start(self, source_of, buf, send, recv):
+        for j in range(1, self.n_z):
+            to = (self.z + j) % self.n_z
+            push(source_of(to), buf.at[self.z], send.at[j], recv.at[self.z], (self.f, to)).start()
+
+    def wait(self, buf, send, recv):
+        for j in range(1, self.n_z):
+            came = (self.z + j) % self.n_z
+            push(buf.at[came], buf.at[came], send.at[j], recv.at[came], (self.f, came)).wait_recv()
+
+    def drain(self, source_of, buf, send, recv):
+        for j in range(1, self.n_z):
+            to = (self.z + j) % self.n_z
+            push(source_of(to), buf.at[self.z], send.at[j], recv.at[self.z], (self.f, to)).wait_send()
+
+
+def text_tools(n_z, pad, width, f, z, lmask_ref, part_ref, mine_ref, out_buf, in_buf, rs_send, rs_recv, ag_send, ag_recv):
+    ring = ZRing(f, z, n_z)
+    bf16, f32 = jnp.bfloat16, jnp.float32
+
+    def scatter(turn, main, rank_part):
+        full = jnp.concatenate([main, rank_part], axis=1)
+        full = full.reshape(n_z, pad, full.shape[1])
+        part_ref[...] = full
+        mine_ref[turn] = part_ref[z]
+        out_buf[turn] = full.astype(bf16)
+        ring.start(lambda to: out_buf.at[turn, to], in_buf.at[turn], rs_send.at[turn], rs_recv.at[turn])
+
+    def collect(turn):
+        ring.wait(in_buf.at[turn], rs_send.at[turn], rs_recv.at[turn])
+        total = mine_ref[turn]
+        for j in range(1, n_z):
+            total = total + in_buf[turn, (z + j) % n_z].astype(f32)
+        ring.drain(lambda to: out_buf.at[turn, to], in_buf.at[turn], rs_send.at[turn], rs_recv.at[turn])
+        return total[:, :width], (total[:, width:] * lmask_ref[...]).astype(bf16)
+
+    def spread(ref, *parts):
+        offset = 0
+        for part in parts:
+            ref[z, :, offset:offset + part.shape[1]] = part
+            offset += part.shape[1]
+        ring.start(lambda to: ref.at[z], ref, ag_send, ag_recv)
+
+    def spread_end(ref):
+        ring.wait(ref, ag_send, ag_recv)
+        ring.drain(lambda to: ref.at[z], ref, ag_send, ag_recv)
+
+    def gathered(ref, start, count):
+        return ref[:, :, start:start + count].reshape(n_z * pad, count)
+
+    def own_lanes(ref, share):
+        at = pl.ds(pl.multiple_of(z * share, 128), share)
+        return ref[:, :, at].reshape(n_z * pad, share)
+
+    return scatter, collect, spread, spread_end, gathered, own_lanes
+
+
+def rows_of(mod_ref, own_ref):
+    return lambda row: jnp.where(own_ref[...] > 0, mod_ref[row:row + 1, :], mod_ref[8 + row:9 + row, :])
+
+
+def both_fwd_kernel(tiles, n_z, turns, o_ref, x_ref, g_ref, mod_ref, wo_ref, ao_ref, bo_ref, a1_ref, b1_ref, w1_ref, a2_ref, w2_ref, b2_ref,
+                    ot_ref, xt_ref, tmod_ref, owner_ref, own_ref, lmask_ref, two_ref, tao_ref, tbo_ref,
+                    a_out, x1_out, h2_out, u_out, y_out, to_out, t1_out, t2_out, gate_out,
+                    tall_out, att_out, tx1_out, tbr_out,
+                    m_acc, t2_acc, o_got, part_ref, mine_ref, out_buf, in_buf, ag_ref, o_send, o_recv, rs_send, rs_recv, ag_send, ag_recv):
     step = pl.program_id(0)
+    f, z, core, base, column = column_peers(n_z)
+    pad, width_t = xt_ref.shape
+    f32, bf16 = jnp.float32, jnp.bfloat16
+    scatter, collect, spread, spread_end, gathered, own_lanes = text_tools(
+        n_z, pad, width_t, f, z, lmask_ref, part_ref, mine_ref, out_buf, in_buf, rs_send, rs_recv, ag_send, ag_recv)
+    home = [(base + z // 2, 2 * core + i) for i in range(2)]
+
+    def is_here(i):
+        return (z // 2 == core) & (2 * core + i == z)
+
+    def o_push(i):
+        return push(ot_ref.at[i], o_got.at[z % 2], o_send.at[i], o_recv.at[z % 2], home[i])
+
+    @pl.when(step == 0)
+    def _():
+        meet(column)
+        for i in range(2):
+            @pl.when(is_here(i))
+            def _():
+                copy = pltpu.make_async_copy(ot_ref.at[i], o_got.at[z % 2], o_recv.at[z % 2])
+                copy.start()
+                copy.wait()
+
+            @pl.when(jnp.logical_not(is_here(i)))
+            def _():
+                o_push(i).start()
+
     rows = o_ref.shape[0]
     width = o_ref.shape[1]
+
 
     @pl.when(step == 0)
     def _():
@@ -420,16 +537,16 @@
 
         def cols(n, _):
             sl = pl.ds(pl.multiple_of(n * 256, 256), 256)
-            a_out[:, sl] = mm_t(o_ref[...], wo_ref[sl, :]) + mm(to_out[...], bo_ref[:, sl])
+            a = mm_t(o_ref[...], wo_ref[sl, :]) + mm(to_out[...], bo_ref[:, sl])
+            a_out[:, sl] = a.astype(jnp.bfloat16)
+            x1_out[:, sl] = x_ref[:, sl].astype(jnp.float32) + mod_ref[2:3, sl] * a
             return 0
 
         lax.fori_loop(0, width // 256, cols, 0)
 
         def norm(r, _):
             sl = pl.ds(pl.multiple_of(r * ROWS, ROWS), ROWS)
-            x1 = x_ref[sl, :].astype(jnp.float32) + mod_ref[2:3, :] * a_out[sl, :]
-            x1_out[sl, :] = x1
-            xh, _inv = norm_rows(x1)
+            xh, _inv = norm_rows(x1_out[sl, :])
             h2_out[sl, :] = (xh * (1.0 + mod_ref[4:5, :]) + mod_ref[3:4, :]).astype(jnp.bfloat16)
             return 0
 
@@ -443,6 +560,35 @@
     f = gelu_parts(u)[0].astype(jnp.bfloat16)
     m_acc[...] += mm_t(f, w2_ref[...])
     t2_acc[...] += mm_t(f, a2_ref[...])
+
+
+    @pl.when(step == turns[0])
+    def _():
+        for i in range(2):
+            @pl.when(jnp.logical_not(is_here(i)))
+            def _():
+                push(o_got.at[i], o_got.at[i], o_send.at[i], o_recv.at[i], home[i]).wait_recv()
+                o_push(i).wait_send()
+        owner = owner_ref[...]
+        att = jnp.where(owner > 0, o_got[0].astype(f32), jnp.where(owner < 0, o_got[1].astype(f32), 0.0)).astype(bf16)
+        att_out[...] = att
+        scatter(0, mm_t(att, two_ref[...]), mm_t(att, tao_ref[...]))
+
+    @pl.when(step == turns[1])
+    def _():
+        modulation = rows_of(tmod_ref, own_ref)
+        branch, to_mine = collect(0)
+        branch = branch + mm(to_mine, tbo_ref[...])
+        tbr_out[...] = branch
+        x1 = xt_ref[...].astype(f32) + modulation(2) * branch
+        tx1_out[...] = x1
+        hat, _inv = norm_rows(x1)
+        spread(ag_ref, (hat * (1.0 + modulation(4)) + modulation(3)).astype(bf16), to_mine)
+
+    @pl.when(step == tiles - 1)
+    def _():
+        spread_end(ag_ref)
+        tall_out[...] = ag_ref[...]
 
     @pl.when(step == tiles - 1)
     def _():
@@ -460,40 +606,54 @@
         lax.fori_loop(0, rows // ROWS, last, 0)
 
 
-def block_fwd(o, x, g, mod, wo, pair_o, pair_1, w1, pair_2, w2, tn=512):
-    rows, width = o.shape
-    hidden = w1.shape[1]
-    tiles = hidden // tn
-    rank = pair_o[0].shape[0]
-    whole = lambda shape: pl.BlockSpec(shape, lambda n: (0,) * len(shape))
-    once = lambda shape: pl.BlockSpec(shape, lambda n: (0,) * len(shape), pipeline_mode=pl.Buffered(1))
-    tile = lambda height: pl.BlockSpec((height, tn), lambda n: (0, n))
+def both_back_kernel(tiles, n_z, turns, g_ref, x1_ref, a_ref, h2_ref, o_ref, mod_ref, u_ref, w2_ref, a2_ref, b2_ref, w1_ref, a1_ref, b1_ref,
+                     wo_ref, ao_ref, bo_ref, to_ref, t1_ref, t2_ref,
+                     gt_ref, tx1_ref, tbr_ref, tmod_ref, own_ref, mask_ref, lmask_ref, tall_ref, att_ref, tdm_ref, two_ref, tw1_ref, tw2_ref,
+                     tao_ref, tbo_ref, ta1_ref, tb1_ref, ta2_ref, tb2_ref,
+                     dx1_out, do_out, sums_out, ga2_out, gb1_out, ga1_out, gb2_out, gao_out, gbo_out,
+                     ty_out, tdx1_out, tdo_out, tsums_out, tgao_out, tgbo_out, tga1_out, tgb1_out, tga2_out, tgb2_out,
+                     dm_ref, dt2_ref, dh_acc, dt1_acc, part_ref, mine_ref, out_buf, in_buf, tda_ref, tdo_buf,
+                     do_send, do_recv, rs_send, rs_recv, ag_send, ag_recv):
+    step = pl.program_id(0)
+    f, z, core, base, column = column_peers(n_z)
+    pad, width_t = gt_ref.shape
+    rank = tao_ref.shape[0]
+    share = tao_ref.shape[1]
     f32, bf16 = jnp.float32, jnp.bfloat16
-    act = (rows, width)
-    return pl.pallas_call(
-        functools.partial(block_fwd_kernel, tiles),
-        grid=(tiles,),
-        in_specs=[once(act), once(act), once(act), once(mod.shape), once((width, width)), once((rank, width)), once((rank, width)),
-                  once((rank, width)), tile(rank), tile(width), tile(rank), tile(width), once((rank, width))],
-        out_specs=[whole(act), whole(act), whole(act), tile(rows), whole(act), whole((rows, rank)), whole((rows, rank)),
-                   whole((rows, rank)), whole((8, width))],
-        out_shape=[jax.ShapeDtypeStruct(act, f32), jax.ShapeDtypeStruct(act, f32), jax.ShapeDtypeStruct(act, bf16),
-                   jax.ShapeDtypeStruct((rows, hidden), f32), jax.ShapeDtypeStruct(act, bf16)]
-        + [jax.ShapeDtypeStruct((rows, rank), bf16)] * 3 + [jax.ShapeDtypeStruct((8, width), f32)],
-        scratch_shapes=[pltpu.VMEM(act, f32), pltpu.VMEM((rows, rank), f32)],
-        compiler_params=pltpu.CompilerParams(vmem_limit_bytes=58 * 1024 * 1024),
-        cost_estimate=pl.CostEstimate(flops=2 * rows * width * (width + 2 * hidden), bytes_accessed=4 * width * hidden, transcendentals=0),
-        name="block_forward",
-    )(o, x, g, mod, wo, *pair_o, pair_1[0], pair_1[1], w1, pair_2[0], w2, pair_2[1])
-
-
-def block_back_kernel(tiles, g_ref, x1_ref, a_ref, h2_ref, o_ref, mod_ref, u_ref, w2_ref, a2_ref, b2_ref, w1_ref, a1_ref, b1_ref,
-                      wo_ref, ao_ref, bo_ref, to_ref, t1_ref, t2_ref,
-                      dx1_out, do_out, sums_out, ga2_out, gb1_out, ga1_out, gb2_out, gao_out, gbo_out,
-                      dm_ref, dt2_ref, dh_acc, dt1_acc, da_ref):
-    step = pl.program_id(0)
+    scatter, collect, spread, spread_end, gathered, own_lanes = text_tools(
+        n_z, pad, width_t, f, z, lmask_ref, part_ref, mine_ref, out_buf, in_buf, rs_send, rs_recv, ag_send, ag_recv)
+    home = [(base + z // 2, 2 * core + i) for i in range(2)]
+
+    def is_here(i):
+        return (z // 2 == core) & (2 * core + i == z)
+
+    def do_push(s):
+        return push(tdo_buf, tdo_out.at[z % 2], do_send.at[s], do_recv.at[z % 2], home[s])
+
+    def collapse(place, values):
+        for s in range(2):
+            tsums_out[2 * place + s:2 * place + s + 1, :] = jnp.sum(
+                jnp.where(own_ref[...] == (1.0 if s == 0 else -1.0), values, 0.0), axis=0, keepdims=True)
+
+    @pl.when(step == 0)
+    def _():
+        meet(column)
+        h2_all = gathered(tall_ref, 0, width_t)
+        t1 = (mm_t(h2_all, ta1_ref[...]) * mask_ref[...]).astype(bf16)
+        u = mm(h2_all, tw1_ref[...]) + mm(t1, tb1_ref[...])
+        act, slope = gelu_parts(u)
+        act = act.astype(bf16)
+        dm_all = tdm_ref[...].reshape(n_z * pad, width_t)
+        dt2 = (mm_t(dm_all, tb2_ref[...]) * mask_ref[...]).astype(bf16)
+        du = ((mm(dm_all, tw2_ref[...]) + mm(dt2, ta2_ref[...])) * slope).astype(bf16)
+        scatter(1, mm_t(du, tw1_ref[...]), mm_t(du, tb1_ref[...]))
+        scatter(0, mm_t(act, tw2_ref[...]), mm_t(act, ta2_ref[...]))
+        tga2_out[...] = t_mm(dt2, act)
+        tgb1_out[...] = t_mm(t1, du)
+
     rows, width = g_ref.shape
     bf16 = jnp.bfloat16
+
 
     @pl.when(step == 0)
     def _():
@@ -515,6 +675,49 @@
     gb1_out[...] = t_mm(t1_ref[...], du)
     dh_acc[...] += mm_t(du, w1_ref[...])
     dt1_acc[...] += mm_t(du, b1_ref[...])
+
+
+    @pl.when(step == turns[0])
+    def _():
+        modulation = rows_of(tmod_ref, own_ref)
+        dh, dt1_mine = collect(1)
+        dh = dh + mm(dt1_mine, ta1_ref[...])
+        hat, inverse = norm_rows(tx1_ref[...])
+        dz = dh * (1.0 + modulation(4))
+        dx1 = gt_ref[...].astype(f32) + inverse * (
+            dz - jnp.mean(dz, axis=-1, keepdims=True) - hat * jnp.mean(dz * hat, axis=-1, keepdims=True))
+        feed, t2_mine = collect(0)
+        spread(tda_ref, (modulation(2) * dx1).astype(bf16), dt1_mine, t2_mine)
+        tdx1_out[...] = dx1
+        collapse(0, dx1 * tbr_ref[...])
+        collapse(1, dh)
+        collapse(2, dh * hat)
+        feed = feed + mm(t2_mine, tb2_ref[...])
+        ty_out[...] = (tx1_ref[...] + modulation(5) * feed).astype(bf16)
+        collapse(3, gt_ref[...].astype(f32) * feed)
+
+    @pl.when(step == turns[1])
+    def _():
+        spread_end(tda_ref)
+        da_all = gathered(tda_ref, 0, width_t)
+        dt1 = gathered(tda_ref, width_t, rank)
+        t2 = gathered(tda_ref, width_t + rank, rank)
+        dto = (mm_t(da_all, tbo_ref[...]) * mask_ref[...]).astype(bf16)
+        tdo_buf[...] = (mm(da_all, two_ref[...]) + mm(dto, tao_ref[...])).astype(bf16)
+        for s in range(2):
+            @pl.when(is_here(s))
+            def _():
+                copy = pltpu.make_async_copy(tdo_buf, tdo_out.at[z % 2], do_recv.at[z % 2])
+                copy.start()
+                copy.wait()
+
+            @pl.when(jnp.logical_not(is_here(s)))
+            def _():
+                do_push(s).start()
+        tgao_out[...] = t_mm(dto, att_ref[...])
+        tgbo_out[...] = t_mm(gathered(tall_ref, width_t, rank), own_lanes(tda_ref, share))
+        tgb2_out[...] = t_mm(t2, own_lanes(tdm_ref, share))
+        tga1_out[...] = t_mm(dt1, own_lanes(tall_ref, share))
 
     @pl.when(step == tiles - 1)
     def _():
@@ -531,291 +734,111 @@
             dx1 = g_ref[sl, :].astype(jnp.float32) + inverse * (
                 dz - jnp.mean(dz, axis=-1, keepdims=True) - xh * jnp.mean(dz * xh, axis=-1, keepdims=True))
             dx1_out[sl, :] = dx1
-            da_ref[sl, :] = (mod_ref[2:3, :] * dx1).astype(bf16)
+            dm_ref[sl, :] = (mod_ref[2:3, :] * dx1).astype(bf16)
             fold = lambda v: sum(v[8 * i:8 * i + 8, :] for i in range(ROWS // 8))
-            sums_out[0:8, :] += fold(dx1 * a_ref[sl, :])
+            sums_out[0:8, :] += fold(dx1 * a_ref[sl, :].astype(jnp.float32))
             sums_out[8:16, :] += fold(dh)
             sums_out[16:24, :] += fold(dh * xh)
             return 0
 
         lax.fori_loop(0, rows // ROWS, last, 0)
-        dto = mm_t(da_ref[...], bo_ref[...]).astype(bf16)
+        dto = mm_t(dm_ref[...], bo_ref[...]).astype(bf16)
         dt2_ref[...] = dto
         gao_out[...] = t_mm(dto, o_ref[...])
-        gbo_out[...] = t_mm(to_ref[...], da_ref[...])
+        gbo_out[...] = t_mm(to_ref[...], dm_ref[...])
 
         def cols(n, _):
             sl = pl.ds(pl.multiple_of(n * 256, 256), 256)
-            do_out[:, sl] = (mm(da_ref[...], wo_ref[:, sl]) + mm(dt2_ref[...], ao_ref[:, sl])).astype(bf16)
+            do_out[:, sl] = (mm(dm_ref[...], wo_ref[:, sl]) + mm(dt2_ref[...], ao_ref[:, sl])).astype(bf16)
             return 0
 
         lax.fori_loop(0, width // 256, cols, 0)
 
-
-def block_back(g, x1, a, h2, o, mod, u, w2, pair_2, w1, pair_1, wo, pair_o, mids, tn=512):
+    @pl.when(step == tiles - 1)
+    def _():
+        for i in range(2):
+            @pl.when(jnp.logical_not(is_here(i)))
+            def _():
+                push(tdo_out.at[i], tdo_out.at[i], do_send.at[i], do_recv.at[i], home[i]).wait_recv()
+                do_push(i).wait_send()
+
+
+def both_fwd(o, x, g, mod, wo, pair_o, pair_1, w1, pair_2, w2, ot, xt, tmod, owner, own, lmask, two, tpair_o, n_z, cid, tn=512, turns=(2, 7)):
     rows, width = o.shape
     hidden = w1.shape[1]
     tiles = hidden // tn
     rank = pair_o[0].shape[0]
-    whole = lambda shape: pl.BlockSpec(shape, lambda n: (0,) * len(shape))
     once = lambda shape: pl.BlockSpec(shape, lambda n: (0,) * len(shape), pipeline_mode=pl.Buffered(1))
+    whole = once
     tile = lambda height: pl.BlockSpec((height, tn), lambda n: (0, n))
     f32, bf16 = jnp.float32, jnp.bfloat16
+    shape, vmem, dma = jax.ShapeDtypeStruct, pltpu.VMEM, pltpu.SemaphoreType.DMA
+    act = (rows, width)
+    pad = xt.shape[0]
+    total, share = n_z * pad, two.shape[1]
+    thick = tpair_o[0].shape[0]
+    wide = width + thick
+    texts = (xt, tmod, owner, own, lmask, two, *tpair_o)
+    return pl.pallas_call(
+        functools.partial(both_fwd_kernel, tiles, n_z, turns),
+        grid=(tiles,),
+        in_specs=[once(act), once(act), once(act), once(mod.shape), once((width, width)), once((rank, width)), once((rank, width)),
+                  once((rank, width)), tile(rank), tile(width), tile(rank), tile(width), once((rank, width)),
+                  pl.BlockSpec(memory_space=pl.ANY)] + [once(v.shape) for v in texts],
+        out_specs=[whole(act), whole(act), whole(act), tile(rows), whole(act), whole((rows, rank)), whole((rows, rank)),
+                   whole((rows, rank)), whole((8, width)), whole((n_z, pad, wide)), whole((total, share)), whole((pad, width)),
+                   whole((pad, width))],
+        out_shape=[shape(act, bf16), shape(act, f32), shape(act, bf16), shape((rows, hidden), f32), shape(act, bf16)]
+        + [shape((rows, rank), bf16)] * 3
+        + [shape((8, width), f32), shape((n_z, pad, wide), bf16), shape((total, share), bf16), shape((pad, width), f32),
+           shape((pad, width), f32)],
+        scratch_shapes=[vmem(act, f32), vmem((rows, rank), f32), vmem((2, total, share), bf16), vmem((n_z, pad, wide), f32), vmem((1, pad, wide), f32),
+                        vmem((1, n_z, pad, wide), bf16), vmem((1, n_z, pad, wide), bf16), vmem((n_z, pad, wide), bf16),
+                        dma((2,)), dma((2,)), dma((1, n_z)), dma((1, n_z)), dma((n_z,)), dma((n_z,))],
+        compiler_params=pltpu.CompilerParams(collective_id=cid, has_side_effects=True, vmem_limit_bytes=60 * 1024 * 1024),
+        name="block_forward",
+    )(o, x, g, mod, wo, *pair_o, pair_1[0], pair_1[1], w1, pair_2[0], w2, pair_2[1], ot, *texts)
+
+
+def both_back(g, x1, a, h2, o, mod, u, w2, pair_2, w1, pair_1, wo, pair_o, mids,
+              gt, tx1, tbr, tmod, own, mask, lmask, tall, att, tdm, two, tw1, tw2, tpair_o, tpair_1, tpair_2, n_z, cid, tn=512, turns=(5, 9)):
+    rows, width = o.shape
+    hidden = w1.shape[1]
+    tiles = hidden // tn
+    rank = pair_o[0].shape[0]
+    once = lambda shape: pl.BlockSpec(shape, lambda n: (0,) * len(shape), pipeline_mode=pl.Buffered(1))
+    whole = once
+    tile = lambda height: pl.BlockSpec((height, tn), lambda n: (0, n))
+    f32, bf16 = jnp.float32, jnp.bfloat16
+    shape, vmem, dma = jax.ShapeDtypeStruct, pltpu.VMEM, pltpu.SemaphoreType.DMA
     act = (rows, width)
     side = (rank, width)
     thin = (rows, rank)
+    pad = gt.shape[0]
+    total, share = n_z * pad, two.shape[1]
+    thick = tpair_o[0].shape[0]
+    t_hidden = tw1.shape[1]
+    wide = width + thick
+    texts = (gt, tx1, tbr, tmod, own, mask, lmask, tall, att, tdm, two, tw1, tw2, *tpair_o, *tpair_1, *tpair_2)
     return pl.pallas_call(
-        functools.partial(block_back_kernel, tiles),
+        functools.partial(both_back_kernel, tiles, n_z, turns),
         grid=(tiles,),
         in_specs=[once(act)] * 5 + [once(mod.shape), tile(rows), tile(width), tile(rank), once(side), tile(width), once(side), tile(rank),
-                  once((width, width)), once(side), once(side)] + [once(thin)] * 3,
-        out_specs=[whole(act), whole(act), whole((24, width)), tile(rank), tile(rank)] + [whole(side)] * 4,
-        out_shape=[jax.ShapeDtypeStruct(act, f32), jax.ShapeDtypeStruct(act, bf16), jax.ShapeDtypeStruct((24, width), f32)]
-        + [jax.ShapeDtypeStruct((rank, hidden), f32)] * 2 + [jax.ShapeDtypeStruct(side, f32)] * 4,
-        scratch_shapes=[pltpu.VMEM(act, bf16), pltpu.VMEM(thin, bf16), pltpu.VMEM(act, f32), pltpu.VMEM(thin, f32), pltpu.VMEM(act, bf16)],
-        compiler_params=pltpu.CompilerParams(vmem_limit_bytes=58 * 1024 * 1024),
-        cost_estimate=pl.CostEstimate(flops=2 * rows * width * (width + 2 * hidden), bytes_accessed=4 * width * hidden, transcendentals=0),
+                  once((width, width)), once(side), once(side)] + [once(thin)] * 3 + [once(v.shape) for v in texts],
+        out_specs=[whole(act), whole(act), whole((24, width)), tile(rank), tile(rank)] + [whole(side)] * 4
+        + [whole((pad, width)), whole((pad, width)), pl.BlockSpec(memory_space=pl.ANY), whole((8, width)), whole((thick, share)),
+           whole((thick, share)), whole((thick, share)), whole((thick, t_hidden)), whole((thick, t_hidden)), whole((thick, share))],
+        out_shape=[shape(act, f32), shape(act, bf16), shape((24, width), f32)] + [shape((rank, hidden), f32)] * 2 + [shape(side, f32)] * 4
+        + [shape((pad, width), bf16), shape((pad, width), f32), shape((2, total, share), bf16), shape((8, width), f32),
+           shape((thick, share), f32), shape((thick, share), f32), shape((thick, share), f32), shape((thick, t_hidden), f32),
+           shape((thick, t_hidden), f32), shape((thick, share), f32)],
+        scratch_shapes=[vmem(act, bf16), vmem(thin, bf16), vmem(act, f32), vmem(thin, f32),
+                        vmem((n_z, pad, wide), f32), vmem((2, pad, wide), f32), vmem((2, n_z, pad, wide), bf16), vmem((2, n_z, pad, wide), bf16),
+                        vmem((n_z, pad, wide + thick), bf16), vmem((total, share), bf16),
+                        dma((2,)), dma((2,)), dma((2, n_z)), dma((2, n_z)), dma((n_z,)), dma((n_z,))],
+        compiler_params=pltpu.CompilerParams(collective_id=cid, has_side_effects=True, vmem_limit_bytes=60 * 1024 * 1024),
         name="block_backward",
-    )(g, x1, a, h2, o, mod, u, w2, pair_2[0], pair_2[1], w1, pair_1[0], pair_1[1], wo, *pair_o, *mids)
-
-
-def column_peers(n_z):
-    f, z = lax.axis_index("fsdp"), lax.axis_index("tp")
-    core = f % 2
-    base = f - core
-    peers = [(f, (z + j) % n_z) for j in range(1, n_z)]
-    peers += [(base + 1 - core, (z + j) % n_z) for j in range(n_z)]
-    return f, z, core, base, peers
-
-
-def meet(peers):
-    barrier = pltpu.get_barrier_semaphore()
-    for peer in peers:
-        pl.semaphore_signal(barrier, inc=1, device_id=peer, device_id_type=MESH)
-    pl.semaphore_wait(barrier, len(peers))
-
-
-def push(src, dst, send, recv, peer):
-    return pltpu.make_async_remote_copy(
-        src_ref=src, dst_ref=dst, send_sem=send, recv_sem=recv, device_id=peer, device_id_type=MESH)
-
-
-class ZRing:
-    def __init__(self, f, z, n_z):
-        self.f, self.z, self.n_z = f, z, n_z
-
-    def start(self, source_of, buf, send, recv):
-        for j in range(1, self.n_z):
-            to = (self.z + j) % self.n_z
-            push(source_of(to), buf.at[self.z], send.at[j], recv.at[self.z], (self.f, to)).start()
-
-    def wait(self, buf, send, recv):
-        for j in range(1, self.n_z):
-            came = (self.z + j) % self.n_z
-            push(buf.at[came], buf.at[came], send.at[j], recv.at[came], (self.f, came)).wait_recv()
-
-    def drain(self, source_of, buf, send, recv):
-        for j in range(1, self.n_z):
-            to = (self.z + j) % self.n_z
-            push(source_of(to), buf.at[self.z], send.at[j], recv.at[self.z], (self.f, to)).wait_send()
-
-
-def text_mid_kernel(n_z, o_ref, x_ref, g_ref, mod_ref, owner_ref, own_ref, mask_ref, lmask_ref, wo_ref, w1_ref, w2_ref,
-                    ao_ref, bo_ref, a1_ref, b1_ref, a2_ref, b2_ref,
-                    y_out, dx1_out, do_out, sums_out, gao_out, gbo_out, ga1_out, gb1_out, ga2_out, gb2_out,
-                    o_got, part_ref, out_buf, in_buf, ag_ref, da_ref, dm_ref, u_ref, f_ref, att_ref, do_buf, x1_ref, br_ref, t_ref,
-                    o_send, o_recv, rs_send, rs_recv, ag_send, ag_recv, dm_send, dm_recv, do_send, do_recv):
-    f, z, core, base, peers = column_peers(n_z)
-    ring = ZRing(f, z, n_z)
-    bf16, f32 = jnp.bfloat16, jnp.float32
-    pad, width = x_ref.shape
-    rank = ao_ref.shape[0]
-    share = ao_ref.shape[1]
-    meet(peers)
-
-    def modulation(row):
-        return jnp.where(own_ref[...] > 0, mod_ref[row:row + 1, :], mod_ref[8 + row:9 + row, :])
-
-    home = [(base + z // 2, 2 * core + i) for i in range(2)]
-    for i in range(2):
-        here = (z // 2 == core) & (2 * core + i == z)
-
-        @pl.when(here)
-        def _():
-            copy = pltpu.make_async_copy(o_ref.at[i], o_got.at[z % 2], o_recv.at[z % 2])
-            copy.start()
-            copy.wait()
-
-        @pl.when(jnp.logical_not(here))
-        def _():
-            push(o_ref.at[i], o_got.at[z % 2], o_send.at[i], o_recv.at[z % 2], home[i]).start()
-
-    dm_ref[z, :, :] = (modulation(5) * g_ref[...].astype(f32)).astype(bf16)
-    ring.start(lambda to: dm_ref.at[z], dm_ref, dm_send, dm_recv)
-
-    for s in range(2):
-        here = (z // 2 == core) & (2 * core + s == z)
-
-        @pl.when(jnp.logical_not(here))
-        def _():
-            push(o_got.at[s], o_got.at[s], o_send.at[s], o_recv.at[s], home[s]).wait_recv()
-
-    owner = owner_ref[...]
-    att_ref[...] = jnp.where(
-        owner > 0, o_got[0].astype(f32), jnp.where(owner < 0, o_got[1].astype(f32), 0.0)).astype(bf16)
-
-    def scatter(turn, main, rank_part):
-        full = jnp.concatenate([main, rank_part], axis=1)
-        full = full.reshape(n_z, pad, full.shape[1])
-        part_ref[...] = full
-        out_buf[...] = full.astype(bf16)
-        ring.start(lambda to: out_buf.at[to], in_buf.at[turn], rs_send.at[turn], rs_recv.at[turn])
-
-    def collect(turn):
-        ring.wait(in_buf.at[turn], rs_send.at[turn], rs_recv.at[turn])
-        total = part_ref[z]
-        for j in range(1, n_z):
-            total = total + in_buf[turn, (z + j) % n_z].astype(f32)
-        ring.drain(lambda to: out_buf.at[to], in_buf.at[turn], rs_send.at[turn], rs_recv.at[turn])
-        return total[:, :width], (total[:, width:] * lmask_ref[...]).astype(bf16)
-
-    def spread(turn, ref, *parts):
-        offset = 0
-        for part in parts:
-            ref[z, :, offset:offset + part.shape[1]] = part
-            offset += part.shape[1]
-        ring.start(lambda to: ref.at[z], ref, ag_send.at[turn], ag_recv.at[turn])
-
-    def spread_end(turn, ref):
-        ring.wait(ref, ag_send.at[turn], ag_recv.at[turn])
-        ring.drain(lambda to: ref.at[z], ref, ag_send.at[turn], ag_recv.at[turn])
-
-    def gathered(ref, start, count):
-        return ref[:, :, start:start + count].reshape(n_z * pad, count)
-
-    def own_lanes(ref):
-        at = pl.ds(pl.multiple_of(z * share, 128), share)
-        return ref[:, :, at].reshape(n_z * pad, share)
-
-    mask = mask_ref[...]
-    att = att_ref[...]
-    scatter(0, mm_t(att, wo_ref[...]), mm_t(att, ao_ref[...]))
-    branch, to_mine = collect(0)
-    branch = branch + mm(to_mine, bo_ref[...])
-    br_ref[...] = branch
-    x1 = x_ref[...].astype(f32) + modulation(2) * branch
-    x1_ref[...] = x1
-    xh, _inv = norm_rows(x1)
-    h2 = (xh * (1.0 + modulation(4)) + modulation(3)).astype(bf16)
-    spread(0, ag_ref, h2, to_mine)
-    spread_end(0, ag_ref)
-    h2_all = gathered(ag_ref, 0, width)
-    to_all = gathered(ag_ref, width, rank)
-    t1 = (mm_t(h2_all, a1_ref[...]) * mask).astype(bf16)
-    u = mm(h2_all, w1_ref[...]) + mm(t1, b1_ref[...])
-    u_ref[...] = u
-    act = gelu_parts(u)[0].astype(bf16)
-    f_ref[...] = act
-    scatter(1, mm_t(act, w2_ref[...]), mm_t(act, a2_ref[...]))
-    t_ref[0] = to_all
-    t_ref[1] = t1
-    feed, t2_mine = collect(1)
-    feed = feed + mm(t2_mine, b2_ref[...])
-    y_out[...] = (x1_ref[...] + modulation(5) * feed).astype(bf16)
-
-    def collapse(place, values):
-        for s in range(2):
-            sums_out[2 * place + s:2 * place + s + 1, :] = jnp.sum(
-                jnp.where(own_ref[...] == (1.0 if s == 0 else -1.0), values, 0.0), axis=0, keepdims=True)
-
-    collapse(3, g_ref[...].astype(f32) * feed)
-
-    ring.wait(dm_ref, dm_send, dm_recv)
-    ring.drain(lambda to: dm_ref.at[z], dm_ref, dm_send, dm_recv)
-    dm_all = dm_ref[...].reshape(n_z * pad, width)
-    dt2 = (mm_t(dm_all, b2_ref[...]) * mask).astype(bf16)
-    df = mm(dm_all, w2_ref[...]) + mm(dt2, a2_ref[...])
-    ga2_out[...] = t_mm(dt2, f_ref[...])
-    du = (df * gelu_parts(u_ref[...])[1]).astype(bf16)
-    scatter(2, mm_t(du, w1_ref[...]), mm_t(du, b1_ref[...]))
-    gb1_out[...] = t_mm(t_ref[1], du)
-    dh, dt1_mine = collect(2)
-    dh = dh + mm(dt1_mine, a1_ref[...])
-    xh, inverse = norm_rows(x1_ref[...])
-    dz = dh * (1.0 + modulation(4))
-    dx1 = g_ref[...].astype(f32) + inverse * (
-        dz - jnp.mean(dz, axis=-1, keepdims=True) - xh * jnp.mean(dz * xh, axis=-1, keepdims=True))
-    spread(1, da_ref, (modulation(2) * dx1).astype(bf16), dt1_mine, t2_mine)
-    dx1_out[...] = dx1
-    collapse(0, dx1 * br_ref[...])
-    collapse(1, dh)
-    collapse(2, dh * xh)
-    spread_end(1, da_ref)
-    da_all = gathered(da_ref, 0, width)
-    dt1 = gathered(da_ref, width, rank)
-    t2 = gathered(da_ref, width + rank, rank)
-    dto = (mm_t(da_all, bo_ref[...]) * mask).astype(bf16)
-    do_buf[...] = (mm(da_all, wo_ref[...]) + mm(dto, ao_ref[...])).astype(bf16)
-    for s in range(2):
-        here = (z // 2 == core) & (2 * core + s == z)
-
-        @pl.when(here)
-        def _():
-            copy = pltpu.make_async_copy(do_buf, do_out.at[z % 2], do_recv.at[z % 2])
-            copy.start()
-            copy.wait()
-
-        @pl.when(jnp.logical_not(here))
-        def _():
-            push(do_buf, do_out.at[z % 2], do_send.at[s], do_recv.at[z % 2], (base + z // 2, 2 * core + s)).start()
-
-    gao_out[...] = t_mm(dto, att_ref[...])
-    gbo_out[...] = t_mm(t_ref[0], own_lanes(da_ref))
-    gb2_out[...] = t_mm(t2, own_lanes(dm_ref))
-    ga1_out[...] = t_mm(dt1, own_lanes(ag_ref))
-    for i in range(2):
-        here = (z // 2 == core) & (2 * core + i == z)
-
-        @pl.when(jnp.logical_not(here))
-        def _():
-            push(do_out.at[i], do_out.at[i], do_send.at[i], do_recv.at[i], home[i]).wait_recv()
-            push(do_buf, do_out.at[i], do_send.at[i], do_recv.at[i], home[i]).wait_send()
-            push(o_ref.at[i], o_got.at[z % 2], o_send.at[i], o_recv.at[z % 2], home[i]).wait_send()
-
-
-def text_mid(o, x, g, mod, owner, own, mask, lmask, wo, w1, w2, pair_o, pair_1, pair_2, n_z, cid):
-    pad, width = x.shape
-    rank, share = pair_o[0].shape
-    total = n_z * pad
-    hidden = w1.shape[1]
-    wide = width + rank
-    f32, bf16 = jnp.float32, jnp.bfloat16
-    shape = jax.ShapeDtypeStruct
-    vmem = pltpu.VMEM
-    dma = pltpu.SemaphoreType.DMA
-    args = (o, x, g, mod, owner, own, mask, lmask, wo, w1, w2, *pair_o, *pair_1, *pair_2)
-    out_shape = [
-        shape((pad, width), bf16), shape((pad, width), f32), shape((2, total, share), bf16), shape((8, width), f32),
-        shape((rank, share), f32), shape((rank, share), f32), shape((rank, share), f32), shape((rank, hidden), f32),
-        shape((rank, hidden), f32), shape((rank, share), f32),
-    ]
-    return pl.pallas_call(
-        functools.partial(text_mid_kernel, n_z),
-        out_shape=out_shape,
-        in_specs=[pl.BlockSpec(memory_space=vmem)] * len(args),
-        out_specs=[pl.BlockSpec(memory_space=vmem)] * len(out_shape),
-        scratch_shapes=[
-            vmem((2, total, share), bf16), vmem((n_z, pad, wide), f32), vmem((n_z, pad, wide), bf16),
-            vmem((3, n_z, pad, wide), bf16), vmem((n_z, pad, wide), bf16), vmem((n_z, pad, wide + rank), bf16),
-            vmem((n_z, pad, width), bf16),
-            vmem((total, hidden), f32), vmem((total, hidden), bf16), vmem((total, share), bf16),
-            vmem((total, share), bf16), vmem((pad, width), f32), vmem((pad, width), f32), vmem((2, total, rank), bf16),
-            dma((2,)), dma((2,)), dma((3, n_z)), dma((3, n_z)), dma((2, n_z)), dma((2, n_z)), dma((n_z,)), dma((n_z,)),
-            dma((2,)), dma((2,)),
-        ],
-        compiler_params=pltpu.CompilerParams(collective_id=cid, has_side_effects=True, vmem_limit_bytes=50 * 1024 * 1024),
-        name="text_block",
-    )(*args)
+    )(g, x1, a, h2, o, mod, u, w2, pair_2[0], pair_2[1], w1, pair_1[0], pair_1[1], wo, *pair_o, *mids, *texts)
 
 
 def flip_bits(chip, mask, nbits):
@@ -829,13 +852,17 @@
 def tail_kernel(n_f, n_z, fans, cols, *refs):
     it = iter(refs)
     take = lambda count: [next(it) for _ in range(count)]
-    grad_ref, = take(1)
-    img_a, img_b, txt_a, txt_b = take(4), take(4), take(4), take(4)
-    hot4_ref, hot2_ref, dmod_ref, wmod_ref, bmod_ref, tmod_ref, cond_ref, smask_ref = take(8)
-    grad_out, cond_out, rank_out, shard_out = take(4)
+    dq_in, tdq_in, wq_ref = take(3)
+    (x_ref, dx1_ref, h_ref, imod_ref, mid_ref, qa_ref, qb_ref, isum_ref, igate_ref, tx_ref, tdx1_ref, th_ref, tmodr_ref, owner_ref,
+     own_ref, lmask_ref, tmid_ref, twq_ref, tqa_ref, tqb_ref, tsum_ref) = take(21)
+    img_a, img_b, txt_a, txt_b = take(3), take(3), take(3), take(3)
+    hot4_ref, hot2_ref, wmod_ref, bmod_ref, tmod_ref, cond_ref, smask_ref = take(7)
+    grad_out, tgrad_out, cond_out, rank_out, shard_out = take(5)
+    (dq_ref, wtile, dh_ref, dt_ref, grad_ref, gaq_ref, gbq_ref, tgot, part_ref, mine_ref, out_buf, in_buf, dt_ag, tgb_ref, dmod_ref,
+     isums) = take(16)
     zmsg, zgot, dense, snd1, rcv1, snd2, rcv2, dgot, own_dm, all_dm, cpart, cgot, zsum, zall, dts = take(15)
     (g_send, g_recv, z_send, z_recv, c_send, c_recv, s_send, s_recv, d_send, d_recv, f_send, f_recv, p_send, p_recv,
-     q_send, q_recv, t_send, t_recv) = take(18)
+     q_send, q_recv, t_send, t_recv, dq_send, dq_recv, dq_own, w_sem, h_send, h_recv, rs_send, rs_recv, ag_send, ag_recv) = take(28)
     f32, bf16 = jnp.float32, jnp.bfloat16
     f, z, core, base, column = column_peers(n_z)
     chip = f // 2
@@ -849,16 +876,86 @@
     blk = shard_out.shape[0]
     hidden_rank = hot2_ref.shape[0]
 
-    def dmod_copy(index, peer):
-        return push(dmod_ref.at[peer[1]], dgot.at[core * n_z + z], d_send.at[index], d_recv.at[core * n_z + z], peer)
-
-    for index, peer in enumerate(column):
-        dmod_copy(index, peer).start()
-    dgot[core * n_z + z] = dmod_ref[z]
+    home = [(base + z // 2, 2 * core + i) for i in range(2)]
+
+    def is_here(i):
+        return (z // 2 == core) & (2 * core + i == z)
+
+    swap = push(dq_in.at[1 - core], dq_ref.at[core], dq_send, dq_recv, (partner, z))
+    swap.start()
+    keep = pltpu.make_async_copy(dq_in.at[core], dq_ref.at[core], dq_own)
+    keep.start()
+
+    def t_push(i):
+        return push(tdq_in.at[i], tgot.at[z % 2], h_send.at[i], h_recv.at[z % 2], home[i])
+
+    for i in range(2):
+        @pl.when(is_here(i))
+        def _():
+            copy = pltpu.make_async_copy(tdq_in.at[i], tgot.at[z % 2], h_recv.at[z % 2])
+            copy.start()
+            copy.wait()
+
+        @pl.when(jnp.logical_not(is_here(i)))
+        def _():
+            t_push(i).start()
+
+    pad, width = tx_ref.shape
+    thick = tqa_ref.shape[0]
+    scatter, collect, spread, spread_end, gathered, own_lanes = text_tools(
+        n_z, pad, width, f, z, lmask_ref, part_ref, mine_ref, out_buf, in_buf, rs_send, rs_recv, ag_send, ag_recv)
+    tn = wtile.shape[3]
+    per_half = dq_ref.shape[2] // tn
+
+    def tile_of(n):
+        side = core if n < per_half else 1 - core
+        return side, side * per_half + n % per_half
+
+    def tile_load(n):
+        at = pl.ds(pl.multiple_of(tile_of(n)[1] * tn, 128), tn)
+        return pltpu.make_async_copy(wq_ref.at[:, :, at], wtile.at[n % 2], w_sem.at[n % 2])
+
+    def tile_back(n):
+        if n + 1 < 2 * per_half:
+            tile_load(n + 1).start()
+        tile_load(n).wait()
+        side, number = tile_of(n)
+        at = pl.ds(pl.multiple_of(number * tn, 128), tn)
+        part = dq_ref[side, :, n % per_half * tn:(n % per_half + 1) * tn]
+        main = mm_t(part, wtile[n % 2].reshape(width, tn))
+        thin = mm_t(part, qb_ref[:, at])
+        if n == 0:
+            dh_ref[...] = main
+            dt_ref[...] = thin
+        else:
+            dh_ref[...] += main
+            dt_ref[...] += thin
+        gbq_ref[:, at] = t_mm(mid_ref[...], part)
+
+    tile_load(0).start()
+    keep.wait()
+    for n in range(per_half):
+        tile_back(n)
+
+    for i in range(2):
+        @pl.when(jnp.logical_not(is_here(i)))
+        def _():
+            push(tgot.at[i], tgot.at[i], h_send.at[i], h_recv.at[i], home[i]).wait_recv()
+            t_push(i).wait_send()
+    owner = owner_ref[...]
+    tdq = jnp.where(owner > 0, tgot[0].astype(f32), jnp.where(owner < 0, tgot[1].astype(f32), 0.0)).astype(bf16)
+    scatter(0, mm_t(tdq, twq_ref[...]), mm_t(tdq, tqb_ref[...]))
+    tgb_ref[...] = t_mm(tmid_ref[...], tdq)
+
+    push(dq_in.at[1 - core], dq_ref.at[1 - core], dq_send, dq_recv, (partner, z)).wait_recv()
+    for n in range(per_half, 2 * per_half):
+        tile_back(n)
+    dt_low = dt_ref[...].astype(bf16)
+    gaq_ref[...] = t_mm(dt_low, h_ref[...])
 
     offset = 0
     spans = []
-    for part, sizes in ((img_a, fans), (img_b, cols)):
+    for part, sizes in (([gaq_ref] + img_a, fans), ([gbq_ref] + img_b, cols)):
         for index in range(4):
             count = sizes[index + 1] // n_z
             for t in range(n_z):
@@ -867,6 +964,60 @@
             offset += count
     ring.start(lambda to: zmsg.at[to], zgot, z_send, z_recv)
     zgot[z] = zmsg[z]
+
+    isums[...] = jnp.zeros_like(isums)
+    quarter = grad_ref.shape[1]
+    dh_ref[...] += mm(dt_low, qa_ref[...])
+    for i in range(2):
+        def last(r, _):
+            sl = pl.ds(pl.multiple_of(i * quarter + r * ROWS, ROWS), ROWS)
+            dh = dh_ref[sl, :]
+            xh, inverse = norm_rows(x_ref[sl, :].astype(f32))
+            dz = dh * (1.0 + imod_ref[1:2, :])
+            dx = dx1_ref[sl, :] + inverse * (
+                dz - jnp.mean(dz, axis=-1, keepdims=True) - xh * jnp.mean(dz * xh, axis=-1, keepdims=True))
+            grad_ref[i, pl.ds(pl.multiple_of(r * ROWS, ROWS), ROWS), :] = dx.astype(bf16)
+            fold = lambda v: sum(v[8 * j:8 * j + 8, :] for j in range(ROWS // 8))
+            isums[0:8, :] += fold(dh)
+            isums[8:16, :] += fold(dh * xh)
+            return 0
+
+        lax.fori_loop(0, quarter // ROWS, last, 0)
+
+    pick = rows_of(tmodr_ref, own_ref)
+    tdh, tdt = collect(0)
+    spread(dt_ag, tdt)
+    tdh = tdh + mm(tdt, tqa_ref[...])
+    hat, inverse = norm_rows(tx_ref[...].astype(f32))
+    dz = tdh * (1.0 + pick(1))
+    tgrad_out[...] = tdx1_ref[...] + inverse * (
+        dz - jnp.mean(dz, axis=-1, keepdims=True) - hat * jnp.mean(dz * hat, axis=-1, keepdims=True))
+
+    def total_of(v):
+        return jnp.sum(v, axis=0, keepdims=True)
+
+    rows_img = [total_of(isums[0:8, :]), total_of(isums[8:16, :])]
+    rows_img += [total_of(isum_ref[8 * p:8 * p + 8, :]) for p in range(3)] + [total_of(igate_ref[...])]
+    rows_txt = []
+    for s in range(2):
+        chosen = own_ref[...] == (1.0 if s == 0 else -1.0)
+        rows_txt.append([total_of(jnp.where(chosen, tdh, 0.0)), total_of(jnp.where(chosen, tdh * hat, 0.0))]
+                        + [tsum_ref[2 * p + s:2 * p + s + 1, :] for p in range(4)])
+    dmod_ref[...] = jnp.zeros_like(dmod_ref)
+    chunk = dmod_ref.shape[-1]
+    per_row = width // chunk
+    per_block = 6 * per_row // n_z
+    for r, parts in enumerate([rows_img] + rows_txt):
+        for q in range(6 * per_row):
+            dmod_ref[q // per_block, r, q % per_block:q % per_block + 1, :] = (
+                parts[q // per_row][:, q % per_row * chunk:(q % per_row + 1) * chunk])
+
+    def dmod_copy(index, peer):
+        return push(dmod_ref.at[peer[1]], dgot.at[core * n_z + z], d_send.at[index], d_recv.at[core * n_z + z], peer)
+
+    for index, peer in enumerate(column):
+        dmod_copy(index, peer).start()
+    dgot[core * n_z + z] = dmod_ref[z]
 
     for index, peer in enumerate(column):
         place = peer[0] % 2 * n_z + peer[1]
@@ -879,7 +1030,6 @@
         for t in range(1, n_z):
             total = total + dgot[core * n_z + t, 1 + slot]
         rows.append(total)
-    chunk = dmod_ref.shape[-1]
     own_dm[...] = jnp.zeros_like(own_dm)
     for r, total in enumerate(rows):
         for j in range(own_dm.shape[1] // chunk):
@@ -895,6 +1045,10 @@
     row = lax.broadcasted_iota(jnp.int32, rank_img.shape, 0)
     rank_part = jnp.where(row < 2, rank_img, rank_txt)
 
+    spread_end(dt_ag)
+    tga = t_mm(gathered(dt_ag, 0, thick), own_lanes(th_ref, cols[2] // n_z))
+    txt_a = [tga[:hidden_rank]] + [ref[...] for ref in txt_a]
+    txt_b = [tgb_ref[:hidden_rank, :]] + [ref[...] for ref in txt_b]
     hot2 = hot2_ref[...]
     starts = []
     offset = 0
@@ -917,8 +1071,8 @@
             dense[at_a:at_b, :] = jnp.zeros((at_b - at_a, 128), f32)
             put_b(at_b, gb_mod[stream].astype(bf16), hot2)
         elif stream == 1:
-            put_a(at_a, txt_a[index - 1][...].astype(bf16), hot2)
-            put_b(at_b, txt_b[index - 1][...].astype(bf16), hot2)
+            put_a(at_a, txt_a[index - 1].astype(bf16), hot2)
+            put_b(at_b, txt_b[index - 1].astype(bf16), hot2)
 
     ring.wait(zgot, z_send, z_recv)
     hot4 = hot4_ref[...]
@@ -927,11 +1081,6 @@
             for at, put, (begin, count) in ((at_a, put_a, spans[index - 1]), (at_b, put_b, spans[index + 3])):
                 part = zgot[:, :, begin:begin + count].reshape(hot4.shape[0], count)
                 put(at, part, hot4)
-
-    home = [(base + z // 2, 2 * core + i) for i in range(2)]
-
-    def is_here(i):
-        return (z // 2 == core) & (2 * core + i == z)
 
     for i in range(2):
         @pl.when(is_here(i))
@@ -1045,6 +1194,7 @@
         count = mod_a[stream].shape[0]
         shard_out[:count, :] += own * mod_a[stream]
 
+    swap.wait_send()
     ring.drain(lambda to: zmsg.at[to], zgot, z_send, z_recv)
     ring.drain(lambda to: zsum, zall, q_send, q_recv)
     for index, peer in enumerate(column):
@@ -1071,35 +1221,47 @@
             push(grad_ref.at[i], grad_out.at[z % 2], g_send.at[i], g_recv.at[z % 2], home[i]).wait_send()
 
 
-def tail(grad, img_a, img_b, txt_a, txt_b, hot4, hot2, dmod, wmod, bmod, tmod, cond, smask, n_f, n_z, fans, cols, cid):
+def tail(dq, tdq, wq, smalls, img_a, img_b, txt_a, txt_b, hot4, hot2, wmod, bmod, tmod, cond, smask, n_f, n_z, fans, cols, cid, tn=768):
     f32, bf16 = jnp.float32, jnp.bfloat16
     vmem, dma = pltpu.VMEM, pltpu.SemaphoreType.DMA
     shape = jax.ShapeDtypeStruct
-    args = (grad, *img_a, *img_b, *txt_a, *txt_b, hot4, hot2, dmod, wmod, bmod, tmod, cond, smask)
+    args = (dq, tdq, wq, *smalls, *img_a, *img_b, *txt_a, *txt_b, hot4, hot2, wmod, bmod, tmod, cond, smask)
     lanes = (sum(fans[1:]) + sum(cols[1:])) // n_z
     rows = 2 * (sum(fans) + sum(cols)) // n_z
     blk = rows // n_f
     chips = n_f // 2
     cut = cols[0] // n_z
     rank = hot2.shape[0]
-    inside = pl.BlockSpec(memory_space=vmem)
+    _, img_rows, half = dq.shape
+    _, k_local, _ = wq.shape
+    width = cols[2]
+    tx = smalls[9]
+    thick = smalls[18].shape[0]
+    pad = tx.shape[0]
+    wide = width + thick
+    inside, outside = pl.BlockSpec(memory_space=vmem), pl.BlockSpec(memory_space=pl.ANY)
     return pl.pallas_call(
         functools.partial(tail_kernel, n_f, n_z, tuple(fans), tuple(cols)),
-        out_shape=[shape(grad.shape, bf16), shape((n_f, 8, 256), f32), shape((8, rank), f32), shape((blk, 128), f32)],
-        in_specs=[pl.BlockSpec(memory_space=pl.ANY)] + [inside] * (len(args) - 1),
-        out_specs=[pl.BlockSpec(memory_space=pl.ANY)] + [inside] * 3,
+        out_shape=[shape((2, img_rows // 2, width), bf16), shape((pad, width), f32), shape((n_f, 8, 256), f32), shape((8, rank), f32),
+                   shape((blk, 128), f32)],
+        in_specs=[outside] * 3 + [inside] * (len(args) - 3),
+        out_specs=[outside] + [inside] * 4,
         scratch_shapes=[
+            vmem((2, img_rows, half), bf16), vmem((2, n_f, k_local, tn), bf16), vmem((img_rows, width), f32), vmem((img_rows, RANK), f32),
+            vmem((2, img_rows // 2, width), bf16), vmem((RANK, fans[1]), f32), vmem((RANK, cols[1]), f32), vmem(tdq.shape, bf16),
+            vmem((n_z, pad, wide), f32), vmem((1, pad, wide), f32), vmem((1, n_z, pad, wide), bf16), vmem((1, n_z, pad, wide), bf16),
+            vmem((n_z, pad, thick), bf16), vmem((thick, cols[1] // n_z), f32), vmem((n_z, 3, 8, width // n_z), f32), vmem((16, width), f32),
             vmem((n_z, RANK, lanes), bf16), vmem((n_z, RANK, lanes), bf16), vmem((rows, 128), f32),
             vmem((chips, blk, 128), bf16), vmem((chips, blk, 128), bf16),
-            vmem((2, 4, blk // 2, 128), bf16), vmem((2, 4, blk // 2, 128), bf16),
-            vmem((2 * n_z,) + dmod.shape[1:], f32), vmem((8, cut), f32), vmem((n_f, 8, cut), f32),
+            vmem((2, 3, blk // 2, 128), bf16), vmem((2, 3, blk // 2, 128), bf16),
+            vmem((2 * n_z, 3, 8, width // n_z), f32), vmem((8, cut), f32), vmem((n_f, 8, cut), f32),
             vmem((n_f, 8, 256), f32), vmem((n_f, 8, 256), f32), vmem((n_f + 1, 8, 256), f32),
             vmem((n_z, n_f + 1, 8, 256), f32), vmem((n_f, 8, 128), f32),
-            dma((2,)), dma((2,)), dma((n_z,)), dma((n_z,)), dma((chips,)), dma((chips,)), dma((2, 4)), dma((2, 4)),
+            dma((2,)), dma((2,)), dma((n_z,)), dma((n_z,)), dma((chips,)), dma((chips,)), dma((2, 3)), dma((2, 3)),
             dma((2 * n_z,)), dma((2 * n_z,)), dma((n_f,)), dma((n_f,)), dma((n_f,)), dma((n_f,)), dma((n_z,)), dma((n_z,)),
-            dma((n_f,)), dma((n_f,)),
+            dma((n_f,)), dma((n_f,)), dma, dma, dma, dma((2,)), dma((2,)), dma((2,)), dma((1, n_z)), dma((1, n_z)), dma((n_z,)), dma((n_z,)),
         ],
-        compiler_params=pltpu.CompilerParams(collective_id=cid, has_side_effects=True, vmem_limit_bytes=56 * 1024 * 1024),
+        compiler_params=pltpu.CompilerParams(collective_id=cid, has_side_effects=True, vmem_limit_bytes=60 * 1024 * 1024),
         name="gradient_exchange",
     )(*args)
 
@@ -1111,16 +1273,16 @@
     it = iter(refs)
     take = lambda count: [next(it) for _ in range(count)]
     ins = take(FULL + PART + 1)
-    (x_ref, g_ref, picks_ref, hot2_ref, cblk_ref, clane_ref, c8_ref, smask_ref, wmod_ref, xt_ref, own_ref, tmask_ref) = take(12)
+    (x_ref, g_ref, picks_ref, hot2_ref, cblk_ref, clane_ref, c8_ref, smask_ref, wmod_ref, xt_ref, gt_ref, own_ref, tmask_ref) = take(13)
     outs = take(FULL + PART)
     x_out, g_out, imod_out, tmod_out = take(4)
     img_a, img_b, txt_a, txt_b = take(4), take(4), take(4), take(4)
-    moda_out, modb_out, midm_out, cond_out = take(4)
+    moda_out, modb_out, midm_out, cond_out, dm_out = take(5)
     h_out, mid_out, heads_out, th_out, tmid_out, theads_out = take(6)
     (row_ref, fl_ref, img_msg, img_got, txt_msg, txt_got, cgot, mpart, mgot, own_mod, mod_got, wtile, wtxt, stage, tq_ref) = take(15)
     (z_send, z_recv, xy_send, xy_recv, core_send, core_recv, own_sem, x_send, x_recv, g_send, g_recv, c_send, c_recv, l_send,
      l_recv, m_send, m_recv, i_send, i_recv, t_send, t_recv, d_send, d_recv, a_send, a_recv, w_sem, tw_sem, h_send, h_recv,
-     h_sem, q_send, q_recv) = take(32)
+     h_sem, q_send, q_recv, dm_send, dm_recv) = take(34)
     f32, bf16 = jnp.float32, jnp.bfloat16
     f, z, core, base, column = column_peers(n_z)
     chip = f // 2
@@ -1517,6 +1679,8 @@
     hat, _inv = norm_rows(xt_ref[...].astype(f32))
     th_out[z] = (hat * (1.0 + pick(1)) + pick(0)).astype(bf16)
     ring.start(lambda to: th_out.at[z], th_out, a_send, a_recv)
+    dm_out[z] = (pick(5) * gt_ref[...].astype(f32)).astype(bf16)
+    ring.start(lambda to: dm_out.at[z], dm_out, dm_send, dm_recv)
     tokens_wait(x_ref, x_out, x_send, x_recv)
     quarter = x_ref.shape[1]
     for i in range(2):
@@ -1619,6 +1783,8 @@
     around_wait(cond_out, l_send, l_recv)
     ring.drain(lambda to: txt_msg, txt_got, t_send, t_recv)
     ring.drain(lambda to: th_out.at[z], th_out, a_send, a_recv)
+    ring.wait(dm_out, dm_send, dm_recv)
+    ring.drain(lambda to: dm_out.at[z], dm_out, dm_send, dm_recv)
     for index, peer in enumerate(column):
         mod_push(index, peer).wait_send()
     for s in range(2):
@@ -1639,7 +1805,7 @@
             push(tq_ref, theads_out.at[z % 2], q_send.at[s], q_recv.at[z % 2], there[s]).wait_send()
 
 
-def front(full, part, adapter_rows, x, g, picks, hot2, cond, wmod, x_txt, own, tmask, smask, n_f, n_z, fans, cols, cid):
+def front(full, part, adapter_rows, x, g, picks, hot2, cond, wmod, x_txt, g_txt, own, tmask, smask, n_f, n_z, fans, cols, cid):
     f32, bf16 = jnp.float32, jnp.bfloat16
     vmem, dma = pltpu.VMEM, pltpu.SemaphoreType.DMA
     shape = jax.ShapeDtypeStruct
@@ -1650,7 +1816,7 @@
     cond8 = jnp.concatenate([cond, cond, jnp.zeros((4, width), f32)])
     lane = jnp.pad(lax.dynamic_slice_in_dim(cond, z * (width // n_z), width // n_z, 1), ((0, 6), (0, 0)))
     chosen = (picks[:, None] == jnp.arange(NAD)[None, :]).astype(f32).reshape(-1, 1)
-    smalls = (jnp.broadcast_to(chosen, (slots * NAD, 128)), hot2, blocks, lane, cond8, smask, wmod, x_txt, own, tmask)
+    smalls = (jnp.broadcast_to(chosen, (slots * NAD, 128)), hot2, blocks, lane, cond8, smask, wmod, x_txt, g_txt, own, tmask)
     args = (*full, *part, adapter_rows, x, g, *smalls)
     any_spec, in_vmem = pl.BlockSpec(memory_space=pl.ANY), pl.BlockSpec(memory_space=vmem)
     rows = 2 * (sum(fans) + sum(cols)) // n_z
@@ -1672,7 +1838,7 @@
     outs += [shape(x.shape, bf16), shape(g.shape, bf16), shape((8, width), f32), shape((16, width), f32)]
     outs += [shape((RANK, n), bf16) for n in fans[1:]] + [shape((RANK, n), bf16) for n in cols[1:]]
     outs += [shape((thick, n), bf16) for n in own_a] + [shape((thick, n), bf16) for n in own_b]
-    outs += [shape((2, rank2, width), bf16), shape((2, rank2, cut), bf16), shape((2, 8, rank2), f32), shape((n_f, 8, share), f32)]
+    outs += [shape((2, rank2, width), bf16), shape((2, rank2, cut), bf16), shape((2, 8, rank2), f32), shape((n_f, 8, share), f32), shape((n_z, pad, width), bf16)]
     outs += [shape((img_rows, width), bf16), shape((img_rows, RANK), bf16), shape((2, img_rows, cols[1] // 2), bf16),
              shape((n_z, pad, width), bf16), shape((n_z * pad, thick), bf16), shape((2, n_z * pad, qkv_part), bf16)]
     specs = [any_spec] * in_hbm + [in_vmem, any_spec] + [in_vmem] * (len(outs) - in_hbm - 2)
@@ -1693,7 +1859,7 @@
             dma((total, n_z, 2, chips)), dma((total, n_z, 2, chips)), dma((total,)),
             dma((2,)), dma((2,)), dma((2,)), dma((2,)), dma((n_f,)), dma((n_f,)), dma((n_f,)), dma((n_f,)), dma((n_f,)), dma((n_f,)),
             dma((2, 2)), dma((n_z,)), dma((n_z,)), dma((n_z,)), dma((2 * n_z,)), dma((2 * n_z,)), dma((n_z,)), dma((n_z,)),
-            dma((2,)), dma, dma, dma, dma, dma((2,)), dma((2,)),
+            dma((2,)), dma, dma, dma, dma, dma((2,)), dma((2,)), dma((n_z,)), dma((n_z,)),
         ],
         compiler_params=pltpu.CompilerParams(collective_id=cid, has_side_effects=True, vmem_limit_bytes=58 * 1024 * 1024),
         name="front",
@@ -1853,7 +2019,7 @@
     out_t = jnp.swapaxes(out_weight, 1, 2)
     fc2_t = jnp.swapaxes(fc2_weight, 1, 2)
     local = [qkv_weight, out_t, fc1_weight, fc2_t]
-    adapter_rows = adapters.astype(BF16).reshape(-1, 128)
+    adapter_rows = lax.optimization_barrier(adapters.reshape(-1, 128)).astype(BF16)
     txt_pad = (txt_local + 15) // 16 * 16
 
     def padded(values):
@@ -1944,7 +2110,7 @@
         made = front(
             [w[0] for w in local], [w[1] for w in local], adapter_rows, image_tokens, image_cot,
             adapter_index, own_hot.T.astype(BF16), cond_act.astype(F32), mod_weight, x_txt_low,
-            sign(owner_local), lanes_pad(txt_mask), slot_mask, n_f, n_z, fans, cols, 1,
+            g_txt_low, sign(owner_local), lanes_pad(txt_mask), slot_mask, n_f, n_z, fans, cols, 1,
         )
         made = iter(made)
         take = lambda count: [next(made) for _ in range(count)]
@@ -1954,11 +2120,10 @@
         img_rows_mod, txt_mod = take(2)
         img_pairs = [None] + list(zip(take(4), take(4)))
         thick_pairs = [None] + list(zip(take(4), take(4)))
-        mod_a, mod_b, tmod, cond_own = take(4)
+        mod_a, mod_b, tmod, cond_own, txt_dm = take(5)
         img_in, img_qkv_mid, img_heads, txt_in, txt_qkv_mid, txt_heads = take(6)
         img_heads = img_heads.reshape(img_n, -1)
         txt_in = txt_in.reshape(-1, width)
-        txt_qkv_mid = txt_qkv_mid[:, :rank_cols]
         txt_pairs = [None, tuple(part[:rank_cols] for part in thick_pairs[1])]
         img_mod = img_rows_mod[:6].reshape(1, -1)
         txt_mods = txt_mod.reshape(slots, 8, width)[:, :6].reshape(slots, -1)
@@ -2075,6 +2240,7 @@
         img_heads = to_heads(img_qkv)
         txt_heads = jnp.stack(to_chip([txt_qkv, txt_qkv]))
         img_in = heads_in[0]
+        txt_dm = jnp.stack(z_gather((stretch(1, 5) * g_txt_low.astype(F32)).astype(BF16)))
 
     inputs = [x_img.astype(F32), x_txt]
     norm_one = [layer_norm(values) for values in inputs]
@@ -2095,18 +2261,22 @@
         return jnp.where(owner_group[:, 0:1] > 0, got[0], jnp.where(owner_group[:, 1:2] > 0, got[1], 0))
 
     attended = to_tokens(o_img)
-    (txt_result, txt_grad_after, do_txt, txt_sums, *txt_sides) = text_mid(
-        o_txt, x_txt_low, g_txt_low, txt_mod, sign(owner_group), sign(owner_local), lanes_pad(txt_mask),
-        lanes_pad(txt_mask_local), txt_w[1], txt_w[2], txt_w[3], thick_pairs[2], thick_pairs[3], thick_pairs[4],
+    (img_branch, img_after, img_mlp, img_pre, img_result, *img_mids, img_gate, txt_mlp, txt_att, txt_after, txt_branch) = both_fwd(
+        attended, x_img, g_img, img_rows_mod, img_w[1], img_pairs[2], img_pairs[3], img_w[2], img_pairs[4], img_w[3],
+        o_txt, x_txt_low, txt_mod, sign(owner_group), sign(owner_local), lanes_pad(txt_mask_local), txt_w[1], thick_pairs[2],
         n_z, 2,
     )
+    made = both_back(
+        g_img, img_after, img_branch, img_mlp, attended, img_rows_mod, img_pre, img_w[3], img_pairs[4], img_w[2], img_pairs[3],
+        img_w[1], img_pairs[2], img_mids, g_txt_low, txt_after, txt_branch, txt_mod, sign(owner_local), lanes_pad(txt_mask),
+        lanes_pad(txt_mask_local), txt_mlp, txt_att, txt_dm, txt_w[1], txt_w[2], txt_w[3], thick_pairs[2], thick_pairs[3],
+        thick_pairs[4], n_z, 4,
+    )
+    img_grad_after, img_grad_att, img_sums, *sides = made[:9]
+    txt_result, txt_grad_after, do_txt, txt_sums, *txt_sides = made[9:]
     txt_sides = [part[:rank_cols] for part in txt_sides]
+    txt_sum_rows = txt_sums
     txt_sums = txt_sums.reshape(4, slots, width)
-
-    (img_branch, img_after, img_mlp, img_pre, img_result, *img_mids, img_gate) = block_fwd(
-        attended, x_img, g_img, img_rows_mod, img_w[1], img_pairs[2], img_pairs[3], img_w[2],
-        img_pairs[4], img_w[3],
-    )
     image_out = unshard(img_result)
 
     grads = [[None] * 5 for stream in range(2)]
@@ -2119,10 +2289,6 @@
         main = matmul(grad, weight) if flipped else inner_right(grad, weight)
         return middle, main + matmul(middle, pair[0])
 
-    (img_grad_after, img_grad_att, img_sums, *sides) = block_back(
-        g_img, img_after, img_branch, img_mlp, attended, img_rows_mod, img_pre, img_w[3],
-        img_pairs[4], img_w[2], img_pairs[3], img_w[1], img_pairs[2], img_mids,
-    )
     grads[0][4] = (sides[0], sides[3])
     grads[0][3] = (sides[2], sides[1])
     grads[0][2] = (sides[4], sides[5])
@@ -2132,6 +2298,7 @@
     grads[1][2] = (txt_sides[0], txt_sides[1])
     grads[1][3] = (txt_sides[2], txt_sides[3])
     grads[1][4] = (txt_sides[4], txt_sides[5])
+    img_sum_rows = img_sums
     img_sums = jnp.sum(jnp.concatenate([img_sums, img_gate]).reshape(4, 8, width), axis=1)
     for place in range(4):
         mod_parts[0][2 + place] = img_sums[place : place + 1]
@@ -2139,6 +2306,26 @@
 
     do_img = to_heads(img_grad_att)
     d_img, d_txt = attend_back(img_heads, txt_heads, bias, do_img, do_txt, lse, HD)
+    if n_f == 8:
+        sides_of = lambda stream, side: [grads[stream][index][side] for index in range(2, 5)]
+        smalls = (
+            x_img, img_grad_after, img_in, img_rows_mod, img_qkv_mid, *img_pairs[1], img_sum_rows, img_gate,
+            x_txt_low, txt_grad_after, txt_in.reshape(n_z, txt_pad, width), txt_mod, sign(owner_group), sign(owner_local),
+            lanes_pad(txt_mask_local), txt_qkv_mid, txt_w[0], *thick_pairs[1], txt_sum_rows,
+        )
+        image_low, txt_grad, cond_slices, mod_rank, shard = tail(
+            d_img.reshape(2, img_half, -1), d_txt, img_w[0].reshape(n_f, k_local, -1), smalls,
+            sides_of(0, 0), sides_of(0, 1), sides_of(1, 0), sides_of(1, 1),
+            one_hot.T.astype(BF16), own_hot.T.astype(BF16), mod_weight, mod_b, tmod, cond_own, slot_mask,
+            n_f, n_z, fans, cols, 3,
+        )
+        image_grad = image_low.astype(F32)
+        cond_rows = jnp.swapaxes(cond_slices[:, :slots, :k_local], 0, 1).reshape(slots, width)
+        for s in range(2):
+            cond_rows = cond_rows + matmul(mod_rank[2 * s : 2 * s + 2].astype(BF16), mod_a[s])
+        cond_grad = jax.vjp(jax.nn.silu, conditioning)[1](cond_rows)[0]
+        adapter_grad = shard.reshape(1, -1)
+        return (image_out, txt_result[:txt_local], image_grad, txt_grad[:txt_local], cond_grad, adapter_grad)
     img_grad_qkv = to_tokens(d_img)
     txt_grad_qkv = txt_home(d_txt)
 
@@ -2163,27 +2350,6 @@
         mod_parts[s][1] = collapse(s, grad_norm[s] * norm_one[s][0])
     img_dmod = jnp.concatenate(mod_parts[0], axis=1)
     txt_dmod = jnp.concatenate(mod_parts[1], axis=1)
-    if n_f == 8:
-        cut = width // n_z
-        dmod = jnp.concatenate([img_dmod, txt_dmod]).reshape(1 + slots, n_z, -1, cut)
-        dmod = jnp.pad(jnp.swapaxes(dmod, 0, 1), ((0, 0), (0, 0), (0, 8 - dmod.shape[2]), (0, 0)))
-        sides_of = lambda stream, side: [grads[stream][index][side] for index in range(1, 5)]
-        image_low, cond_slices, mod_rank, shard = tail(
-            grad_inputs[0].astype(BF16).reshape(2, quarter, width),
-            sides_of(0, 0), sides_of(0, 1), sides_of(1, 0), sides_of(1, 1),
-            one_hot.T.astype(BF16), own_hot.T.astype(BF16), dmod, mod_weight, mod_b, tmod, cond_own,
-            slot_mask,
-            n_f, n_z, fans, cols, 3,
-        )
-        image_grad = image_low.astype(F32)
-        cond_rows = jnp.swapaxes(cond_slices[:, :slots, :k_local], 0, 1).reshape(slots, width)
-        for s in range(2):
-            cond_rows = cond_rows + matmul(mod_rank[2 * s : 2 * s + 2].astype(BF16), mod_a[s])
-        cond_grad = jax.vjp(jax.nn.silu, conditioning)[1](cond_rows)[0]
-        adapter_grad = shard.reshape(1, -1)
-        return (
-            image_out, txt_result[:txt_local], image_grad, grad_inputs[1][:txt_local], cond_grad, adapter_grad
-        )
     image_grad = unshard(grad_inputs[0].astype(BF16)).astype(F32)
 
     img_dmod = (img_dmod + swap_core(img_dmod)).astype(BF16)

time: 924 us -> 799 us (0.86)
  other arithmetic: 49.9 us -> 17.1 us
  Pallas kernels: 763 us -> 732 us
  matrix products: 30.2 us -> 0.86 us
  waiting for transfers between devices: 27.9 us -> 0.46 us
    pallas_call x3 -> x2, Pallas kernels: 218 us -> 144 us  [the longest x1 86.1 us: both_back(): pl.pallas_call(functools.partial(both_back_kernel, tiles, n_z, turns), gr...]
    pallas_call x1, Pallas kernels: 77.4 us -> 121 us  [tail(): pl.pallas_call(functools.partial(tail_kernel, n_f, n_z, tuple(fans), tupl...]
    dot_general x11 -> x0, matrix products: 26 us -> none  [the longest x4 19.6 us: inner_right(): lax.dot_general(left, right, (((left.ndim - 1,), (right.ndim - 1,)), ((),...]
    convert_element_type x4 -> x1, other arithmetic: 18.7 us -> 0.88 us  [shards(): lax.optimization_barrier(adapters.reshape(-1, 128)).astype(BF16)]
    ppermute x4 -> x2, waiting for transfers between devices: 14 us -> 0.01 us  [from_chip(): got.append(lax.ppermute(mine, BOTH, [(b, a) for a, b in round_pairs(r)]))]
    ppermute x6 -> x0, waiting for transfers between devices: 12.2 us -> none  [z_swap(): return lax.ppermute(values, 'tp', [(i, i ^ step) for i in range(n_z)])]
  transfers between devices with their start and end apart: 15 -> 6, of which waited for: 6 -> 1; matrix products, arithmetic and copies ran while one was open for 6% -> 4% of each run, Pallas kernels for 20% -> 23%
where the time goes in v6:
time: 799 us; the launch traced here: 787 us
  Pallas kernels  732 us (92%)
  local copies, waits for them, and re-layouts  28.2 us (4%)
  other arithmetic  17.1 us (2%)
    pallas_call x1, Pallas kernels, front(): pl.pallas_call(functools.partial(front_kernel, n_f, n_z, tuple(fans), tup...  368 us
    pallas_call x1, Pallas kernels, tail(): pl.pallas_call(functools.partial(tail_kernel, n_f, n_z, tuple(fans), tupl...  121 us
    pallas_call x1, Pallas kernels, both_back(): pl.pallas_call(functools.partial(both_back_kernel, tiles, n_z, turns), gr...  86.1 us
    pallas_call x1, Pallas kernels, attend_back(): pl.pallas_call(functools.partial(attend_back_kernel, hd, bq), grid=(pairs...  61.6 us
    pallas_call x1, Pallas kernels, both_fwd(): pl.pallas_call(functools.partial(both_fwd_kernel, tiles, n_z, turns), gri...  57.8 us
    pallas_call x1, Pallas kernels, attend(): pl.pallas_call(functools.partial(attend_kernel, hd, bq), grid=(pairs,), i...  37.6 us
  transfers between devices with their start and end apart: 6, of which 1 were waited for; matrix products, arithmetic and copies ran while one was open for 4% of the time, Pallas kernels for 23%

profile of v6, /device:TPU:11, one launch (start us, length us, event | category | flops | bytes accessed | tf_op | source)
XLA Modules:
  0.0 787.4 jit_solution(14029073964656220852)
XLA Ops:
  0.6 0.7 collective-permute-start.5
  1.5 0.7 compare_convert_fusion.4
  2.3 2.2 slice_bitcast_fusion.4
  4.5 0.7 slice_bitcast_fusion.6
  5.3 0.9 convert_element_type.75.refs_8_
  6.4 0.6 pad.30.refs_13_
  7.0 0.6 pad.31.refs_14_
  7.7 0.7 maximum_maximum_fusion.refs_15_
  8.5 0.6 select_maximum_fusion.refs_16_.refs_42_
  9.1 1.6 pad.33.refs_18_.xt_ref.refs_12_
  10.7 1.6 pad.34.refs_19_.gt_ref
  12.6 0.7 slice_subtract_fusion.1.refs_20_.own_ref.refs_17_
  13.3 1.4 slice_bitcast_fusion
  14.9 0.7 convert_convert_fusion.1.refs_12_.refs_37_
  16.2 0.7 pad.35.refs_21_.mask_ref
  17.0 0.7 broadcast_in_dim.42.refs_11_
  17.6 368.0 %front.1 = (bf16[8,192,4608]{2,1,0:T(8,128)(2,1)}, bf16[8,192,1536]{2,1,0:T(8,128)(2,1)}, bf16[8,192,6144]{2,1,0:T(8,128)(2,1)}, bf16[8,192,6144]{2,1,0:T(8,128)...) custom-call(bf16[192,1152]{1,0:T(8,128)(2,1)} %get-tuple-element.183, ...), custom_call_target="tpu_custom_call" | custom-call | tf_op jit(solution)/shard_map/front/pallas_call | solution.py:1847
  385.7 1.2 copy-done
  386.8 37.6 %attend.1 = (bf16[1024,768]{1,0:T(8,128)(2,1)S(1)}, bf16[2,192,384]{2,1,0:T(8,128)(2,1)S(1)}, f32[6,2,1216]{2,1,0:T(2,128)S(1)}) custom-call(bf16[1024,2304]{1,0:T(8,128)(2,1)} %bitcast.61, bf16[2,192,1152]{2,1,0:T(8,128)(2,1)S(1)} %copy-done, f32[192,1]{1,0:T(8,128)S(1)} %fusion.9.bias_ref), custom_call_target="tpu_custom_call" | custom-call | tf_op jit(solution)/shard_map/attend/pallas_call | solution.py:288
  424.4 0.7 copy-done.3
  425.7 0.6 pad.36.lmask_ref.refs_18_
  426.4 0.7 slice_subtract_fusion.owner_ref.refs_16_
  427.7 1.3 pad_maximum_fusion.o_ref
  429.0 57.8 %block_forward.1 = (bf16[512,1536]{1,0:T(8,128)(2,1)}, f32[512,1536]{1,0:T(8,128)}, bf16[512,1536]{1,0:T(8,128)(2,1)}, f32[512,6144]{1,0:T(8,128)}, bf16[512,153...) custom-call(bf16[512,1536]{1,0:T(8,128)(2,1)} %pad_maximum_fusion.o_, ...), custom_call_target="tpu_custom_call" | custom-call | tf_op jit(solution)/shard_map/block_forward/pallas_call | solution.py:782
  486.8 86.1 %block_backward.1 = (f32[512,1536]{1,0:T(8,128)}, bf16[512,1536]{1,0:T(8,128)(2,1)}, f32[24,1536]{1,0:T(8,128)}, f32[16,6144]{1,0:T(8,128)}, f32[16,6144]{1,0:T(...) custom-call(bf16[512,1536]{1,0:T(8,128)(2,1)} %bitcast.66, ...), custom_call_target="tpu_custom_call" | custom-call | tf_op jit(solution)/shard_map/block_backward/pallas_call | solution.py:823
  572.9 1.6 broadcast_select_fusion.3
  574.4 1.8 collective-permute-start.4
  576.4 0.7 convert_convert_fusion.refs_36_
  577.1 1.0 broadcast_select_fusion.9
  578.0 4.9 collective-permute-start.2
  583.0 0.7 slice.119
  583.7 1.4 slice.122.refs_30_
  585.1 1.4 slice.123.refs_31_
  586.5 1.6 slice.124.refs_32_
  588.1 1.4 slice.125.refs_33_
  589.5 1.6 slice.126.refs_34_
  591.1 1.4 slice.127.refs_35_
  592.5 1.3 broadcast_select_fusion.2
  594.0 1.0 copy-done.1
  595.1 61.6 %attend_back.1 = (bf16[1024,2304]{1,0:T(8,128)(2,1)}, bf16[2,192,1152]{2,1,0:T(8,128)(2,1)S(1)}) custom-call(bf16[1024,2304]{1,0:T(8,128)(2,1)} %bitcast.62, bf16[2,192,1152]{2,1,0:T(8,128)(2,1)S(1)} %copy-done.1, f32[192,1]{1,0:T(8,128)S(1)} %fusion.9.bias_ref, bf16[1024,768]{1,0:T(8,128)(2,1)S(1)} %pad_maximum_fusion.2.doi_ref, ...), custom_call_target="tpu_custom_call" | custom-call | tf_op jit(solution)/shard_map/attend_back/pallas_call | solution.py:363
  656.7 0.9 copy-done.2
  657.6 120.7 %gradient_exchange.1 = (bf16[2,256,1536]{2,1,0:T(8,128)(2,1)}, f32[48,1536]{1,0:T(8,128)}, f32[8,8,256]{2,1,0:T(8,128)}, f32[8,32]{1,0:T(8,128)}, f32[2208,128]{1,0:T(8,128)}) custom-call(bf16[2,512,2304]{2,1,0:T(8,128)(2,1)} %bitcast.69, bf16[2,192,1152]{2,1,0:T(8,128)(2,1)} %copy-done.2, bf16[8,192,4608]{2,1,0:T(8,128)(2,1)} %get-tuple-element.132.refs_2_, ...), custom_call_target="tpu_custom_call" | custom-call | tf_op jit(solution)/shard_map/gradient_exchange/pallas_call | solution.py:1243
  778.3 3.5 convert_element_type.90
  781.9 0.7 slice.128
  782.6 0.8 slice_bitcast_fusion.8
  783.7 0.7 fusion.11
  784.5 1.3 pad_maximum_fusion.1
  786.2 1.0 copy.37
  (88 shorter events, 4.2 us)
Async XLA Ops:
  0.6 4.6 copy-start.9
  0.6 14.1 %collective-permute-start.5 = (s32[2]{0:T(128)}, s32[2]{0:T(128)S(1)}, u32[]{:S(2)}, u32[]{:S(2)}) collective-permute-start(s32[2]{0:T(128)} %param.17), channel_id=1, source_target_pairs={{0,4},{4,0},{8,12},{12,8},{16,20},{20,16},{24,28},{28,24},{1,5},{5... | collective-permute-start | bytes 32 | tf_op jit(solution)/shard_map/ppermute | solution.py:1980
  1.4 14.2 %collective-permute-start = (s32[1,2]{1,0:T(1,128)}, s32[1,2]{1,0:T(1,128)S(1)}, u32[]{:S(2)}, u32[]{:S(2)}) collective-permute-start(s32[1,2]{1,0:T(1,128)} %param.16), channel_id=1, source_target_pairs={{0,4},{4,0},{8,12},{12,8},{16,20},{20,16},{24,28},{28,24},{1,5},{5... | collective-permute-start | bytes 32 | tf_op jit(solution)/shard_map/ppermute | solution.py:1980
  2.3 2.2 copy-start.11
  4.5 1.7 copy-start.15
  4.5 7.8 copy-start.17
  4.5 8.8 %copy-start.7 = (bf16[2,1536,192]{1,2,0:T(8,128)(2,1)S(1)}, bf16[2,1536,192]{1,2,0:T(8,128)(2,1)}, u32[]{:S(2)}) copy-start(bf16[2,1536,192]{1,2,0:T(8,128)(2,1)} %param.23) | copy-start | bytes 3538948
  4.5 8.8 %copy-start.8 = (bf16[2,192,1536]{2,1,0:T(8,128)(2,1)S(1)}, bf16[2,192,1536]{2,1,0:T(8,128)(2,1)}, u32[]{:S(2)}) copy-start(bf16[2,192,1536]{2,1,0:T(8,128)(2,1)} %param.22) | copy-start | bytes 3538948
  13.3 1.5 copy-start.18
  385.7 1.2 copy-start
  424.4 0.7 copy-start.3
  425.2 2.4 collective-permute-start.1
  572.9 4.2 copy-start.6
  574.4 18.1 %collective-permute-start.4 = (bf16[512,768]{1,0:T(8,128)(2,1)S(1)}, bf16[512,768]{1,0:T(8,128)(2,1)}, u32[]{:S(2)}, u32[]{:S(2)}) collective-permute-start(bf16[512,768]{1,0:T(8,128)(2,1)S(1)} %broadcast_select_fusion.3), channel_id=1, source_target_pairs={{0,4},{4,0},{8,12},{12,8},{16,20},{20,16},{24,28},{28,24},{1,5},{5... | collective-permute-start | bytes 2359304 | tf_op jit(solution)/shard_map/ppermute | solution.py:1980
  577.1 5.9 copy-start.13
  577.1 15.5 %copy-start.5 = (bf16[512,1536]{1,0:T(8,128)(2,1)S(1)}, bf16[512,1536]{1,0:T(8,128)(2,1)}, u32[]{:S(2)}) copy-start(bf16[512,1536]{1,0:T(8,128)(2,1)} %get-tuple-element.127) | copy-start | bytes 4718596
  578.0 206.3 %collective-permute-start.2 = (bf16[256,1536]{1,0:T(8,128)(2,1)}, bf16[256,1536]{1,0:T(8,128)(2,1)S(1)}, u32[]{:S(2)}, u32[]{:S(2)}) collective-permute-start(bf16[256,1536]{1,0:T(8,128)(2,1)} %get-tuple-element.176), channel_id=1, source_target_pairs={{0,0},{1,1},{4,2},{5,3},{2,4},{3,5},{6,6},{7,7},{8,8},{9,9},{12,10... | collective-permute-start | bytes 2359304 | tf_op jit(solution)/shard_map/ppermute | solution.py:1970
  582.9 201.5 %collective-permute-start.3 = (bf16[256,1536]{1,0:T(8,128)(2,1)S(1)}, bf16[256,1536]{1,0:T(8,128)(2,1)S(1)}, u32[]{:S(2)}, u32[]{:S(2)}) collective-permute-start(bf16[256,1536]{1,0:T(8,128)(2,1)S(1)} %get-tuple-element.177), channel_id=1, source_target_pairs={{1,0},{0,1},{5,2},{4,3},{3,4},{2,5},{7,6},{6,7},{9,8},{8,9},{13,10... | collective-permute-start | bytes 2359304 | tf_op jit(solution)/shard_map/ppermute | solution.py:1970
  593.9 1.2 copy-start.1
  593.9 1.2 copy-start.4
  656.7 0.9 copy-start.2
  778.3 3.6 copy-start.12
  778.3 5.2 copy-start.16
  778.3 5.2 copy-start.14
  784.5 1.7 copy-start.10

commit v7 on v6

--- a/solution.py
+++ b/solution.py
@@ -250,6 +250,18 @@
 def dots(left, right, lc, rc):
     return lax.dot_general(left, right, (((lc,), (rc,)), ((), ())), preferred_element_type=jnp.float32)
 
+def attend_block(q, ki, vi, kt, vt, bias):
+    q = q * jnp.bfloat16(0.125)
+    si = dots(ki, q, 1, 1)
+    st = dots(kt, q, 1, 1) + bias
+    top = jnp.maximum(jnp.max(si, axis=0, keepdims=True), jnp.max(st, axis=0, keepdims=True))
+    ei = jnp.exp(si - top)
+    et = jnp.exp(st - top)
+    total = jnp.sum(ei, axis=0, keepdims=True) + jnp.sum(et, axis=0, keepdims=True)
+    o = dots(vi, ei.astype(jnp.bfloat16), 0, 0) + dots(vt, et.astype(jnp.bfloat16), 0, 0)
+    return (o / total).T.astype(jnp.bfloat16), top + jnp.log(total)
+
+
 def attend_kernel(hd, bq, img_ref, txt_ref, bias_ref, oi_ref, ot_ref, lse_ref):
     img_n, txt_n = img_ref.shape[0], txt_ref.shape[1]
     heads = img_ref.shape[1] // (3 * hd)
@@ -1047,8 +1059,8 @@
 
     spread_end(dt_ag)
     tga = t_mm(gathered(dt_ag, 0, thick), own_lanes(th_ref, cols[2] // n_z))
-    txt_a = [tga[:hidden_rank]] + [ref[...] for ref in txt_a]
-    txt_b = [tgb_ref[:hidden_rank, :]] + [ref[...] for ref in txt_b]
+    txt_a = [tga[:hidden_rank]] + [ref[:hidden_rank, :] for ref in txt_a]
+    txt_b = [tgb_ref[:hidden_rank, :]] + [ref[:hidden_rank, :] for ref in txt_b]
     hot2 = hot2_ref[...]
     starts = []
     offset = 0
@@ -1273,16 +1285,17 @@
     it = iter(refs)
     take = lambda count: [next(it) for _ in range(count)]
     ins = take(FULL + PART + 1)
-    (x_ref, g_ref, picks_ref, hot2_ref, cblk_ref, clane_ref, c8_ref, smask_ref, wmod_ref, xt_ref, gt_ref, own_ref, tmask_ref) = take(13)
+    (x_ref, g_ref, picks_ref, hot2_ref, cblk_ref, clane_ref, c8_ref, smask_ref, wmod_ref, xt_ref, gt_ref, own_ref, tmask_ref, sign_ref) = take(14)
     outs = take(FULL + PART)
     x_out, g_out, imod_out, tmod_out = take(4)
     img_a, img_b, txt_a, txt_b = take(4), take(4), take(4), take(4)
     moda_out, modb_out, midm_out, cond_out, dm_out = take(5)
-    h_out, mid_out, heads_out, th_out, tmid_out, theads_out = take(6)
-    (row_ref, fl_ref, img_msg, img_got, txt_msg, txt_got, cgot, mpart, mgot, own_mod, mod_got, wtile, wtxt, stage, tq_ref) = take(15)
+    ot_out, lse_out, bias_out, hot4_out = take(4)
+    h_out, mid_out, heads_out, th_out, tmid_out, theads_out, att_out = take(7)
+    (row_ref, fl_ref, img_msg, img_got, txt_msg, txt_got, cgot, mpart, mgot, own_mod, mod_got, wtile, wtxt, stage, tq_ref, sign_got, hot_got, img_buf, txt_buf, o_stage) = take(20)
     (z_send, z_recv, xy_send, xy_recv, core_send, core_recv, own_sem, x_send, x_recv, g_send, g_recv, c_send, c_recv, l_send,
      l_recv, m_send, m_recv, i_send, i_recv, t_send, t_recv, d_send, d_recv, a_send, a_recv, w_sem, tw_sem, h_send, h_recv,
-     h_sem, q_send, q_recv, dm_send, dm_recv) = take(34)
+     h_sem, q_send, q_recv, dm_send, dm_recv, s_send, s_recv, b_sem, o_send, o_recv, o_sem) = take(40)
     f32, bf16 = jnp.float32, jnp.bfloat16
     f, z, core, base, column = column_peers(n_z)
     chip = f // 2
@@ -1501,6 +1514,11 @@
     lane_sends = around(lambda to: clane_ref, cond_out, l_send, l_recv)
     mod_sends = around(lambda to: mpart.at[to], mgot, m_send, m_recv)
 
+    sign_push = push(sign_ref, sign_got, s_send.at[0], s_recv.at[0], (partner, z))
+    hot_push = push(hot2_ref, hot_got, s_send.at[1], s_recv.at[1], (partner, z))
+
+    sign_push.start()
+    hot_push.start()
     for copy in cond_sends + lane_sends:
         copy.start()
     launch_own(adapters)
@@ -1526,13 +1544,10 @@
         launch_own(m)
     for k in range(1, n_z):
         arrive(0, k)
-        at_distance(k - 1, lambda zz: forward(0, zz))
     for m in (1, 2, 3):
         arrive(m, 1)
-        at_distance(0, lambda zz: forward(m, zz))
-    at_distance(n_z - 1, lambda zz: forward(0, zz))
-    for m in (FULL + 1, FULL + 2, FULL + 3):
-        forward(m, z)
+    for k in range(n_z):
+        at_distance(k, lambda zz: forward(0, zz))
 
     finish(adapters, z)
     settle(adapters, z)
@@ -1614,9 +1629,13 @@
                 ref[s * RANK:(s + 1) * RANK, at:at + 128] = value
             pick_b(stream, index, s, put)
 
+    for k in (2, 3):
+        for m in (1, 2, 3):
+            arrive(m, k)
     for m in (1, 2, 3):
-        arrive(m, 2)
-        at_distance(1, lambda zz: forward(m, zz))
+        forward(m, z)
+    for m in (FULL + 1, FULL + 2, FULL + 3):
+        forward(m, z)
 
     ring.wait(txt_got, t_send, t_recv)
     for t in range(n_z):
@@ -1695,8 +1714,7 @@
     tokens_start(g_ref, g_out, g_send, g_recv)
 
     for m in (1, 2, 3):
-        arrive(m, 3)
-        at_distance(2, lambda zz: forward(m, zz))
+        at_distance(1, lambda zz: forward(m, zz))
 
     finish(FULL, z)
     settle(FULL, z)
@@ -1754,6 +1772,81 @@
     keep = pltpu.make_async_copy(stage.at[1], heads_out.at[core], h_sem)
     keep.start()
 
+    sign_push.wait_recv()
+    chip_sign = jnp.where(z // 2 == core, sign_ref[...], sign_got[...])
+    chip_sign = jnp.where(z % 2 == 0, chip_sign, -chip_sign)
+    bias_out[...] = jnp.where(chip_sign > 0, 0.0, -1e30)
+    hot_push.wait_recv()
+    hot4_out[:rank2, :] = jnp.where(core == 0, hot2_ref[...].astype(f32), hot_got[...].astype(f32)).astype(bf16)
+    hot4_out[rank2:, :] = jnp.where(core == 0, hot_got[...].astype(f32), hot2_ref[...].astype(f32)).astype(bf16)
+    keep.wait()
+    push(stage.at[0], heads_out.at[1 - core], h_send, h_recv, (partner, z)).wait_recv()
+    for s in range(2):
+        @pl.when(jnp.logical_not(is_here(s)))
+        def _():
+            push(theads_out.at[s], theads_out.at[s], q_send.at[s], q_recv.at[s], there[s]).wait_recv()
+    pairs = heads_out.shape[2] // (6 * HD)
+    per_part = pairs // 2
+
+    def pair_loads(i):
+        lanes = pl.ds(pl.multiple_of(i * (6 * HD), 128), 6 * HD)
+        part = pl.ds(pl.multiple_of(i % per_part * (6 * HD), 128), 6 * HD)
+        return [pltpu.make_async_copy(heads_out.at[:, :, lanes], img_buf.at[i % 2], b_sem.at[i % 2, 0]),
+                pltpu.make_async_copy(theads_out.at[i // per_part, :, part], txt_buf.at[i % 2], b_sem.at[i % 2, 1])]
+
+    def pair_lanes(i):
+        return pl.ds(pl.multiple_of((core * pairs + i) * (2 * HD), 128), 2 * HD)
+
+    def o_keep(i):
+        return pltpu.make_async_copy(o_stage.at[i, core], att_out.at[:, pair_lanes(i)], o_sem.at[i])
+
+    def o_push(i):
+        return push(o_stage.at[i, 1 - core], att_out.at[:, pair_lanes(i)], o_send.at[i], o_recv.at[i], (partner, z))
+
+    for copy in pair_loads(0):
+        copy.start()
+    tokens = img_buf.shape[1] * img_buf.shape[2]
+
+    def pair_step(i, _):
+        at = i % 2
+
+        @pl.when(i + 1 < pairs)
+        def _():
+            for copy in pair_loads(i + 1):
+                copy.start()
+
+        for copy in pair_loads(i):
+            copy.wait()
+        bias = bias_out[:, 0:1]
+        for h in range(2):
+            low = 3 * HD * h
+            ki = img_buf[at, :, :, low + HD:low + 2 * HD].reshape(tokens, HD)
+            vi = img_buf[at, :, :, low + 2 * HD:low + 3 * HD].reshape(tokens, HD)
+            kt = txt_buf[at, :, low + HD:low + 2 * HD]
+            vt = txt_buf[at, :, low + 2 * HD:low + 3 * HD]
+            for b in range(3):
+                q = img_buf[at, b, :, low:low + HD] if b < 2 else txt_buf[at, :, low:low + HD]
+                o, lse = attend_block(q, ki, vi, kt, vt, bias)
+                rows = img_buf.shape[2]
+                if b < 2:
+                    o_stage[i, b, :, h * HD:(h + 1) * HD] = o
+                    lse_out[i, h:h + 1, b * rows:(b + 1) * rows] = lse
+                else:
+                    ot_stage = o
+                    lse_out[i, h:h + 1, tokens:tokens + q.shape[0]] = lse
+            if h == 0:
+                first = ot_stage
+        both = jnp.concatenate([first, ot_stage], axis=1)
+        ot_out[i // per_part, :, pl.ds(pl.multiple_of(i % per_part * (2 * HD), 128), 2 * HD)] = both
+        o_keep(i).start()
+        o_push(i).start()
+        return 0
+
+    lax.fori_loop(0, pairs // 2, pair_step, 0)
+    for m in (1, 2, 3):
+        at_distance(2, lambda zz: forward(m, zz))
+    lax.fori_loop(pairs // 2, pairs, pair_step, 0)
+
     for m in (1, 2, 3):
         at_distance(n_z - 1, lambda zz: forward(m, zz))
     for m in range(total - 1):
@@ -1795,17 +1888,25 @@
     tokens_wait(g_ref, g_out, g_send, g_recv)
     tokens_drain(x_ref, x_out, x_send, x_recv)
     tokens_drain(g_ref, g_out, g_send, g_recv)
-    keep.wait()
     heads_push().wait_send()
-    push(stage.at[0], heads_out.at[1 - core], h_send, h_recv, (partner, z)).wait_recv()
+    sign_push.wait_send()
+    hot_push.wait_send()
+
+    def o_done(i, _):
+        o_keep(i).wait()
+        o_push(i).wait_send()
+        other = pl.ds(pl.multiple_of(((1 - core) * pairs + i) * (2 * HD), 128), 2 * HD)
+        push(o_stage.at[i, 0], att_out.at[:, other], o_send.at[i], o_recv.at[i], (partner, z)).wait_recv()
+        return 0
+
+    lax.fori_loop(0, pairs, o_done, 0)
     for s in range(2):
         @pl.when(jnp.logical_not(is_here(s)))
         def _():
-            push(theads_out.at[s], theads_out.at[s], q_send.at[s], q_recv.at[s], there[s]).wait_recv()
             push(tq_ref, theads_out.at[z % 2], q_send.at[s], q_recv.at[z % 2], there[s]).wait_send()
 
 
-def front(full, part, adapter_rows, x, g, picks, hot2, cond, wmod, x_txt, g_txt, own, tmask, smask, n_f, n_z, fans, cols, cid):
+def front(full, part, adapter_rows, x, g, picks, hot2, cond, wmod, x_txt, g_txt, own, tmask, smask, sign_rows, n_f, n_z, fans, cols, cid):
     f32, bf16 = jnp.float32, jnp.bfloat16
     vmem, dma = pltpu.VMEM, pltpu.SemaphoreType.DMA
     shape = jax.ShapeDtypeStruct
@@ -1816,7 +1917,7 @@
     cond8 = jnp.concatenate([cond, cond, jnp.zeros((4, width), f32)])
     lane = jnp.pad(lax.dynamic_slice_in_dim(cond, z * (width // n_z), width // n_z, 1), ((0, 6), (0, 0)))
     chosen = (picks[:, None] == jnp.arange(NAD)[None, :]).astype(f32).reshape(-1, 1)
-    smalls = (jnp.broadcast_to(chosen, (slots * NAD, 128)), hot2, blocks, lane, cond8, smask, wmod, x_txt, g_txt, own, tmask)
+    smalls = (jnp.broadcast_to(chosen, (slots * NAD, 128)), hot2, blocks, lane, cond8, smask, wmod, x_txt, g_txt, own, tmask, sign_rows)
     args = (*full, *part, adapter_rows, x, g, *smalls)
     any_spec, in_vmem = pl.BlockSpec(memory_space=pl.ANY), pl.BlockSpec(memory_space=vmem)
     rows = 2 * (sum(fans) + sum(cols)) // n_z
@@ -1839,11 +1940,15 @@
     outs += [shape((RANK, n), bf16) for n in fans[1:]] + [shape((RANK, n), bf16) for n in cols[1:]]
     outs += [shape((thick, n), bf16) for n in own_a] + [shape((thick, n), bf16) for n in own_b]
     outs += [shape((2, rank2, width), bf16), shape((2, rank2, cut), bf16), shape((2, 8, rank2), f32), shape((n_f, 8, share), f32), shape((n_z, pad, width), bf16)]
+    heads_half = cols[1] // (6 * HD)
+    pairs = heads_half // 2
+    outs += [shape((2, n_z * pad, width // n_z), bf16), shape((pairs, 2, 2 * img_rows + n_z * pad), f32), shape(sign_rows.shape, f32),
+             shape((2 * rank2, NAD * RANK), bf16)]
     outs += [shape((img_rows, width), bf16), shape((img_rows, RANK), bf16), shape((2, img_rows, cols[1] // 2), bf16),
-             shape((n_z, pad, width), bf16), shape((n_z * pad, thick), bf16), shape((2, n_z * pad, qkv_part), bf16)]
+             shape((n_z, pad, width), bf16), shape((n_z * pad, thick), bf16), shape((2, n_z * pad, qkv_part), bf16), shape((img_rows, width), bf16)]
     specs = [any_spec] * in_hbm + [in_vmem, any_spec] + [in_vmem] * (len(outs) - in_hbm - 2)
-    specs[len(outs) - 4] = any_spec
-    specs[len(outs) - 1] = any_spec
+    for place in (1, 2, 5):
+        specs[len(outs) - place] = any_spec
     return pl.pallas_call(
         functools.partial(front_kernel, n_f, n_z, tuple(fans), tuple(cols)),
         out_shape=outs,
@@ -1854,12 +1959,14 @@
             vmem((rank2, 6 * share), bf16), vmem((n_z, rank2, 6 * share), bf16), vmem((n_f, 8, 256), f32),
             vmem((n_f, 8, cut), f32), vmem((n_f, 8, cut), f32), vmem((8, cut), f32), vmem((2 * n_z, 8, cut), f32),
             vmem((2, n_f, k_local, 768), bf16), vmem((n_f, k_local, qkv_part), bf16), vmem((2, img_rows, cols[1] // 2), bf16),
-            vmem((n_z * pad, qkv_part), bf16),
+            vmem((n_z * pad, qkv_part), bf16), vmem(sign_rows.shape, f32), vmem((rank2, NAD * RANK), bf16),
+            vmem((2, 2, img_rows, 6 * HD), bf16), vmem((2, n_z * pad, 6 * HD), bf16), vmem((pairs, 2, img_rows, 2 * HD), bf16),
             dma((total, n_z, 2)), dma((total, n_z)), dma((total, n_z, 2, chips, nbits)), dma((total, n_z, 2, chips)),
             dma((total, n_z, 2, chips)), dma((total, n_z, 2, chips)), dma((total,)),
             dma((2,)), dma((2,)), dma((2,)), dma((2,)), dma((n_f,)), dma((n_f,)), dma((n_f,)), dma((n_f,)), dma((n_f,)), dma((n_f,)),
             dma((2, 2)), dma((n_z,)), dma((n_z,)), dma((n_z,)), dma((2 * n_z,)), dma((2 * n_z,)), dma((n_z,)), dma((n_z,)),
             dma((2,)), dma, dma, dma, dma, dma((2,)), dma((2,)), dma((n_z,)), dma((n_z,)),
+            dma((2,)), dma((2,)), dma((2, 2)), dma((pairs,)), dma((pairs,)), dma((pairs,)),
         ],
         compiler_params=pltpu.CompilerParams(collective_id=cid, has_side_effects=True, vmem_limit_bytes=58 * 1024 * 1024),
         name="front",
@@ -2053,12 +2160,6 @@
     def by_group(mine, other):
         return by_core(mine, other, 0)
 
-    column_picks = by_group(adapter_index, swap_core(adapter_index))
-    column_count = 2 * slots
-    one_hot = (
-        jnp.arange(NAD * RANK)[:, None]
-        == (column_picks[:, None] * RANK + jnp.arange(RANK)[None, :]).reshape(1, -1)
-    ).astype(F32)
     def stretch(stream, index):
         if stream == 0:
             return img_mod[:, index * width : (index + 1) * width]
@@ -2110,7 +2211,8 @@
         made = front(
             [w[0] for w in local], [w[1] for w in local], adapter_rows, image_tokens, image_cot,
             adapter_index, own_hot.T.astype(BF16), cond_act.astype(F32), mod_weight, x_txt_low,
-            g_txt_low, sign(owner_local), lanes_pad(txt_mask), slot_mask, n_f, n_z, fans, cols, 1,
+            g_txt_low, sign(owner_local), lanes_pad(txt_mask), slot_mask,
+            jnp.broadcast_to(sign(owner_group), (owner_group.shape[0], thick)), n_f, n_z, fans, cols, 1,
         )
         made = iter(made)
         take = lambda count: [next(made) for _ in range(count)]
@@ -2121,13 +2223,21 @@
         img_pairs = [None] + list(zip(take(4), take(4)))
         thick_pairs = [None] + list(zip(take(4), take(4)))
         mod_a, mod_b, tmod, cond_own, txt_dm = take(5)
-        img_in, img_qkv_mid, img_heads, txt_in, txt_qkv_mid, txt_heads = take(6)
+        o_txt, lse, bias, hot_four = take(4)
+        bias = bias[:, :1]
+        img_in, img_qkv_mid, img_heads, txt_in, txt_qkv_mid, txt_heads, attended = take(7)
         img_heads = img_heads.reshape(img_n, -1)
         txt_in = txt_in.reshape(-1, width)
         txt_pairs = [None, tuple(part[:rank_cols] for part in thick_pairs[1])]
         img_mod = img_rows_mod[:6].reshape(1, -1)
         txt_mods = txt_mod.reshape(slots, 8, width)[:, :6].reshape(slots, -1)
     else:
+        column_picks = by_group(adapter_index, swap_core(adapter_index))
+        column_count = 2 * slots
+        one_hot = (
+            jnp.arange(NAD * RANK)[:, None]
+            == (column_picks[:, None] * RANK + jnp.arange(RANK)[None, :]).reshape(1, -1)
+        ).astype(F32)
         got = gather([w[0] for w in local], [w[1] for w in local] + [adapter_rows], n_f, n_z)
         got = [g.reshape(-1, g.shape[-1]) for g in got]
         img_w, txt_w, row = got[:4], got[4:8], got[8]
@@ -2244,23 +2354,24 @@
 
     inputs = [x_img.astype(F32), x_txt]
     norm_one = [layer_norm(values) for values in inputs]
-    lengths = by_group(text_lengths[0:1], swap_core(text_lengths[0:1]))
-    chip_lengths = jnp.cumsum(lax.dynamic_index_in_dim(lengths, z // slots, 0, keepdims=False))
-    chip_slot = z % slots
-    chip_segment = jnp.sum(
-        (position(txt_rows)[:, None] >= chip_lengths[None, :]).astype(jnp.int32),
-        axis=1,
-        keepdims=True,
-    )
-    chip_owner = (chip_segment == chip_slot) & (txt_rows % txt_pad < txt_local)[:, None]
-    bias = jnp.where(chip_owner, 0.0, -1e30).astype(F32)
-    o_img, o_txt, lse = attend(img_heads, txt_heads, bias, HD)
-
     def txt_home(values):
         got = from_chip([values[0], values[1]])
         return jnp.where(owner_group[:, 0:1] > 0, got[0], jnp.where(owner_group[:, 1:2] > 0, got[1], 0))
 
-    attended = to_tokens(o_img)
+    if n_f != 8:
+        lengths = by_group(text_lengths[0:1], swap_core(text_lengths[0:1]))
+        chip_lengths = jnp.cumsum(lax.dynamic_index_in_dim(lengths, z // slots, 0, keepdims=False))
+        chip_slot = z % slots
+        chip_segment = jnp.sum(
+            (position(txt_rows)[:, None] >= chip_lengths[None, :]).astype(jnp.int32),
+            axis=1,
+            keepdims=True,
+        )
+        chip_owner = (chip_segment == chip_slot) & (txt_rows % txt_pad < txt_local)[:, None]
+        bias = jnp.where(chip_owner, 0.0, -1e30).astype(F32)
+        o_img, o_txt, lse = attend(img_heads, txt_heads, bias, HD)
+
+        attended = to_tokens(o_img)
     (img_branch, img_after, img_mlp, img_pre, img_result, *img_mids, img_gate, txt_mlp, txt_att, txt_after, txt_branch) = both_fwd(
         attended, x_img, g_img, img_rows_mod, img_w[1], img_pairs[2], img_pairs[3], img_w[2], img_pairs[4], img_w[3],
         o_txt, x_txt_low, txt_mod, sign(owner_group), sign(owner_local), lanes_pad(txt_mask_local), txt_w[1], thick_pairs[2],
@@ -2274,7 +2385,8 @@
     )
     img_grad_after, img_grad_att, img_sums, *sides = made[:9]
     txt_result, txt_grad_after, do_txt, txt_sums, *txt_sides = made[9:]
-    txt_sides = [part[:rank_cols] for part in txt_sides]
+    if n_f != 8:
+        txt_sides = [part[:rank_cols] for part in txt_sides]
     txt_sum_rows = txt_sums
     txt_sums = txt_sums.reshape(4, slots, width)
     image_out = unshard(img_result)
@@ -2316,7 +2428,7 @@
         image_low, txt_grad, cond_slices, mod_rank, shard = tail(
             d_img.reshape(2, img_half, -1), d_txt, img_w[0].reshape(n_f, k_local, -1), smalls,
             sides_of(0, 0), sides_of(0, 1), sides_of(1, 0), sides_of(1, 1),
-            one_hot.T.astype(BF16), own_hot.T.astype(BF16), mod_weight, mod_b, tmod, cond_own, slot_mask,
+            hot_four, own_hot.T.astype(BF16), mod_weight, mod_b, tmod, cond_own, slot_mask,
             n_f, n_z, fans, cols, 3,
         )
         image_grad = image_low.astype(F32)

time: 799 us -> 755 us (0.945)
  Pallas kernels: 732 us -> 703 us
  local copies, waits for them, and re-layouts: 28.2 us -> 18 us
    pallas_call x1 -> x0, Pallas kernels: 37.6 us -> none  [attend(): pl.pallas_call(functools.partial(attend_kernel, hd, bq), grid=(pairs,), i...]
    slice x6 -> x0, local copies, waits for them, and re-layouts: 8.89 us -> none  [shards(): txt_sides = [part[:rank_cols] for part in txt_sides]]
  transfers between devices with their start and end apart: 6 -> 3, of which waited for: 1 -> 0; matrix products, arithmetic and copies ran while one was open for 4% -> 1% of each run, Pallas kernels for 23% -> 25%
where the time goes in v7:
time: 755 us; the launch traced here: 745 us
  Pallas kernels  703 us (93%)
  local copies, waits for them, and re-layouts  18 us (2%)
  other arithmetic  16 us (2%)
    pallas_call x1, Pallas kernels, front(): pl.pallas_call(functools.partial(front_kernel, n_f, n_z, tuple(fans), tup...  370 us
    pallas_call x1, Pallas kernels, tail(): pl.pallas_call(functools.partial(tail_kernel, n_f, n_z, tuple(fans), tupl...  121 us
    pallas_call x1, Pallas kernels, both_back(): pl.pallas_call(functools.partial(both_back_kernel, tiles, n_z, turns), gr...  86.1 us
    pallas_call x1, Pallas kernels, both_fwd(): pl.pallas_call(functools.partial(both_fwd_kernel, tiles, n_z, turns), gri...  63.9 us
    pallas_call x1, Pallas kernels, attend_back(): pl.pallas_call(functools.partial(attend_back_kernel, hd, bq), grid=(pairs...  61.8 us
  transfers between devices with their start and end apart: 3, of which 0 were waited for; matrix products, arithmetic and copies ran while one was open for 1% of the time, Pallas kernels for 25%

profile of v7, /device:TPU:11, one launch (start us, length us, event | category | flops | bytes accessed | tf_op | source)
XLA Modules:
  0.0 745.1 jit_solution(16026430977531337742)
XLA Ops:
  0.7 0.8 compare_convert_fusion.3
  1.5 0.7 broadcast_multiply_fusion
  2.2 0.8 reduce-window.8
  3.0 0.1 fusion.9
  3.1 0.1 convert_select_fusion
  3.3 0.7 fusion.16
  4.0 0.1 fusion.12
  4.2 0.7 slice_subtract_fusion.1.refs_20_.own_ref.refs_17_
  5.0 2.1 slice_bitcast_fusion.4
  7.1 0.7 slice_bitcast_fusion.6
  7.9 0.9 convert_element_type.65.refs_8_
  9.0 0.7 convert_convert_fusion.refs_12_.refs_37_
  9.8 0.6 pad.30.refs_13_
  10.4 0.6 pad.31.refs_14_
  11.1 0.7 maximum_maximum_fusion.refs_15_
  11.9 0.1 reshape.164
  12.0 0.6 select_maximum_fusion.refs_16_.refs_42_
  12.6 1.6 pad.33.refs_18_.xt_ref.refs_12_
  14.1 1.6 pad.34.refs_19_.gt_ref
  15.7 0.1 copy.28
  15.8 0.7 pad.35.refs_21_.mask_ref
  16.5 0.6 pad.36.lmask_ref.refs_18_
  17.2 1.5 slice_bitcast_fusion
  18.7 0.7 broadcast_in_dim.40.refs_11_
  19.3 0.7 broadcast_in_dim.74.refs_22_
  20.0 369.8 %front.1 = (bf16[8,192,4608]{2,1,0:T(8,128)(2,1)}, bf16[8,192,1536]{2,1,0:T(8,128)(2,1)}, bf16[8,192,6144]{2,1,0:T(8,128)(2,1)}, bf16[8,192,6144]{2,1,0:T(8,128)...) custom-call(bf16[192,1152]{1,0:T(8,128)(2,1)} %get-tuple-element.185, ...), custom_call_target="tpu_custom_call" | custom-call | tf_op jit(solution)/shard_map/front/pallas_call | solution.py:1952
  389.9 63.9 %block_forward.1 = (bf16[512,1536]{1,0:T(8,128)(2,1)}, f32[512,1536]{1,0:T(8,128)}, bf16[512,1536]{1,0:T(8,128)(2,1)}, f32[512,6144]{1,0:T(8,128)}, bf16[512,153...) custom-call(bf16[512,1536]{1,0:T(8,128)(2,1)} %get-tuple-element.89., ...), custom_call_target="tpu_custom_call" | custom-call | tf_op jit(solution)/shard_map/block_forward/pallas_call | solution.py:794
  453.7 86.1 %block_backward.1 = (f32[512,1536]{1,0:T(8,128)}, bf16[512,1536]{1,0:T(8,128)(2,1)}, f32[24,1536]{1,0:T(8,128)}, f32[16,6144]{1,0:T(8,128)}, f32[16,6144]{1,0:T(...) custom-call(bf16[512,1536]{1,0:T(8,128)(2,1)} %bitcast.63, ...), custom_call_target="tpu_custom_call" | custom-call | tf_op jit(solution)/shard_map/block_backward/pallas_call | solution.py:835
  539.9 1.6 broadcast_select_fusion.2
  541.4 1.8 collective-permute-start.2
  543.2 1.0 broadcast_select_fusion.5
  544.2 4.7 collective-permute-start
  549.0 0.7 slice.98
  549.7 1.3 broadcast_select_fusion.1
  551.0 0.1 pad_maximum_fusion.1.doi_ref
  551.1 1.0 copy-done.1
  552.2 61.8 %attend_back.1 = (bf16[1024,2304]{1,0:T(8,128)(2,1)}, bf16[2,192,1152]{2,1,0:T(8,128)(2,1)S(1)}) custom-call(bf16[1024,2304]{1,0:T(8,128)(2,1)} %bitcast.67, bf16[2,192,1152]{2,1,0:T(8,128)(2,1)S(1)} %copy-done.1, f32[192,1]{1,0:T(8,128)S(1)} %bitcast.53, bf16[1024,768]{1,0:T(8,128)(2,1)S(1)} %pad_maximum_fusion.1.doi_ref, ...), custom_call_target="tpu_custom_call" | custom-call | tf_op jit(solution)/shard_map/attend_back/pallas_call | solution.py:375
  614.1 0.9 copy-done
  615.0 121.0 %gradient_exchange.1 = (bf16[2,256,1536]{2,1,0:T(8,128)(2,1)}, f32[48,1536]{1,0:T(8,128)}, f32[8,8,256]{2,1,0:T(8,128)}, f32[8,32]{1,0:T(8,128)}, f32[2208,128]{1,0:T(8,128)}) custom-call(bf16[2,512,2304]{2,1,0:T(8,128)(2,1)} %bitcast.66, bf16[2,192,1152]{2,1,0:T(8,128)(2,1)} %copy-done, bf16[8,192,4608]{2,1,0:T(8,128)(2,1)} %get-tuple-element.135.refs_2_, ...), custom_call_target="tpu_custom_call" | custom-call | tf_op jit(solution)/shard_map/gradient_exchange/pallas_call | solution.py:1255
  736.0 3.5 convert_element_type.77
  739.6 0.7 slice.102
  740.3 0.8 slice_bitcast_fusion.8
  741.2 0.1 convolution_add_fusion.1
  741.4 0.7 fusion.5
  742.1 0.1 select_bitcast_fusion.1
  742.2 1.3 pad_maximum_fusion
  743.5 0.4 copy-done.10
  743.9 1.0 copy.35
  (59 shorter events, 1.2 us)
Async XLA Ops:
  0.6 6.5 copy-start.11
  0.6 7.2 copy-start.9
  7.1 2.5 copy-start.15
  7.8 9.3 %copy-start.7 = (bf16[2,1536,192]{1,2,0:T(8,128)(2,1)S(1)}, bf16[2,1536,192]{1,2,0:T(8,128)(2,1)}, u32[]{:S(2)}) copy-start(bf16[2,1536,192]{1,2,0:T(8,128)(2,1)} %param.23) | copy-start | bytes 3538948
  7.9 9.3 %copy-start.8 = (bf16[2,192,1536]{2,1,0:T(8,128)(2,1)S(1)}, bf16[2,192,1536]{2,1,0:T(8,128)(2,1)}, u32[]{:S(2)}) copy-start(bf16[2,192,1536]{2,1,0:T(8,128)(2,1)} %param.22) | copy-start | bytes 3538948
  539.8 3.4 copy-start.6
  541.4 8.2 %collective-permute-start.2 = (bf16[512,768]{1,0:T(8,128)(2,1)S(1)}, bf16[512,768]{1,0:T(8,128)(2,1)}, u32[]{:S(2)}, u32[]{:S(2)}) collective-permute-start(bf16[512,768]{1,0:T(8,128)(2,1)S(1)} %broadcast_select_fusion.2), channel_id=1, source_target_pairs={{0,4},{4,0},{8,12},{12,8},{16,20},{20,16},{24,28},{28,24},{1,5},{5... | collective-permute-start | bytes 2359304 | tf_op jit(solution)/shard_map/ppermute | solution.py:2087
  543.2 5.8 copy-start.13
  543.2 6.5 copy-start.5
  544.2 197.9 %collective-permute-start = (bf16[256,1536]{1,0:T(8,128)(2,1)}, bf16[256,1536]{1,0:T(8,128)(2,1)S(1)}, u32[]{:S(2)}, u32[]{:S(2)}) collective-permute-start(bf16[256,1536]{1,0:T(8,128)(2,1)} %get-tuple-element.178), channel_id=1, source_target_pairs={{0,0},{1,1},{4,2},{5,3},{2,4},{3,5},{6,6},{7,7},{8,8},{9,9},{12,10... | collective-permute-start | bytes 2359304 | tf_op jit(solution)/shard_map/ppermute | solution.py:2077
  548.9 193.2 %collective-permute-start.1 = (bf16[256,1536]{1,0:T(8,128)(2,1)S(1)}, bf16[256,1536]{1,0:T(8,128)(2,1)S(1)}, u32[]{:S(2)}, u32[]{:S(2)}) collective-permute-start(bf16[256,1536]{1,0:T(8,128)(2,1)S(1)} %get-tuple-element.179), channel_id=1, source_target_pairs={{1,0},{0,1},{5,2},{4,3},{3,4},{2,5},{7,6},{6,7},{9,8},{8,9},{13,10... | collective-permute-start | bytes 2359304 | tf_op jit(solution)/shard_map/ppermute | solution.py:2077
  551.0 1.2 copy-start.1
  551.0 1.2 copy-start.2
  551.0 1.2 copy-start.3
  551.0 1.2 copy-start.4
  614.0 0.9 copy-start
  736.0 3.6 copy-start.12
  736.0 5.2 copy-start.16
  736.0 5.2 copy-start.14
  742.2 1.7 copy-start.10

commit v8 on v7

--- a/solution.py
+++ b/solution.py
@@ -365,6 +365,97 @@
         dt_ref[0, :, base + hd:base + 2 * hd] = acc_t[0].astype(jnp.bfloat16)
         dt_ref[0, :, base + 2 * hd:base + 3 * hd] = acc_t[1].astype(jnp.bfloat16)
 
+def attend_back_far_kernel(hd, bq, n_z, fans, cols, img_ref, txt_ref, bias_ref, doi_ref, dot_ref, lse_ref, y_ref, *refs):
+    img_a, img_b, rest = refs[:3], refs[3:6], refs[6:]
+    di_ref, dt_ref, y_out, z_out, acc_i, acc_t, zmsg, y_send, y_recv, z_send, z_recv = rest
+    step = pl.program_id(0)
+    f, z, core, base, column = column_peers(n_z)
+    ring = ZRing(f, z, n_z)
+    there = [(base + z // 2, 2 * core + i) for i in range(2)]
+
+    def is_here(i):
+        return (z // 2 == core) & (2 * core + i == z)
+
+    def y_keep(i):
+        return pltpu.make_async_copy(y_ref.at[i], y_out.at[z % 2], y_recv.at[z % 2])
+
+    def y_push(i):
+        return push(y_ref.at[i], y_out.at[z % 2], y_send.at[i], y_recv.at[z % 2], there[i])
+
+    def z_keep():
+        return pltpu.make_async_copy(zmsg.at[z], z_out.at[z], z_recv.at[z])
+
+    @pl.when(step == 0)
+    def _():
+        meet(column)
+        offset = 0
+        for part, sizes in ((img_a, fans), (img_b, cols)):
+            for index in range(3):
+                count = sizes[index + 2] // n_z
+                for t in range(n_z):
+                    zmsg[t, :, offset:offset + count] = part[index][:, t * count:(t + 1) * count].astype(jnp.bfloat16)
+                offset += count
+        ring.start(lambda to: zmsg.at[to], z_out, z_send, z_recv)
+        z_keep().start()
+        for i in range(2):
+            @pl.when(is_here(i))
+            def _():
+                y_keep(i).start()
+
+            @pl.when(jnp.logical_not(is_here(i)))
+            def _():
+                y_push(i).start()
+
+    attend_back_kernel(hd, bq, img_ref, txt_ref, bias_ref, doi_ref, dot_ref, lse_ref, di_ref, dt_ref, acc_i, acc_t)
+
+    @pl.when(step == pl.num_programs(0) - 1)
+    def _():
+        z_keep().wait()
+        ring.wait(z_out, z_send, z_recv)
+        ring.drain(lambda to: zmsg.at[to], z_out, z_send, z_recv)
+        for i in range(2):
+            @pl.when(is_here(i))
+            def _():
+                y_keep(i).wait()
+
+            @pl.when(jnp.logical_not(is_here(i)))
+            def _():
+                push(y_out.at[i], y_out.at[i], y_send.at[i], y_recv.at[i], there[i]).wait_recv()
+                y_push(i).wait_send()
+
+
+def attend_back_far(img, txt, bias, doi, dot, lse, hd, y, img_a, img_b, n_z, fans, cols, cid, bq=512):
+    img_n, wide_n = img.shape
+    parts, txt_n, _ = txt.shape
+    pairs = wide_n // (6 * hd)
+    per = pairs // parts
+    vmem, dma = pltpu.VMEM, pltpu.SemaphoreType.DMA
+    bf16, shape = jnp.bfloat16, jax.ShapeDtypeStruct
+    wide = pl.BlockSpec((img_n, 6 * hd), lambda i: (0, i))
+    wide_t = pl.BlockSpec((1, txt_n, 6 * hd), lambda i: (i // per, 0, i % per))
+    outside = pl.BlockSpec(memory_space=pl.ANY)
+    sides = (*img_a, *img_b)
+    lanes = (sum(fans[2:]) + sum(cols[2:])) // n_z
+    return pl.pallas_call(
+        functools.partial(attend_back_far_kernel, hd, bq, n_z, tuple(fans), tuple(cols)),
+        grid=(pairs,),
+        in_specs=[
+            wide, wide_t,
+            pl.BlockSpec((txt_n, 1), lambda i: (0, 0)),
+            pl.BlockSpec((img_n, 2 * hd), lambda i: (0, i)),
+            pl.BlockSpec((1, txt_n, 2 * hd), lambda i: (i // per, 0, i % per)),
+            pl.BlockSpec((1, 2, img_n + txt_n), lambda i: (i, 0, 0)),
+            outside,
+        ] + [pl.BlockSpec(v.shape, lambda i: (0, 0)) for v in sides],
+        out_specs=[wide, wide_t, outside, outside],
+        out_shape=[shape(img.shape, bf16), shape(txt.shape, bf16), shape(y.shape, bf16), shape((n_z, RANK, lanes), bf16)],
+        scratch_shapes=[vmem((2, img_n, hd), jnp.float32), vmem((2, txt_n, hd), jnp.float32), vmem((n_z, RANK, lanes), bf16),
+                        dma((2,)), dma((2,)), dma((n_z,)), dma((n_z,))],
+        compiler_params=pltpu.CompilerParams(collective_id=cid, has_side_effects=True, vmem_limit_bytes=56 * 1024 * 1024),
+        name="attend_back",
+    )(img, txt, bias, doi, dot, lse, y, *sides)
+
+
 def attend_back(img, txt, bias, doi, dot, lse, hd, bq=512):
     img_n, cols = img.shape
     parts, txt_n, _ = txt.shape
@@ -624,8 +715,8 @@
                      tao_ref, tbo_ref, ta1_ref, tb1_ref, ta2_ref, tb2_ref,
                      dx1_out, do_out, sums_out, ga2_out, gb1_out, ga1_out, gb2_out, gao_out, gbo_out,
                      ty_out, tdx1_out, tdo_out, tsums_out, tgao_out, tgbo_out, tga1_out, tgb1_out, tga2_out, tgb2_out,
-                     dm_ref, dt2_ref, dh_acc, dt1_acc, part_ref, mine_ref, out_buf, in_buf, tda_ref, tdo_buf,
-                     do_send, do_recv, rs_send, rs_recv, ag_send, ag_recv):
+                     dm_ref, dt2_ref, dh_acc, dt1_acc, part_ref, mine_ref, out_buf, in_buf, tda_ref, tdo_buf, heads_buf,
+                     do_send, do_recv, rs_send, rs_recv, ag_send, ag_recv, hd_send, hd_recv, hd_own):
     step = pl.program_id(0)
     f, z, core, base, column = column_peers(n_z)
     pad, width_t = gt_ref.shape
@@ -759,12 +850,23 @@
         gao_out[...] = t_mm(dto, o_ref[...])
         gbo_out[...] = t_mm(to_ref[...], dm_ref[...])
 
+        per_half = width // 512
+
         def cols(n, _):
             sl = pl.ds(pl.multiple_of(n * 256, 256), 256)
-            do_out[:, sl] = (mm(dm_ref[...], wo_ref[:, sl]) + mm(dt2_ref[...], ao_ref[:, sl])).astype(bf16)
+            into = pl.ds(pl.multiple_of(n % per_half * 256, 256), 256)
+            heads_buf[n // per_half, :, into] = (mm(dm_ref[...], wo_ref[:, sl]) + mm(dt2_ref[...], ao_ref[:, sl])).astype(bf16)
             return 0
 
         lax.fori_loop(0, width // 256, cols, 0)
+        partner = base + 1 - core
+        swap = push(heads_buf.at[1 - core], do_out.at[core], hd_send, hd_recv, (partner, z))
+        swap.start()
+        keep = pltpu.make_async_copy(heads_buf.at[core], do_out.at[core], hd_own)
+        keep.start()
+        keep.wait()
+        swap.wait_send()
+        push(heads_buf.at[0], do_out.at[1 - core], hd_send, hd_recv, (partner, z)).wait_recv()
 
     @pl.when(step == tiles - 1)
     def _():
@@ -813,7 +915,7 @@
 
 
 def both_back(g, x1, a, h2, o, mod, u, w2, pair_2, w1, pair_1, wo, pair_o, mids,
-              gt, tx1, tbr, tmod, own, mask, lmask, tall, att, tdm, two, tw1, tw2, tpair_o, tpair_1, tpair_2, n_z, cid, tn=512, turns=(5, 9)):
+              gt, tx1, tbr, tmod, own, mask, lmask, tall, att, tdm, two, tw1, tw2, tpair_o, tpair_1, tpair_2, n_z, cid, tn=512, turns=(8, 11)):
     rows, width = o.shape
     hidden = w1.shape[1]
     tiles = hidden // tn
@@ -837,17 +939,17 @@
         grid=(tiles,),
         in_specs=[once(act)] * 5 + [once(mod.shape), tile(rows), tile(width), tile(rank), once(side), tile(width), once(side), tile(rank),
                   once((width, width)), once(side), once(side)] + [once(thin)] * 3 + [once(v.shape) for v in texts],
-        out_specs=[whole(act), whole(act), whole((24, width)), tile(rank), tile(rank)] + [whole(side)] * 4
+        out_specs=[whole(act), pl.BlockSpec(memory_space=pl.ANY), whole((24, width)), tile(rank), tile(rank)] + [whole(side)] * 4
         + [whole((pad, width)), whole((pad, width)), pl.BlockSpec(memory_space=pl.ANY), whole((8, width)), whole((thick, share)),
            whole((thick, share)), whole((thick, share)), whole((thick, t_hidden)), whole((thick, t_hidden)), whole((thick, share))],
-        out_shape=[shape(act, f32), shape(act, bf16), shape((24, width), f32)] + [shape((rank, hidden), f32)] * 2 + [shape(side, f32)] * 4
+        out_shape=[shape(act, f32), shape((2, rows, width // 2), bf16), shape((24, width), f32)] + [shape((rank, hidden), f32)] * 2 + [shape(side, f32)] * 4
         + [shape((pad, width), bf16), shape((pad, width), f32), shape((2, total, share), bf16), shape((8, width), f32),
            shape((thick, share), f32), shape((thick, share), f32), shape((thick, share), f32), shape((thick, t_hidden), f32),
            shape((thick, t_hidden), f32), shape((thick, share), f32)],
         scratch_shapes=[vmem(act, bf16), vmem(thin, bf16), vmem(act, f32), vmem(thin, f32),
                         vmem((n_z, pad, wide), f32), vmem((2, pad, wide), f32), vmem((2, n_z, pad, wide), bf16), vmem((2, n_z, pad, wide), bf16),
-                        vmem((n_z, pad, wide + thick), bf16), vmem((total, share), bf16),
-                        dma((2,)), dma((2,)), dma((2, n_z)), dma((2, n_z)), dma((n_z,)), dma((n_z,))],
+                        vmem((n_z, pad, wide + thick), bf16), vmem((total, share), bf16), vmem((2, rows, width // 2), bf16),
+                        dma((2,)), dma((2,)), dma((2, n_z)), dma((2, n_z)), dma((n_z,)), dma((n_z,)), dma, dma, dma],
         compiler_params=pltpu.CompilerParams(collective_id=cid, has_side_effects=True, vmem_limit_bytes=60 * 1024 * 1024),
         name="block_backward",
     )(g, x1, a, h2, o, mod, u, w2, pair_2[0], pair_2[1], w1, pair_1[0], pair_1[1], wo, *pair_o, *mids, *texts)
@@ -867,7 +969,8 @@
     dq_in, tdq_in, wq_ref = take(3)
     (x_ref, dx1_ref, h_ref, imod_ref, mid_ref, qa_ref, qb_ref, isum_ref, igate_ref, tx_ref, tdx1_ref, th_ref, tmodr_ref, owner_ref,
      own_ref, lmask_ref, tmid_ref, twq_ref, tqa_ref, tqb_ref, tsum_ref) = take(21)
-    img_a, img_b, txt_a, txt_b = take(3), take(3), take(3), take(3)
+    early_ref, = take(1)
+    txt_a, txt_b = take(3), take(3)
     hot4_ref, hot2_ref, wmod_ref, bmod_ref, tmod_ref, cond_ref, smask_ref = take(7)
     grad_out, tgrad_out, cond_out, rank_out, shard_out = take(5)
     (dq_ref, wtile, dh_ref, dt_ref, grad_ref, gaq_ref, gbq_ref, tgot, part_ref, mine_ref, out_buf, in_buf, dt_ag, tgb_ref, dmod_ref,
@@ -965,17 +1068,20 @@
     dt_low = dt_ref[...].astype(bf16)
     gaq_ref[...] = t_mm(dt_low, h_ref[...])
 
+    spans = {}
     offset = 0
-    spans = []
-    for part, sizes in (([gaq_ref] + img_a, fans), ([gbq_ref] + img_b, cols)):
-        for index in range(4):
-            count = sizes[index + 1] // n_z
-            for t in range(n_z):
-                zmsg[t, :, offset:offset + count] = part[index][:, t * count:(t + 1) * count].astype(bf16)
-            spans.append((offset, count))
-            offset += count
+    for part, count, name in ((gaq_ref, fans[1] // n_z, (0, 1)), (gbq_ref, cols[1] // n_z, (1, 1))):
+        for t in range(n_z):
+            zmsg[t, :, offset:offset + count] = part[:, t * count:(t + 1) * count].astype(bf16)
+        spans[name] = (offset, count)
+        offset += count
     ring.start(lambda to: zmsg.at[to], zgot, z_send, z_recv)
     zgot[z] = zmsg[z]
+    offset = 0
+    for side, sizes in ((0, fans), (1, cols)):
+        for index in range(2, 5):
+            spans[side, index] = (offset, sizes[index] // n_z)
+            offset += sizes[index] // n_z
 
     isums[...] = jnp.zeros_like(isums)
     quarter = grad_ref.shape[1]
@@ -1030,6 +1136,33 @@
     for index, peer in enumerate(column):
         dmod_copy(index, peer).start()
     dgot[core * n_z + z] = dmod_ref[z]
+
+    hot2, hot4 = hot2_ref[...], hot4_ref[...]
+    starts = []
+    offset = 0
+    for stream in range(2):
+        for index in range(5):
+            starts.append((stream, index, offset, offset + fans[index] // n_z))
+            offset += fans[index] // n_z + cols[index] // n_z
+
+    def put_a(at, part, hot):
+        dense[at:at + part.shape[1], :] = dots(part, hot, 0, 0)
+
+    def put_b(at, part, hot):
+        full = dots(hot, part, 0, 0)
+        blocks = part.shape[1] // 128
+        for j in range(blocks):
+            dense[pl.ds(at + j, 128, stride=blocks), :] = full[:, j * 128:(j + 1) * 128]
+
+    def put_image(index, ref):
+        for side, put in ((0, put_a), (1, put_b)):
+            begin, count = spans[side, index]
+            put(starts[index][2 + side], ref[:, :, begin:begin + count].reshape(hot4.shape[0], count), hot4)
+
+    for index in range(2, 5):
+        put_image(index, early_ref)
+        put_a(starts[5 + index][2], txt_a[index - 2][:hidden_rank, :].astype(bf16), hot2)
+        put_b(starts[5 + index][3], txt_b[index - 2][:hidden_rank, :].astype(bf16), hot2)
 
     for index, peer in enumerate(column):
         place = peer[0] % 2 * n_z + peer[1]
@@ -1059,40 +1192,15 @@
 
     spread_end(dt_ag)
     tga = t_mm(gathered(dt_ag, 0, thick), own_lanes(th_ref, cols[2] // n_z))
-    txt_a = [tga[:hidden_rank]] + [ref[:hidden_rank, :] for ref in txt_a]
-    txt_b = [tgb_ref[:hidden_rank, :]] + [ref[:hidden_rank, :] for ref in txt_b]
-    hot2 = hot2_ref[...]
-    starts = []
-    offset = 0
-    for stream in range(2):
-        for index in range(5):
-            starts.append((stream, index, offset, offset + fans[index] // n_z))
-            offset += fans[index] // n_z + cols[index] // n_z
-
-    def put_a(at, part, hot):
-        dense[at:at + part.shape[1], :] = dots(part, hot, 0, 0)
-
-    def put_b(at, part, hot):
-        full = dots(hot, part, 0, 0)
-        blocks = part.shape[1] // 128
-        for j in range(blocks):
-            dense[pl.ds(at + j, 128, stride=blocks), :] = full[:, j * 128:(j + 1) * 128]
-
     for stream, index, at_a, at_b in starts:
         if index == 0:
             dense[at_a:at_b, :] = jnp.zeros((at_b - at_a, 128), f32)
             put_b(at_b, gb_mod[stream].astype(bf16), hot2)
-        elif stream == 1:
-            put_a(at_a, txt_a[index - 1].astype(bf16), hot2)
-            put_b(at_b, txt_b[index - 1].astype(bf16), hot2)
-
+        elif index == 1 and stream == 1:
+            put_a(at_a, tga[:hidden_rank].astype(bf16), hot2)
+            put_b(at_b, tgb_ref[:hidden_rank, :].astype(bf16), hot2)
     ring.wait(zgot, z_send, z_recv)
-    hot4 = hot4_ref[...]
-    for stream, index, at_a, at_b in starts:
-        if stream == 0 and index > 0:
-            for at, put, (begin, count) in ((at_a, put_a, spans[index - 1]), (at_b, put_b, spans[index + 3])):
-                part = zgot[:, :, begin:begin + count].reshape(hot4.shape[0], count)
-                put(at, part, hot4)
+    put_image(1, zgot)
 
     for i in range(2):
         @pl.when(is_here(i))
@@ -1233,12 +1341,12 @@
             push(grad_ref.at[i], grad_out.at[z % 2], g_send.at[i], g_recv.at[z % 2], home[i]).wait_send()
 
 
-def tail(dq, tdq, wq, smalls, img_a, img_b, txt_a, txt_b, hot4, hot2, wmod, bmod, tmod, cond, smask, n_f, n_z, fans, cols, cid, tn=768):
+def tail(dq, tdq, wq, smalls, early, txt_a, txt_b, hot4, hot2, wmod, bmod, tmod, cond, smask, n_f, n_z, fans, cols, cid, tn=768):
     f32, bf16 = jnp.float32, jnp.bfloat16
     vmem, dma = pltpu.VMEM, pltpu.SemaphoreType.DMA
     shape = jax.ShapeDtypeStruct
-    args = (dq, tdq, wq, *smalls, *img_a, *img_b, *txt_a, *txt_b, hot4, hot2, wmod, bmod, tmod, cond, smask)
-    lanes = (sum(fans[1:]) + sum(cols[1:])) // n_z
+    args = (dq, tdq, wq, *smalls, early, *txt_a, *txt_b, hot4, hot2, wmod, bmod, tmod, cond, smask)
+    lanes = (fans[1] + cols[1]) // n_z
     rows = 2 * (sum(fans) + sum(cols)) // n_z
     blk = rows // n_f
     chips = n_f // 2
@@ -2389,7 +2497,8 @@
         txt_sides = [part[:rank_cols] for part in txt_sides]
     txt_sum_rows = txt_sums
     txt_sums = txt_sums.reshape(4, slots, width)
-    image_out = unshard(img_result)
+    if n_f != 8:
+        image_out = unshard(img_result)
 
     grads = [[None] * 5 for stream in range(2)]
 
@@ -2416,10 +2525,15 @@
         mod_parts[0][2 + place] = img_sums[place : place + 1]
     grad_after = [img_grad_after, txt_grad_after]
 
-    do_img = to_heads(img_grad_att)
-    d_img, d_txt = attend_back(img_heads, txt_heads, bias, do_img, do_txt, lse, HD)
+    do_img = img_grad_att.reshape(img_n, -1)
+    if n_f != 8:
+        d_img, d_txt = attend_back(img_heads, txt_heads, bias, do_img, do_txt, lse, HD)
     if n_f == 8:
         sides_of = lambda stream, side: [grads[stream][index][side] for index in range(2, 5)]
+        d_img, d_txt, image_out, early = attend_back_far(
+            img_heads, txt_heads, bias, do_img, do_txt, lse, HD, img_result.reshape(2, quarter, width),
+            sides_of(0, 0), sides_of(0, 1), n_z, fans, cols, 5,
+        )
         smalls = (
             x_img, img_grad_after, img_in, img_rows_mod, img_qkv_mid, *img_pairs[1], img_sum_rows, img_gate,
             x_txt_low, txt_grad_after, txt_in.reshape(n_z, txt_pad, width), txt_mod, sign(owner_group), sign(owner_local),
@@ -2427,7 +2541,7 @@
         )
         image_low, txt_grad, cond_slices, mod_rank, shard = tail(
             d_img.reshape(2, img_half, -1), d_txt, img_w[0].reshape(n_f, k_local, -1), smalls,
-            sides_of(0, 0), sides_of(0, 1), sides_of(1, 0), sides_of(1, 1),
+            early, sides_of(1, 0), sides_of(1, 1),
             hot_four, own_hot.T.astype(BF16), mod_weight, mod_b, tmod, cond_own, slot_mask,
             n_f, n_z, fans, cols, 3,
         )

time: 755 us -> 733 us (0.971)
  Pallas kernels: 703 us -> 693 us
    pallas_call x1, Pallas kernels: 121 us -> 110 us  [tail(): pl.pallas_call(functools.partial(tail_kernel, n_f, n_z, tuple(fans), tupl...]
  transfers between devices with their start and end apart: 3 -> 0, of which waited for: 0 -> 0; matrix products, arithmetic and copies ran while one was open for 1% -> 0% of each run, Pallas kernels for 25% -> 0%
where the time goes in v8:
time: 733 us; the launch traced here: 724 us
  Pallas kernels  693 us (95%)
  local copies, waits for them, and re-layouts  16.2 us (2%)
  other arithmetic  12.1 us (2%)
    pallas_call x1, Pallas kernels, front(): pl.pallas_call(functools.partial(front_kernel, n_f, n_z, tuple(fans), tup...  370 us
    pallas_call x1, Pallas kernels, tail(): pl.pallas_call(functools.partial(tail_kernel, n_f, n_z, tuple(fans), tupl...  110 us
    pallas_call x1, Pallas kernels, both_back(): pl.pallas_call(functools.partial(both_back_kernel, tiles, n_z, turns), gr...  83.5 us
    pallas_call x1, Pallas kernels, attend_back_far(): pl.pallas_call(functools.partial(attend_back_far_kernel, hd, bq, n_z, tup...  66.2 us
    pallas_call x1, Pallas kernels, both_fwd(): pl.pallas_call(functools.partial(both_fwd_kernel, tiles, n_z, turns), gri...  63.9 us

profile of v8, /device:TPU:11, one launch (start us, length us, event | category | flops | bytes accessed | tf_op | source)
XLA Modules:
  0.0 723.6 jit_solution(11625210129929857483)
XLA Ops:
  0.7 0.9 reduce-window.8
  1.6 0.1 fusion.12
  1.7 0.7 broadcast_multiply_fusion
  2.4 0.1 add.96
  2.5 0.1 pad.41.clone
  2.6 0.7 compare_convert_fusion.3
  3.3 0.1 reshape.190
  3.4 0.1 fusion.9
  3.6 0.1 reshape.170
  3.7 0.6 select_maximum_fusion.refs_16_.refs_37_
  4.3 0.7 convert_convert_fusion.refs_12_.refs_32_
  5.0 0.7 broadcast_in_dim.40.refs_11_
  5.6 0.7 fusion.8
  6.4 0.6 pad.31.refs_14_
  7.0 0.1 reshape.169
  7.1 0.1 convert_select_fusion.1
  7.2 0.7 slice_subtract_fusion.1.refs_20_.own_ref.refs_17_
  8.0 0.1 copy.30
  8.0 0.6 pad.36.lmask_ref.refs_18_
  8.6 0.7 maximum_maximum_fusion.refs_15_
  9.3 0.6 pad.30.refs_13_
  10.0 0.1 convert_select_fusion
  10.2 0.7 fusion.16
  10.9 0.1 copy.28
  11.0 0.7 pad.35.refs_21_.mask_ref
  11.7 0.7 broadcast_in_dim.74.refs_22_
  12.4 1.6 pad.33.refs_18_.xt_ref.refs_12_
  14.0 0.7 pad.34.refs_19_.gt_ref
  14.6 0.7 slice_bitcast_fusion.6
  15.4 0.9 convert_element_type.65.refs_8_
  16.3 1.0 slice_bitcast_fusion.4
  17.3 1.4 slice_bitcast_fusion
  18.7 369.8 %front.1 = (bf16[8,192,4608]{2,1,0:T(8,128)(2,1)}, bf16[8,192,1536]{2,1,0:T(8,128)(2,1)}, bf16[8,192,6144]{2,1,0:T(8,128)(2,1)}, bf16[8,192,6144]{2,1,0:T(8,128)...) custom-call(bf16[192,1152]{1,0:T(8,128)(2,1)} %get-tuple-element.183, ...), custom_call_target="tpu_custom_call" | custom-call | tf_op jit(solution)/shard_map/front/pallas_call | solution.py:2060
  388.5 63.9 %block_forward.1 = (bf16[512,1536]{1,0:T(8,128)(2,1)}, f32[512,1536]{1,0:T(8,128)}, bf16[512,1536]{1,0:T(8,128)(2,1)}, f32[512,6144]{1,0:T(8,128)}, bf16[512,153...) custom-call(bf16[512,1536]{1,0:T(8,128)(2,1)} %get-tuple-element.95., ...), custom_call_target="tpu_custom_call" | custom-call | tf_op jit(solution)/shard_map/block_forward/pallas_call | solution.py:896
  452.4 83.5 %block_backward.1 = (f32[512,1536]{1,0:T(8,128)}, bf16[2,512,768]{2,1,0:T(8,128)(2,1)}, f32[24,1536]{1,0:T(8,128)}, f32[16,6144]{1,0:T(8,128)}, f32[16,6144]{1,0...) custom-call(bf16[512,1536]{1,0:T(8,128)(2,1)} %bitcast.60, ...), custom_call_target="tpu_custom_call" | custom-call | tf_op jit(solution)/shard_map/block_backward/pallas_call | solution.py:937
  535.9 66.2 %attend_back.1 = (bf16[1024,2304]{1,0:T(8,128)(2,1)}, bf16[2,192,1152]{2,1,0:T(8,128)(2,1)}, bf16[2,256,1536]{2,1,0:T(8,128)(2,1)}, bf16[4,16,4608]{2,1,0:T(8,128)(2,1)}) custom-call(bf16[1024,2304]{1,0:T(8,128)(2,1)} %bitcast.64, bf16[2,192,1152]{2,1,0:T(8,128)(2,1)} %get-tuple-element.92.txt_ref, f32[192,1]{1,0:T(8,128)} %bitcast.75, ...), custom_call_target="tpu_custom_call" | custom-call | tf_op jit(solution)/shard_map/attend_back/pallas_call | solution.py:439
  602.1 110.0 %gradient_exchange.1 = (bf16[2,256,1536]{2,1,0:T(8,128)(2,1)}, f32[48,1536]{1,0:T(8,128)}, f32[8,8,256]{2,1,0:T(8,128)}, f32[8,32]{1,0:T(8,128)}, f32[2208,128]{1,0:T(8,128)}) custom-call(bf16[2,512,2304]{2,1,0:T(8,128)(2,1)} %bitcast.63, bf16[2,192,1152]{2,1,0:T(8,128)(2,1)} %get-tuple-element.143.refs_1_, ...), custom_call_target="tpu_custom_call" | custom-call | tf_op jit(solution)/shard_map/gradient_exchange/pallas_call | solution.py:1363
  712.2 0.7 convert.5
  712.9 0.8 slice_bitcast_fusion.8
  713.7 0.1 reshape.188
  713.8 0.1 convolution_add_fusion.1
  713.9 0.7 fusion.5
  714.7 0.7 slice.85
  715.3 1.7 slice.86
  717.0 3.6 convert_element_type.77
  720.6 1.1 copy.36
  721.7 0.7 copy-done.4
  722.4 1.0 copy.37
  (36 shorter events, 0.4 us)
Async XLA Ops:
  0.6 13.3 %copy-start.7 = (bf16[40,1536]{1,0:T(8,128)(2,1)S(1)}, bf16[40,1536]{1,0:T(8,128)(2,1)}, u32[]{:S(2)}) copy-start(bf16[40,1536]{1,0:T(8,128)(2,1)} %param.25) | copy-start | bytes 368644
  0.6 14.0 %copy-start.6 = (bf16[2,384,192]{1,2,0:T(8,128)(2,1)S(1)}, bf16[2,384,192]{1,2,0:T(8,128)(2,1)}, u32[]{:S(2)}) copy-start(bf16[2,384,192]{1,2,0:T(8,128)(2,1)} %param.21) | copy-start | bytes 884740
  0.7 14.7 %copy-start.3 = (f32[1,282624]{1,0:T(1,128)S(1)}, f32[1,282624]{1,0:T(1,128)}, u32[]{:S(2)}) copy-start(f32[1,282624]{1,0:T(1,128)} %param.18) | copy-start | bytes 3391492
  11.0 5.2 copy-start.5
  15.4 1.9 copy-start.1
  15.4 1.9 copy-start.2
  602.1 111.7 %copy-start.9 = (bf16[2,32,1536]{2,1,0:T(8,128)(2,1)S(1)}, bf16[2,32,1536]{2,1,0:T(8,128)(2,1)}, u32[]{:S(2)}) copy-start(bf16[2,32,1536]{2,1,0:T(8,128)(2,1)} %get-tuple-element.174) | copy-start | bytes 589828
  602.1 111.8 %copy-start.10 = (f32[2,1536]{1,0:T(2,128)S(1)}, f32[2,1536]{1,0:T(2,128)}, u32[]{:S(2)}) copy-start(f32[2,1536]{1,0:T(2,128)} %param.15) | copy-start | bytes 36868
  602.1 112.5 %copy-start.8 = (bf16[48,1536]{1,0:T(8,128)(2,1)S(1)}, bf16[48,1536]{1,0:T(8,128)(2,1)}, u32[]{:S(2)}) copy-start(bf16[48,1536]{1,0:T(8,128)(2,1)} %get-tuple-element.141) | copy-start | bytes 442372
  717.0 3.6 copy-start
  720.6 1.8 copy-start.4

commit v9 on v8

--- a/solution.py
+++ b/solution.py
@@ -1428,7 +1428,10 @@
     def cuts(m):
         if m == adapters:
             return [(0, (0, blk // 2)), (1, (blk // 2, blk // 2))]
-        return list(enumerate(halves(wide_of(m))))
+        parts = halves(wide_of(m))
+        if m % FULL == 1:
+            parts = [(0, parts[1][1]), (parts[1][1], parts[0][1])]
+        return list(enumerate(parts))
 
     def place(m, who, zz, cut):
         off, w = cut
@@ -1646,15 +1649,17 @@
 
     forward(adapters, z)
     forward(FULL, z)
+    for k in range(1, n_z):
+        arrive(0, k)
+    forward(0, z)
     for m in (1, 2, 3):
         launch_own(m)
     for m in (FULL + 1, FULL + 2, FULL + 3):
         launch_own(m)
-    for k in range(1, n_z):
-        arrive(0, k)
+    at_distance(1, lambda zz: forward(0, zz))
     for m in (1, 2, 3):
         arrive(m, 1)
-    for k in range(n_z):
+    for k in range(2, n_z):
         at_distance(k, lambda zz: forward(0, zz))
 
     finish(adapters, z)
@@ -1821,8 +1826,6 @@
         lax.fori_loop(0, quarter // ROWS, norm, 0)
     tokens_start(g_ref, g_out, g_send, g_recv)
 
-    for m in (1, 2, 3):
-        at_distance(1, lambda zz: forward(m, zz))
 
     finish(FULL, z)
     settle(FULL, z)
@@ -1879,6 +1882,9 @@
             heads_push().start()
     keep = pltpu.make_async_copy(stage.at[1], heads_out.at[core], h_sem)
     keep.start()
+
+    for m in (1, 2, 3):
+        at_distance(1, lambda zz: forward(m, zz))
 
     sign_push.wait_recv()
     chip_sign = jnp.where(z // 2 == core, sign_ref[...], sign_got[...])
@@ -1950,13 +1956,13 @@
         o_push(i).start()
         return 0
 
+    for m in (1, 2, 3):
+        at_distance(2, lambda zz: forward(m, zz))
     lax.fori_loop(0, pairs // 2, pair_step, 0)
     for m in (1, 2, 3):
-        at_distance(2, lambda zz: forward(m, zz))
+        at_distance(n_z - 1, lambda zz: forward(m, zz))
     lax.fori_loop(pairs // 2, pairs, pair_step, 0)
 
-    for m in (1, 2, 3):
-        at_distance(n_z - 1, lambda zz: forward(m, zz))
     for m in range(total - 1):
         if m not in (0, FULL):
             every_z(m, finish)

time: 733 us -> 709 us (0.967)
  Pallas kernels: 693 us -> 669 us
    pallas_call x1, Pallas kernels: 370 us -> 345 us  [front(): pl.pallas_call(functools.partial(front_kernel, n_f, n_z, tuple(fans), tup...]
where the time goes in v9:
time: 709 us; the launch traced here: 699 us
  Pallas kernels  669 us (94%)
  local copies, waits for them, and re-layouts  16.2 us (2%)
  other arithmetic  12.1 us (2%)
    pallas_call x1, Pallas kernels, front(): pl.pallas_call(functools.partial(front_kernel, n_f, n_z, tuple(fans), tup...  345 us
    pallas_call x1, Pallas kernels, tail(): pl.pallas_call(functools.partial(tail_kernel, n_f, n_z, tuple(fans), tupl...  110 us
    pallas_call x1, Pallas kernels, both_back(): pl.pallas_call(functools.partial(both_back_kernel, tiles, n_z, turns), gr...  83.7 us
    pallas_call x1, Pallas kernels, attend_back_far(): pl.pallas_call(functools.partial(attend_back_far_kernel, hd, bq, n_z, tup...  66.2 us
    pallas_call x1, Pallas kernels, both_fwd(): pl.pallas_call(functools.partial(both_fwd_kernel, tiles, n_z, turns), gri...  64 us

profile of v9, /device:TPU:11, one launch (start us, length us, event | category | flops | bytes accessed | tf_op | source)
XLA Modules:
  0.0 698.9 jit_solution(16979611989453476307)
XLA Ops:
  0.7 0.9 reduce-window.8
  1.6 0.1 fusion.12
  1.7 0.7 broadcast_multiply_fusion
  2.4 0.1 add.96
  2.5 0.1 pad.41.clone
  2.6 0.7 compare_convert_fusion.3
  3.3 0.1 reshape.190
  3.4 0.1 fusion.9
  3.6 0.1 reshape.170
  3.7 0.6 select_maximum_fusion.refs_16_.refs_37_
  4.3 0.7 convert_convert_fusion.refs_12_.refs_32_
  5.0 0.7 broadcast_in_dim.40.refs_11_
  5.6 0.7 fusion.8
  6.4 0.6 pad.31.refs_14_
  7.0 0.1 reshape.169
  7.1 0.1 convert_select_fusion.1
  7.2 0.7 slice_subtract_fusion.1.refs_20_.own_ref.refs_17_
  8.0 0.1 copy.30
  8.0 0.6 pad.36.lmask_ref.refs_18_
  8.6 0.7 maximum_maximum_fusion.refs_15_
  9.3 0.6 pad.30.refs_13_
  10.0 0.1 convert_select_fusion
  10.2 0.7 fusion.16
  10.9 0.1 copy.28
  11.0 0.7 pad.35.refs_21_.mask_ref
  11.7 0.7 broadcast_in_dim.74.refs_22_
  12.4 1.6 pad.33.refs_18_.xt_ref.refs_12_
  14.0 0.7 pad.34.refs_19_.gt_ref
  14.6 0.7 slice_bitcast_fusion.6
  15.4 0.9 convert_element_type.65.refs_8_
  16.3 1.0 slice_bitcast_fusion.4
  17.3 1.4 slice_bitcast_fusion
  18.7 344.9 %front.1 = (bf16[8,192,4608]{2,1,0:T(8,128)(2,1)}, bf16[8,192,1536]{2,1,0:T(8,128)(2,1)}, bf16[8,192,6144]{2,1,0:T(8,128)(2,1)}, bf16[8,192,6144]{2,1,0:T(8,128)...) custom-call(bf16[192,1152]{1,0:T(8,128)(2,1)} %get-tuple-element.183, ...), custom_call_target="tpu_custom_call" | custom-call | tf_op jit(solution)/shard_map/front/pallas_call | solution.py:2066
  363.6 64.0 %block_forward.1 = (bf16[512,1536]{1,0:T(8,128)(2,1)}, f32[512,1536]{1,0:T(8,128)}, bf16[512,1536]{1,0:T(8,128)(2,1)}, f32[512,6144]{1,0:T(8,128)}, bf16[512,153...) custom-call(bf16[512,1536]{1,0:T(8,128)(2,1)} %get-tuple-element.95., ...), custom_call_target="tpu_custom_call" | custom-call | tf_op jit(solution)/shard_map/block_forward/pallas_call | solution.py:896
  427.7 83.7 %block_backward.1 = (f32[512,1536]{1,0:T(8,128)}, bf16[2,512,768]{2,1,0:T(8,128)(2,1)}, f32[24,1536]{1,0:T(8,128)}, f32[16,6144]{1,0:T(8,128)}, f32[16,6144]{1,0...) custom-call(bf16[512,1536]{1,0:T(8,128)(2,1)} %bitcast.60, ...), custom_call_target="tpu_custom_call" | custom-call | tf_op jit(solution)/shard_map/block_backward/pallas_call | solution.py:937
  511.4 66.2 %attend_back.1 = (bf16[1024,2304]{1,0:T(8,128)(2,1)}, bf16[2,192,1152]{2,1,0:T(8,128)(2,1)}, bf16[2,256,1536]{2,1,0:T(8,128)(2,1)}, bf16[4,16,4608]{2,1,0:T(8,128)(2,1)}) custom-call(bf16[1024,2304]{1,0:T(8,128)(2,1)} %bitcast.64, bf16[2,192,1152]{2,1,0:T(8,128)(2,1)} %get-tuple-element.92.txt_ref, f32[192,1]{1,0:T(8,128)} %bitcast.75, ...), custom_call_target="tpu_custom_call" | custom-call | tf_op jit(solution)/shard_map/attend_back/pallas_call | solution.py:439
  577.6 110.0 %gradient_exchange.1 = (bf16[2,256,1536]{2,1,0:T(8,128)(2,1)}, f32[48,1536]{1,0:T(8,128)}, f32[8,8,256]{2,1,0:T(8,128)}, f32[8,32]{1,0:T(8,128)}, f32[2208,128]{1,0:T(8,128)}) custom-call(bf16[2,512,2304]{2,1,0:T(8,128)(2,1)} %bitcast.63, bf16[2,192,1152]{2,1,0:T(8,128)(2,1)} %get-tuple-element.143.refs_1_, ...), custom_call_target="tpu_custom_call" | custom-call | tf_op jit(solution)/shard_map/gradient_exchange/pallas_call | solution.py:1363
  687.5 0.7 convert.5
  688.2 0.8 slice_bitcast_fusion.8
  689.1 0.1 reshape.188
  689.1 0.1 convolution_add_fusion.1
  689.3 0.7 fusion.5
  690.0 0.7 slice.85
  690.7 1.7 slice.86
  692.3 3.6 convert_element_type.77
  695.9 1.1 copy.36
  697.1 0.7 copy-done.4
  697.7 1.0 copy.37
  (36 shorter events, 0.4 us)
Async XLA Ops:
  0.6 13.3 %copy-start.7 = (bf16[40,1536]{1,0:T(8,128)(2,1)S(1)}, bf16[40,1536]{1,0:T(8,128)(2,1)}, u32[]{:S(2)}) copy-start(bf16[40,1536]{1,0:T(8,128)(2,1)} %param.25) | copy-start | bytes 368644
  0.6 14.0 %copy-start.6 = (bf16[2,384,192]{1,2,0:T(8,128)(2,1)S(1)}, bf16[2,384,192]{1,2,0:T(8,128)(2,1)}, u32[]{:S(2)}) copy-start(bf16[2,384,192]{1,2,0:T(8,128)(2,1)} %param.21) | copy-start | bytes 884740
  0.7 14.7 %copy-start.3 = (f32[1,282624]{1,0:T(1,128)S(1)}, f32[1,282624]{1,0:T(1,128)}, u32[]{:S(2)}) copy-start(f32[1,282624]{1,0:T(1,128)} %param.18) | copy-start | bytes 3391492
  11.0 5.2 copy-start.5
  15.4 1.9 copy-start.1
  15.4 1.9 copy-start.2
  577.5 111.6 %copy-start.9 = (bf16[2,32,1536]{2,1,0:T(8,128)(2,1)S(1)}, bf16[2,32,1536]{2,1,0:T(8,128)(2,1)}, u32[]{:S(2)}) copy-start(bf16[2,32,1536]{2,1,0:T(8,128)(2,1)} %get-tuple-element.174) | copy-start | bytes 589828
  577.5 111.7 %copy-start.10 = (f32[2,1536]{1,0:T(2,128)S(1)}, f32[2,1536]{1,0:T(2,128)}, u32[]{:S(2)}) copy-start(f32[2,1536]{1,0:T(2,128)} %param.15) | copy-start | bytes 36868
  577.5 112.5 %copy-start.8 = (bf16[48,1536]{1,0:T(8,128)(2,1)S(1)}, bf16[48,1536]{1,0:T(8,128)(2,1)}, u32[]{:S(2)}) copy-start(bf16[48,1536]{1,0:T(8,128)(2,1)} %get-tuple-element.141) | copy-start | bytes 442372
  692.3 3.6 copy-start
  695.9 1.8 copy-start.4

commit v10 on v9

--- a/solution.py
+++ b/solution.py
@@ -1652,9 +1652,9 @@
     for k in range(1, n_z):
         arrive(0, k)
     forward(0, z)
+    for m in (FULL + 1, FULL + 2, FULL + 3):
+        launch_own(m)
     for m in (1, 2, 3):
-        launch_own(m)
-    for m in (FULL + 1, FULL + 2, FULL + 3):
         launch_own(m)
     at_distance(1, lambda zz: forward(0, zz))
     for m in (1, 2, 3):

time: 709 us -> 709 us (level)
  no operation moved by 1% of the time
where the time goes in v10:
time: 709 us; the launch traced here: 699 us
  Pallas kernels  669 us (94%)
  local copies, waits for them, and re-layouts  16.2 us (2%)
  other arithmetic  12.1 us (2%)
    pallas_call x1, Pallas kernels, front(): pl.pallas_call(functools.partial(front_kernel, n_f, n_z, tuple(fans), tup...  345 us
    pallas_call x1, Pallas kernels, tail(): pl.pallas_call(functools.partial(tail_kernel, n_f, n_z, tuple(fans), tupl...  110 us
    pallas_call x1, Pallas kernels, both_back(): pl.pallas_call(functools.partial(both_back_kernel, tiles, n_z, turns), gr...  83.7 us
    pallas_call x1, Pallas kernels, attend_back_far(): pl.pallas_call(functools.partial(attend_back_far_kernel, hd, bq, n_z, tup...  66.2 us
    pallas_call x1, Pallas kernels, both_fwd(): pl.pallas_call(functools.partial(both_fwd_kernel, tiles, n_z, turns), gri...  64 us

profile of v10, /device:TPU:11, one launch (start us, length us, event | category | flops | bytes accessed | tf_op | source)
XLA Modules:
  0.0 698.9 jit_solution(17366636902494132740)
XLA Ops:
  0.7 0.9 reduce-window.8
  1.6 0.1 fusion.12
  1.7 0.7 broadcast_multiply_fusion
  2.4 0.1 add.96
  2.5 0.1 pad.41.clone
  2.6 0.7 compare_convert_fusion.3
  3.3 0.1 reshape.190
  3.4 0.1 fusion.9
  3.6 0.1 reshape.170
  3.7 0.6 select_maximum_fusion.refs_16_.refs_37_
  4.3 0.7 convert_convert_fusion.refs_12_.refs_32_
  5.0 0.7 broadcast_in_dim.40.refs_11_
  5.6 0.7 fusion.8
  6.4 0.6 pad.31.refs_14_
  7.0 0.1 reshape.169
  7.1 0.1 convert_select_fusion.1
  7.2 0.7 slice_subtract_fusion.1.refs_20_.own_ref.refs_17_
  8.0 0.1 copy.30
  8.0 0.6 pad.36.lmask_ref.refs_18_
  8.6 0.7 maximum_maximum_fusion.refs_15_
  9.3 0.6 pad.30.refs_13_
  10.0 0.1 convert_select_fusion
  10.2 0.7 fusion.16
  10.9 0.1 copy.28
  11.0 0.7 pad.35.refs_21_.mask_ref
  11.7 0.7 broadcast_in_dim.74.refs_22_
  12.4 1.6 pad.33.refs_18_.xt_ref.refs_12_
  14.0 0.7 pad.34.refs_19_.gt_ref
  14.6 0.7 slice_bitcast_fusion.6
  15.4 0.9 convert_element_type.65.refs_8_
  16.3 1.0 slice_bitcast_fusion.4
  17.3 1.4 slice_bitcast_fusion
  18.7 344.9 %front.1 = (bf16[8,192,4608]{2,1,0:T(8,128)(2,1)}, bf16[8,192,1536]{2,1,0:T(8,128)(2,1)}, bf16[8,192,6144]{2,1,0:T(8,128)(2,1)}, bf16[8,192,6144]{2,1,0:T(8,128)...) custom-call(bf16[192,1152]{1,0:T(8,128)(2,1)} %get-tuple-element.183, ...), custom_call_target="tpu_custom_call" | custom-call | tf_op jit(solution)/shard_map/front/pallas_call | solution.py:2066
  363.6 64.0 %block_forward.1 = (bf16[512,1536]{1,0:T(8,128)(2,1)}, f32[512,1536]{1,0:T(8,128)}, bf16[512,1536]{1,0:T(8,128)(2,1)}, f32[512,6144]{1,0:T(8,128)}, bf16[512,153...) custom-call(bf16[512,1536]{1,0:T(8,128)(2,1)} %get-tuple-element.95., ...), custom_call_target="tpu_custom_call" | custom-call | tf_op jit(solution)/shard_map/block_forward/pallas_call | solution.py:896
  427.7 83.7 %block_backward.1 = (f32[512,1536]{1,0:T(8,128)}, bf16[2,512,768]{2,1,0:T(8,128)(2,1)}, f32[24,1536]{1,0:T(8,128)}, f32[16,6144]{1,0:T(8,128)}, f32[16,6144]{1,0...) custom-call(bf16[512,1536]{1,0:T(8,128)(2,1)} %bitcast.60, ...), custom_call_target="tpu_custom_call" | custom-call | tf_op jit(solution)/shard_map/block_backward/pallas_call | solution.py:937
  511.4 66.2 %attend_back.1 = (bf16[1024,2304]{1,0:T(8,128)(2,1)}, bf16[2,192,1152]{2,1,0:T(8,128)(2,1)}, bf16[2,256,1536]{2,1,0:T(8,128)(2,1)}, bf16[4,16,4608]{2,1,0:T(8,128)(2,1)}) custom-call(bf16[1024,2304]{1,0:T(8,128)(2,1)} %bitcast.64, bf16[2,192,1152]{2,1,0:T(8,128)(2,1)} %get-tuple-element.92.txt_ref, f32[192,1]{1,0:T(8,128)} %bitcast.75, ...), custom_call_target="tpu_custom_call" | custom-call | tf_op jit(solution)/shard_map/attend_back/pallas_call | solution.py:439
  577.6 110.0 %gradient_exchange.1 = (bf16[2,256,1536]{2,1,0:T(8,128)(2,1)}, f32[48,1536]{1,0:T(8,128)}, f32[8,8,256]{2,1,0:T(8,128)}, f32[8,32]{1,0:T(8,128)}, f32[2208,128]{1,0:T(8,128)}) custom-call(bf16[2,512,2304]{2,1,0:T(8,128)(2,1)} %bitcast.63, bf16[2,192,1152]{2,1,0:T(8,128)(2,1)} %get-tuple-element.143.refs_1_, ...), custom_call_target="tpu_custom_call" | custom-call | tf_op jit(solution)/shard_map/gradient_exchange/pallas_call | solution.py:1363
  687.5 0.7 convert.5
  688.2 0.8 slice_bitcast_fusion.8
  689.1 0.1 reshape.188
  689.1 0.1 convolution_add_fusion.1
  689.3 0.7 fusion.5
  690.0 0.7 slice.85
  690.7 1.7 slice.86
  692.3 3.6 convert_element_type.77
  695.9 1.1 copy.36
  697.1 0.7 copy-done.4
  697.7 1.0 copy.37
  (36 shorter events, 0.4 us)
Async XLA Ops:
  0.6 13.3 %copy-start.7 = (bf16[40,1536]{1,0:T(8,128)(2,1)S(1)}, bf16[40,1536]{1,0:T(8,128)(2,1)}, u32[]{:S(2)}) copy-start(bf16[40,1536]{1,0:T(8,128)(2,1)} %param.25) | copy-start | bytes 368644
  0.6 14.0 %copy-start.6 = (bf16[2,384,192]{1,2,0:T(8,128)(2,1)S(1)}, bf16[2,384,192]{1,2,0:T(8,128)(2,1)}, u32[]{:S(2)}) copy-start(bf16[2,384,192]{1,2,0:T(8,128)(2,1)} %param.21) | copy-start | bytes 884740
  0.7 14.7 %copy-start.3 = (f32[1,282624]{1,0:T(1,128)S(1)}, f32[1,282624]{1,0:T(1,128)}, u32[]{:S(2)}) copy-start(f32[1,282624]{1,0:T(1,128)} %param.18) | copy-start | bytes 3391492
  11.0 5.2 copy-start.5
  15.4 1.9 copy-start.1
  15.4 1.9 copy-start.2
  577.5 111.6 %copy-start.9 = (bf16[2,32,1536]{2,1,0:T(8,128)(2,1)S(1)}, bf16[2,32,1536]{2,1,0:T(8,128)(2,1)}, u32[]{:S(2)}) copy-start(bf16[2,32,1536]{2,1,0:T(8,128)(2,1)} %get-tuple-element.174) | copy-start | bytes 589828
  577.5 111.7 %copy-start.10 = (f32[2,1536]{1,0:T(2,128)S(1)}, f32[2,1536]{1,0:T(2,128)}, u32[]{:S(2)}) copy-start(f32[2,1536]{1,0:T(2,128)} %param.15) | copy-start | bytes 36868
  577.5 112.5 %copy-start.8 = (bf16[48,1536]{1,0:T(8,128)(2,1)S(1)}, bf16[48,1536]{1,0:T(8,128)(2,1)}, u32[]{:S(2)}) copy-start(bf16[48,1536]{1,0:T(8,128)(2,1)} %get-tuple-element.141) | copy-start | bytes 442372
  692.3 3.6 copy-start
  695.9 1.8 copy-start.4
